TPU v7x, 32 devices: a whole 2x2x4 slice. The times are simulated.
32 devices in a mesh: lat: 4 (over x, core), lon: 8 (over z, y).
Axes of the slice: x: 2, y: 2, z: 4, core: 2. Of those that a mesh axis runs over, the one named last changes fastest.
Arguments:
- spectra: bfloat16 [16384, 616], P(('lat', 'lon')), may hold values from -6 to 6
- owner: int32 [16384, 1], P(('lat', 'lon')), may hold values from 0 to 31; in each aligned block of 512 rows (0 to 511, 512 to 1023, ...) at most 32 rows name the same one
- cell: int32 [16384], P(('lat', 'lon')), may hold values from 0 to 2047
- w_in: bfloat16 [616, 512], replicated, may hold values from -0.25 to 0.25
- w_out: bfloat16 [512, 512], replicated, may hold values from -0.25 to 0.25
- w_point: bfloat16 [512, 512], replicated, may hold values from -0.25 to 0.25
- w_depth: float32 [9, 512], replicated, may hold values from -2 to 2
- cotangent: bfloat16 [64, 1024, 512], P('lat', 'lon'), may hold values from -6 to 6
Outputs:
- latent: bfloat16 [64, 1024, 512], P('lat', 'lon')
- grad_in: float32 [616, 512], replicated
- grad_out: float32 [512, 512], replicated
- grad_point: float32 [512, 512], replicated
- grad_depth: float32 [9, 512], replicated
Inputs may be any that keep to these rules, and one draw needn't show every extreme that they name: `owner`: among the 512 rows of one device at most 32 name the same tile, a bound that some block reaches.
All inputs are finite; a program needn't handle non-finite values.
Results may differ from a plain program's by a relative error of at most 0.007.
Values may be sent and summed in bfloat16 or wider, within the bound.
No kernel may reach another device: no remote copies, remote signals or barrier semaphores. Data moves between devices by JAX's collectives and lax.ppermute only.
A program may use at most 64 MiB of HBM per device.

v0:
```python
import jax
import jax.numpy as jnp
from jax import lax
from jax.sharding import PartitionSpec as P

offsets = [(a, b) for a in (-1, 0, 1) for b in (-1, 0, 1)]


def extended(block, sides, width, periodic):
    for axis, dim in sides:
        count = lax.axis_size(axis)
        forward = [(i, i + 1) for i in range(count - 1)]
        if periodic:
            forward.append((count - 1, 0))
        backward = [(target, source) for source, target in forward]
        low = lax.ppermute(
            lax.slice_in_dim(block, block.shape[dim] - width, None, axis=dim), axis, forward
        )
        high = lax.ppermute(lax.slice_in_dim(block, 0, width, axis=dim), axis, backward)
        block = jnp.concatenate([low, block, high], axis=dim)
    return block


def send_out(values, places, tiles, cap):
    width = values.shape[1]
    moved, arrived = (
        lax.all_to_all(
            values.reshape(tiles, cap, width),
            ("lat", "lon"),
            split_axis=0,
            concat_axis=0,
            tiled=True,
        ),
        lax.all_to_all(
            places.reshape(tiles, cap), ("lat", "lon"), split_axis=0, concat_axis=0, tiled=True
        ),
    )
    return (moved.reshape(tiles * cap, width), arrived.reshape(tiles * cap))


def send_back(values, tiles, cap):
    width = values.shape[1]
    moved = lax.all_to_all(
        values.reshape(tiles, cap, width), ("lat", "lon"), split_axis=0, concat_axis=0, tiled=True
    )
    return moved.reshape(tiles * cap, width)


def extend(field):
    wide = extended(field, (("lon", 1),), 1, True)
    return extended(wide, (("lat", 0),), 1, False)


def encode(features, w_in, w_out):
    preact = jnp.dot(features, w_in, preferred_element_type=jnp.float32)
    hidden = jax.nn.silu(preact).astype(jnp.bfloat16)
    embedded = jnp.dot(hidden, w_out, preferred_element_type=jnp.float32).astype(jnp.bfloat16)
    return (preact, hidden, embedded)


def on_device(spectra, owner, cell, w_in, w_out, w_point, w_depth, cotangent):
    tiles = lax.axis_size("lat") * lax.axis_size("lon")
    rows_here = spectra.shape[0]
    cap = max(2, 2 * rows_here // tiles)
    clat, clon, width = cotangent.shape
    cells = clat * clon
    target = owner[:, 0]
    hits = (target[:, None] == jnp.arange(tiles, dtype=jnp.int32)[None, :]).astype(jnp.int32)
    position = jnp.sum(jnp.cumsum(hits, axis=0) * hits, axis=1) - 1
    slot_index = target * cap + position
    cells_sent = jnp.full((tiles * cap,), -1, jnp.int32).at[slot_index].set(cell)
    preact, hidden, embedded = encode(spectra, w_in, w_out)
    outgoing = jnp.zeros((tiles * cap, width), jnp.bfloat16).at[slot_index].set(embedded)
    arrived, places = send_out(outgoing, cells_sent, tiles, cap)
    one_hot = (places[None, :] == jnp.arange(cells, dtype=jnp.int32)[:, None]).astype(jnp.bfloat16)
    grid_rows = jnp.dot(one_hot, arrived, preferred_element_type=jnp.float32).astype(jnp.bfloat16)
    grid = grid_rows.reshape(clat, clon, width)
    padded = extend(grid).astype(jnp.float32)
    mixed = jnp.zeros((clat, clon, width), jnp.float32)
    for k, (a, b) in enumerate(offsets):
        mixed = mixed + w_depth[k] * padded[1 + a : 1 + a + clat, 1 + b : 1 + b + clon]
    mixed = mixed.astype(jnp.bfloat16)
    mixed_rows = mixed.reshape(cells, width)
    latent = grid_rows.astype(jnp.float32) + jnp.dot(
        mixed_rows, w_point, preferred_element_type=jnp.float32
    )
    latent = latent.astype(jnp.bfloat16).reshape(clat, clon, width)
    cot_rows = cotangent.reshape(cells, width)
    grad_point = lax.dot_general(
        mixed_rows, cot_rows, (((0,), (0,)), ((), ())), preferred_element_type=jnp.float32
    )
    g_mixed = (
        jnp.dot(cot_rows, w_point.T, preferred_element_type=jnp.float32)
        .astype(jnp.bfloat16)
        .reshape(clat, clon, width)
    )
    g_mixed_f = g_mixed.astype(jnp.float32)
    grad_depth = jnp.stack(
        [
            jnp.sum(g_mixed_f * padded[1 + a : 1 + a + clat, 1 + b : 1 + b + clon], axis=(0, 1))
            for a, b in offsets
        ]
    )
    padded_g = extend(g_mixed).astype(jnp.float32)
    g_grid = cotangent.astype(jnp.float32)
    for k, (a, b) in enumerate(offsets):
        g_grid = g_grid + w_depth[k] * padded_g[1 - a : 1 - a + clat, 1 - b : 1 - b + clon]
    g_grid = g_grid.astype(jnp.bfloat16).reshape(cells, width)
    g_arrived = lax.dot_general(
        one_hot, g_grid, (((0,), (0,)), ((), ())), preferred_element_type=jnp.float32
    ).astype(jnp.bfloat16)
    returned = send_back(g_arrived, tiles, cap)
    g_embedded = returned[slot_index]
    grad_out = lax.dot_general(
        hidden, g_embedded, (((0,), (0,)), ((), ())), preferred_element_type=jnp.float32
    )
    g_hidden = jnp.dot(g_embedded, w_out.T, preferred_element_type=jnp.float32)
    sigmoid_pre = jax.nn.sigmoid(preact)
    g_preact = (g_hidden * sigmoid_pre * (1.0 + preact * (1.0 - sigmoid_pre))).astype(jnp.bfloat16)
    grad_in = lax.dot_general(
        spectra, g_preact, (((0,), (0,)), ((), ())), preferred_element_type=jnp.float32
    )
    grad_in, grad_out, grad_point, grad_depth = lax.psum(
        (grad_in, grad_out, grad_point, grad_depth), ("lat", "lon")
    )
    obs_scale = 1.0 / jnp.sqrt(jnp.float32(rows_here * tiles))
    cell_scale = 1.0 / jnp.sqrt(jnp.float32(cells * tiles))
    return (
        latent,
        grad_in * obs_scale,
        grad_out * obs_scale,
        grad_point * cell_scale,
        grad_depth * cell_scale,
    )


def solution(mesh):
    in_specs = (
        P(("lat", "lon"), None),
        P(("lat", "lon"), None),
        P(("lat", "lon")),
        P(),
        P(),
        P(),
        P(),
        P("lat", "lon", None),
    )
    out_specs = (P("lat", "lon", None), P(), P(), P(), P())
    return jax.shard_map(
        on_device, mesh=mesh, in_specs=in_specs, out_specs=out_specs, check_vma=False
    )
```

profile of v0, /device:TPU:0, one launch (start us, length us, event | category | flops | bytes accessed | tf_op | source)
XLA Modules:
  0.0 306.6 jit_solution(5156814113194592299)
XLA Ops:
  7.2 0.0 copy-start
  7.2 0.8 fusion.35
  7.9 1.2 reduce-window.6
  9.1 0.2 slice_reduce_fusion
  9.4 0.8 fusion.34
  10.2 0.7 compare_select_fusion
  10.8 2.6 scatter_custom_fusion
  13.5 0.7 all_to_all.12
  14.1 7.3 %all-to-all-start = ((s32[32,1,32]{2,1,0:T(1,128)}), s32[32,1,32]{2,1,0:T(1,128)S(1)}, u32[]{:S(2)}, u32[]{:S(2)}) async-start(s32[32,1,32]{2,1,0:T(1,128)} %all_to_all.12), calls=%async_computation | async-start | bytes 32768 | tf_op jit(solution)/shard_map/all_to_all | solution.py:34
  21.5 1.7 fusion.43
  23.1 0.0 copy-start.6
  23.2 1.9 convolution_convert_fusion.1
  25.0 3.5 %scatter_custom_fusion.1 = bf16[1024,512]{1,0:T(8,128)(2,1)} fusion(s32[512]{0:T(512)S(1)} %bitcast.109, bf16[512,512]{1,0:T(8,128)(2,1)S(1)} %convolution_convert_fusion.1, bf16[]{:T(256)} %constant.13.clone.1), kind=kCustom, calls=%fused_computation.67 | custom fusion | bytes 1048578 | tf_op jit(solution)/shard_map/scatter | solution.py:73
  28.5 0.0 all-to-all-done
  28.5 5.8 %all-to-all-start.1 = ((bf16[32,32,512]{2,1,0:T(8,128)(2,1)}), bf16[32,32,512]{2,1,0:T(8,128)(2,1)S(1)}, u32[]{:S(2)}, u32[]{:S(2)}) async-start(bf16[32,32,512]{2,1,0:T(8,128)(2,1)} %bitcast.5), calls=%async_computation.1 | async-start | bytes 2097152 | tf_op jit(solution)/shard_map/all_to_all | solution.py:27
  34.4 0.5 broadcast.56
  34.9 0.7 reduce.5
  35.6 0.1 eq.48
  35.6 26.3 %all-to-all-done.1 = bf16[32,32,512]{2,1,0:T(8,128)(2,1)S(1)} async-done(((bf16[32,32,512]{2,1,0:T(8,128)(2,1)}), bf16[32,32,512]{2,1,0:T(8,128)(2,1)S(1)}, u32[]{:S(2)}, u32[]{:S(2)}) %all-to-all-start.1) | async-done | bytes 1048608 | tf_op jit(solution)/shard_map/all_to_all | solution.py:27
  61.9 1.0 copy-done.8
  62.9 3.6 %fusion.23 = bf16[2048,512]{1,0:T(8,128)(2,1)S(1)} fusion(bf16[1024,512]{1,0:T(8,128)(2,1)} %bitcast.87, s32[1024]{0:T(1024)S(1)} %eq.48), kind=kOutput, calls=%fused_computation.48 | convolution fusion | flops 2150629376 | bytes 3149824 | tf_op jit(solution)/shard_map/dot_general | solution.py:76
  66.5 0.0 copy-start.2
  66.5 0.1 fusion.41
  66.6 0.7 collective-permute-start
  67.3 4.1 %collective-permute-start.1 = (bf16[16,1,512]{2,1,0:T(2,128)(2,1)S(1)}, bf16[16,1,512]{2,1,0:T(2,128)(2,1)S(1)}, u32[]{:S(2)}, u32[]{:S(2)}) collective-permute-start(bf16[16,1,512]{2,1,0:T(2,128)(2,1)S(1)} %get-tuple-element.24), channel_id=1, source_target_pairs={{1,0},{2,1},{3,2},{4,3},{5,4},{6,5},{7,6},{0,7},{9,8},{10,9},{11,1... | collective-permute-start | bytes 49160 | tf_op jit(solution)/shard_map/ppermute | solution.py:19
  71.3 1.9 collective-permute-done
  73.2 0.1 pad_maximum_fusion.5
  73.3 1.3 collective-permute-start.2
  74.6 1.3 collective-permute-start.3
  75.9 0.0 collective-permute-done.2
  75.9 2.7 collective-permute-done.3
  78.7 0.9 maximum_convert_fusion
  79.5 0.0 copy-start.9
  79.6 8.6 %fusion.10 = (f32[512]{0:T(512)S(1)}, f32[512]{0:T(512)S(1)}, f32[512]{0:T(512)S(1)}, f32[512]{0:T(512)S(1)}, f32[512]{0:T(512)S(1)}, /*index=5*/f32[512]{0:T(51...) fusion(f32[18,130,512]{2,1,0:T(8,128)S(1)} %maximum_convert_fusion, ...), kind=kOutput, calls=%fused_computation.23 | convolution fusion | flops 1094708736 | bytes 42485760 | tf_op jit(solution)/shard_map/dot_general | solution.py:93
  88.2 0.1 fusion.40
  88.2 0.1 collective-permute-start.4
  88.3 4.8 %collective-permute-start.5 = (bf16[16,1,512]{2,1,0:T(2,128)(2,1)S(1)}, bf16[16,1,512]{2,1,0:T(2,128)(2,1)S(1)}, u32[]{:S(2)}, u32[]{:S(2)}) collective-permute-start(bf16[16,1,512]{2,1,0:T(2,128)(2,1)S(1)} %get-tuple-element.22), channel_id=1, source_target_pairs={{1,0},{2,1},{3,2},{4,3},{5,4},{6,5},{7,6},{0,7},{9,8},{10,9},{11,1... | collective-permute-start | bytes 49160 | tf_op jit(solution)/shard_map/ppermute | solution.py:19
  93.1 1.9 collective-permute-done.4
  94.9 0.1 pad_maximum_fusion.2
  95.0 0.0 copy-start.4
  95.0 4.8 %collective-permute-start.6 = (bf16[1,130,512]{2,1,0:T(8,128)(2,1)S(1)}, bf16[1,130,512]{2,1,0:T(8,128)(2,1)S(1)}, u32[]{:S(2)}, u32[]{:S(2)}) collective-permute-start(bf16[1,130,512]{2,1,0:T(8,128)(2,1)S(1)} %get-tuple-element.17), channel_id=1, source_target_pairs={{0,8},{8,16},{16,24},{1,9},{9,17},{17,25},{2,10},{10,18},{18,26},{... | collective-permute-start | bytes 399368 | tf_op jit(solution)/shard_map/ppermute | solution.py:16
  99.8 1.5 collective-permute-start.7
  101.3 0.0 collective-permute-done.6
  101.3 2.0 collective-permute-done.7
  103.3 0.9 maximum_convert_fusion.1
  104.2 5.4 %fusion.12 = bf16[16,128,512]{2,1,0:T(8,128)(2,1)S(1)} fusion(f32[18,130,512]{2,1,0:T(8,128)S(1)} %maximum_convert_fusion.1, bf16[16,128,512]{2,1,0:T(8,128)(2,1)S(1)} %copy-done.4, f32[512]{0:T(512)S(1)} %bitcast.102, f32[512]{0:T(512)S(1)} %bitcast.104, f32[512]{0:T(512)S(1)} %bitcast.90, f32[512]{0:T(512)S(1)} %bitcast.92, f32[512]{0:T(512)S(1)} %bitcast.94, ...), kind=kLoop, calls=%fused_computation.26 | loop fusion | flops 20971520 | bytes 41961472 | tf_op jit(solution)/shard_map/convert_element_type | solution.py:108
  109.6 3.3 %fusion.24 = bf16[1024,512]{1,0:T(8,128)(2,1)} fusion(bf16[2048,512]{1,0:T(8,128)(2,1)S(1)} %bitcast.85, s32[1024]{0:T(1024)S(1)} %eq.48), kind=kOutput, calls=%fused_computation.51 | convolution fusion | flops 2150105088 | bytes 3149824 | tf_op jit(solution)/shard_map/dot_general | solution.py:109
  112.9 8.4 %all-to-all-start.2 = ((bf16[32,32,512]{2,1,0:T(8,128)(2,1)}), bf16[32,32,512]{2,1,0:T(8,128)(2,1)S(1)}, u32[]{:S(2)}, u32[]{:S(2)}) async-start(bf16[32,32,512]{2,1,0:T(8,128)(2,1)} %bitcast.86), calls=%async_computation.2 | async-start | bytes 2097152 | tf_op jit(solution)/shard_map/all_to_all | solution.py:43
  121.3 0.0 all-reduce.3.cloned.1.call-start
  121.4 0.0 copy-start.5
  121.4 17.2 %add_convert_fusion.1 = bf16[16,128,512]{2,1,0:T(8,128)(2,1)} fusion(f32[18,130,512]{2,1,0:T(8,128)} %copy-done.1, f32[512]{0:T(512)S(1)} %bitcast.103, f32[512]{0:T(512)S(1)} %bitcast.105, f32[512]{0:T(512)S(1)} %bitcast.91, f32[512]{0:T(512)S(1)} %bitcast.93, f32[512]{0:T(512)S(1)} %bitcast.95, f32[512]{0:T(512)S(1)} %bitcast.97, f32[512]{0:T(512)S(1)} %bitcast.99, ...), kind=kLoop, calls=%fused_computation.44 | loop fusion | flops 18874368 | bytes 39864320 | tf_op jit(solution)/shard_map/convert_element_type | solution.py:82
  138.6 3.9 %convolution_bitcast_fusion.1 = f32[512,512]{1,0:T(8,128)} fusion(bf16[16,128,512]{2,1,0:T(8,128)(2,1)} %add_convert_fusion.1, bf16[16,128,512]{2,1,0:T(8,128)(2,1)S(1)} %copy-done.5), kind=kOutput, calls=%fused_computation.53 | convolution fusion | flops 1073741824 | bytes 5242880 | tf_op jit(solution)/shard_map/dot_general | solution.py:89
  142.4 6.4 %all-to-all-done.2 = bf16[32,32,512]{2,1,0:T(8,128)(2,1)S(1)} async-done(((bf16[32,32,512]{2,1,0:T(8,128)(2,1)}), bf16[32,32,512]{2,1,0:T(8,128)(2,1)S(1)}, u32[]{:S(2)}, u32[]{:S(2)}) %all-to-all-start.2) | async-done | bytes 1048608 | tf_op jit(solution)/shard_map/all_to_all | solution.py:43
  148.9 2.0 gather_fusion
  150.9 1.5 fusion.39
  152.3 3.6 %convolution_bitcast_fusion = f32[616,512]{1,0:T(8,128)} fusion(bf16[512,616]{0,1:T(8,128)(2,1)S(1)} %copy-done, bf16[512,512]{1,0:T(8,128)(2,1)S(1)} %gather_fusion, bf16[512,512]{1,0:T(8,128)(2,1)} %param.12, f32[512,512]{1,0:T(8,128)} %copy-done.6), kind=kOutput, calls=%fused_computation.52 | convolution fusion | flops 593756160 | bytes 3989504 | tf_op jit(solution)/shard_map/dot_general | solution.py:120
  155.9 0.0 all-reduce.3.cloned.1.call-update
  155.9 0.1 stack.39
  156.0 38.4 %psum.31 = f32[9,512]{1,0:T(8,128)S(1)} all-reduce(f32[9,512]{1,0:T(8,128)S(1)} %stack.39), channel_id=1, replica_groups=mesh['lat'=4,'lon'=8] {'lat','lon'}, use_global_device_ids=true, to_apply=%region_17.18 | all-reduce | flops 4608 | bytes 36864 | tf_op jit(solution)/shard_map/psum | solution.py:123
  194.4 0.6 broadcast_multiply_fusion.3
  195.0 4.3 %add_convert_fusion = bf16[2048,512]{1,0:T(8,128)(2,1)} fusion(bf16[2048,512]{1,0:T(8,128)(2,1)S(1)} %copy-done.3, bf16[2048,512]{1,0:T(8,128)(2,1)} %bitcast.17, bf16[512,512]{1,0:T(8,128)(2,1)} %param.13), kind=kOutput, calls=%fused_computation.43 | convolution fusion | flops 1076887552 | bytes 6815744 | tf_op jit(solution)/shard_map/dot_general | solution.py:84
  199.2 94.9 %all-reduce.3.cloned.1.call-done = (f32[616,512]{1,0:T(8,128)}, f32[512,512]{1,0:T(8,128)}, f32[512,512]{1,0:T(8,128)}) async-done(((f32[616,512]{1,0:T(8,128)}, f32[512,512]{1,0:T(8,128)}, f32[512,512]{1,0:T(8,128)}), (f32[616,512]{1,0:T(8,128)}, f32[512,512]{1,0:T(8,128)}, f32[512,512]{1,0:T(8,128)})) %all-reduce.3.cloned.1.call-update) | async-done | bytes 3358736 | tf_op jit(solution)/shard_map/psum | solution.py:123
  294.2 2.5 broadcast_multiply_fusion
  296.7 3.1 %broadcast_multiply_fusion.1 = (f32[512,512]{1,0:T(8,128)}, f32[512,512]{1,0:T(8,128)}) fusion(f32[512,512]{1,0:T(8,128)} %get-tuple-element.16, f32[512,512]{1,0:T(8,128)} %get-tuple-element.15), kind=kLoop, calls=%fused_computation.64 | loop fusion | flops 524288 | bytes 4194304 | tf_op jit(solution)/shard_map/mul | solution.py:132
  (20 shorter events, 0.1 us)
Async XLA Ops:
  7.2 14.3 %copy-start = (bf16[512,616]{0,1:T(8,128)(2,1)S(1)}, bf16[512,616]{0,1:T(8,128)(2,1)}, u32[]{:S(2)}) copy-start(bf16[512,616]{0,1:T(8,128)(2,1)} %param.8) | copy-start | bytes 1892356
  14.1 14.4 %all-to-all-start = ((s32[32,1,32]{2,1,0:T(1,128)}), s32[32,1,32]{2,1,0:T(1,128)S(1)}, u32[]{:S(2)}, u32[]{:S(2)}) async-start(s32[32,1,32]{2,1,0:T(1,128)} %all_to_all.12), calls=%async_computation | async-start | bytes 32768 | tf_op jit(solution)/shard_map/all_to_all | solution.py:34
  23.1 38.8 %copy-start.6 = (f32[512,512]{1,0:T(8,128)}, f32[512,512]{1,0:T(8,128)S(1)}, u32[]{:S(2)}) copy-start(f32[512,512]{1,0:T(8,128)S(1)} %fusion.43) | copy-start | bytes 3145732
  28.5 33.4 %all-to-all-start.1 = ((bf16[32,32,512]{2,1,0:T(8,128)(2,1)}), bf16[32,32,512]{2,1,0:T(8,128)(2,1)S(1)}, u32[]{:S(2)}, u32[]{:S(2)}) async-start(bf16[32,32,512]{2,1,0:T(8,128)(2,1)} %bitcast.5), calls=%async_computation.1 | async-start | bytes 2097152 | tf_op jit(solution)/shard_map/all_to_all | solution.py:27
  61.9 1.0 copy-start.8
  66.5 13.0 %copy-start.2 = (bf16[2048,512]{1,0:T(8,128)(2,1)}, bf16[2048,512]{1,0:T(8,128)(2,1)S(1)}, u32[]{:S(2)}) copy-start(bf16[2048,512]{1,0:T(8,128)(2,1)S(1)} %fusion.23) | copy-start | bytes 6291460
  66.6 6.7 %collective-permute-start = (bf16[16,1,512]{2,1,0:T(2,128)(2,1)S(1)}, bf16[16,1,512]{2,1,0:T(2,128)(2,1)S(1)}, u32[]{:S(2)}, u32[]{:S(2)}) collective-permute-start(bf16[16,1,512]{2,1,0:T(2,128)(2,1)S(1)} %get-tuple-element.23), channel_id=1, source_target_pairs={{0,1},{1,2},{2,3},{3,4},{4,5},{5,6},{6,7},{7,0},{8,9},{9,10},{10,1... | collective-permute-start | bytes 49160 | tf_op jit(solution)/shard_map/ppermute | solution.py:16
  67.3 5.9 %collective-permute-start.1 = (bf16[16,1,512]{2,1,0:T(2,128)(2,1)S(1)}, bf16[16,1,512]{2,1,0:T(2,128)(2,1)S(1)}, u32[]{:S(2)}, u32[]{:S(2)}) collective-permute-start(bf16[16,1,512]{2,1,0:T(2,128)(2,1)S(1)} %get-tuple-element.24), channel_id=1, source_target_pairs={{1,0},{2,1},{3,2},{4,3},{5,4},{6,5},{7,6},{0,7},{9,8},{10,9},{11,1... | collective-permute-start | bytes 49160 | tf_op jit(solution)/shard_map/ppermute | solution.py:19
  73.3 2.6 collective-permute-start.2
  74.6 4.0 %collective-permute-start.3 = (bf16[1,130,512]{2,1,0:T(8,128)(2,1)S(1)}, bf16[1,130,512]{2,1,0:T(8,128)(2,1)S(1)}, u32[]{:S(2)}, u32[]{:S(2)}) collective-permute-start(bf16[1,130,512]{2,1,0:T(8,128)(2,1)S(1)} %get-tuple-element.20), channel_id=1, source_target_pairs={{8,0},{16,8},{24,16},{9,1},{17,9},{25,17},{10,2},{18,10},{26,18},{... | collective-permute-start | bytes 399368 | tf_op jit(solution)/shard_map/ppermute | solution.py:19
  79.5 8.6 %copy-start.1 = (f32[18,130,512]{2,1,0:T(8,128)}, f32[18,130,512]{2,1,0:T(8,128)S(1)}, u32[]{:S(2)}) copy-start(f32[18,130,512]{2,1,0:T(8,128)S(1)} %maximum_convert_fusion) | copy-start | bytes 14376964
  79.5 21.7 %copy-start.9 = (f32[9,512]{1,0:T(8,128)S(1)}, f32[9,512]{1,0:T(8,128)}, u32[]{:S(2)}) copy-start(f32[9,512]{1,0:T(8,128)} %param.14) | copy-start | bytes 55300
  88.2 6.7 %collective-permute-start.4 = (bf16[16,1,512]{2,1,0:T(2,128)(2,1)S(1)}, bf16[16,1,512]{2,1,0:T(2,128)(2,1)S(1)}, u32[]{:S(2)}, u32[]{:S(2)}) collective-permute-start(bf16[16,1,512]{2,1,0:T(2,128)(2,1)S(1)} %get-tuple-element.21), channel_id=1, source_target_pairs={{0,1},{1,2},{2,3},{3,4},{4,5},{5,6},{6,7},{7,0},{8,9},{9,10},{10,1... | collective-permute-start | bytes 49160 | tf_op jit(solution)/shard_map/ppermute | solution.py:16
  88.3 6.6 %collective-permute-start.5 = (bf16[16,1,512]{2,1,0:T(2,128)(2,1)S(1)}, bf16[16,1,512]{2,1,0:T(2,128)(2,1)S(1)}, u32[]{:S(2)}, u32[]{:S(2)}) collective-permute-start(bf16[16,1,512]{2,1,0:T(2,128)(2,1)S(1)} %get-tuple-element.22), channel_id=1, source_target_pairs={{1,0},{2,1},{3,2},{4,3},{5,4},{6,5},{7,6},{0,7},{9,8},{10,9},{11,1... | collective-permute-start | bytes 49160 | tf_op jit(solution)/shard_map/ppermute | solution.py:19
  95.0 9.1 %copy-start.4 = (bf16[16,128,512]{2,1,0:T(8,128)(2,1)S(1)}, bf16[16,128,512]{2,1,0:T(8,128)(2,1)}, u32[]{:S(2)}) copy-start(bf16[16,128,512]{2,1,0:T(8,128)(2,1)} %param.15) | copy-start | bytes 6291460
  95.0 6.3 %collective-permute-start.6 = (bf16[1,130,512]{2,1,0:T(8,128)(2,1)S(1)}, bf16[1,130,512]{2,1,0:T(8,128)(2,1)S(1)}, u32[]{:S(2)}, u32[]{:S(2)}) collective-permute-start(bf16[1,130,512]{2,1,0:T(8,128)(2,1)S(1)} %get-tuple-element.17), channel_id=1, source_target_pairs={{0,8},{8,16},{16,24},{1,9},{9,17},{17,25},{2,10},{10,18},{18,26},{... | collective-permute-start | bytes 399368 | tf_op jit(solution)/shard_map/ppermute | solution.py:16
  99.8 3.5 %collective-permute-start.7 = (bf16[1,130,512]{2,1,0:T(8,128)(2,1)S(1)}, bf16[1,130,512]{2,1,0:T(8,128)(2,1)S(1)}, u32[]{:S(2)}, u32[]{:S(2)}) collective-permute-start(bf16[1,130,512]{2,1,0:T(8,128)(2,1)S(1)} %get-tuple-element.18), channel_id=1, source_target_pairs={{8,0},{16,8},{24,16},{9,1},{17,9},{25,17},{10,2},{18,10},{26,18},{... | collective-permute-start | bytes 399368 | tf_op jit(solution)/shard_map/ppermute | solution.py:19
  112.9 36.0 %all-to-all-start.2 = ((bf16[32,32,512]{2,1,0:T(8,128)(2,1)}), bf16[32,32,512]{2,1,0:T(8,128)(2,1)S(1)}, u32[]{:S(2)}, u32[]{:S(2)}) async-start(bf16[32,32,512]{2,1,0:T(8,128)(2,1)} %bitcast.86), calls=%async_computation.2 | async-start | bytes 2097152 | tf_op jit(solution)/shard_map/all_to_all | solution.py:43
  121.3 172.9 %all-reduce.3.cloned.1.call-start = ((), (), s32[]{:S(2)}) async-start(), calls=%async_computation.3 | async-start | bytes 6717440 | tf_op jit(solution)/shard_map/psum | solution.py:123
  121.4 17.2 %copy-start.5 = (bf16[16,128,512]{2,1,0:T(8,128)(2,1)S(1)}, bf16[16,128,512]{2,1,0:T(8,128)(2,1)}, u32[]{:S(2)}) copy-start(bf16[16,128,512]{2,1,0:T(8,128)(2,1)} %param.15) | copy-start | bytes 6291460
  142.4 8.4 %copy-start.7 = (f32[512,512]{1,0:T(8,128)S(1)}, f32[512,512]{1,0:T(8,128)}, u32[]{:S(2)}) copy-start(f32[512,512]{1,0:T(8,128)} %copy-done.6) | copy-start | bytes 3145732
  152.3 42.6 %copy-start.3 = (bf16[2048,512]{1,0:T(8,128)(2,1)S(1)}, bf16[2048,512]{1,0:T(8,128)(2,1)}, u32[]{:S(2)}) copy-start(bf16[2048,512]{1,0:T(8,128)(2,1)} %copy-done.2) | copy-start | bytes 6291460
Sparse Core Ops, SparseCore 0:
  156.0 138.1 all-reduce.2
where the time goes:
time: 307 us
  waiting for transfers between devices  136 us (44%)
  starting transfers between devices  40 us (13%)
  blocking collectives  38.4 us (13%)
  other arithmetic  34.8 us (11%)
  matrix products  32.2 us (10%)
  between operations  14.4 us (5%)
  local copies, waits for them, and re-layouts  10.7 us (3%)
    psum x1, waiting for transfers between devices, on_device(): lax.psum((grad_in, grad_out, grad_point, grad_depth), ('lat', 'lon'))  94.9 us
    psum x1, blocking collectives, on_device(): lax.psum((grad_in, grad_out, grad_point, grad_depth), ('lat', 'lon'))  38.4 us
    all_to_all x1, waiting for transfers between devices, send_out(): lax.all_to_all(values.reshape(tiles, cap, width), ('lat', 'lon'), split_a...  26.3 us
    convert_element_type x1, other arithmetic, on_device(): mixed = mixed.astype(jnp.bfloat16)  17.2 us
    ppermute x4, starting transfers between devices, extended(): lax.ppermute(lax.slice_in_dim(block, 0, width, axis=dim), axis, backward)  11.6 us
    dot_general x1, matrix products, on_device(): jnp.dot(cot_rows, w_point.T, preferred_element_type=jnp.float32)  8.6 us
    all_to_all x1, starting transfers between devices, send_back(): lax.all_to_all(values.reshape(tiles, cap, width), ('lat', 'lon'), split_a...  8.37 us
    all_to_all x1, starting transfers between devices, send_out(): lax.all_to_all(places.reshape(tiles, cap), ('lat', 'lon'), split_axis=0,...  7.3 us
  transfers between devices with their start and end apart: 12, of which 7 were waited for; matrix products, arithmetic and copies ran while one was open for 11% of the time, Pallas kernels for 0%

commit v1 on v0

v1 whole, which is shorter than its diff:
```python
import functools

import jax
import jax.numpy as jnp
from jax import lax
from jax.experimental import pallas as pl
from jax.experimental.pallas import tpu as pltpu
from jax.sharding import Mesh
from jax.sharding import PartitionSpec as P

LANES = 128
bf16 = jnp.bfloat16
f32 = jnp.float32
i32 = jnp.int32


def params(mib):
    return pltpu.CompilerParams(vmem_limit_bytes=mib * 1024 * 1024)


def round_up(n, m):
    return -(-n // m) * m


def dot(a, b, dims=(1, 0)):
    return lax.dot_general(
        a, b, (((dims[0],), (dims[1],)), ((), ())), preferred_element_type=f32
    )


def cost(us):
    return pl.CostEstimate(flops=us * 1153500000, bytes_accessed=0, transcendentals=0)


def smem():
    return pl.BlockSpec(memory_space=pltpu.SMEM)


def anywhere():
    return pl.BlockSpec(memory_space=pl.ANY)


def vmem():
    return pl.BlockSpec(memory_space=pltpu.VMEM)


def route_kernel(tiles, cap, clon, places_ref, rows_ref, out_ref):
    spec, n = rows_ref.shape
    head = out_ref.shape[1] - LANES
    owner = places_ref[0:1, :]
    hits = owner == lax.broadcasted_iota(i32, (tiles, n), 0)
    above = lax.broadcasted_iota(i32, (n, n), 0) < lax.broadcasted_iota(i32, (n, n), 1)
    count = dot(hits.astype(f32).astype(bf16), above.astype(f32).astype(bf16))
    rank = jnp.sum(jnp.where(hits, count, 0.0), axis=0, keepdims=True)
    slot = owner * cap + rank.astype(i32)
    cell = places_ref[1:2, :]
    line = lax.broadcasted_iota(i32, (LANES - (spec - head), n), 0)
    high = cell // clon
    spots = jnp.where(line == 0, high, jnp.where(line == 1, cell - high * clon, 0)).astype(f32)
    last = jnp.concatenate([rows_ref[head:, :].astype(f32), spots], axis=0).astype(bf16)
    first = rows_ref[:head, :]
    step = min(256, tiles * cap)

    def body(t, carry):
        base = t * step
        place = lax.broadcasted_iota(i32, (step, n), 0) + base
        pick = (slot == place).astype(f32).astype(bf16)
        at = pl.ds(pl.multiple_of(base, step), step)
        out_ref[at, :head] = dot(pick, first, (1, 1)).astype(bf16)
        out_ref[at, head:] = dot(pick, last, (1, 1)).astype(bf16)
        return carry

    lax.fori_loop(0, tiles * cap // step, body, 0)


def route(places, rows, tiles, cap, clon, spec_wide):
    return pl.pallas_call(
        functools.partial(route_kernel, tiles, cap, clon),
        out_shape=jax.ShapeDtypeStruct((tiles * cap, spec_wide), bf16),
        in_specs=[vmem()] * 2,
        out_specs=vmem(),
        compiler_params=params(12),
        cost_estimate=cost(3),
        name="route",
    )(places, rows)


def grid_grad_kernel(
    clat, clon, wide, cot_ref, east_ref, west_ref, north_ref, south_ref, wp_ref, wd_ref,
    cot_ext, gm_ref, gg_ref, east, west,
):
    width = wp_ref.shape[0]
    w_point = wp_ref[...]
    east[...] = east_ref[...].astype(f32)
    west[...] = west_ref[...].astype(f32)
    line = lax.broadcasted_iota(i32, (wide - clon, width), 0)

    def matmul(i, carry):
        at = pl.multiple_of((i + 1) * wide, 16)
        cot_ext[pl.ds(at, clon), :] = cot_ref[pl.ds(pl.multiple_of(i * clon, 16), clon), :]
        tail = jnp.where(
            line == 0, east[pl.ds(i, 1), :], jnp.where(line == wide - clon - 1, west[pl.ds(i, 1), :], 0.0)
        )
        cot_ext[pl.ds(at + clon, wide - clon), :] = tail.astype(bf16)
        at = pl.ds(at, wide)
        gm_ref[at, :] = dot(cot_ext[at, :], w_point, (1, 1)).astype(bf16)
        return carry

    for ref, at in ((north_ref, 0), (south_ref, (clat + 1) * wide)):
        cot_ext[at : at + wide, :] = ref[...]
        gm_ref[at : at + wide, :] = dot(ref[...], w_point, (1, 1)).astype(bf16)
    lax.fori_loop(0, clat, matmul, 0)

    def conv(i, carry):
        out_at = pl.ds(pl.multiple_of(i * clon, 16), clon)
        mid = pl.ds(pl.multiple_of((i + 1) * wide, 16), wide)
        for lane in range(0, width, LANES):
            cols = slice(lane, lane + LANES)
            sums = []
            for b in range(3):
                total = None
                for a in range(3):
                    at = pl.ds(pl.multiple_of((i + 2 - a) * wide, 16), wide)
                    term = wd_ref[3 * a + b : 3 * a + b + 1, cols] * gm_ref[at, cols].astype(f32)
                    total = term if total is None else total + term
                sums.append(total)
            out = cot_ext[mid, cols].astype(f32) + sums[1]
            out = out + pltpu.roll(sums[2], 1, 0) + pltpu.roll(sums[0], wide - 1, 0)
            gg_ref[out_at, cols] = out[:clon].astype(bf16)
        return carry

    lax.fori_loop(0, clat, conv, 0)


def grid_grad(cot, sides, w_point, w_depth, clat, clon, wide):
    width = w_point.shape[0]
    ext = jax.ShapeDtypeStruct(((clat + 2) * wide, width), bf16)
    return pl.pallas_call(
        functools.partial(grid_grad_kernel, clat, clon, wide),
        out_shape=(ext, ext, jax.ShapeDtypeStruct((clat * clon, width), bf16)),
        in_specs=[vmem()] * 7,
        out_specs=(vmem(),) * 3,
        scratch_shapes=[pltpu.VMEM((clat, width), f32)] * 2,
        compiler_params=params(8),
        cost_estimate=cost(10),
        name="grid_grad",
    )(cot, *sides, w_point, w_depth)


def write_halves(core, total, start, mine_ref, other_ref, first=0, size=None):
    size = total.shape[0] if size is None else size
    half = total.shape[1] // 2
    for ref, base in ((mine_ref, core * half), (other_ref, (1 - core) * half)):
        for n in range(half // LANES):
            cols = pl.ds(pl.multiple_of(base + n * LANES, LANES), LANES)
            ref[n, start : start + size, :] = total[first : first + size, cols].astype(bf16)


def clear_tail(start, *refs):
    for ref in refs:
        unused = ref.shape[1] - start
        if unused:
            ref[:, start:, :] = jnp.zeros((ref.shape[0], unused, LANES), bf16)


def owner_kernel(
    spec, clat, clon, wide, core_ref, rows_hbm, wi_hbm, wo_hbm, gg_hbm, cot_hbm, gm_hbm, wd_hbm,
    grid_hbm, mix_hbm, east_hbm, west_hbm, mine_hbm, other_hbm,
    rows_ref, wi_ref, wo_ref, gg_ref, cot_ref, gm_ref, wd_ref,
    padded, mix_ref, east_ref, west_ref, mine_ref, other_ref,
    emb_ref, gi, go, gp, gd, sems,
):
    core = core_ref[0]
    slots, spec_wide = rows_ref.shape
    cells, width = gg_ref.shape
    sources = rows_hbm, wi_hbm, wo_hbm, gg_hbm, wd_hbm, cot_hbm, gm_hbm
    targets = rows_ref, wi_ref, wo_ref, gg_ref, wd_ref, cot_ref, gm_ref
    loads = [
        pltpu.make_async_copy(source, target, sems.at[i])
        for i, (source, target) in enumerate(zip(sources, targets))
    ]
    for load in loads:
        load.start()
    gi[...] = jnp.zeros_like(gi)
    go[...] = jnp.zeros_like(go)
    gd[...] = jnp.zeros_like(gd)
    gp[...] = jnp.zeros_like(gp)
    padded[pl.ds(0, 2 * clon), :] = jnp.zeros((2 * clon, width), bf16)
    padded[pl.ds((clat + 2) * clon, 2 * clon), :] = jnp.zeros((2 * clon, width), bf16)
    for load in loads[:4]:
        load.wait()

    step = min(256, slots)

    def encode(t, carry):
        at = pl.ds(pl.multiple_of(t * step, step), step)
        rows = rows_ref[at, :]
        preact = dot(rows, wi_ref[...])
        sig = 1.0 / (1.0 + jnp.exp(-preact))
        hidden = (preact * sig).astype(bf16)
        emb_ref[at, :] = dot(hidden, wo_ref[...]).astype(bf16)
        place = rows[:, spec : spec + 1].astype(f32) * clon + rows[:, spec + 1 : spec + 2].astype(f32)
        hits = place.astype(i32) == lax.broadcasted_iota(i32, (step, cells), 1)
        g_emb = dot(hits.astype(f32).astype(bf16), gg_ref[...]).astype(bf16)
        go[...] += dot(hidden, g_emb, (0, 0))
        g_hid = dot(g_emb, wo_ref[...], (1, 1))
        g_pre = (g_hid * (sig * (1.0 + preact * (1.0 - sig)))).astype(bf16)
        gi[...] += dot(rows, g_pre, (0, 0))
        return carry

    lax.fori_loop(0, slots // step, encode, 0)

    last = rows_ref[:, spec_wide - LANES :]
    col = spec - (spec_wide - LANES)
    lane = lax.broadcasted_iota(i32, (16, LANES), 1)
    pick = jnp.where(lane == col, float(clon), jnp.where(lane == col + 1, 1.0, 0.0)).astype(bf16)
    place = dot(pick, last, (1, 1))[0:1, :].astype(i32)
    block = 2 * clon

    def bins(t, carry):
        cell = lax.broadcasted_iota(i32, (block, slots), 0) + t * block
        hits = (place == cell).astype(f32).astype(bf16)
        grid = dot(hits, emb_ref[...]).astype(bf16)
        padded[pl.ds(pl.multiple_of((t + 1) * block, 16), block), :] = grid
        return carry

    lax.fori_loop(0, clat // 2, bins, 0)
    put_grid = pltpu.make_async_copy(padded.at[pl.ds(2 * clon, cells)], grid_hbm, sems.at[7])
    put_grid.start()
    for load in loads[4:]:
        load.wait()

    fill = jnp.zeros((wide - clon, LANES), f32)

    def conv(e, carry):
        out_at = pl.ds(pl.multiple_of(e * wide, 16), wide)
        for lane in range(0, width, LANES):
            cols = slice(lane, lane + LANES)
            near = [
                padded[pl.ds(pl.multiple_of((e + a) * clon, 16), clon), cols].astype(f32)
                for a in range(3)
            ]
            sums = []
            for b in range(3):
                total = None
                for a in range(3):
                    term = wd_ref[3 * a + b : 3 * a + b + 1, cols] * near[a]
                    total = term if total is None else total + term
                sums.append(jnp.concatenate([total, fill], axis=0))
            mixed = sums[1] + pltpu.roll(sums[2], wide - 1, 0) + pltpu.roll(sums[0], 1, 0)
            mix_ref[out_at, cols] = mixed.astype(bf16)
            east_ref[e, :, cols] = mixed[clon : clon + 8]
            west_ref[e, :, cols] = mixed[wide - 8 : wide]
            g_mid = gm_ref[out_at, cols].astype(f32)
            for b, g in ((0, pltpu.roll(g_mid, wide - 1, 0)), (1, g_mid), (2, pltpu.roll(g_mid, 1, 0))):
                g = g[:clon]
                for a in range(3):
                    part = jnp.sum((g * near[a]).reshape(clon // 8, 8, LANES), axis=0)
                    gd[8 * (3 * a + b) : 8 * (3 * a + b) + 8, cols] += part
        return carry

    lax.fori_loop(0, clat + 2, conv, 0)
    puts = [
        pltpu.make_async_copy(mix_ref, mix_hbm, sems.at[8]),
        pltpu.make_async_copy(east_ref, east_hbm, sems.at[9]),
        pltpu.make_async_copy(west_ref, west_hbm, sems.at[10]),
    ]
    for put in puts:
        put.start()

    def point(t, carry):
        at = pl.ds(pl.multiple_of(t * 3 * wide, 16), 3 * wide)
        gp[...] += dot(mix_ref[at, :], cot_ref[at, :], (0, 0))
        return carry

    lax.fori_loop(0, (clat + 2) // 3, point, 0)
    taps = [jnp.sum(gd[8 * k : 8 * k + 8, :], axis=0, keepdims=True) for k in range(9)]
    gd[0:16, :] = jnp.concatenate(taps + [jnp.zeros((7, width), f32)], axis=0)
    start = 0
    for total, size in ((go, width), (gi, round_up(spec, 16)), (gp, width), (gd, 16)):
        write_halves(core, total, start, mine_ref, other_ref, 0, size)
        start += size
    clear_tail(start, mine_ref, other_ref)
    puts += [put_grid] + [
        pltpu.make_async_copy(mine_ref, mine_hbm, sems.at[11]),
        pltpu.make_async_copy(other_ref, other_hbm, sems.at[12]),
    ]
    for put in puts[-2:]:
        put.start()
    for put in puts:
        put.wait()


def owner_part(core, rows, w_in, w_out, g_grid, cot_ext, gm_ext, w_depth, spec, clat, clon, wide, out_rows):
    slots, spec_wide = rows.shape
    width = w_out.shape[0]
    half = jax.ShapeDtypeStruct((width // LANES // 2, out_rows, LANES), bf16)
    column = jax.ShapeDtypeStruct((clat + 2, 8, width), f32)
    operands = rows, w_in, w_out, g_grid, cot_ext, gm_ext, w_depth
    padded = pltpu.VMEM(((clat + 4) * clon, width), bf16)
    outs = jax.ShapeDtypeStruct(cot_ext.shape, bf16), column, column, half, half
    return pl.pallas_call(
        functools.partial(owner_kernel, spec, clat, clon, wide),
        out_shape=(jax.ShapeDtypeStruct((clat * clon, width), bf16),) + outs,
        in_specs=[smem()] + [anywhere()] * 7,
        out_specs=(anywhere(),) * 6,
        scratch_shapes=[pltpu.VMEM(x.shape, x.dtype) for x in operands]
        + [padded]
        + [pltpu.VMEM(x.shape, x.dtype) for x in outs]
        + [
            pltpu.VMEM((slots, width), bf16),
            pltpu.VMEM((spec_wide, width), f32),
            pltpu.VMEM((width, width), f32),
            pltpu.VMEM((width, width), f32),
            pltpu.VMEM((72, width), f32),
            pltpu.SemaphoreType.DMA((13,)),
        ],
        compiler_params=params(56),
        cost_estimate=cost(22),
        name="owner",
    )(core, *operands)


def latent_kernel(
    clat, clon, wide, grid_ref, mix_ref, top_ref, bottom_ref, left_ref, right_ref, wp_ref, out_ref
):
    width = wp_ref.shape[0]
    w_point = wp_ref[...]
    line = lax.broadcasted_iota(i32, (clon, width), 0)

    def body(i, carry):
        at = pl.ds(pl.multiple_of(i * clon, 16), clon)
        mixed = mix_ref[pl.ds(pl.multiple_of((i + 1) * wide, 16), clon), :].astype(f32)
        mixed = mixed + (i == 0).astype(f32) * top_ref[:clon, :].astype(f32)
        mixed = mixed + (i == clat - 1).astype(f32) * bottom_ref[:clon, :].astype(f32)
        mixed = mixed + jnp.where(
            line == 0, left_ref[pl.ds(i, 1), :], jnp.where(line == clon - 1, right_ref[pl.ds(i, 1), :], 0.0)
        )
        out = grid_ref[at, :].astype(f32) + dot(mixed.astype(bf16), w_point)
        out_ref[at, :] = out.astype(bf16)
        return carry

    lax.fori_loop(0, clat, body, 0)


def finish_latent(grid, mix_ext, sides, w_point, clat, clon, wide):
    return pl.pallas_call(
        functools.partial(latent_kernel, clat, clon, wide),
        out_shape=jax.ShapeDtypeStruct(grid.shape, bf16),
        in_specs=[vmem()] * 7,
        out_specs=vmem(),
        compiler_params=params(6),
        cost_estimate=cost(5),
        name="latent",
    )(grid, mix_ext, *sides, w_point)


def totals_kernel(parts_ref, *refs):
    out_ref = refs[-1]
    total = jnp.sum(parts_ref[...].astype(f32), axis=0).astype(bf16)
    out_ref[...] = jnp.broadcast_to(total[None], parts_ref.shape)


def totals(parts, *after):
    return pl.pallas_call(
        totals_kernel,
        out_shape=jax.ShapeDtypeStruct(parts.shape, bf16),
        in_specs=[vmem()] + [anywhere()] * len(after),
        out_specs=vmem(),
        compiler_params=params(6),
        cost_estimate=cost(1),
        name="totals",
    )(parts, *after)


def unpack_kernel(
    obs_scale, cell_scale, core_ref, own_ref, sibling_ref, gi_ref, go_ref, gp_ref, gd_ref
):
    spec, width = gi_ref.shape
    chips = own_ref.shape[0]
    count = width // (2 * LANES)
    per = chips // count
    core = core_ref[0]
    for ref, half in ((own_ref, core), (sibling_ref, 1 - core)):
        for n in range(count):
            cols = pl.ds(pl.multiple_of((half * count + n) * LANES, LANES), LANES)
            block = ref[n * per : (n + 1) * per].astype(f32)
            block = block.reshape(per * block.shape[1], LANES)
            start = 0
            for out_ref, scale in (
                (go_ref, obs_scale), (gi_ref, obs_scale), (gp_ref, cell_scale), (gd_ref, cell_scale)
            ):
                size = out_ref.shape[0]
                out_ref[:, cols] = block[start : start + size] * scale
                start += round_up(size, 16)


def unpack(core, own, sibling, spec, width, obs_scale, cell_scale):
    return pl.pallas_call(
        functools.partial(unpack_kernel, obs_scale, cell_scale),
        out_shape=tuple(
            jax.ShapeDtypeStruct((rows, width), f32) for rows in (spec, width, width, 9)
        ),
        in_specs=[smem()] + [vmem()] * 2,
        out_specs=(vmem(),) * 4,
        compiler_params=params(8),
        cost_estimate=cost(3),
        name="unpack",
    )(core, own, sibling)


def neighbours(axes, periodic):
    count = lax.axis_size(axes)
    up = [(i, i + 1) for i in range(count - 1)]
    if periodic:
        up.append((count - 1, 0))
    return up, [(t, s) for s, t in up]


LAT = ("x", "core")
CHIPS = ("x", "lon")


SWAP = [(0, 1), (1, 0)]


def core_sum(mine, other):
    got = lax.ppermute(other, "core", SWAP)
    return (mine.astype(f32) + got.astype(f32)).astype(bf16)


def spread(values):
    chips = lax.axis_size(CHIPS)
    blocks, rows, _ = values.shape
    values = values.reshape(chips, blocks * rows // chips, LANES)
    return lax.all_to_all(values, CHIPS, split_axis=0, concat_axis=0, tiled=True)


def on_device(spectra, owner, cell, w_in, w_out, w_point, w_depth, cotangent):
    tiles = lax.axis_size(LAT) * lax.axis_size("lon")
    rows_here, spec = spectra.shape
    cap = max(2, 2 * rows_here // tiles)
    clat, clon, width = cotangent.shape
    cells = clat * clon
    wide = clon + 16
    spec_wide = round_up(spec + 2, LANES)
    core = lax.axis_index("core").reshape(1)
    east_way, west_way = neighbours("lon", True)
    south_way, north_way = neighbours(LAT, False)

    from_west = lax.ppermute(cotangent[:, -1], "lon", east_way)
    from_east = lax.ppermute(cotangent[:, 0], "lon", west_way)

    places = jnp.concatenate([owner.reshape(1, rows_here), cell.reshape(1, rows_here)], axis=0)
    outgoing = route(places, spectra.T, tiles, cap, clon, spec_wide)
    outgoing, from_west, from_east = lax.optimization_barrier((outgoing, from_west, from_east))
    arrived = lax.all_to_all(
        outgoing.reshape(tiles, cap, spec_wide), ("x", "core", "lon"), 0, 0, tiled=True
    ).reshape(tiles * cap, spec_wide)

    fill = jnp.zeros((wide - clon - 2, width), bf16)

    def edge_row(i):
        return jnp.concatenate([cotangent[i], from_east[i, None], fill, from_west[i, None]], axis=0)

    from_north = lax.ppermute(edge_row(clat - 1), LAT, south_way)
    from_south = lax.ppermute(edge_row(0), LAT, north_way)
    cot_ext, gm_ext, g_grid = grid_grad(
        cotangent.reshape(cells, width),
        (from_east, from_west, from_north, from_south),
        w_point, w_depth, clat, clon, wide,
    )
    w_in_wide = jnp.pad(w_in, ((0, spec_wide - spec), (0, 0)))

    out_rows = round_up(2 * width + round_up(spec, 16) + 16, 16 * tiles * LANES // width)
    grid, mix_ext, east, west, mine, other = owner_part(
        core, arrived, w_in_wide, w_out, g_grid, cot_ext, gm_ext, w_depth,
        spec, clat, clon, wide, out_rows,
    )
    summed = core_sum(mine, other)
    summed, grid, mix_ext, east, west = lax.optimization_barrier((summed, grid, mix_ext, east, west))
    parts = spread(summed)

    ext = mix_ext.reshape(clat + 2, wide, width)
    top = lax.ppermute(ext[clat + 1], LAT, south_way)
    bottom = lax.ppermute(ext[0], LAT, north_way)

    def edge_column(own, at):
        return own[1:-1].at[0].add(top[at].astype(f32)).at[-1].add(bottom[at].astype(f32))

    left = lax.ppermute(edge_column(east[:, 0], clon), "lon", east_way)
    right = lax.ppermute(edge_column(west[:, 7], wide - 1), "lon", west_way)
    sent = totals(parts, left, right)
    full = lax.all_to_all(sent, CHIPS, split_axis=0, concat_axis=0, tiled=True)
    latent = finish_latent(grid, mix_ext, (top, bottom, left, right), w_point, clat, clon, wide)

    obs_scale = float((rows_here * tiles) ** -0.5)
    cell_scale = float((cells * tiles) ** -0.5)
    full, latent = lax.optimization_barrier((full, latent))
    sibling = lax.ppermute(full, "core", SWAP)
    grad_in, grad_out, grad_point, grad_depth = unpack(
        core, full, sibling, spec, width, obs_scale, cell_scale
    )
    return latent.reshape(clat, clon, width), grad_in, grad_out, grad_point, grad_depth


def solution(mesh):
    lat, lon = mesh.devices.shape
    fine = Mesh(mesh.devices.reshape(lat // 2, 2, lon), ("x", "core", "lon"))
    everyone = P(("x", "core", "lon"))
    field = P(LAT, "lon", None)
    in_specs = (everyone, everyone, everyone, P(), P(), P(), P(), field)
    out_specs = (field, P(), P(), P(), P())
    return jax.shard_map(
        on_device, mesh=fine, in_specs=in_specs, out_specs=out_specs, check_vma=False
    )
```

time: 307 us -> 141 us (0.46)
  waiting for transfers between devices: 136 us -> 30.3 us
  Pallas kernels: 0 us -> 47.8 us
  blocking collectives: 38.4 us -> 0 us
  matrix products: 32.2 us -> 0 us
  other arithmetic: 34.8 us -> 4.76 us
  between operations: 14.4 us -> 0.88 us
  local copies, waits for them, and re-layouts: 10.7 us -> 21.8 us
  starting transfers between devices: 40 us -> 34.4 us
    psum x1 -> x0, waiting for transfers between devices: 94.9 us -> none  [on_device(): lax.psum((grad_in, grad_out, grad_point, grad_depth), ('lat', 'lon'))]
    pallas_call x0 -> x6, Pallas kernels: none -> 47.8 us  [the longest x1 26 us: owner_part(): pl.pallas_call(functools.partial(owner_kernel, spec, clat, clon, wide), o...]
    psum x1 -> x0, blocking collectives: 38.4 us -> none  [on_device(): lax.psum((grad_in, grad_out, grad_point, grad_depth), ('lat', 'lon'))]
    dot_general x9 -> x0, matrix products: 32.2 us -> none  [the longest x1 8.6 us: on_device(): jnp.dot(cot_rows, w_point.T, preferred_element_type=jnp.float32)]
    convert_element_type x5 -> x1, other arithmetic: 25.1 us -> 2.43 us  [core_sum(): return (mine.astype(f32) + got.astype(f32)).astype(bf16)]
    unnamed x20 -> x34, local copies, waits for them, and re-layouts: 1.02 us -> 12.3 us
    all_to_all x3, waiting for transfers between devices: 32.7 us -> 23.1 us  [the longest x1 12.9 us: on_device(): lax.all_to_all(outgoing.reshape(tiles, cap, spec_wide), ('x', 'core', 'lo...]
    all_to_all x3, starting transfers between devices: 21.5 us -> 14.9 us  [the longest x1 7.69 us: on_device(): full = lax.all_to_all(sent, CHIPS, split_axis=0, concat_axis=0, tiled=True)]
  transfers between devices with their start and end apart: 12 -> 13, of which waited for: 7 -> 6; matrix products, arithmetic and copies ran while one was open for 11% -> 8% of each run, Pallas kernels for 0% -> 13%
where the time goes in v1:
time: 141 us; the launch traced here: 140 us
  Pallas kernels  47.8 us (34%)
  starting transfers between devices  34.4 us (24%)
  waiting for transfers between devices  30.3 us (21%)
  local copies, waits for them, and re-layouts  21.8 us (15%)
  other arithmetic  4.76 us (3%)
    pallas_call x1, Pallas kernels, owner_part(): pl.pallas_call(functools.partial(owner_kernel, spec, clat, clon, wide), o...  26 us
    all_to_all x1, waiting for transfers between devices, on_device(): lax.all_to_all(outgoing.reshape(tiles, cap, spec_wide), ('x', 'core', 'lo...  12.9 us
    unnamed x34, local copies, waits for them, and re-layouts  12.3 us
    pallas_call x1, Pallas kernels, grid_grad(): pl.pallas_call(functools.partial(grid_grad_kernel, clat, clon, wide), out...  9.42 us
    all_to_all x1, waiting for transfers between devices, on_device(): full = lax.all_to_all(sent, CHIPS, split_axis=0, concat_axis=0, tiled=True)  8.43 us
    all_to_all x1, starting transfers between devices, on_device(): full = lax.all_to_all(sent, CHIPS, split_axis=0, concat_axis=0, tiled=True)  7.69 us
    pallas_call x1, Pallas kernels, finish_latent(): pl.pallas_call(functools.partial(latent_kernel, clat, clon, wide), out_sh...  6.26 us
    all_to_all x1, starting transfers between devices, spread(): lax.all_to_all(values, CHIPS, split_axis=0, concat_axis=0, tiled=True)  3.62 us
  transfers between devices with their start and end apart: 13, of which 6 were waited for; matrix products, arithmetic and copies ran while one was open for 8% of the time, Pallas kernels for 13%

profile of v1, /device:TPU:0, one launch (start us, length us, event | category | flops | bytes accessed | tf_op | source)
XLA Modules:
  0.0 140.0 jit_solution(7259686134222186265)
XLA Ops:
  0.6 1.0 fusion.5
  1.7 3.0 %collective-permute-start = (bf16[16,512]{1,0:T(8,128)(2,1)S(1)}, bf16[16,512]{1,0:T(8,128)(2,1)S(1)}, u32[]{:S(2)}, u32[]{:S(2)}) collective-permute-start(bf16[16,512]{1,0:T(8,128)(2,1)S(1)} %bitcast.30), channel_id=1, source_target_pairs={{0,1},{1,2},{2,3},{3,4},{4,5},{5,6},{6,7},{7,0},{8,9},{9,10},{10,1... | collective-permute-start | bytes 49160 | tf_op jit(solution)/shard_map/ppermute | solution.py:451
  4.7 3.1 %collective-permute-start.1 = (bf16[16,512]{1,0:T(8,128)(2,1)S(1)}, bf16[16,512]{1,0:T(8,128)(2,1)S(1)}, u32[]{:S(2)}, u32[]{:S(2)}) collective-permute-start(bf16[16,512]{1,0:T(8,128)(2,1)S(1)} %bitcast.31), channel_id=1, source_target_pairs={{1,0},{2,1},{3,2},{4,3},{5,4},{6,5},{7,6},{0,7},{9,8},{10,9},{11,1... | collective-permute-start | bytes 49160 | tf_op jit(solution)/shard_map/ppermute | solution.py:452
  7.8 0.7 pad_add_fusion.places_ref
  8.5 1.1 copy-done.4
  9.6 3.0 %route.1 = bf16[1024,640]{1,0:T(8,128)(2,1)} custom-call(s32[2,512]{1,0:T(2,128)S(1)} %pad_add_fusion.places_ref, bf16[616,512]{1,0:T(8,128)(2,1)S(1)} %bitcast.28), custom_call_target="tpu_custom_call" | custom-call | flops 3460499968 | tf_op jit(solution)/shard_map/route/pallas_call | solution.py:77
  12.6 0.0 collective-permute-done.west_ref
  12.6 0.0 collective-permute-done.1.east_ref
  12.6 0.0 copy-start.5
  12.6 0.0 copy-start.7
  12.6 3.5 %all-to-all-start = ((bf16[32,32,640]{2,1,0:T(8,128)(2,1)}), bf16[32,32,640]{2,1,0:T(8,128)(2,1)}, u32[]{:S(2)}, u32[]{:S(2)}) async-start(bf16[32,32,640]{2,1,0:T(8,128)(2,1)} %bitcast.6), calls=%async_computation | async-start | bytes 2621440 | tf_op jit(solution)/shard_map/all_to_all | solution.py:457
  16.2 0.1 pad.19.clone
  16.3 0.1 pad_maximum_fusion.1
  16.4 1.3 collective-permute-start.3
  17.7 3.0 %collective-permute-start.2 = (bf16[144,512]{1,0:T(8,128)(2,1)S(1)}, bf16[144,512]{1,0:T(8,128)(2,1)S(1)}, u32[]{:S(2)}, u32[]{:S(2)}) collective-permute-start(bf16[144,512]{1,0:T(8,128)(2,1)S(1)} %get-tuple-element.114), channel_id=1, source_target_pairs={{0,8},{8,16},{16,24},{1,9},{9,17},{17,25},{2,10},{10,18},{18,26},{... | collective-permute-start | bytes 442376 | tf_op jit(solution)/shard_map/ppermute | solution.py:466
  20.8 2.0 %pad.12.wi_hbm = bf16[640,512]{1,0:T(8,128)(2,1)} pad(bf16[616,512]{1,0:T(8,128)(2,1)} %param.19, bf16[]{:T(256)} %constant.105.clone.1), padding=0_24x0_0 | pad | bytes 1286146 | tf_op jit(solution)/shard_map/jit(_pad)/pad | solution.py:473
  22.7 0.0 collective-permute-done.3.south_ref
  22.7 0.0 collective-permute-done.2.north_ref
  22.7 9.4 %grid_grad.1 = (bf16[2592,512]{1,0:T(8,128)(2,1)S(1)}, bf16[2592,512]{1,0:T(8,128)(2,1)S(1)}, bf16[2048,512]{1,0:T(8,128)(2,1)S(1)}) custom-call(bf16[2048,512]{1,0:T(8,128)(2,1)S(1)} %bitcast.27, bf16[16,512]{1,0:T(8,128)(2,1)S(1)} %collective-permute-done.1.east_ref, bf16[16,512]{1,0:T(8,128)(2,1)S(1)} %collective-permute-done.west_ref, ...), custom_call_target="tpu_custom_call" | custom-call | flops 11534999552 | tf_op jit(solution)/shard_map/grid_grad/pallas_call | solution.py:138
  32.2 0.0 copy-start.12
  32.2 1.5 %copy-done.12 = bf16[2592,512]{1,0:T(8,128)(2,1)} copy-done((bf16[2592,512]{1,0:T(8,128)(2,1)}, bf16[2592,512]{1,0:T(8,128)(2,1)S(1)}, u32[]{:S(2)}) %copy-start.12) | copy-done | bytes 2654232
  33.7 1.5 %copy-done.13 = bf16[2592,512]{1,0:T(8,128)(2,1)} copy-done((bf16[2592,512]{1,0:T(8,128)(2,1)}, bf16[2592,512]{1,0:T(8,128)(2,1)S(1)}, u32[]{:S(2)}) %copy-start.13) | copy-done | bytes 2654232
  35.2 1.3 copy-done.14
  36.5 12.9 %all-to-all-done = bf16[32,32,640]{2,1,0:T(8,128)(2,1)} async-done(((bf16[32,32,640]{2,1,0:T(8,128)(2,1)}), bf16[32,32,640]{2,1,0:T(8,128)(2,1)}, u32[]{:S(2)}, u32[]{:S(2)}) %all-to-all-start) | async-done | bytes 1310752 | tf_op jit(solution)/shard_map/all_to_all | solution.py:457
  49.4 26.0 %owner.1 = (bf16[2048,512]{1,0:T(8,128)(2,1)}, bf16[2592,512]{1,0:T(8,128)(2,1)}, f32[18,8,512]{2,1,0:T(8,128)}, f32[18,8,512]{2,1,0:T(8,128)}, bf16[2,1664,128]...) custom-call(s32[1]{0:T(128)} %bitcast.core_ref, bf16[1024,640]{1,0:T(8,128)(2,1)} %bitcast.7.rows_hbm, ...), custom_call_target="tpu_custom_call" | custom-call | flops 25376999424 | tf_op jit(solution)/shard_map/owner/pallas_call | solution.py:302
  75.4 0.1 collective-permute-start.4
  75.4 2.6 %collective-permute-done.4 = bf16[2,1664,128]{2,1,0:T(8,128)(2,1)S(1)} collective-permute-done((bf16[2,1664,128]{2,1,0:T(8,128)(2,1)}, bf16[2,1664,128]{2,1,0:T(8,128)(2,1)S(1)}, u32[]{:S(2)}, u32[]{:S(2)}) %collective-permute-start.4) | collective-permute-done | bytes 852000 | tf_op jit(solution)/shard_map/ppermute | solution.py:428
  78.0 2.4 %add_convert_fusion = bf16[2,1664,128]{2,1,0:T(8,128)(2,1)} fusion(bf16[2,1664,128]{2,1,0:T(8,128)(2,1)S(1)} %collective-permute-done.4, bf16[2,1664,128]{2,1,0:T(8,128)(2,1)} %get-tuple-element.82), kind=kLoop, calls=%fused_computation | loop fusion | flops 1703936 | bytes 2555904 | tf_op jit(solution)/shard_map/convert_element_type | solution.py:429
  80.4 3.6 %all-to-all-start.1 = ((bf16[16,208,128]{2,1,0:T(8,128)(2,1)}), bf16[16,208,128]{2,1,0:T(8,128)(2,1)S(1)}, u32[]{:S(2)}, u32[]{:S(2)}) async-start(bf16[16,208,128]{2,1,0:T(8,128)(2,1)} %bitcast.29), calls=%async_computation.1 | async-start | bytes 1703936 | tf_op jit(solution)/shard_map/all_to_all | solution.py:436
  84.1 0.7 fusion.4
  84.8 1.3 collective-permute-start.6
  86.1 3.0 %collective-permute-start.5 = (bf16[144,512]{1,0:T(8,128)(2,1)S(1)}, bf16[144,512]{1,0:T(8,128)(2,1)S(1)}, u32[]{:S(2)}, u32[]{:S(2)}) collective-permute-start(bf16[144,512]{1,0:T(8,128)(2,1)S(1)} %get-tuple-element.100), channel_id=1, source_target_pairs={{0,8},{8,16},{16,24},{1,9},{9,17},{17,25},{2,10},{10,18},{18,26},{... | collective-permute-start | bytes 442376 | tf_op jit(solution)/shard_map/ppermute | solution.py:485
  89.1 1.1 copy.15
  90.2 1.1 copy.16
  91.4 0.6 slice_bitcast_fusion.3
  92.0 0.0 collective-permute-done.5.top_ref
  92.0 0.7 fusion.1
  92.8 0.7 copy-done.2
  93.4 1.3 scatter-add.14
  94.8 0.0 collective-permute-done.6.bottom_ref
  94.8 0.8 fusion
  95.6 0.1 scatter-add.19
  95.6 0.0 copy-start.15
  95.7 0.6 copy-done.15
  96.3 1.3 scatter-add.15
  97.6 1.8 %collective-permute-start.7 = (f32[16,512]{1,0:T(8,128)}, f32[16,512]{1,0:T(8,128)S(1)}, u32[]{:S(2)}, u32[]{:S(2)}) collective-permute-start(f32[16,512]{1,0:T(8,128)} %scatter-add.15), channel_id=1, source_target_pairs={{0,1},{1,2},{2,3},{3,4},{4,5},{5,6},{6,7},{7,0},{8,9},{9,10},{10,1... | collective-permute-start | bytes 98312 | tf_op jit(solution)/shard_map/ppermute | solution.py:491
  99.4 2.9 %collective-permute-start.8 = (f32[16,512]{1,0:T(8,128)}, f32[16,512]{1,0:T(8,128)S(1)}, u32[]{:S(2)}, u32[]{:S(2)}) collective-permute-start(f32[16,512]{1,0:T(8,128)} %copy-done.15), channel_id=1, source_target_pairs={{1,0},{2,1},{3,2},{4,3},{5,4},{6,5},{7,6},{0,7},{9,8},{10,9},{11,1... | collective-permute-start | bytes 98312 | tf_op jit(solution)/shard_map/ppermute | solution.py:492
  102.3 2.3 %collective-permute-done.7.refs_0_.left_ref = f32[16,512]{1,0:T(8,128)S(1)} collective-permute-done((f32[16,512]{1,0:T(8,128)}, f32[16,512]{1,0:T(8,128)S(1)}, u32[]{:S(2)}, u32[]{:S(2)}) %collective-permute-start.7) | collective-permute-done | bytes 32800 | tf_op jit(solution)/shard_map/ppermute | solution.py:491
  104.6 0.0 collective-permute-done.8.refs_1_.right_ref
  104.6 0.6 copy-done.8
  105.3 1.8 %all-to-all-done.1.parts_ref = bf16[16,208,128]{2,1,0:T(8,128)(2,1)S(1)} async-done(((bf16[16,208,128]{2,1,0:T(8,128)(2,1)}), bf16[16,208,128]{2,1,0:T(8,128)(2,1)S(1)}, u32[]{:S(2)}, u32[]{:S(2)}) %all-to-all-start.1) | async-done | bytes 852000 | tf_op jit(solution)/shard_map/all_to_all | solution.py:436
  107.0 0.8 copy-done.9
  107.8 1.0 totals.1
  108.8 7.7 %all-to-all-start.2 = ((bf16[16,208,128]{2,1,0:T(8,128)(2,1)}), bf16[16,208,128]{2,1,0:T(8,128)(2,1)S(1)}, u32[]{:S(2)}, u32[]{:S(2)}) async-start(bf16[16,208,128]{2,1,0:T(8,128)(2,1)} %totals.1), calls=%async_computation.2 | async-start | bytes 1703936 | tf_op jit(solution)/shard_map/all_to_all | solution.py:494
  116.5 0.0 copy-start.3
  116.5 0.9 copy-done.3
  117.4 1.0 copy-done.6
  118.4 0.8 copy-done.10
  119.2 1.6 %copy-done.11 = bf16[2048,512]{1,0:T(8,128)(2,1)S(1)} copy-done((bf16[2048,512]{1,0:T(8,128)(2,1)S(1)}, bf16[2048,512]{1,0:T(8,128)(2,1)}, u32[]{:S(2)}) %copy-start.11) | copy-done | bytes 2097176
  120.8 6.3 %latent.1 = bf16[2048,512]{1,0:T(8,128)(2,1)} custom-call(bf16[2048,512]{1,0:T(8,128)(2,1)S(1)} %copy-done.11, bf16[2592,512]{1,0:T(8,128)(2,1)S(1)} %copy-done.1, bf16[144,512]{1,0:T(8,128)(2,1)S(1)} %copy-done.3, bf16[144,512]{1,0:T(8,128)(2,1)} %collective-permute-done.6.bottom_ref, f32[16,512]{1,0:T(8,128)S(1)} %collective-permute-done.7.refs_0_.left_ref, ...), custom_call_target="tpu_custom_call" | custom-call | flops 5767499776 | tf_op jit(solution)/shard_map/latent/pallas_call | solution.py:347
  127.0 8.4 %all-to-all-done.2.own_ref = bf16[16,208,128]{2,1,0:T(8,128)(2,1)S(1)} async-done(((bf16[16,208,128]{2,1,0:T(8,128)(2,1)}), bf16[16,208,128]{2,1,0:T(8,128)(2,1)S(1)}, u32[]{:S(2)}, u32[]{:S(2)}) %all-to-all-start.2) | async-done | bytes 852000 | tf_op jit(solution)/shard_map/all_to_all | solution.py:494
  135.5 0.0 collective-permute-start.9
  135.5 2.4 %collective-permute-done.9.sibling_ref = bf16[16,208,128]{2,1,0:T(8,128)(2,1)S(1)} collective-permute-done((bf16[16,208,128]{2,1,0:T(8,128)(2,1)S(1)}, bf16[16,208,128]{2,1,0:T(8,128)(2,1)S(1)}, u32[]{:S(2)}, u32[]{:S(2)}) %collective-permute-start.9) | collective-permute-done | bytes 852000 | tf_op jit(solution)/shard_map/ppermute | solution.py:500
  137.9 2.1 %unpack.1 = (f32[616,512]{1,0:T(8,128)}, f32[512,512]{1,0:T(8,128)}, f32[512,512]{1,0:T(8,128)}, f32[9,512]{1,0:T(8,128)}) custom-call(s32[1]{0:T(128)} %bitcast.core_ref, bf16[16,208,128]{2,1,0:T(8,128)(2,1)S(1)} %all-to-all-done.2.own_ref, bf16[16,208,128]{2,1,0:T(8,128)(2,1)S(1)} %collective-permute-done.9.sibling_ref), custom_call_target="tpu_custom_call" | custom-call | flops 3460499968 | tf_op jit(solution)/shard_map/unpack/pallas_call | solution.py:399
  (22 shorter events, 0.1 us)
Async XLA Ops:
  1.7 10.9 %collective-permute-start = (bf16[16,512]{1,0:T(8,128)(2,1)S(1)}, bf16[16,512]{1,0:T(8,128)(2,1)S(1)}, u32[]{:S(2)}, u32[]{:S(2)}) collective-permute-start(bf16[16,512]{1,0:T(8,128)(2,1)S(1)} %bitcast.30), channel_id=1, source_target_pairs={{0,1},{1,2},{2,3},{3,4},{4,5},{5,6},{6,7},{7,0},{8,9},{9,10},{10,1... | collective-permute-start | bytes 49160 | tf_op jit(solution)/shard_map/ppermute | solution.py:451
  4.7 7.9 %collective-permute-start.1 = (bf16[16,512]{1,0:T(8,128)(2,1)S(1)}, bf16[16,512]{1,0:T(8,128)(2,1)S(1)}, u32[]{:S(2)}, u32[]{:S(2)}) collective-permute-start(bf16[16,512]{1,0:T(8,128)(2,1)S(1)} %bitcast.31), channel_id=1, source_target_pairs={{1,0},{2,1},{3,2},{4,3},{5,4},{6,5},{7,6},{0,7},{9,8},{10,9},{11,1... | collective-permute-start | bytes 49160 | tf_op jit(solution)/shard_map/ppermute | solution.py:452
  8.5 1.1 copy-start.4
  12.6 3.7 %copy-start = (bf16[16,128,512]{2,1,0:T(8,128)(2,1)S(1)}, bf16[16,128,512]{2,1,0:T(8,128)(2,1)}, u32[]{:S(2)}) copy-start(bf16[16,128,512]{2,1,0:T(8,128)(2,1)} %param.23) | copy-start | bytes 6291460
  12.6 10.2 %copy-start.5 = (bf16[512,512]{1,0:T(8,128)(2,1)S(1)}, bf16[512,512]{1,0:T(8,128)(2,1)}, u32[]{:S(2)}) copy-start(bf16[512,512]{1,0:T(8,128)(2,1)} %wp_ref.3) | copy-start | bytes 1572868
  12.6 10.1 %copy-start.7 = (f32[9,512]{1,0:T(8,128)S(1)}, f32[9,512]{1,0:T(8,128)}, u32[]{:S(2)}) copy-start(f32[9,512]{1,0:T(8,128)} %wd_hbm.1) | copy-start | bytes 55300
  12.6 36.8 %all-to-all-start = ((bf16[32,32,640]{2,1,0:T(8,128)(2,1)}), bf16[32,32,640]{2,1,0:T(8,128)(2,1)}, u32[]{:S(2)}, u32[]{:S(2)}) async-start(bf16[32,32,640]{2,1,0:T(8,128)(2,1)} %bitcast.6), calls=%async_computation | async-start | bytes 2621440 | tf_op jit(solution)/shard_map/all_to_all | solution.py:457
  16.4 6.3 %collective-permute-start.3 = (bf16[144,512]{1,0:T(8,128)(2,1)S(1)}, bf16[144,512]{1,0:T(8,128)(2,1)S(1)}, u32[]{:S(2)}, u32[]{:S(2)}) collective-permute-start(bf16[144,512]{1,0:T(8,128)(2,1)S(1)} %get-tuple-element.113), channel_id=1, source_target_pairs={{8,0},{16,8},{24,16},{9,1},{17,9},{25,17},{10,2},{18,10},{26,18},{... | collective-permute-start | bytes 442376 | tf_op jit(solution)/shard_map/ppermute | solution.py:467
  17.7 5.0 %collective-permute-start.2 = (bf16[144,512]{1,0:T(8,128)(2,1)S(1)}, bf16[144,512]{1,0:T(8,128)(2,1)S(1)}, u32[]{:S(2)}, u32[]{:S(2)}) collective-permute-start(bf16[144,512]{1,0:T(8,128)(2,1)S(1)} %get-tuple-element.114), channel_id=1, source_target_pairs={{0,8},{8,16},{16,24},{1,9},{9,17},{17,25},{2,10},{10,18},{18,26},{... | collective-permute-start | bytes 442376 | tf_op jit(solution)/shard_map/ppermute | solution.py:466
  32.2 1.5 %copy-start.12 = (bf16[2592,512]{1,0:T(8,128)(2,1)}, bf16[2592,512]{1,0:T(8,128)(2,1)S(1)}, u32[]{:S(2)}) copy-start(bf16[2592,512]{1,0:T(8,128)(2,1)S(1)} %get-tuple-element.80.cot_hbm) | copy-start | bytes 7962628
  33.7 1.5 %copy-start.13 = (bf16[2592,512]{1,0:T(8,128)(2,1)}, bf16[2592,512]{1,0:T(8,128)(2,1)S(1)}, u32[]{:S(2)}) copy-start(bf16[2592,512]{1,0:T(8,128)(2,1)S(1)} %get-tuple-element.81.gm_hbm) | copy-start | bytes 7962628
  35.2 1.3 copy-start.14
  75.4 2.7 %collective-permute-start.4 = (bf16[2,1664,128]{2,1,0:T(8,128)(2,1)}, bf16[2,1664,128]{2,1,0:T(8,128)(2,1)S(1)}, u32[]{:S(2)}, u32[]{:S(2)}) collective-permute-start(bf16[2,1664,128]{2,1,0:T(8,128)(2,1)} %get-tuple-element.83), channel_id=1, source_target_pairs={{0,8},{8,0},{1,9},{9,1},{2,10},{10,2},{3,11},{11,3},{4,12},{12,4},... | collective-permute-start | bytes 2555912 | tf_op jit(solution)/shard_map/ppermute | solution.py:428
  78.0 6.1 %copy-start.1 = (bf16[2592,512]{1,0:T(8,128)(2,1)S(1)}, bf16[2592,512]{1,0:T(8,128)(2,1)}, u32[]{:S(2)}) copy-start(bf16[2592,512]{1,0:T(8,128)(2,1)} %get-tuple-element.90.mix_ref) | copy-start | bytes 7962628
  80.4 26.6 %all-to-all-start.1 = ((bf16[16,208,128]{2,1,0:T(8,128)(2,1)}), bf16[16,208,128]{2,1,0:T(8,128)(2,1)S(1)}, u32[]{:S(2)}, u32[]{:S(2)}) async-start(bf16[16,208,128]{2,1,0:T(8,128)(2,1)} %bitcast.29), calls=%async_computation.1 | async-start | bytes 1703936 | tf_op jit(solution)/shard_map/all_to_all | solution.py:436
  84.8 10.0 %collective-permute-start.6 = (bf16[144,512]{1,0:T(8,128)(2,1)}, bf16[144,512]{1,0:T(8,128)(2,1)}, u32[]{:S(2)}, u32[]{:S(2)}) collective-permute-start(bf16[144,512]{1,0:T(8,128)(2,1)} %get-tuple-element.99), channel_id=1, source_target_pairs={{8,0},{16,8},{24,16},{9,1},{17,9},{25,17},{10,2},{18,10},{26,18},{... | collective-permute-start | bytes 442376 | tf_op jit(solution)/shard_map/ppermute | solution.py:486
  86.1 6.0 %collective-permute-start.5 = (bf16[144,512]{1,0:T(8,128)(2,1)S(1)}, bf16[144,512]{1,0:T(8,128)(2,1)S(1)}, u32[]{:S(2)}, u32[]{:S(2)}) collective-permute-start(bf16[144,512]{1,0:T(8,128)(2,1)S(1)} %get-tuple-element.100), channel_id=1, source_target_pairs={{0,8},{8,16},{16,24},{1,9},{9,17},{17,25},{2,10},{10,18},{18,26},{... | collective-permute-start | bytes 442376 | tf_op jit(solution)/shard_map/ppermute | solution.py:485
  92.8 0.7 copy-start.2
  95.6 0.6 copy-start.15
  97.6 7.0 %collective-permute-start.7 = (f32[16,512]{1,0:T(8,128)}, f32[16,512]{1,0:T(8,128)S(1)}, u32[]{:S(2)}, u32[]{:S(2)}) collective-permute-start(f32[16,512]{1,0:T(8,128)} %scatter-add.15), channel_id=1, source_target_pairs={{0,1},{1,2},{2,3},{3,4},{4,5},{5,6},{6,7},{7,0},{8,9},{9,10},{10,1... | collective-permute-start | bytes 98312 | tf_op jit(solution)/shard_map/ppermute | solution.py:491
  99.4 5.2 %collective-permute-start.8 = (f32[16,512]{1,0:T(8,128)}, f32[16,512]{1,0:T(8,128)S(1)}, u32[]{:S(2)}, u32[]{:S(2)}) collective-permute-start(f32[16,512]{1,0:T(8,128)} %copy-done.15), channel_id=1, source_target_pairs={{1,0},{2,1},{3,2},{4,3},{5,4},{6,5},{7,6},{0,7},{9,8},{10,9},{11,1... | collective-permute-start | bytes 98312 | tf_op jit(solution)/shard_map/ppermute | solution.py:492
  104.6 0.6 copy-start.8
  107.0 0.8 copy-start.9
  108.8 26.7 %all-to-all-start.2 = ((bf16[16,208,128]{2,1,0:T(8,128)(2,1)}), bf16[16,208,128]{2,1,0:T(8,128)(2,1)S(1)}, u32[]{:S(2)}, u32[]{:S(2)}) async-start(bf16[16,208,128]{2,1,0:T(8,128)(2,1)} %totals.1), calls=%async_computation.2 | async-start | bytes 1703936 | tf_op jit(solution)/shard_map/all_to_all | solution.py:494
  116.5 0.9 copy-start.3
  117.4 1.0 copy-start.6
  118.4 0.8 copy-start.10
  119.2 1.6 %copy-start.11 = (bf16[2048,512]{1,0:T(8,128)(2,1)S(1)}, bf16[2048,512]{1,0:T(8,128)(2,1)}, u32[]{:S(2)}) copy-start(bf16[2048,512]{1,0:T(8,128)(2,1)} %get-tuple-element.92.grid_ref) | copy-start | bytes 6291460
  135.5 2.4 %collective-permute-start.9 = (bf16[16,208,128]{2,1,0:T(8,128)(2,1)S(1)}, bf16[16,208,128]{2,1,0:T(8,128)(2,1)S(1)}, u32[]{:S(2)}, u32[]{:S(2)}) collective-permute-start(bf16[16,208,128]{2,1,0:T(8,128)(2,1)S(1)} %all-to-all-done.2.own_ref), channel_id=1, source_target_pairs={{0,8},{8,0},{1,9},{9,1},{2,10},{10,2},{3,11},{11,3},{4,12},{12,4},... | collective-permute-start | bytes 2555912 | tf_op jit(solution)/shard_map/ppermute | solution.py:500

commit v2 on v1

--- a/solution.py
+++ b/solution.py
@@ -85,15 +85,38 @@
     )(places, rows)
 
 
+PAD = 16
+CHUNK = 32
+
+
+def shifted(ref, n, row, start, by, size):
+    return ref[n, row, pl.ds(start + by, size), :]
+
+
 def grid_grad_kernel(
-    clat, clon, wide, cot_ref, east_ref, west_ref, north_ref, south_ref, wp_ref, wd_ref,
-    cot_ext, gm_ref, gg_ref, east, west,
+    clat, clon, wide, one_ref, cot_ref, east_ref, west_ref, north_ref, south_ref, wp_ref, wd_ref,
+    cott_hbm, gm_hbm, gg_hbm, cott_ref, gm_ref, gg_ref, cot_ext, east, west, sems,
 ):
     width = wp_ref.shape[0]
     w_point = wp_ref[...]
+    one = one_ref[0]
     east[...] = east_ref[...].astype(f32)
     west[...] = west_ref[...].astype(f32)
     line = lax.broadcasted_iota(i32, (wide - clon, width), 0)
+    puts = [
+        pltpu.make_async_copy(source, target, sems.at[i])
+        for i, (source, target) in enumerate(
+            ((gg_ref, gg_hbm), (gm_ref, gm_hbm), (cott_ref, cott_hbm))
+        )
+    ]
+
+    def mixed_grad(e, rows):
+        g = dot(rows, w_point, (1, 1)).astype(bf16).astype(f32)
+        for n in range(width // LANES):
+            cols = slice(n * LANES, (n + 1) * LANES)
+            gm_ref[n, e, 0:PAD, :] = g[clon:, cols]
+            gm_ref[n, e, PAD : PAD + clon, :] = g[:clon, cols]
+            gm_ref[n, e, PAD + clon :, :] = g[clon:, cols]
 
     def matmul(i, carry):
         at = pl.multiple_of((i + 1) * wide, 16)
@@ -102,49 +125,66 @@
             line == 0, east[pl.ds(i, 1), :], jnp.where(line == wide - clon - 1, west[pl.ds(i, 1), :], 0.0)
         )
         cot_ext[pl.ds(at + clon, wide - clon), :] = tail.astype(bf16)
-        at = pl.ds(at, wide)
-        gm_ref[at, :] = dot(cot_ext[at, :], w_point, (1, 1)).astype(bf16)
-        return carry
-
-    for ref, at in ((north_ref, 0), (south_ref, (clat + 1) * wide)):
-        cot_ext[at : at + wide, :] = ref[...]
-        gm_ref[at : at + wide, :] = dot(ref[...], w_point, (1, 1)).astype(bf16)
+        mixed_grad(i + 1, cot_ext[pl.ds(at, wide), :])
+        return carry
+
+    for ref, e in ((north_ref, 0), (south_ref, clat + 1)):
+        cot_ext[e * wide : (e + 1) * wide, :] = ref[...]
+        mixed_grad(e, ref[...])
+    used = (clat + 2) * wide
+    cot_ext[used:, :] = jnp.zeros((cot_ext.shape[0] - used, width), bf16)
     lax.fori_loop(0, clat, matmul, 0)
+    puts[1].start()
 
     def conv(i, carry):
-        out_at = pl.ds(pl.multiple_of(i * clon, 16), clon)
-        mid = pl.ds(pl.multiple_of((i + 1) * wide, 16), wide)
-        for lane in range(0, width, LANES):
-            cols = slice(lane, lane + LANES)
-            sums = []
-            for b in range(3):
-                total = None
+        for n in range(width // LANES):
+            cols = slice(n * LANES, (n + 1) * LANES)
+            for j in range(0, clon, CHUNK):
+                at = pl.ds(pl.multiple_of(i * clon + j, CHUNK), CHUNK)
+                out = cot_ref[at, cols].astype(f32)
                 for a in range(3):
-                    at = pl.ds(pl.multiple_of((i + 2 - a) * wide, 16), wide)
-                    term = wd_ref[3 * a + b : 3 * a + b + 1, cols] * gm_ref[at, cols].astype(f32)
-                    total = term if total is None else total + term
-                sums.append(total)
-            out = cot_ext[mid, cols].astype(f32) + sums[1]
-            out = out + pltpu.roll(sums[2], 1, 0) + pltpu.roll(sums[0], wide - 1, 0)
-            gg_ref[out_at, cols] = out[:clon].astype(bf16)
+                    for b in range(3):
+                        k = 3 * a + b
+                        g = shifted(gm_ref, n, i + 2 - a, PAD + j, (1 - b) * one, CHUNK)
+                        out = out + wd_ref[k : k + 1, cols] * g
+                gg_ref[at, cols] = out.astype(bf16)
         return carry
 
     lax.fori_loop(0, clat, conv, 0)
-
-
-def grid_grad(cot, sides, w_point, w_depth, clat, clon, wide):
+    puts[0].start()
+
+    def transpose(k, carry):
+        at = pl.ds(pl.multiple_of(k * LANES, LANES), LANES)
+        cott_ref[:, at] = cot_ext[at, :].T
+        return carry
+
+    lax.fori_loop(0, cot_ext.shape[0] // LANES, transpose, 0)
+    puts[2].start()
+    for put in puts:
+        put.wait()
+
+
+def grid_grad(one, cot, sides, w_point, w_depth, clat, clon, wide):
     width = w_point.shape[0]
-    ext = jax.ShapeDtypeStruct(((clat + 2) * wide, width), bf16)
+    ext_rows = round_up((clat + 2) * wide, LANES)
+    outs = (
+        jax.ShapeDtypeStruct((width, ext_rows), bf16),
+        jax.ShapeDtypeStruct((width // LANES, clat + 2, clon + 2 * PAD, LANES), f32),
+        jax.ShapeDtypeStruct((clat * clon, width), bf16),
+    )
     return pl.pallas_call(
         functools.partial(grid_grad_kernel, clat, clon, wide),
-        out_shape=(ext, ext, jax.ShapeDtypeStruct((clat * clon, width), bf16)),
-        in_specs=[vmem()] * 7,
-        out_specs=(vmem(),) * 3,
-        scratch_shapes=[pltpu.VMEM((clat, width), f32)] * 2,
-        compiler_params=params(8),
+        out_shape=outs,
+        in_specs=[smem()] + [vmem()] * 7,
+        out_specs=(anywhere(),) * 3,
+        scratch_shapes=[pltpu.VMEM(x.shape, x.dtype) for x in outs]
+        + [pltpu.VMEM((ext_rows, width), bf16)]
+        + [pltpu.VMEM((clat, width), f32)] * 2
+        + [pltpu.SemaphoreType.DMA((3,))],
+        compiler_params=params(50),
         cost_estimate=cost(10),
         name="grid_grad",
-    )(cot, *sides, w_point, w_depth)
+    )(one, cot, *sides, w_point, w_depth)
 
 
 def write_halves(core, total, start, mine_ref, other_ref, first=0, size=None):
@@ -164,48 +204,61 @@
 
 
 def owner_kernel(
-    spec, clat, clon, wide, core_ref, rows_hbm, wi_hbm, wo_hbm, gg_hbm, cot_hbm, gm_hbm, wd_hbm,
+    spec, clat, clon, wide, core_ref, rows_hbm, wit_hbm, wot_hbm, wo_hbm, gg_hbm, wd_hbm, gm_hbm, cott_hbm,
     grid_hbm, mix_hbm, east_hbm, west_hbm, mine_hbm, other_hbm,
-    rows_ref, wi_ref, wo_ref, gg_ref, cot_ref, gm_ref, wd_ref,
-    padded, mix_ref, east_ref, west_ref, mine_ref, other_ref,
-    emb_ref, gi, go, gp, gd, sems,
+    rows_ref, wit_ref, wot_ref, wo_ref, gg_ref, wd_ref, gm_ref, cott_ref,
+    grid_ref, mix_ref, east_ref, west_ref, mine_ref, other_ref,
+    padded, emb_ref, gi, gi_out, go, gp, gd, sems,
 ):
-    core = core_ref[0]
+    core, one = core_ref[0], core_ref[1]
     slots, spec_wide = rows_ref.shape
     cells, width = gg_ref.shape
-    sources = rows_hbm, wi_hbm, wo_hbm, gg_hbm, wd_hbm, cot_hbm, gm_hbm
-    targets = rows_ref, wi_ref, wo_ref, gg_ref, wd_ref, cot_ref, gm_ref
+    sources = rows_hbm, wit_hbm, wot_hbm, wo_hbm, gg_hbm, wd_hbm, gm_hbm, cott_hbm
+    targets = rows_ref, wit_ref, wot_ref, wo_ref, gg_ref, wd_ref, gm_ref, cott_ref
     loads = [
         pltpu.make_async_copy(source, target, sems.at[i])
         for i, (source, target) in enumerate(zip(sources, targets))
     ]
     for load in loads:
         load.start()
+    outs = (
+        (grid_ref, grid_hbm), (mix_ref, mix_hbm), (east_ref, east_hbm), (west_ref, west_hbm),
+        (mine_ref, mine_hbm), (other_ref, other_hbm),
+    )
+    puts = [
+        pltpu.make_async_copy(source, target, sems.at[len(loads) + i])
+        for i, (source, target) in enumerate(outs)
+    ]
     gi[...] = jnp.zeros_like(gi)
     go[...] = jnp.zeros_like(go)
     gd[...] = jnp.zeros_like(gd)
-    gp[...] = jnp.zeros_like(gp)
-    padded[pl.ds(0, 2 * clon), :] = jnp.zeros((2 * clon, width), bf16)
-    padded[pl.ds((clat + 2) * clon, 2 * clon), :] = jnp.zeros((2 * clon, width), bf16)
-    for load in loads[:4]:
+    blocks = width // LANES
+    side = jnp.zeros((blocks, clat + 4, PAD, LANES), f32)
+    padded[:, :, :PAD, :] = side
+    padded[:, :, PAD + clon :, :] = side
+    for e in (0, 1, clat + 2, clat + 3):
+        padded[:, e, PAD : PAD + clon, :] = jnp.zeros((blocks, clon, LANES), f32)
+    used = (clat + 2) * wide
+    mix_ref[used:, :] = jnp.zeros((mix_ref.shape[0] - used, width), bf16)
+    for load in loads[:5]:
         load.wait()
 
-    step = min(256, slots)
+    step = min(512, slots)
 
     def encode(t, carry):
         at = pl.ds(pl.multiple_of(t * step, step), step)
         rows = rows_ref[at, :]
-        preact = dot(rows, wi_ref[...])
+        preact = dot(wit_ref[...], rows, (1, 1))
         sig = 1.0 / (1.0 + jnp.exp(-preact))
         hidden = (preact * sig).astype(bf16)
-        emb_ref[at, :] = dot(hidden, wo_ref[...]).astype(bf16)
+        emb_ref[:, at] = dot(wot_ref[...], hidden).astype(bf16)
         place = rows[:, spec : spec + 1].astype(f32) * clon + rows[:, spec + 1 : spec + 2].astype(f32)
         hits = place.astype(i32) == lax.broadcasted_iota(i32, (step, cells), 1)
         g_emb = dot(hits.astype(f32).astype(bf16), gg_ref[...]).astype(bf16)
-        go[...] += dot(hidden, g_emb, (0, 0))
-        g_hid = dot(g_emb, wo_ref[...], (1, 1))
+        go[...] += dot(hidden, g_emb)
+        g_hid = dot(wo_ref[...], g_emb, (1, 1))
         g_pre = (g_hid * (sig * (1.0 + preact * (1.0 - sig)))).astype(bf16)
-        gi[...] += dot(rows, g_pre, (0, 0))
+        gi[...] += dot(g_pre, rows)
         return carry
 
     lax.fori_loop(0, slots // step, encode, 0)
@@ -215,108 +268,104 @@
     lane = lax.broadcasted_iota(i32, (16, LANES), 1)
     pick = jnp.where(lane == col, float(clon), jnp.where(lane == col + 1, 1.0, 0.0)).astype(bf16)
     place = dot(pick, last, (1, 1))[0:1, :].astype(i32)
-    block = 2 * clon
+    block = 4 * clon
 
     def bins(t, carry):
         cell = lax.broadcasted_iota(i32, (block, slots), 0) + t * block
         hits = (place == cell).astype(f32).astype(bf16)
-        grid = dot(hits, emb_ref[...]).astype(bf16)
-        padded[pl.ds(pl.multiple_of((t + 1) * block, 16), block), :] = grid
-        return carry
-
-    lax.fori_loop(0, clat // 2, bins, 0)
-    put_grid = pltpu.make_async_copy(padded.at[pl.ds(2 * clon, cells)], grid_hbm, sems.at[7])
-    put_grid.start()
-    for load in loads[4:]:
+        grid = dot(hits, emb_ref[...], (1, 1)).astype(bf16)
+        grid_ref[pl.ds(pl.multiple_of(t * block, 16), block), :] = grid
+        for n in range(blocks):
+            part = grid[:, n * LANES : (n + 1) * LANES].astype(f32)
+            padded[n, pl.ds(4 * t + 2, 4), PAD : PAD + clon, :] = part.reshape(4, clon, LANES)
+        return carry
+
+    lax.fori_loop(0, cells // block, bins, 0)
+    puts[0].start()
+    for load in loads[5:]:
         load.wait()
 
-    fill = jnp.zeros((wide - clon, LANES), f32)
-
     def conv(e, carry):
-        out_at = pl.ds(pl.multiple_of(e * wide, 16), wide)
-        for lane in range(0, width, LANES):
-            cols = slice(lane, lane + LANES)
-            near = [
-                padded[pl.ds(pl.multiple_of((e + a) * clon, 16), clon), cols].astype(f32)
-                for a in range(3)
-            ]
-            sums = []
-            for b in range(3):
-                total = None
+        for n in range(blocks):
+            cols = slice(n * LANES, (n + 1) * LANES)
+            weights = [wd_ref[k : k + 1, cols] for k in range(9)]
+            taps = [gd[8 * k : 8 * k + 8, cols] for k in range(9)]
+            for j in range(0, clon, CHUNK):
+                at = PAD + j
+                grads = [shifted(gm_ref, n, e, at, (1 - b) * one, CHUNK) for b in range(3)]
+                mixed = None
                 for a in range(3):
-                    term = wd_ref[3 * a + b : 3 * a + b + 1, cols] * near[a]
-                    total = term if total is None else total + term
-                sums.append(jnp.concatenate([total, fill], axis=0))
-            mixed = sums[1] + pltpu.roll(sums[2], wide - 1, 0) + pltpu.roll(sums[0], 1, 0)
-            mix_ref[out_at, cols] = mixed.astype(bf16)
-            east_ref[e, :, cols] = mixed[clon : clon + 8]
-            west_ref[e, :, cols] = mixed[wide - 8 : wide]
-            g_mid = gm_ref[out_at, cols].astype(f32)
-            for b, g in ((0, pltpu.roll(g_mid, wide - 1, 0)), (1, g_mid), (2, pltpu.roll(g_mid, 1, 0))):
-                g = g[:clon]
+                    for b in range(3):
+                        k = 3 * a + b
+                        cell = shifted(padded, n, e + a, at, (b - 1) * one, CHUNK)
+                        mixed = weights[k] * cell if mixed is None else mixed + weights[k] * cell
+                    middle = padded[n, e + a, at : at + CHUNK, :]
+                    for b in range(3):
+                        k = 3 * a + b
+                        part = (grads[b] * middle).reshape(CHUNK // 8, 8, LANES)
+                        taps[k] = taps[k] + jnp.sum(part, axis=0)
+                out_at = pl.ds(pl.multiple_of(e * wide + j, 16), CHUNK)
+                mix_ref[out_at, cols] = mixed.astype(bf16)
+            for k in range(9):
+                gd[8 * k : 8 * k + 8, cols] = taps[k]
+            ends = []
+            for b, at in ((0, PAD + clon), (2, PAD - 8)):
+                end = None
                 for a in range(3):
-                    part = jnp.sum((g * near[a]).reshape(clon // 8, 8, LANES), axis=0)
-                    gd[8 * (3 * a + b) : 8 * (3 * a + b) + 8, cols] += part
+                    term = weights[3 * a + b] * shifted(padded, n, e + a, at, (b - 1) * one, 8)
+                    end = term if end is None else end + term
+                ends.append(end)
+            east_ref[e, :, cols] = ends[0]
+            west_ref[e, :, cols] = ends[1]
+            out_at = pl.ds(pl.multiple_of(e * wide + clon, 16), wide - clon)
+            mix_ref[out_at, cols] = jnp.concatenate(ends, axis=0).astype(bf16)
         return carry
 
     lax.fori_loop(0, clat + 2, conv, 0)
-    puts = [
-        pltpu.make_async_copy(mix_ref, mix_hbm, sems.at[8]),
-        pltpu.make_async_copy(east_ref, east_hbm, sems.at[9]),
-        pltpu.make_async_copy(west_ref, west_hbm, sems.at[10]),
-    ]
-    for put in puts:
+    for put in puts[1:4]:
         put.start()
-
-    def point(t, carry):
-        at = pl.ds(pl.multiple_of(t * 3 * wide, 16), 3 * wide)
-        gp[...] += dot(mix_ref[at, :], cot_ref[at, :], (0, 0))
-        return carry
-
-    lax.fori_loop(0, (clat + 2) // 3, point, 0)
+    gp[...] = dot(cott_ref[...], mix_ref[...]).T
+    gi_out[...] = gi[...].T
+    gi_rows = round_up(spec, 16)
     taps = [jnp.sum(gd[8 * k : 8 * k + 8, :], axis=0, keepdims=True) for k in range(9)]
     gd[0:16, :] = jnp.concatenate(taps + [jnp.zeros((7, width), f32)], axis=0)
     start = 0
-    for total, size in ((go, width), (gi, round_up(spec, 16)), (gp, width), (gd, 16)):
+    for total, size in ((go, width), (gi_out, gi_rows), (gp, width), (gd, 16)):
         write_halves(core, total, start, mine_ref, other_ref, 0, size)
         start += size
     clear_tail(start, mine_ref, other_ref)
-    puts += [put_grid] + [
-        pltpu.make_async_copy(mine_ref, mine_hbm, sems.at[11]),
-        pltpu.make_async_copy(other_ref, other_hbm, sems.at[12]),
-    ]
-    for put in puts[-2:]:
+    for put in puts[4:]:
         put.start()
     for put in puts:
         put.wait()
 
 
-def owner_part(core, rows, w_in, w_out, g_grid, cot_ext, gm_ext, w_depth, spec, clat, clon, wide, out_rows):
-    slots, spec_wide = rows.shape
-    width = w_out.shape[0]
+def owner_part(core, operands, spec, clat, clon, wide, out_rows):
+    slots, spec_wide = operands[0].shape
+    width = operands[2].shape[0]
     half = jax.ShapeDtypeStruct((width // LANES // 2, out_rows, LANES), bf16)
     column = jax.ShapeDtypeStruct((clat + 2, 8, width), f32)
-    operands = rows, w_in, w_out, g_grid, cot_ext, gm_ext, w_depth
-    padded = pltpu.VMEM(((clat + 4) * clon, width), bf16)
-    outs = jax.ShapeDtypeStruct(cot_ext.shape, bf16), column, column, half, half
+    grid = jax.ShapeDtypeStruct((clat * clon, width), bf16)
+    ext = jax.ShapeDtypeStruct(operands[-1].shape[::-1], bf16)
+    outs = grid, ext, column, column, half, half
     return pl.pallas_call(
         functools.partial(owner_kernel, spec, clat, clon, wide),
-        out_shape=(jax.ShapeDtypeStruct((clat * clon, width), bf16),) + outs,
-        in_specs=[smem()] + [anywhere()] * 7,
-        out_specs=(anywhere(),) * 6,
-        scratch_shapes=[pltpu.VMEM(x.shape, x.dtype) for x in operands]
-        + [padded]
-        + [pltpu.VMEM(x.shape, x.dtype) for x in outs]
+        out_shape=outs,
+        in_specs=[smem()] + [anywhere()] * len(operands),
+        out_specs=(anywhere(),) * len(outs),
+        scratch_shapes=[pltpu.VMEM(x.shape, x.dtype) for x in operands + outs]
         + [
-            pltpu.VMEM((slots, width), bf16),
+            pltpu.VMEM((width // LANES, clat + 4, clon + 2 * PAD, LANES), f32),
+            pltpu.VMEM((width, slots), bf16),
+            pltpu.VMEM((width, spec_wide), f32),
             pltpu.VMEM((spec_wide, width), f32),
             pltpu.VMEM((width, width), f32),
             pltpu.VMEM((width, width), f32),
             pltpu.VMEM((72, width), f32),
-            pltpu.SemaphoreType.DMA((13,)),
+            pltpu.SemaphoreType.DMA((len(operands) + len(outs),)),
         ],
         compiler_params=params(56),
-        cost_estimate=cost(22),
+        cost_estimate=cost(20),
         name="owner",
     )(core, *operands)
 
@@ -444,7 +493,8 @@
     cells = clat * clon
     wide = clon + 16
     spec_wide = round_up(spec + 2, LANES)
-    core = lax.axis_index("core").reshape(1)
+    core = jnp.stack([lax.axis_index("core"), jnp.int32(1)])
+    one = jnp.ones((1,), i32)
     east_way, west_way = neighbours("lon", True)
     south_way, north_way = neighbours(LAT, False)
 
@@ -453,7 +503,9 @@
 
     places = jnp.concatenate([owner.reshape(1, rows_here), cell.reshape(1, rows_here)], axis=0)
     outgoing = route(places, spectra.T, tiles, cap, clon, spec_wide)
-    outgoing, from_west, from_east = lax.optimization_barrier((outgoing, from_west, from_east))
+    outgoing, from_west, from_east, w_in, w_out = lax.optimization_barrier(
+        (outgoing, from_west, from_east, w_in, w_out)
+    )
     arrived = lax.all_to_all(
         outgoing.reshape(tiles, cap, spec_wide), ("x", "core", "lon"), 0, 0, tiled=True
     ).reshape(tiles * cap, spec_wide)
@@ -465,25 +517,25 @@
 
     from_north = lax.ppermute(edge_row(clat - 1), LAT, south_way)
     from_south = lax.ppermute(edge_row(0), LAT, north_way)
-    cot_ext, gm_ext, g_grid = grid_grad(
+    cot_t, g_mixed, g_grid = grid_grad(
+        one,
         cotangent.reshape(cells, width),
         (from_east, from_west, from_north, from_south),
         w_point, w_depth, clat, clon, wide,
     )
-    w_in_wide = jnp.pad(w_in, ((0, spec_wide - spec), (0, 0)))
+    w_in_t = jnp.pad(w_in.T, ((0, 0), (0, spec_wide - spec)))
 
     out_rows = round_up(2 * width + round_up(spec, 16) + 16, 16 * tiles * LANES // width)
+    operands = arrived, w_in_t, w_out.T, w_out, g_grid, w_depth, g_mixed, cot_t
     grid, mix_ext, east, west, mine, other = owner_part(
-        core, arrived, w_in_wide, w_out, g_grid, cot_ext, gm_ext, w_depth,
-        spec, clat, clon, wide, out_rows,
+        core, operands, spec, clat, clon, wide, out_rows
     )
     summed = core_sum(mine, other)
     summed, grid, mix_ext, east, west = lax.optimization_barrier((summed, grid, mix_ext, east, west))
     parts = spread(summed)
 
-    ext = mix_ext.reshape(clat + 2, wide, width)
-    top = lax.ppermute(ext[clat + 1], LAT, south_way)
-    bottom = lax.ppermute(ext[0], LAT, north_way)
+    top = lax.ppermute(mix_ext[(clat + 1) * wide : (clat + 2) * wide], LAT, south_way)
+    bottom = lax.ppermute(mix_ext[:wide], LAT, north_way)
 
     def edge_column(own, at):
         return own[1:-1].at[0].add(top[at].astype(f32)).at[-1].add(bottom[at].astype(f32))

time: 141 us -> 138 us (0.979)
  local copies, waits for them, and re-layouts: 21.8 us -> 12.8 us
  waiting for transfers between devices: 30.3 us -> 37.9 us
  starting transfers between devices: 34.4 us -> 30.3 us
  Pallas kernels: 47.8 us -> 50.5 us
    ppermute x1, waiting for transfers between devices: 2.32 us -> 8.5 us  [on_device(): left = lax.ppermute(edge_column(east[:, 0], clon), 'lon', east_way)]
    unnamed x34 -> x26, local copies, waits for them, and re-layouts: 12.3 us -> 6.85 us
    pallas_call x1, Pallas kernels: 9.42 us -> 14.9 us  [grid_grad(): pl.pallas_call(functools.partial(grid_grad_kernel, clat, clon, wide), out...]
    all_to_all x1, waiting for transfers between devices: 12.9 us -> 7.81 us  [on_device(): lax.all_to_all(outgoing.reshape(tiles, cap, spec_wide), ('x', 'core', 'lo...]
    all_to_all x1, waiting for transfers between devices: 8.43 us -> 13 us  [on_device(): full = lax.all_to_all(sent, CHIPS, split_axis=0, concat_axis=0, tiled=True)]
    all_to_all x1, starting transfers between devices: 7.69 us -> 3.62 us  [on_device(): full = lax.all_to_all(sent, CHIPS, split_axis=0, concat_axis=0, tiled=True)]
    scatter-add x4, local copies, waits for them, and re-layouts: 2.76 us -> 0.23 us  [edge_column(): own[1:-1].at[0].add(top[at].astype(f32)).at[-1].add(bottom[at].astype(f32))]
    pallas_call x1, Pallas kernels: 26 us -> 23.7 us  [owner_part(): pl.pallas_call(functools.partial(owner_kernel, spec, clat, clon, wide), o...]
  transfers between devices with their start and end apart: 13 -> 13, of which waited for: 6 -> 7; matrix products, arithmetic and copies ran while one was open for 8% -> 5% of each run, Pallas kernels for 13% -> 17%
where the time goes in v2:
time: 138 us; the launch traced here: 137 us
  Pallas kernels  50.5 us (37%)
  waiting for transfers between devices  37.9 us (27%)
  starting transfers between devices  30.3 us (22%)
  local copies, waits for them, and re-layouts  12.8 us (9%)
  other arithmetic  4.51 us (3%)
    pallas_call x1, Pallas kernels, owner_part(): pl.pallas_call(functools.partial(owner_kernel, spec, clat, clon, wide), o...  23.7 us
    pallas_call x1, Pallas kernels, grid_grad(): pl.pallas_call(functools.partial(grid_grad_kernel, clat, clon, wide), out...  14.9 us
    all_to_all x1, waiting for transfers between devices, on_device(): full = lax.all_to_all(sent, CHIPS, split_axis=0, concat_axis=0, tiled=True)  13 us
    ppermute x1, waiting for transfers between devices, on_device(): left = lax.ppermute(edge_column(east[:, 0], clon), 'lon', east_way)  8.5 us
    all_to_all x1, waiting for transfers between devices, on_device(): lax.all_to_all(outgoing.reshape(tiles, cap, spec_wide), ('x', 'core', 'lo...  7.81 us
    unnamed x26, local copies, waits for them, and re-layouts  6.85 us
    pallas_call x1, Pallas kernels, finish_latent(): pl.pallas_call(functools.partial(latent_kernel, clat, clon, wide), out_sh...  5.4 us
    all_to_all x1, starting transfers between devices, spread(): lax.all_to_all(values, CHIPS, split_axis=0, concat_axis=0, tiled=True)  3.76 us
  transfers between devices with their start and end apart: 13, of which 7 were waited for; matrix products, arithmetic and copies ran while one was open for 5% of the time, Pallas kernels for 17%

profile of v2, /device:TPU:0, one launch (start us, length us, event | category | flops | bytes accessed | tf_op | source)
XLA Modules:
  0.0 136.9 jit_solution(1254787541127716390)
XLA Ops:
  0.6 1.0 fusion.5
  1.7 3.0 %collective-permute-start = (bf16[16,512]{1,0:T(8,128)(2,1)S(1)}, bf16[16,512]{1,0:T(8,128)(2,1)S(1)}, u32[]{:S(2)}, u32[]{:S(2)}) collective-permute-start(bf16[16,512]{1,0:T(8,128)(2,1)S(1)} %bitcast.34), channel_id=1, source_target_pairs={{0,1},{1,2},{2,3},{3,4},{4,5},{5,6},{6,7},{7,0},{8,9},{9,10},{10,1... | collective-permute-start | bytes 49160 | tf_op jit(solution)/shard_map/ppermute | solution.py:501
  4.7 3.1 %collective-permute-start.1 = (bf16[16,512]{1,0:T(8,128)(2,1)S(1)}, bf16[16,512]{1,0:T(8,128)(2,1)S(1)}, u32[]{:S(2)}, u32[]{:S(2)}) collective-permute-start(bf16[16,512]{1,0:T(8,128)(2,1)S(1)} %bitcast.35), channel_id=1, source_target_pairs={{1,0},{2,1},{3,2},{4,3},{5,4},{6,5},{7,6},{0,7},{9,8},{10,9},{11,1... | collective-permute-start | bytes 49160 | tf_op jit(solution)/shard_map/ppermute | solution.py:502
  7.8 0.7 pad_add_fusion.places_ref
  8.5 1.1 copy-done.1
  9.6 2.9 %route.1 = bf16[1024,640]{1,0:T(8,128)(2,1)} custom-call(s32[2,512]{1,0:T(2,128)S(1)} %pad_add_fusion.places_ref, bf16[616,512]{1,0:T(8,128)(2,1)S(1)} %bitcast.29), custom_call_target="tpu_custom_call" | custom-call | flops 3460499968 | tf_op jit(solution)/shard_map/route/pallas_call | solution.py:77
  12.5 0.0 collective-permute-done.west_ref
  12.5 0.0 collective-permute-done.1.east_ref
  12.5 0.0 copy-start.8
  12.5 3.2 %all-to-all-start = ((bf16[32,32,640]{2,1,0:T(8,128)(2,1)}), bf16[32,32,640]{2,1,0:T(8,128)(2,1)S(1)}, u32[]{:S(2)}, u32[]{:S(2)}) async-start(bf16[32,32,640]{2,1,0:T(8,128)(2,1)} %bitcast.6), calls=%async_computation | async-start | bytes 2621440 | tf_op jit(solution)/shard_map/all_to_all | solution.py:509
  15.8 0.1 pad.19.clone
  15.9 1.0 slice_bitcast_fusion
  16.9 0.0 copy-start.2
  16.9 0.0 copy-start.3
  16.9 0.8 pad_maximum_fusion.1
  17.7 1.3 collective-permute-start.3
  19.0 3.0 %collective-permute-start.2 = (bf16[144,512]{1,0:T(8,128)(2,1)}, bf16[144,512]{1,0:T(8,128)(2,1)S(1)}, u32[]{:S(2)}, u32[]{:S(2)}) collective-permute-start(bf16[144,512]{1,0:T(8,128)(2,1)} %get-tuple-element.118), channel_id=1, source_target_pairs={{0,8},{8,16},{16,24},{1,9},{9,17},{17,25},{2,10},{10,18},{18,26},{... | collective-permute-start | bytes 442376 | tf_op jit(solution)/shard_map/ppermute | solution.py:518
  22.1 0.6 pad_add_fusion.1.core_ref
  22.7 0.0 copy-done.9
  22.7 1.0 copy.16
  23.7 0.0 copy-done.8
  23.7 0.3 copy.15
  24.0 0.9 pad.12.wit_hbm
  24.9 0.0 collective-permute-done.3.south_ref
  24.9 0.0 collective-permute-done.2.north_ref
  24.9 0.0 copy-done.2
  24.9 0.0 copy-done.3
  25.0 14.9 %grid_grad.1 = (bf16[512,2688]{1,0:T(8,128)(2,1)}, f32[4,18,160,128]{3,2,1,0:T(8,128)}, bf16[2048,512]{1,0:T(8,128)(2,1)S(1)}) custom-call(s32[1]{0:T(128)} %constant.106.clone.1.one_ref, bf16[2048,512]{1,0:T(8,128)(2,1)} %bitcast.33, bf16[16,512]{1,0:T(8,128)(2,1)S(1)} %collective-permute-done.1.east_ref, ...), custom_call_target="tpu_custom_call" | custom-call | flops 11534999552 | tf_op jit(solution)/shard_map/grid_grad/pallas_call | solution.py:175
  39.9 0.0 copy-start.6
  39.9 1.3 copy-done.6
  41.2 7.8 %all-to-all-done = bf16[32,32,640]{2,1,0:T(8,128)(2,1)S(1)} async-done(((bf16[32,32,640]{2,1,0:T(8,128)(2,1)}), bf16[32,32,640]{2,1,0:T(8,128)(2,1)S(1)}, u32[]{:S(2)}, u32[]{:S(2)}) %all-to-all-start) | async-done | bytes 1310752 | tf_op jit(solution)/shard_map/all_to_all | solution.py:509
  49.0 1.1 copy-done.7
  50.0 23.7 %owner.1 = (bf16[2048,512]{1,0:T(8,128)(2,1)}, bf16[2688,512]{1,0:T(8,128)(2,1)}, f32[18,8,512]{2,1,0:T(8,128)}, f32[18,8,512]{2,1,0:T(8,128)}, bf16[2,1664,128]...) custom-call(s32[2]{0:T(128)} %pad_add_fusion.1.core_ref, bf16[1024,640]{1,0:T(8,128)(2,1)} %bitcast.31, ...), custom_call_target="tpu_custom_call" | custom-call | flops 23069999104 | tf_op jit(solution)/shard_map/owner/pallas_call | solution.py:351
  73.7 0.1 collective-permute-start.4
  73.8 2.6 %collective-permute-done.4 = bf16[2,1664,128]{2,1,0:T(8,128)(2,1)S(1)} collective-permute-done((bf16[2,1664,128]{2,1,0:T(8,128)(2,1)}, bf16[2,1664,128]{2,1,0:T(8,128)(2,1)S(1)}, u32[]{:S(2)}, u32[]{:S(2)}) %collective-permute-start.4) | collective-permute-done | bytes 852000 | tf_op jit(solution)/shard_map/ppermute | solution.py:477
  76.4 2.3 %add_convert_fusion = bf16[2,1664,128]{2,1,0:T(8,128)(2,1)} fusion(bf16[2,1664,128]{2,1,0:T(8,128)(2,1)S(1)} %collective-permute-done.4, bf16[2,1664,128]{2,1,0:T(8,128)(2,1)} %get-tuple-element.86), kind=kLoop, calls=%fused_computation | loop fusion | flops 1703936 | bytes 2555904 | tf_op jit(solution)/shard_map/convert_element_type | solution.py:478
  78.7 3.8 %all-to-all-start.1 = ((bf16[16,208,128]{2,1,0:T(8,128)(2,1)}), bf16[16,208,128]{2,1,0:T(8,128)(2,1)S(1)}, u32[]{:S(2)}, u32[]{:S(2)}) async-start(bf16[16,208,128]{2,1,0:T(8,128)(2,1)} %bitcast.13), calls=%async_computation.1 | async-start | bytes 1703936 | tf_op jit(solution)/shard_map/all_to_all | solution.py:485
  82.5 1.0 fusion.4
  83.5 1.3 collective-permute-start.6
  84.8 3.0 %collective-permute-start.5 = (bf16[144,512]{1,0:T(8,128)(2,1)S(1)}, bf16[144,512]{1,0:T(8,128)(2,1)S(1)}, u32[]{:S(2)}, u32[]{:S(2)}) collective-permute-start(bf16[144,512]{1,0:T(8,128)(2,1)S(1)} %get-tuple-element.104), channel_id=1, source_target_pairs={{0,8},{8,16},{16,24},{1,9},{9,17},{17,25},{2,10},{10,18},{18,26},{... | collective-permute-start | bytes 442376 | tf_op jit(solution)/shard_map/ppermute | solution.py:537
  87.8 0.0 copy-done.10
  87.8 0.2 copy.17
  88.0 0.0 copy-done.11
  88.0 0.2 copy.18
  88.2 0.6 collective-permute-done.5.top_ref
  88.9 0.1 scatter-add.16
  88.9 0.0 collective-permute-done.6.bottom_ref
  89.0 0.1 scatter-add.19
  89.0 0.1 scatter-add.15
  89.1 1.9 %collective-permute-start.7 = (f32[16,512]{1,0:T(8,128)S(1)}, f32[16,512]{1,0:T(8,128)S(1)}, u32[]{:S(2)}, u32[]{:S(2)}) collective-permute-start(f32[16,512]{1,0:T(8,128)S(1)} %scatter-add.15), channel_id=1, source_target_pairs={{0,1},{1,2},{2,3},{3,4},{4,5},{5,6},{6,7},{7,0},{8,9},{9,10},{10,1... | collective-permute-start | bytes 98312 | tf_op jit(solution)/shard_map/ppermute | solution.py:543
  91.0 2.9 %collective-permute-start.8 = (f32[16,512]{1,0:T(8,128)S(1)}, f32[16,512]{1,0:T(8,128)S(1)}, u32[]{:S(2)}, u32[]{:S(2)}) collective-permute-start(f32[16,512]{1,0:T(8,128)S(1)} %scatter-add.19), channel_id=1, source_target_pairs={{1,0},{2,1},{3,2},{4,3},{5,4},{6,5},{7,6},{0,7},{9,8},{10,9},{11,1... | collective-permute-start | bytes 98312 | tf_op jit(solution)/shard_map/ppermute | solution.py:544
  93.9 8.5 %collective-permute-done.7.refs_0_.left_ref = f32[16,512]{1,0:T(8,128)S(1)} collective-permute-done((f32[16,512]{1,0:T(8,128)S(1)}, f32[16,512]{1,0:T(8,128)S(1)}, u32[]{:S(2)}, u32[]{:S(2)}) %collective-permute-start.7) | collective-permute-done | bytes 32800 | tf_op jit(solution)/shard_map/ppermute | solution.py:543
  102.4 0.0 collective-permute-done.8.refs_1_.right_ref
  102.4 3.0 %all-to-all-done.1.parts_ref = bf16[16,208,128]{2,1,0:T(8,128)(2,1)S(1)} async-done(((bf16[16,208,128]{2,1,0:T(8,128)(2,1)}), bf16[16,208,128]{2,1,0:T(8,128)(2,1)S(1)}, u32[]{:S(2)}, u32[]{:S(2)}) %all-to-all-start.1) | async-done | bytes 852000 | tf_op jit(solution)/shard_map/all_to_all | solution.py:485
  105.4 1.0 totals.1
  106.4 3.6 %all-to-all-start.2 = ((bf16[16,208,128]{2,1,0:T(8,128)(2,1)}), bf16[16,208,128]{2,1,0:T(8,128)(2,1)S(1)}, u32[]{:S(2)}, u32[]{:S(2)}) async-start(bf16[16,208,128]{2,1,0:T(8,128)(2,1)} %totals.1), calls=%async_computation.2 | async-start | bytes 1703936 | tf_op jit(solution)/shard_map/all_to_all | solution.py:546
  110.1 0.0 copy-start
  110.1 1.8 %copy-done = bf16[2688,512]{1,0:T(8,128)(2,1)S(1)} copy-done((bf16[2688,512]{1,0:T(8,128)(2,1)S(1)}, bf16[2688,512]{1,0:T(8,128)(2,1)}, u32[]{:S(2)}) %copy-start) | copy-done | bytes 2752536
  111.8 1.6 %copy-done.5 = bf16[2048,512]{1,0:T(8,128)(2,1)S(1)} copy-done((bf16[2048,512]{1,0:T(8,128)(2,1)S(1)}, bf16[2048,512]{1,0:T(8,128)(2,1)}, u32[]{:S(2)}) %copy-start.5) | copy-done | bytes 2097176
  113.4 5.4 %latent.1 = bf16[2048,512]{1,0:T(8,128)(2,1)} custom-call(bf16[2048,512]{1,0:T(8,128)(2,1)S(1)} %copy-done.5, bf16[2688,512]{1,0:T(8,128)(2,1)S(1)} %copy-done, bf16[144,512]{1,0:T(8,128)(2,1)S(1)} %collective-permute-done.5.top_ref, bf16[144,512]{1,0:T(8,128)(2,1)S(1)} %collective-permute-done.6.bottom_ref, ...), custom_call_target="tpu_custom_call" | custom-call | flops 5767499776 | tf_op jit(solution)/shard_map/latent/pallas_call | solution.py:396
  118.8 13.0 %all-to-all-done.2.own_ref = bf16[16,208,128]{2,1,0:T(8,128)(2,1)S(1)} async-done(((bf16[16,208,128]{2,1,0:T(8,128)(2,1)}), bf16[16,208,128]{2,1,0:T(8,128)(2,1)S(1)}, u32[]{:S(2)}, u32[]{:S(2)}) %all-to-all-start.2) | async-done | bytes 852000 | tf_op jit(solution)/shard_map/all_to_all | solution.py:546
  131.8 0.0 collective-permute-start.9
  131.8 2.4 %collective-permute-done.9.sibling_ref = bf16[16,208,128]{2,1,0:T(8,128)(2,1)S(1)} collective-permute-done((bf16[16,208,128]{2,1,0:T(8,128)(2,1)S(1)}, bf16[16,208,128]{2,1,0:T(8,128)(2,1)S(1)}, u32[]{:S(2)}, u32[]{:S(2)}) %collective-permute-start.9) | collective-permute-done | bytes 852000 | tf_op jit(solution)/shard_map/ppermute | solution.py:552
  134.2 2.7 %unpack.1 = (f32[616,512]{1,0:T(8,128)}, f32[512,512]{1,0:T(8,128)}, f32[512,512]{1,0:T(8,128)}, f32[9,512]{1,0:T(8,128)}) custom-call(s32[2]{0:T(128)S(1)} %copy-done.4, bf16[16,208,128]{2,1,0:T(8,128)(2,1)S(1)} %all-to-all-done.2.own_ref, bf16[16,208,128]{2,1,0:T(8,128)(2,1)S(1)} %collective-permute-done.9.sibling_ref), custom_call_target="tpu_custom_call" | custom-call | flops 3460499968 | tf_op jit(solution)/shard_map/unpack/pallas_call | solution.py:448
  (17 shorter events, 0.1 us)
Async XLA Ops:
  1.7 10.8 %collective-permute-start = (bf16[16,512]{1,0:T(8,128)(2,1)S(1)}, bf16[16,512]{1,0:T(8,128)(2,1)S(1)}, u32[]{:S(2)}, u32[]{:S(2)}) collective-permute-start(bf16[16,512]{1,0:T(8,128)(2,1)S(1)} %bitcast.34), channel_id=1, source_target_pairs={{0,1},{1,2},{2,3},{3,4},{4,5},{5,6},{6,7},{7,0},{8,9},{9,10},{10,1... | collective-permute-start | bytes 49160 | tf_op jit(solution)/shard_map/ppermute | solution.py:501
  4.7 7.8 %collective-permute-start.1 = (bf16[16,512]{1,0:T(8,128)(2,1)S(1)}, bf16[16,512]{1,0:T(8,128)(2,1)S(1)}, u32[]{:S(2)}, u32[]{:S(2)}) collective-permute-start(bf16[16,512]{1,0:T(8,128)(2,1)S(1)} %bitcast.35), channel_id=1, source_target_pairs={{1,0},{2,1},{3,2},{4,3},{5,4},{6,5},{7,6},{0,7},{9,8},{10,9},{11,1... | collective-permute-start | bytes 49160 | tf_op jit(solution)/shard_map/ppermute | solution.py:502
  8.5 1.1 copy-start.1
  12.5 10.2 %copy-start.9 = (bf16[512,512]{1,0:T(8,128)(2,1)S(1)}, bf16[512,512]{1,0:T(8,128)(2,1)}, u32[]{:S(2)}) copy-start(bf16[512,512]{1,0:T(8,128)(2,1)} %wo_hbm) | copy-start | bytes 1572868
  12.5 11.2 %copy-start.8 = (bf16[616,512]{1,0:T(8,128)(2,1)S(1)}, bf16[616,512]{1,0:T(8,128)(2,1)}, u32[]{:S(2)}) copy-start(bf16[616,512]{1,0:T(8,128)(2,1)} %param.19) | copy-start | bytes 1892356
  12.5 36.5 %all-to-all-start = ((bf16[32,32,640]{2,1,0:T(8,128)(2,1)}), bf16[32,32,640]{2,1,0:T(8,128)(2,1)S(1)}, u32[]{:S(2)}, u32[]{:S(2)}) async-start(bf16[32,32,640]{2,1,0:T(8,128)(2,1)} %bitcast.6), calls=%async_computation | async-start | bytes 2621440 | tf_op jit(solution)/shard_map/all_to_all | solution.py:509
  16.9 8.1 %copy-start.2 = (bf16[512,512]{1,0:T(8,128)(2,1)S(1)}, bf16[512,512]{1,0:T(8,128)(2,1)}, u32[]{:S(2)}) copy-start(bf16[512,512]{1,0:T(8,128)(2,1)} %wp_ref.3) | copy-start | bytes 1572868
  16.9 8.1 %copy-start.3 = (f32[9,512]{1,0:T(8,128)S(1)}, f32[9,512]{1,0:T(8,128)}, u32[]{:S(2)}) copy-start(f32[9,512]{1,0:T(8,128)} %wd_hbm.1) | copy-start | bytes 55300
  17.7 7.2 %collective-permute-start.3 = (bf16[144,512]{1,0:T(8,128)(2,1)}, bf16[144,512]{1,0:T(8,128)(2,1)S(1)}, u32[]{:S(2)}, u32[]{:S(2)}) collective-permute-start(bf16[144,512]{1,0:T(8,128)(2,1)} %get-tuple-element.117), channel_id=1, source_target_pairs={{8,0},{16,8},{24,16},{9,1},{17,9},{25,17},{10,2},{18,10},{26,18},{... | collective-permute-start | bytes 442376 | tf_op jit(solution)/shard_map/ppermute | solution.py:519
  19.0 5.9 %collective-permute-start.2 = (bf16[144,512]{1,0:T(8,128)(2,1)}, bf16[144,512]{1,0:T(8,128)(2,1)S(1)}, u32[]{:S(2)}, u32[]{:S(2)}) collective-permute-start(bf16[144,512]{1,0:T(8,128)(2,1)} %get-tuple-element.118), channel_id=1, source_target_pairs={{0,8},{8,16},{16,24},{1,9},{9,17},{17,25},{2,10},{10,18},{18,26},{... | collective-permute-start | bytes 442376 | tf_op jit(solution)/shard_map/ppermute | solution.py:518
  39.9 1.3 copy-start.6
  49.0 1.1 copy-start.7
  73.7 2.7 %collective-permute-start.4 = (bf16[2,1664,128]{2,1,0:T(8,128)(2,1)}, bf16[2,1664,128]{2,1,0:T(8,128)(2,1)S(1)}, u32[]{:S(2)}, u32[]{:S(2)}) collective-permute-start(bf16[2,1664,128]{2,1,0:T(8,128)(2,1)} %get-tuple-element.87), channel_id=1, source_target_pairs={{0,8},{8,0},{1,9},{9,1},{2,10},{10,2},{3,11},{11,3},{4,12},{12,4},... | collective-permute-start | bytes 2555912 | tf_op jit(solution)/shard_map/ppermute | solution.py:477
  76.4 11.4 %copy-start.10 = (f32[18,8,512]{2,1,0:T(8,128)S(1)}, f32[18,8,512]{2,1,0:T(8,128)}, u32[]{:S(2)}) copy-start(f32[18,8,512]{2,1,0:T(8,128)} %get-tuple-element.93) | copy-start | bytes 884740
  78.7 9.3 %copy-start.11 = (f32[18,8,512]{2,1,0:T(8,128)S(1)}, f32[18,8,512]{2,1,0:T(8,128)}, u32[]{:S(2)}) copy-start(f32[18,8,512]{2,1,0:T(8,128)} %get-tuple-element.95) | copy-start | bytes 884740
  78.7 26.7 %all-to-all-start.1 = ((bf16[16,208,128]{2,1,0:T(8,128)(2,1)}), bf16[16,208,128]{2,1,0:T(8,128)(2,1)S(1)}, u32[]{:S(2)}, u32[]{:S(2)}) async-start(bf16[16,208,128]{2,1,0:T(8,128)(2,1)} %bitcast.13), calls=%async_computation.1 | async-start | bytes 1703936 | tf_op jit(solution)/shard_map/all_to_all | solution.py:485
  83.5 5.5 %collective-permute-start.6 = (bf16[144,512]{1,0:T(8,128)(2,1)S(1)}, bf16[144,512]{1,0:T(8,128)(2,1)S(1)}, u32[]{:S(2)}, u32[]{:S(2)}) collective-permute-start(bf16[144,512]{1,0:T(8,128)(2,1)S(1)} %get-tuple-element.103), channel_id=1, source_target_pairs={{8,0},{16,8},{24,16},{9,1},{17,9},{25,17},{10,2},{18,10},{26,18},{... | collective-permute-start | bytes 442376 | tf_op jit(solution)/shard_map/ppermute | solution.py:538
  84.8 4.0 %collective-permute-start.5 = (bf16[144,512]{1,0:T(8,128)(2,1)S(1)}, bf16[144,512]{1,0:T(8,128)(2,1)S(1)}, u32[]{:S(2)}, u32[]{:S(2)}) collective-permute-start(bf16[144,512]{1,0:T(8,128)(2,1)S(1)} %get-tuple-element.104), channel_id=1, source_target_pairs={{0,8},{8,16},{16,24},{1,9},{9,17},{17,25},{2,10},{10,18},{18,26},{... | collective-permute-start | bytes 442376 | tf_op jit(solution)/shard_map/ppermute | solution.py:537
  89.1 13.3 %collective-permute-start.7 = (f32[16,512]{1,0:T(8,128)S(1)}, f32[16,512]{1,0:T(8,128)S(1)}, u32[]{:S(2)}, u32[]{:S(2)}) collective-permute-start(f32[16,512]{1,0:T(8,128)S(1)} %scatter-add.15), channel_id=1, source_target_pairs={{0,1},{1,2},{2,3},{3,4},{4,5},{5,6},{6,7},{7,0},{8,9},{9,10},{10,1... | collective-permute-start | bytes 98312 | tf_op jit(solution)/shard_map/ppermute | solution.py:543
  91.0 11.4 %collective-permute-start.8 = (f32[16,512]{1,0:T(8,128)S(1)}, f32[16,512]{1,0:T(8,128)S(1)}, u32[]{:S(2)}, u32[]{:S(2)}) collective-permute-start(f32[16,512]{1,0:T(8,128)S(1)} %scatter-add.19), channel_id=1, source_target_pairs={{1,0},{2,1},{3,2},{4,3},{5,4},{6,5},{7,6},{0,7},{9,8},{10,9},{11,1... | collective-permute-start | bytes 98312 | tf_op jit(solution)/shard_map/ppermute | solution.py:544
  106.4 25.4 %all-to-all-start.2 = ((bf16[16,208,128]{2,1,0:T(8,128)(2,1)}), bf16[16,208,128]{2,1,0:T(8,128)(2,1)S(1)}, u32[]{:S(2)}, u32[]{:S(2)}) async-start(bf16[16,208,128]{2,1,0:T(8,128)(2,1)} %totals.1), calls=%async_computation.2 | async-start | bytes 1703936 | tf_op jit(solution)/shard_map/all_to_all | solution.py:546
  110.1 1.8 %copy-start = (bf16[2688,512]{1,0:T(8,128)(2,1)S(1)}, bf16[2688,512]{1,0:T(8,128)(2,1)}, u32[]{:S(2)}) copy-start(bf16[2688,512]{1,0:T(8,128)(2,1)} %get-tuple-element.94.mix_ref) | copy-start | bytes 8257540
  111.8 1.6 %copy-start.5 = (bf16[2048,512]{1,0:T(8,128)(2,1)S(1)}, bf16[2048,512]{1,0:T(8,128)(2,1)}, u32[]{:S(2)}) copy-start(bf16[2048,512]{1,0:T(8,128)(2,1)} %get-tuple-element.96.grid_ref) | copy-start | bytes 6291460
  113.4 20.8 %copy-start.4 = (s32[2]{0:T(128)S(1)}, s32[2]{0:T(128)}, u32[]{:S(2)}) copy-start(s32[2]{0:T(128)} %pad_add_fusion.1.core_ref) | copy-start | bytes 28
  131.8 2.4 %collective-permute-start.9 = (bf16[16,208,128]{2,1,0:T(8,128)(2,1)S(1)}, bf16[16,208,128]{2,1,0:T(8,128)(2,1)S(1)}, u32[]{:S(2)}, u32[]{:S(2)}) collective-permute-start(bf16[16,208,128]{2,1,0:T(8,128)(2,1)S(1)} %all-to-all-done.2.own_ref), channel_id=1, source_target_pairs={{0,8},{8,0},{1,9},{9,1},{2,10},{10,2},{3,11},{11,3},{4,12},{12,4},... | collective-permute-start | bytes 2555912 | tf_op jit(solution)/shard_map/ppermute | solution.py:552

commit v3 on v2

--- a/solution.py
+++ b/solution.py
@@ -203,36 +203,139 @@
             ref[:, start:, :] = jnp.zeros((ref.shape[0], unused, LANES), bf16)
 
 
-def owner_kernel(
-    spec, clat, clon, wide, core_ref, rows_hbm, wit_hbm, wot_hbm, wo_hbm, gg_hbm, wd_hbm, gm_hbm, cott_hbm,
-    grid_hbm, mix_hbm, east_hbm, west_hbm, mine_hbm, other_hbm,
-    rows_ref, wit_ref, wot_ref, wo_ref, gg_ref, wd_ref, gm_ref, cott_ref,
-    grid_ref, mix_ref, east_ref, west_ref, mine_ref, other_ref,
-    padded, emb_ref, gi, gi_out, go, gp, gd, sems,
-):
-    core, one = core_ref[0], core_ref[1]
-    slots, spec_wide = rows_ref.shape
-    cells, width = gg_ref.shape
-    sources = rows_hbm, wit_hbm, wot_hbm, wo_hbm, gg_hbm, wd_hbm, gm_hbm, cott_hbm
-    targets = rows_ref, wit_ref, wot_ref, wo_ref, gg_ref, wd_ref, gm_ref, cott_ref
+def start_loads(sources, targets, sems):
     loads = [
         pltpu.make_async_copy(source, target, sems.at[i])
         for i, (source, target) in enumerate(zip(sources, targets))
     ]
     for load in loads:
         load.start()
-    outs = (
-        (grid_ref, grid_hbm), (mix_ref, mix_hbm), (east_ref, east_hbm), (west_ref, west_hbm),
-        (mine_ref, mine_hbm), (other_ref, other_hbm),
-    )
+    return loads
+
+
+def encode_kernel(
+    spec, clon, ids_ref, rows_ref, wit_hbm, wot_hbm, gg_hbm, wo_hbm,
+    emb_ref, mine_ref, other_ref, mine_rest, other_rest,
+    wit_ref, wot_ref, gg_ref, wo_ref, gi, gi_out, go, sems,
+):
+    loads = start_loads((wit_hbm, wot_hbm, gg_hbm, wo_hbm), (wit_ref, wot_ref, gg_ref, wo_ref), sems)
+    core = ids_ref[0]
+    slots, spec_wide = rows_ref.shape
+    cells, width = gg_ref.shape
+    step = min(512, slots)
+
+    for t in range(slots // step):
+        at = slice(t * step, (t + 1) * step)
+        rows = rows_ref[at, :]
+        place = rows[:, spec : spec + 1].astype(f32) * clon + rows[:, spec + 1 : spec + 2].astype(f32)
+        hits = place.astype(i32) == lax.broadcasted_iota(i32, (step, cells), 1)
+        hits = hits.astype(f32).astype(bf16)
+        if t == 0:
+            loads[0].wait()
+        preact = dot(wit_ref[...], rows, (1, 1))
+        sig = 1.0 / (1.0 + jnp.exp(-preact))
+        hidden = (preact * sig).astype(bf16)
+        if t == 0:
+            loads[1].wait()
+        emb_ref[:, at] = dot(wot_ref[...], hidden).astype(bf16)
+        if t == 0:
+            loads[2].wait()
+        g_emb = dot(hits, gg_ref[...]).astype(bf16)
+        g_out = dot(hidden, g_emb)
+        if t == 0:
+            loads[3].wait()
+        g_hid = dot(wo_ref[...], g_emb, (1, 1))
+        g_pre = (g_hid * (sig * (1.0 + preact * (1.0 - sig)))).astype(bf16)
+        g_in = dot(g_pre, rows)
+        if t == 0:
+            go[...] = g_out
+            gi[...] = g_in
+        else:
+            go[...] += g_out
+            gi[...] += g_in
+
+    gi_out[...] = gi[...].T
+    head = spec_wide - LANES
+    write_halves(core, go, 0, mine_ref, other_ref)
+    write_halves(core, gi_out, width, mine_ref, other_ref, 0, head)
+    write_halves(core, gi_out, 0, mine_rest, other_rest, head, mine_rest.shape[1])
+    clear_tail(width + head, mine_ref, other_ref)
+
+
+def encode(ids, rows, weights, spec, clon, out_rows, rest_rows):
+    slots, spec_wide = rows.shape
+    width = weights[-1].shape[0]
+    half = jax.ShapeDtypeStruct((width // LANES // 2, out_rows, LANES), bf16)
+    rest = jax.ShapeDtypeStruct((width // LANES // 2, rest_rows, LANES), bf16)
+    return pl.pallas_call(
+        functools.partial(encode_kernel, spec, clon),
+        out_shape=(jax.ShapeDtypeStruct((width, slots), bf16), half, half, rest, rest),
+        in_specs=[smem(), vmem()] + [anywhere()] * len(weights),
+        out_specs=(vmem(),) * 5,
+        scratch_shapes=[pltpu.VMEM(x.shape, x.dtype) for x in weights]
+        + [
+            pltpu.VMEM((width, spec_wide), f32),
+            pltpu.VMEM((spec_wide, width), f32),
+            pltpu.VMEM((width, width), f32),
+            pltpu.SemaphoreType.DMA((len(weights),)),
+        ],
+        compiler_params=params(24),
+        cost_estimate=cost(10),
+        name="encode",
+    )(ids, rows, *weights)
+
+
+def bins_kernel(spec, clon, rows_ref, emb_ref, grid_ref, grid_hbm, sem):
+    slots, spec_wide = rows_ref.shape
+    cells = grid_ref.shape[0]
+    last = rows_ref[:, spec_wide - LANES :]
+    col = spec - (spec_wide - LANES)
+    lane = lax.broadcasted_iota(i32, (16, LANES), 1)
+    pick = jnp.where(lane == col, float(clon), jnp.where(lane == col + 1, 1.0, 0.0)).astype(bf16)
+    place = dot(pick, last, (1, 1))[0:1, :].astype(i32)
+    block = 4 * clon
+
+    def body(t, carry):
+        cell = lax.broadcasted_iota(i32, (block, slots), 0) + t * block
+        hits = (place == cell).astype(f32).astype(bf16)
+        grid = dot(hits, emb_ref[...], (1, 1)).astype(bf16)
+        grid_ref[pl.ds(pl.multiple_of(t * block, 16), block), :] = grid
+        return carry
+
+    lax.fori_loop(0, cells // block, body, 0)
+    put = pltpu.make_async_copy(grid_ref, grid_hbm, sem)
+    put.start()
+    put.wait()
+
+
+def bins(rows, emb, spec, cells, clon):
+    grid = jax.ShapeDtypeStruct((cells, emb.shape[0]), bf16)
+    return pl.pallas_call(
+        functools.partial(bins_kernel, spec, clon),
+        out_shape=(grid, grid),
+        in_specs=[vmem()] * 2,
+        out_specs=(vmem(), anywhere()),
+        scratch_shapes=[pltpu.SemaphoreType.DMA],
+        compiler_params=params(12),
+        cost_estimate=cost(4),
+        name="bins",
+    )(rows, emb)
+
+
+def mix_kernel(
+    clat, clon, wide, ids_ref, grid_ref, wd_ref, gm_ref, after_ref,
+    mix_ref, gd_ref, mix_hbm, east_hbm, west_hbm, east_ref, west_ref, padded, gd, sems,
+):
+    one = ids_ref[1]
+    width = grid_ref.shape[1]
+    blocks = width // LANES
     puts = [
-        pltpu.make_async_copy(source, target, sems.at[len(loads) + i])
-        for i, (source, target) in enumerate(outs)
+        pltpu.make_async_copy(source, target, sems.at[i])
+        for i, (source, target) in enumerate(
+            ((mix_ref, mix_hbm), (east_ref, east_hbm), (west_ref, west_hbm))
+        )
     ]
-    gi[...] = jnp.zeros_like(gi)
-    go[...] = jnp.zeros_like(go)
     gd[...] = jnp.zeros_like(gd)
-    blocks = width // LANES
     side = jnp.zeros((blocks, clat + 4, PAD, LANES), f32)
     padded[:, :, :PAD, :] = side
     padded[:, :, PAD + clon :, :] = side
@@ -240,50 +343,15 @@
         padded[:, e, PAD : PAD + clon, :] = jnp.zeros((blocks, clon, LANES), f32)
     used = (clat + 2) * wide
     mix_ref[used:, :] = jnp.zeros((mix_ref.shape[0] - used, width), bf16)
-    for load in loads[:5]:
-        load.wait()
-
-    step = min(512, slots)
-
-    def encode(t, carry):
-        at = pl.ds(pl.multiple_of(t * step, step), step)
-        rows = rows_ref[at, :]
-        preact = dot(wit_ref[...], rows, (1, 1))
-        sig = 1.0 / (1.0 + jnp.exp(-preact))
-        hidden = (preact * sig).astype(bf16)
-        emb_ref[:, at] = dot(wot_ref[...], hidden).astype(bf16)
-        place = rows[:, spec : spec + 1].astype(f32) * clon + rows[:, spec + 1 : spec + 2].astype(f32)
-        hits = place.astype(i32) == lax.broadcasted_iota(i32, (step, cells), 1)
-        g_emb = dot(hits.astype(f32).astype(bf16), gg_ref[...]).astype(bf16)
-        go[...] += dot(hidden, g_emb)
-        g_hid = dot(wo_ref[...], g_emb, (1, 1))
-        g_pre = (g_hid * (sig * (1.0 + preact * (1.0 - sig)))).astype(bf16)
-        gi[...] += dot(g_pre, rows)
+
+    def widen(i, carry):
+        at = pl.ds(pl.multiple_of(i * clon, 16), clon)
+        for n in range(blocks):
+            part = grid_ref[at, n * LANES : (n + 1) * LANES].astype(f32)
+            padded[n, i + 2, PAD : PAD + clon, :] = part
         return carry
 
-    lax.fori_loop(0, slots // step, encode, 0)
-
-    last = rows_ref[:, spec_wide - LANES :]
-    col = spec - (spec_wide - LANES)
-    lane = lax.broadcasted_iota(i32, (16, LANES), 1)
-    pick = jnp.where(lane == col, float(clon), jnp.where(lane == col + 1, 1.0, 0.0)).astype(bf16)
-    place = dot(pick, last, (1, 1))[0:1, :].astype(i32)
-    block = 4 * clon
-
-    def bins(t, carry):
-        cell = lax.broadcasted_iota(i32, (block, slots), 0) + t * block
-        hits = (place == cell).astype(f32).astype(bf16)
-        grid = dot(hits, emb_ref[...], (1, 1)).astype(bf16)
-        grid_ref[pl.ds(pl.multiple_of(t * block, 16), block), :] = grid
-        for n in range(blocks):
-            part = grid[:, n * LANES : (n + 1) * LANES].astype(f32)
-            padded[n, pl.ds(4 * t + 2, 4), PAD : PAD + clon, :] = part.reshape(4, clon, LANES)
-        return carry
-
-    lax.fori_loop(0, cells // block, bins, 0)
-    puts[0].start()
-    for load in loads[5:]:
-        load.wait()
+    lax.fori_loop(0, clat, widen, 0)
 
     def conv(e, carry):
         for n in range(blocks):
@@ -322,52 +390,62 @@
         return carry
 
     lax.fori_loop(0, clat + 2, conv, 0)
-    for put in puts[1:4]:
+    for put in puts:
         put.start()
-    gp[...] = dot(cott_ref[...], mix_ref[...]).T
-    gi_out[...] = gi[...].T
-    gi_rows = round_up(spec, 16)
     taps = [jnp.sum(gd[8 * k : 8 * k + 8, :], axis=0, keepdims=True) for k in range(9)]
-    gd[0:16, :] = jnp.concatenate(taps + [jnp.zeros((7, width), f32)], axis=0)
-    start = 0
-    for total, size in ((go, width), (gi_out, gi_rows), (gp, width), (gd, 16)):
-        write_halves(core, total, start, mine_ref, other_ref, 0, size)
-        start += size
-    clear_tail(start, mine_ref, other_ref)
-    for put in puts[4:]:
-        put.start()
+    gd_ref[...] = jnp.concatenate(taps + [jnp.zeros((7, width), f32)], axis=0)
     for put in puts:
         put.wait()
 
 
-def owner_part(core, operands, spec, clat, clon, wide, out_rows):
-    slots, spec_wide = operands[0].shape
-    width = operands[2].shape[0]
-    half = jax.ShapeDtypeStruct((width // LANES // 2, out_rows, LANES), bf16)
+def mix(ids, grid, w_depth, g_mixed, after, clat, clon, wide):
+    width = grid.shape[1]
     column = jax.ShapeDtypeStruct((clat + 2, 8, width), f32)
-    grid = jax.ShapeDtypeStruct((clat * clon, width), bf16)
-    ext = jax.ShapeDtypeStruct(operands[-1].shape[::-1], bf16)
-    outs = grid, ext, column, column, half, half
-    return pl.pallas_call(
-        functools.partial(owner_kernel, spec, clat, clon, wide),
-        out_shape=outs,
-        in_specs=[smem()] + [anywhere()] * len(operands),
-        out_specs=(anywhere(),) * len(outs),
-        scratch_shapes=[pltpu.VMEM(x.shape, x.dtype) for x in operands + outs]
+    ext = jax.ShapeDtypeStruct((round_up((clat + 2) * wide, LANES), width), bf16)
+    return pl.pallas_call(
+        functools.partial(mix_kernel, clat, clon, wide),
+        out_shape=(ext, jax.ShapeDtypeStruct((16, width), f32), ext, column, column),
+        in_specs=[smem()] + [vmem()] * 3 + [anywhere()],
+        out_specs=(vmem(),) * 2 + (anywhere(),) * 3,
+        scratch_shapes=[pltpu.VMEM(column.shape, column.dtype)] * 2
         + [
             pltpu.VMEM((width // LANES, clat + 4, clon + 2 * PAD, LANES), f32),
-            pltpu.VMEM((width, slots), bf16),
-            pltpu.VMEM((width, spec_wide), f32),
-            pltpu.VMEM((spec_wide, width), f32),
-            pltpu.VMEM((width, width), f32),
-            pltpu.VMEM((width, width), f32),
             pltpu.VMEM((72, width), f32),
-            pltpu.SemaphoreType.DMA((len(operands) + len(outs),)),
+            pltpu.SemaphoreType.DMA((3,)),
         ],
-        compiler_params=params(56),
-        cost_estimate=cost(20),
-        name="owner",
-    )(core, *operands)
+        compiler_params=params(16),
+        cost_estimate=cost(10),
+        name="mix",
+    )(ids, grid, w_depth, g_mixed, after)
+
+
+def point_kernel(
+    ids_ref, cott_ref, mix_ref, gd_ref, mine_rest, other_rest, after_ref, mine_ref, other_ref, gp
+):
+    core = ids_ref[0]
+    width = mix_ref.shape[1]
+    rest = mine_rest.shape[1]
+    gp[...] = dot(cott_ref[...], mix_ref[...]).T
+    write_halves(core, gp, 0, mine_ref, other_ref)
+    mine_ref[:, width : width + rest, :] = mine_rest[...]
+    other_ref[:, width : width + rest, :] = other_rest[...]
+    write_halves(core, gd_ref, width + rest, mine_ref, other_ref, 0, 16)
+    clear_tail(width + rest + 16, mine_ref, other_ref)
+
+
+def point(ids, cot_t, mix_ext, grad_depth, rest, after, out_rows):
+    width = mix_ext.shape[1]
+    half = jax.ShapeDtypeStruct((width // LANES // 2, out_rows, LANES), bf16)
+    return pl.pallas_call(
+        point_kernel,
+        out_shape=(half, half),
+        in_specs=[smem()] + [vmem()] * 5 + [anywhere()],
+        out_specs=(vmem(),) * 2,
+        scratch_shapes=[pltpu.VMEM((width, width), f32)],
+        compiler_params=params(12),
+        cost_estimate=cost(3),
+        name="point",
+    )(ids, cot_t, mix_ext, grad_depth, *rest, after)
 
 
 def latent_kernel(
@@ -404,49 +482,93 @@
     )(grid, mix_ext, *sides, w_point)
 
 
+def split_kernel(ids_ref, mine_ref, got_ref, keep_ref, send_ref):
+    x = ids_ref[2]
+    for ref, i in ((keep_ref, x), (send_ref, 1 - x)):
+        at = pl.ds(i, 1)
+        ref[...] = (mine_ref[at].astype(f32) + got_ref[at].astype(f32))[0].astype(bf16)
+
+
+def split(ids, mine, got):
+    half = jax.ShapeDtypeStruct(mine.shape[1:], bf16)
+    return pl.pallas_call(
+        split_kernel,
+        out_shape=(half, half),
+        in_specs=[smem()] + [vmem()] * 2,
+        out_specs=(vmem(),) * 2,
+        compiler_params=params(8),
+        cost_estimate=cost(1),
+        name="split",
+    )(ids, mine, got)
+
+
+def merge_kernel(a_keep, a_got, b_keep, b_got, out_ref):
+    count = out_ref.shape[0]
+    start = 0
+    for keep, got in ((a_keep, a_got), (b_keep, b_got)):
+        total = (keep[...].astype(f32) + got[...].astype(f32)).astype(bf16)
+        size = total.shape[0] // count
+        out_ref[:, start : start + size, :] = total.reshape(count, size, LANES)
+        start += size
+
+
+def merge(a_keep, a_got, b_keep, b_got, count):
+    rows = (a_keep.shape[0] + b_keep.shape[0]) // count
+    return pl.pallas_call(
+        merge_kernel,
+        out_shape=jax.ShapeDtypeStruct((count, rows, LANES), bf16),
+        in_specs=[vmem()] * 4,
+        out_specs=vmem(),
+        compiler_params=params(8),
+        cost_estimate=cost(1),
+        name="merge",
+    )(a_keep, a_got, b_keep, b_got)
+
+
 def totals_kernel(parts_ref, *refs):
     out_ref = refs[-1]
     total = jnp.sum(parts_ref[...].astype(f32), axis=0).astype(bf16)
-    out_ref[...] = jnp.broadcast_to(total[None], parts_ref.shape)
-
-
-def totals(parts, *after):
+    out_ref[...] = jnp.broadcast_to(total[None], out_ref.shape)
+
+
+def totals(parts, chips, *after):
     return pl.pallas_call(
         totals_kernel,
-        out_shape=jax.ShapeDtypeStruct(parts.shape, bf16),
+        out_shape=jax.ShapeDtypeStruct((chips,) + parts.shape[1:], bf16),
         in_specs=[vmem()] + [anywhere()] * len(after),
         out_specs=vmem(),
-        compiler_params=params(6),
+        compiler_params=params(8),
         cost_estimate=cost(1),
         name="totals",
     )(parts, *after)
 
 
 def unpack_kernel(
-    obs_scale, cell_scale, core_ref, own_ref, sibling_ref, gi_ref, go_ref, gp_ref, gd_ref
+    rows_a, rest, obs_scale, cell_scale, ids_ref, own_ref, sibling_ref, gi_ref, go_ref, gp_ref, gd_ref
 ):
     spec, width = gi_ref.shape
     chips = own_ref.shape[0]
     count = width // (2 * LANES)
     per = chips // count
-    core = core_ref[0]
+    core = ids_ref[0]
+    cut = rows_a // per
+    head = spec - spec % LANES
     for ref, half in ((own_ref, core), (sibling_ref, 1 - core)):
         for n in range(count):
             cols = pl.ds(pl.multiple_of((half * count + n) * LANES, LANES), LANES)
             block = ref[n * per : (n + 1) * per].astype(f32)
-            block = block.reshape(per * block.shape[1], LANES)
-            start = 0
-            for out_ref, scale in (
-                (go_ref, obs_scale), (gi_ref, obs_scale), (gp_ref, cell_scale), (gd_ref, cell_scale)
-            ):
-                size = out_ref.shape[0]
-                out_ref[:, cols] = block[start : start + size] * scale
-                start += round_up(size, 16)
-
-
-def unpack(core, own, sibling, spec, width, obs_scale, cell_scale):
-    return pl.pallas_call(
-        functools.partial(unpack_kernel, obs_scale, cell_scale),
+            a = block[:, :cut].reshape(rows_a, LANES)
+            b = block[:, cut:].reshape(per * (block.shape[1] - cut), LANES)
+            go_ref[:, cols] = a[:width] * obs_scale
+            gi_ref[:head, cols] = a[width : width + head] * obs_scale
+            gp_ref[:, cols] = b[:width] * cell_scale
+            gi_ref[head:, cols] = b[width : width + spec - head] * obs_scale
+            gd_ref[:, cols] = b[width + rest : width + rest + gd_ref.shape[0]] * cell_scale
+
+
+def unpack(ids, own, sibling, spec, width, rows_a, rest, obs_scale, cell_scale):
+    return pl.pallas_call(
+        functools.partial(unpack_kernel, rows_a, rest, obs_scale, cell_scale),
         out_shape=tuple(
             jax.ShapeDtypeStruct((rows, width), f32) for rows in (spec, width, width, 9)
         ),
@@ -455,7 +577,7 @@
         compiler_params=params(8),
         cost_estimate=cost(3),
         name="unpack",
-    )(core, own, sibling)
+    )(ids, own, sibling)
 
 
 def neighbours(axes, periodic):
@@ -473,16 +595,8 @@
 SWAP = [(0, 1), (1, 0)]
 
 
-def core_sum(mine, other):
-    got = lax.ppermute(other, "core", SWAP)
-    return (mine.astype(f32) + got.astype(f32)).astype(bf16)
-
-
-def spread(values):
-    chips = lax.axis_size(CHIPS)
-    blocks, rows, _ = values.shape
-    values = values.reshape(chips, blocks * rows // chips, LANES)
-    return lax.all_to_all(values, CHIPS, split_axis=0, concat_axis=0, tiled=True)
+def spread(values, axes):
+    return lax.all_to_all(values, axes, split_axis=0, concat_axis=0, tiled=True)
 
 
 def on_device(spectra, owner, cell, w_in, w_out, w_point, w_depth, cotangent):
@@ -493,7 +607,7 @@
     cells = clat * clon
     wide = clon + 16
     spec_wide = round_up(spec + 2, LANES)
-    core = jnp.stack([lax.axis_index("core"), jnp.int32(1)])
+    ids = jnp.stack([lax.axis_index("core"), jnp.int32(1), lax.axis_index("x")])
     one = jnp.ones((1,), i32)
     east_way, west_way = neighbours("lon", True)
     south_way, north_way = neighbours(LAT, False)
@@ -525,14 +639,37 @@
     )
     w_in_t = jnp.pad(w_in.T, ((0, 0), (0, spec_wide - spec)))
 
-    out_rows = round_up(2 * width + round_up(spec, 16) + 16, 16 * tiles * LANES // width)
-    operands = arrived, w_in_t, w_out.T, w_out, g_grid, w_depth, g_mixed, cot_t
-    grid, mix_ext, east, west, mine, other = owner_part(
-        core, operands, spec, clat, clon, wide, out_rows
+    chips, pairs = lax.axis_size(CHIPS), lax.axis_size("x") == 2
+    align = 16 * tiles * LANES // width
+    head = spec - spec % LANES
+    rest = round_up(spec - head, 16)
+    rows_a = round_up(width + head, align)
+    rows_b = round_up(width + rest + 16, align)
+    emb, mine_a, other_a, *rest_halves = encode(
+        ids, arrived, (w_in_t, w_out.T, g_grid, w_out), spec, clon, rows_a, rest
     )
-    summed = core_sum(mine, other)
-    summed, grid, mix_ext, east, west = lax.optimization_barrier((summed, grid, mix_ext, east, west))
-    parts = spread(summed)
+    got_a = lax.ppermute(other_a, "core", SWAP)
+    grid_here, grid = bins(arrived, emb, spec, cells, clon)
+    keep_a, send_a = split(ids, mine_a, got_a) if pairs else (mine_a, got_a)
+
+    mix_here, grad_depth, mix_ext, east, west = mix(
+        ids, grid_here, w_depth, g_mixed, keep_a, clat, clon, wide
+    )
+    got_a = lax.ppermute(send_a, "x", SWAP) if pairs else send_a
+    mine_b, other_b = point(ids, cot_t, mix_here, grad_depth, rest_halves, got_a, rows_b)
+    got_b = lax.ppermute(other_b, "core", SWAP)
+    if pairs:
+        keep_b, send_b = split(ids, mine_b, got_b)
+        got_b = lax.ppermute(send_b, "x", SWAP)
+        summed = merge(keep_a, got_a, keep_b, got_b, lax.axis_size("lon"))
+    else:
+        sums = [
+            (mine.astype(f32) + got.astype(f32)).astype(bf16).reshape(chips, -1, LANES)
+            for mine, got in ((keep_a, send_a), (mine_b, got_b))
+        ]
+        summed = jnp.concatenate(sums, axis=1)
+    summed, mix_ext, east, west = lax.optimization_barrier((summed, mix_ext, east, west))
+    parts = spread(summed, "lon" if pairs else CHIPS)
 
     top = lax.ppermute(mix_ext[(clat + 1) * wide : (clat + 2) * wide], LAT, south_way)
     bottom = lax.ppermute(mix_ext[:wide], LAT, north_way)
@@ -542,8 +679,7 @@
 
     left = lax.ppermute(edge_column(east[:, 0], clon), "lon", east_way)
     right = lax.ppermute(edge_column(west[:, 7], wide - 1), "lon", west_way)
-    sent = totals(parts, left, right)
-    full = lax.all_to_all(sent, CHIPS, split_axis=0, concat_axis=0, tiled=True)
+    full = spread(totals(parts, chips, left, right), CHIPS)
     latent = finish_latent(grid, mix_ext, (top, bottom, left, right), w_point, clat, clon, wide)
 
     obs_scale = float((rows_here * tiles) ** -0.5)
@@ -551,7 +687,7 @@
     full, latent = lax.optimization_barrier((full, latent))
     sibling = lax.ppermute(full, "core", SWAP)
     grad_in, grad_out, grad_point, grad_depth = unpack(
-        core, full, sibling, spec, width, obs_scale, cell_scale
+        ids, full, sibling, spec, width, rows_a, rest, obs_scale, cell_scale
     )
     return latent.reshape(clat, clon, width), grad_in, grad_out, grad_point, grad_depth
 

time: 138 us -> 139 us (level)
  waiting for transfers between devices: 37.9 us -> 29.2 us
  starting transfers between devices: 30.3 us -> 38.3 us
  other arithmetic: 4.51 us -> 1.58 us
  Pallas kernels: 50.5 us -> 52.9 us
  local copies, waits for them, and re-layouts: 12.8 us -> 15.2 us
    ppermute x1, waiting for transfers between devices: 8.5 us -> 1.99 us  [on_device(): left = lax.ppermute(edge_column(east[:, 0], clon), 'lon', east_way)]
    all_to_all x2, starting transfers between devices: 7.38 us -> 13.2 us  [spread(): return lax.all_to_all(values, axes, split_axis=0, concat_axis=0, tiled=True)]
    all_to_all x2, waiting for transfers between devices: 16 us -> 10.6 us  [spread(): return lax.all_to_all(values, axes, split_axis=0, concat_axis=0, tiled=True)]
    ppermute x1 -> x4, waiting for transfers between devices: 2.58 us -> 6.67 us  [the longest x1 5.05 us: on_device(): got_b = lax.ppermute(send_b, 'x', SWAP)]
    convert_element_type x1 -> x0, other arithmetic: 2.32 us -> none  [core_sum(): return (mine.astype(f32) + got.astype(f32)).astype(bf16)]
    unnamed x26 -> x30, local copies, waits for them, and re-layouts: 6.85 us -> 9.04 us
    ppermute x1 -> x4, starting transfers between devices: 0.07 us -> 2.23 us  [the longest x1 1.25 us: on_device(): got_b = lax.ppermute(send_b, 'x', SWAP)]
    pallas_call x3 -> x9, Pallas kernels: 27.3 us -> 29.5 us  [the longest x1 9.02 us: mix(): pl.pallas_call(functools.partial(mix_kernel, clat, clon, wide), out_shape...]
  transfers between devices with their start and end apart: 13 -> 16, of which waited for: 7 -> 7; matrix products, arithmetic and copies ran while one was open for 5% -> 5% of each run, Pallas kernels for 17% -> 26%
where the time goes in v3:
time: 139 us; the launch traced here: 138 us
  Pallas kernels  52.9 us (38%)
  starting transfers between devices  38.3 us (28%)
  waiting for transfers between devices  29.2 us (21%)
  local copies, waits for them, and re-layouts  15.2 us (11%)
  other arithmetic  1.58 us (1%)
    pallas_call x1, Pallas kernels, grid_grad(): pl.pallas_call(functools.partial(grid_grad_kernel, clat, clon, wide), out...  15.1 us
    all_to_all x2, starting transfers between devices, spread(): return lax.all_to_all(values, axes, split_axis=0, concat_axis=0, tiled=True)  13.2 us
    all_to_all x2, waiting for transfers between devices, spread(): return lax.all_to_all(values, axes, split_axis=0, concat_axis=0, tiled=True)  10.6 us
    unnamed x30, local copies, waits for them, and re-layouts  9.04 us
    pallas_call x1, Pallas kernels, mix(): pl.pallas_call(functools.partial(mix_kernel, clat, clon, wide), out_shape...  9.02 us
    pallas_call x1, Pallas kernels, encode(): pl.pallas_call(functools.partial(encode_kernel, spec, clon), out_shape=(j...  8.8 us
    all_to_all x1, waiting for transfers between devices, on_device(): lax.all_to_all(outgoing.reshape(tiles, cap, spec_wide), ('x', 'core', 'lo...  6.92 us
    pallas_call x1, Pallas kernels, finish_latent(): pl.pallas_call(functools.partial(latent_kernel, clat, clon, wide), out_sh...  5.39 us
  transfers between devices with their start and end apart: 16, of which 7 were waited for; matrix products, arithmetic and copies ran while one was open for 5% of the time, Pallas kernels for 26%

profile of v3, /device:TPU:0, one launch (start us, length us, event | category | flops | bytes accessed | tf_op | source)
XLA Modules:
  0.0 138.2 jit_solution(10225763011140757120)
XLA Ops:
  0.6 1.0 fusion.5
  1.7 3.0 %collective-permute-start = (bf16[16,512]{1,0:T(8,128)(2,1)S(1)}, bf16[16,512]{1,0:T(8,128)(2,1)S(1)}, u32[]{:S(2)}, u32[]{:S(2)}) collective-permute-start(bf16[16,512]{1,0:T(8,128)(2,1)S(1)} %bitcast.35), channel_id=1, source_target_pairs={{0,1},{1,2},{2,3},{3,4},{4,5},{5,6},{6,7},{7,0},{8,9},{9,10},{10,1... | collective-permute-start | bytes 49160 | tf_op jit(solution)/shard_map/ppermute | solution.py:615
  4.7 3.1 %collective-permute-start.1 = (bf16[16,512]{1,0:T(8,128)(2,1)S(1)}, bf16[16,512]{1,0:T(8,128)(2,1)S(1)}, u32[]{:S(2)}, u32[]{:S(2)}) collective-permute-start(bf16[16,512]{1,0:T(8,128)(2,1)S(1)} %bitcast.36), channel_id=1, source_target_pairs={{1,0},{2,1},{3,2},{4,3},{5,4},{6,5},{7,6},{0,7},{9,8},{10,9},{11,1... | collective-permute-start | bytes 49160 | tf_op jit(solution)/shard_map/ppermute | solution.py:616
  7.8 0.7 pad_add_fusion.places_ref
  8.5 1.1 copy-done.3
  9.6 2.9 %route.1 = bf16[1024,640]{1,0:T(8,128)(2,1)} custom-call(s32[2,512]{1,0:T(2,128)S(1)} %pad_add_fusion.places_ref, bf16[616,512]{1,0:T(8,128)(2,1)S(1)} %bitcast.32), custom_call_target="tpu_custom_call" | custom-call | flops 3460499968 | tf_op jit(solution)/shard_map/route/pallas_call | solution.py:77
  12.5 0.0 copy-start.13
  12.5 3.2 %all-to-all-start = ((bf16[32,32,640]{2,1,0:T(8,128)(2,1)}), bf16[32,32,640]{2,1,0:T(8,128)(2,1)S(1)}, u32[]{:S(2)}, u32[]{:S(2)}) async-start(bf16[32,32,640]{2,1,0:T(8,128)(2,1)} %bitcast.7), calls=%async_computation | async-start | bytes 2621440 | tf_op jit(solution)/shard_map/all_to_all | solution.py:623
  15.8 0.1 pad.19.clone
  15.9 1.0 slice_bitcast_fusion
  16.9 0.0 copy-start.6
  16.9 0.8 pad_maximum_fusion.1
  17.7 1.3 collective-permute-start.3
  19.0 3.0 %collective-permute-start.2 = (bf16[144,512]{1,0:T(8,128)(2,1)S(1)}, bf16[144,512]{1,0:T(8,128)(2,1)S(1)}, u32[]{:S(2)}, u32[]{:S(2)}) collective-permute-start(bf16[144,512]{1,0:T(8,128)(2,1)S(1)} %get-tuple-element.140), channel_id=1, source_target_pairs={{0,8},{8,16},{16,24},{1,9},{9,17},{17,25},{2,10},{10,18},{18,26},{... | collective-permute-start | bytes 442376 | tf_op jit(solution)/shard_map/ppermute | solution.py:632
  22.0 0.1 pad_add_fusion.1.ids_ref
  22.1 0.2 copy.16
  22.3 1.1 copy.15
  23.4 1.1 pad.12.wit_hbm
  24.6 0.0 collective-permute-done.2.north_ref
  24.6 0.0 copy-start.4
  24.6 1.0 copy-done.4
  25.6 15.1 %grid_grad.1 = (bf16[512,2688]{1,0:T(8,128)(2,1)}, f32[4,18,160,128]{3,2,1,0:T(8,128)}, bf16[2048,512]{1,0:T(8,128)(2,1)S(1)}) custom-call(s32[1]{0:T(128)} %constant.109.clone.1.one_ref, bf16[2048,512]{1,0:T(8,128)(2,1)} %bitcast.34, bf16[16,512]{1,0:T(8,128)(2,1)S(1)} %collective-permute-done.1.east_ref, ...), custom_call_target="tpu_custom_call" | custom-call | flops 11534999552 | tf_op jit(solution)/shard_map/grid_grad/pallas_call | solution.py:175
  40.8 0.0 copy-start.11
  40.8 1.3 copy-done.11
  42.1 6.9 %all-to-all-done = bf16[32,32,640]{2,1,0:T(8,128)(2,1)S(1)} async-done(((bf16[32,32,640]{2,1,0:T(8,128)(2,1)}), bf16[32,32,640]{2,1,0:T(8,128)(2,1)S(1)}, u32[]{:S(2)}, u32[]{:S(2)}) %all-to-all-start) | async-done | bytes 1310752 | tf_op jit(solution)/shard_map/all_to_all | solution.py:623
  49.0 1.6 %copy-done.12 = bf16[2048,512]{1,0:T(8,128)(2,1)S(1)} copy-done((bf16[2048,512]{1,0:T(8,128)(2,1)S(1)}, bf16[2048,512]{1,0:T(8,128)(2,1)}, u32[]{:S(2)}) %copy-start.12) | copy-done | bytes 2097176
  50.6 8.8 %encode.1 = (bf16[512,1024]{1,0:T(8,128)(2,1)S(1)}, bf16[2,1024,128]{2,1,0:T(8,128)(2,1)S(1)}, bf16[2,1024,128]{2,1,0:T(8,128)(2,1)S(1)}, bf16[2,112,128]{2,1,0:T(8,128)(2,1)S(1)}, bf16[2,112,128]{2,1,0:T(8,128)(2,1)S(1)}) custom-call(s32[3]{0:T(128)S(1)} %pad_add_fusion.1.ids_ref, bf16[1024,640]{1,0:T(8,128)(2,1)S(1)} %bitcast.29, ...), custom_call_target="tpu_custom_call" | custom-call | flops 11534999552 | tf_op jit(solution)/shard_map/encode/pallas_call | solution.py:270
  59.4 0.1 collective-permute-start.4
  59.5 3.3 %bins.1 = (bf16[2048,512]{1,0:T(8,128)(2,1)S(1)}, bf16[2048,512]{1,0:T(8,128)(2,1)S(1)}) custom-call(bf16[1024,640]{1,0:T(8,128)(2,1)S(1)} %bitcast.30, bf16[512,1024]{1,0:T(8,128)(2,1)S(1)} %get-tuple-element.100.emb_ref), custom_call_target="tpu_custom_call" | custom-call | flops 4614000128 | tf_op jit(solution)/shard_map/bins/pallas_call | solution.py:313
  62.8 0.0 copy-start.8
  62.9 0.0 collective-permute-done.4.got_ref
  62.9 0.7 split.2
  63.6 0.6 copy-done.8
  64.2 0.8 collective-permute-start.5
  65.0 9.0 %mix.1 = (bf16[2688,512]{1,0:T(8,128)(2,1)S(1)}, f32[16,512]{1,0:T(8,128)S(1)}, bf16[2688,512]{1,0:T(8,128)(2,1)S(1)}, f32[18,8,512]{2,1,0:T(8,128)S(1)}, f32[18,8,512]{2,1,0:T(8,128)S(1)}) custom-call(s32[3]{0:T(128)S(1)} %pad_add_fusion.1.ids_ref, bf16[2048,512]{1,0:T(8,128)(2,1)S(1)} %get-tuple-element.101.grid_ref, f32[9,512]{1,0:T(8,128)S(1)} %copy-done.6, ...), custom_call_target="tpu_custom_call" | custom-call | flops 11534999552 | tf_op jit(solution)/shard_map/mix/pallas_call | solution.py:405
  74.1 2.5 %point.1 = (bf16[2,640,128]{2,1,0:T(8,128)(2,1)S(1)}, bf16[2,640,128]{2,1,0:T(8,128)(2,1)S(1)}) custom-call(s32[3]{0:T(128)S(1)} %pad_add_fusion.1.ids_ref, bf16[512,2688]{1,0:T(8,128)(2,1)S(1)} %copy-done.7, bf16[2688,512]{1,0:T(8,128)(2,1)S(1)} %get-tuple-element.103.mix_ref, f32[16,512]{1,0:T(8,128)S(1)} %get-tuple-element.104.gd_ref, ...), custom_call_target="tpu_custom_call" | custom-call | flops 3460499968 | tf_op jit(solution)/shard_map/point/pallas_call | solution.py:439
  76.6 0.1 collective-permute-start.6
  76.7 1.6 %collective-permute-done.6.got_ref = bf16[2,640,128]{2,1,0:T(8,128)(2,1)S(1)} collective-permute-done((bf16[2,640,128]{2,1,0:T(8,128)(2,1)S(1)}, bf16[2,640,128]{2,1,0:T(8,128)(2,1)S(1)}, u32[]{:S(2)}, u32[]{:S(2)}) %collective-permute-start.6) | collective-permute-done | bytes 327712 | tf_op jit(solution)/shard_map/ppermute | solution.py:660
  78.3 0.6 split.3
  78.9 1.3 collective-permute-start.7
  80.2 5.1 %collective-permute-done.7.b_got = bf16[640,128]{1,0:T(8,128)(2,1)S(1)} collective-permute-done((bf16[640,128]{1,0:T(8,128)(2,1)S(1)}, bf16[640,128]{1,0:T(8,128)(2,1)S(1)}, u32[]{:S(2)}, u32[]{:S(2)}) %collective-permute-start.7) | collective-permute-done | bytes 163872 | tf_op jit(solution)/shard_map/ppermute | solution.py:663
  85.2 0.9 merge.1
  86.1 3.5 %all-to-all-start.1 = ((bf16[8,208,128]{2,1,0:T(8,128)(2,1)}), bf16[8,208,128]{2,1,0:T(8,128)(2,1)S(1)}, u32[]{:S(2)}, u32[]{:S(2)}) async-start(bf16[8,208,128]{2,1,0:T(8,128)(2,1)} %merge.1), calls=%async_computation.1 | async-start | bytes 851968 | tf_op jit(solution)/shard_map/all_to_all | solution.py:599
  89.6 1.0 fusion.4
  90.6 1.3 collective-permute-start.9
  91.9 3.0 %collective-permute-start.8 = (bf16[144,512]{1,0:T(8,128)(2,1)S(1)}, bf16[144,512]{1,0:T(8,128)(2,1)S(1)}, u32[]{:S(2)}, u32[]{:S(2)}) collective-permute-start(bf16[144,512]{1,0:T(8,128)(2,1)S(1)} %get-tuple-element.126), channel_id=1, source_target_pairs={{0,8},{8,16},{16,24},{1,9},{9,17},{17,25},{2,10},{10,18},{18,26},{... | collective-permute-start | bytes 442376 | tf_op jit(solution)/shard_map/ppermute | solution.py:674
  94.9 0.2 copy.17
  95.1 0.2 copy.18
  95.3 0.6 collective-permute-done.8.top_ref
  96.0 0.1 scatter-add.16
  96.1 0.1 scatter-add.19
  96.1 0.1 scatter-add.15
  96.2 0.0 copy-start.5
  96.2 2.0 %collective-permute-start.10 = (f32[16,512]{1,0:T(8,128)S(1)}, f32[16,512]{1,0:T(8,128)S(1)}, u32[]{:S(2)}, u32[]{:S(2)}) collective-permute-start(f32[16,512]{1,0:T(8,128)S(1)} %scatter-add.15), channel_id=1, source_target_pairs={{0,1},{1,2},{2,3},{3,4},{4,5},{5,6},{6,7},{7,0},{8,9},{9,10},{10,1... | collective-permute-start | bytes 98312 | tf_op jit(solution)/shard_map/ppermute | solution.py:680
  98.2 2.8 %collective-permute-start.11 = (f32[16,512]{1,0:T(8,128)S(1)}, f32[16,512]{1,0:T(8,128)S(1)}, u32[]{:S(2)}, u32[]{:S(2)}) collective-permute-start(f32[16,512]{1,0:T(8,128)S(1)} %scatter-add.19), channel_id=1, source_target_pairs={{1,0},{2,1},{3,2},{4,3},{5,4},{6,5},{7,6},{0,7},{9,8},{10,9},{11,1... | collective-permute-start | bytes 98312 | tf_op jit(solution)/shard_map/ppermute | solution.py:681
  101.0 2.0 %collective-permute-done.10.refs_0_.left_ref = f32[16,512]{1,0:T(8,128)S(1)} collective-permute-done((f32[16,512]{1,0:T(8,128)S(1)}, f32[16,512]{1,0:T(8,128)S(1)}, u32[]{:S(2)}, u32[]{:S(2)}) %collective-permute-start.10) | collective-permute-done | bytes 32800 | tf_op jit(solution)/shard_map/ppermute | solution.py:680
  103.0 1.0 totals.1
  104.0 9.8 %all-to-all-start.2 = ((bf16[16,208,128]{2,1,0:T(8,128)(2,1)}), bf16[16,208,128]{2,1,0:T(8,128)(2,1)S(1)}, u32[]{:S(2)}, u32[]{:S(2)}) async-start(bf16[16,208,128]{2,1,0:T(8,128)(2,1)} %totals.1), calls=%async_computation.2 | async-start | bytes 1703936 | tf_op jit(solution)/shard_map/all_to_all | solution.py:599
  113.8 1.8 %copy-done.2 = bf16[2688,512]{1,0:T(8,128)(2,1)S(1)} copy-done((bf16[2688,512]{1,0:T(8,128)(2,1)S(1)}, bf16[2688,512]{1,0:T(8,128)(2,1)}, u32[]{:S(2)}) %copy-start.2) | copy-done | bytes 2752536
  115.5 1.6 %copy-done.9 = bf16[2048,512]{1,0:T(8,128)(2,1)S(1)} copy-done((bf16[2048,512]{1,0:T(8,128)(2,1)S(1)}, bf16[2048,512]{1,0:T(8,128)(2,1)}, u32[]{:S(2)}) %copy-start.9) | copy-done | bytes 2097176
  117.1 5.4 %latent.1 = bf16[2048,512]{1,0:T(8,128)(2,1)} custom-call(bf16[2048,512]{1,0:T(8,128)(2,1)S(1)} %copy-done.9, bf16[2688,512]{1,0:T(8,128)(2,1)S(1)} %copy-done.2, bf16[144,512]{1,0:T(8,128)(2,1)S(1)} %collective-permute-done.8.top_ref, bf16[144,512]{1,0:T(8,128)(2,1)S(1)} %collective-permute-done.9.bottom_ref, ...), custom_call_target="tpu_custom_call" | custom-call | flops 5767499776 | tf_op jit(solution)/shard_map/latent/pallas_call | solution.py:474
  122.5 10.6 %all-to-all-done.2.own_ref = bf16[16,208,128]{2,1,0:T(8,128)(2,1)S(1)} async-done(((bf16[16,208,128]{2,1,0:T(8,128)(2,1)}), bf16[16,208,128]{2,1,0:T(8,128)(2,1)S(1)}, u32[]{:S(2)}, u32[]{:S(2)}) %all-to-all-start.2) | async-done | bytes 852000 | tf_op jit(solution)/shard_map/all_to_all | solution.py:599
  133.2 2.4 %collective-permute-done.12.sibling_ref = bf16[16,208,128]{2,1,0:T(8,128)(2,1)S(1)} collective-permute-done((bf16[16,208,128]{2,1,0:T(8,128)(2,1)S(1)}, bf16[16,208,128]{2,1,0:T(8,128)(2,1)S(1)}, u32[]{:S(2)}, u32[]{:S(2)}) %collective-permute-start.12) | collective-permute-done | bytes 852000 | tf_op jit(solution)/shard_map/ppermute | solution.py:688
  135.5 2.7 %unpack.1 = (f32[616,512]{1,0:T(8,128)}, f32[512,512]{1,0:T(8,128)}, f32[512,512]{1,0:T(8,128)}, f32[9,512]{1,0:T(8,128)}) custom-call(s32[3]{0:T(128)S(1)} %pad_add_fusion.1.ids_ref, bf16[16,208,128]{2,1,0:T(8,128)(2,1)S(1)} %all-to-all-done.2.own_ref, bf16[16,208,128]{2,1,0:T(8,128)(2,1)S(1)} %collective-permute-done.12.sibling_ref), custom_call_target="tpu_custom_call" | custom-call | flops 3460499968 | tf_op jit(solution)/shard_map/unpack/pallas_call | solution.py:570
  (32 shorter events, 0.2 us)
Async XLA Ops:
  1.7 10.8 %collective-permute-start = (bf16[16,512]{1,0:T(8,128)(2,1)S(1)}, bf16[16,512]{1,0:T(8,128)(2,1)S(1)}, u32[]{:S(2)}, u32[]{:S(2)}) collective-permute-start(bf16[16,512]{1,0:T(8,128)(2,1)S(1)} %bitcast.35), channel_id=1, source_target_pairs={{0,1},{1,2},{2,3},{3,4},{4,5},{5,6},{6,7},{7,0},{8,9},{9,10},{10,1... | collective-permute-start | bytes 49160 | tf_op jit(solution)/shard_map/ppermute | solution.py:615
  4.7 7.8 %collective-permute-start.1 = (bf16[16,512]{1,0:T(8,128)(2,1)S(1)}, bf16[16,512]{1,0:T(8,128)(2,1)S(1)}, u32[]{:S(2)}, u32[]{:S(2)}) collective-permute-start(bf16[16,512]{1,0:T(8,128)(2,1)S(1)} %bitcast.36), channel_id=1, source_target_pairs={{1,0},{2,1},{3,2},{4,3},{5,4},{6,5},{7,6},{0,7},{9,8},{10,9},{11,1... | collective-permute-start | bytes 49160 | tf_op jit(solution)/shard_map/ppermute | solution.py:616
  8.5 1.1 copy-start.3
  12.5 9.6 %copy-start = (bf16[512,512]{1,0:T(8,128)(2,1)S(1)}, bf16[512,512]{1,0:T(8,128)(2,1)}, u32[]{:S(2)}) copy-start(bf16[512,512]{1,0:T(8,128)(2,1)} %wo_hbm) | copy-start | bytes 1572868
  12.5 9.8 %copy-start.13 = (bf16[616,512]{1,0:T(8,128)(2,1)S(1)}, bf16[616,512]{1,0:T(8,128)(2,1)}, u32[]{:S(2)}) copy-start(bf16[616,512]{1,0:T(8,128)(2,1)} %param.19) | copy-start | bytes 1892356
  12.5 36.5 %all-to-all-start = ((bf16[32,32,640]{2,1,0:T(8,128)(2,1)}), bf16[32,32,640]{2,1,0:T(8,128)(2,1)S(1)}, u32[]{:S(2)}, u32[]{:S(2)}) async-start(bf16[32,32,640]{2,1,0:T(8,128)(2,1)} %bitcast.7), calls=%async_computation | async-start | bytes 2621440 | tf_op jit(solution)/shard_map/all_to_all | solution.py:623
  16.9 7.7 %copy-start.6 = (f32[9,512]{1,0:T(8,128)S(1)}, f32[9,512]{1,0:T(8,128)}, u32[]{:S(2)}) copy-start(f32[9,512]{1,0:T(8,128)} %wd_ref.3) | copy-start | bytes 55300
  17.7 6.9 %collective-permute-start.3 = (bf16[144,512]{1,0:T(8,128)(2,1)}, bf16[144,512]{1,0:T(8,128)(2,1)S(1)}, u32[]{:S(2)}, u32[]{:S(2)}) collective-permute-start(bf16[144,512]{1,0:T(8,128)(2,1)} %get-tuple-element.139), channel_id=1, source_target_pairs={{8,0},{16,8},{24,16},{9,1},{17,9},{25,17},{10,2},{18,10},{26,18},{... | collective-permute-start | bytes 442376 | tf_op jit(solution)/shard_map/ppermute | solution.py:633
  19.0 5.6 %collective-permute-start.2 = (bf16[144,512]{1,0:T(8,128)(2,1)S(1)}, bf16[144,512]{1,0:T(8,128)(2,1)S(1)}, u32[]{:S(2)}, u32[]{:S(2)}) collective-permute-start(bf16[144,512]{1,0:T(8,128)(2,1)S(1)} %get-tuple-element.140), channel_id=1, source_target_pairs={{0,8},{8,16},{16,24},{1,9},{9,17},{17,25},{2,10},{10,18},{18,26},{... | collective-permute-start | bytes 442376 | tf_op jit(solution)/shard_map/ppermute | solution.py:632
  24.6 1.0 copy-start.4
  40.8 1.3 copy-start.11
  49.0 1.6 %copy-start.12 = (bf16[2048,512]{1,0:T(8,128)(2,1)S(1)}, bf16[2048,512]{1,0:T(8,128)(2,1)}, u32[]{:S(2)}) copy-start(bf16[2048,512]{1,0:T(8,128)(2,1)} %copy-done.11) | copy-start | bytes 6291460
  59.4 3.5 %collective-permute-start.4 = (bf16[2,1024,128]{2,1,0:T(8,128)(2,1)S(1)}, bf16[2,1024,128]{2,1,0:T(8,128)(2,1)S(1)}, u32[]{:S(2)}, u32[]{:S(2)}) collective-permute-start(bf16[2,1024,128]{2,1,0:T(8,128)(2,1)S(1)} %get-tuple-element.96), channel_id=1, source_target_pairs={{0,8},{8,0},{1,9},{9,1},{2,10},{10,2},{3,11},{11,3},{4,12},{12,4},... | collective-permute-start | bytes 1572872 | tf_op jit(solution)/shard_map/ppermute | solution.py:651
  59.5 5.5 %copy-start.10 = (f32[4,18,160,128]{3,2,1,0:T(8,128)S(1)}, f32[4,18,160,128]{3,2,1,0:T(8,128)}, u32[]{:S(2)}) copy-start(f32[4,18,160,128]{3,2,1,0:T(8,128)} %get-tuple-element.102.gm_ref) | copy-start | bytes 17694724
  62.8 1.3 copy-start.8
  64.2 9.9 %collective-permute-start.5 = (bf16[1024,128]{1,0:T(8,128)(2,1)S(1)}, bf16[1024,128]{1,0:T(8,128)(2,1)S(1)}, u32[]{:S(2)}, u32[]{:S(2)}) collective-permute-start(bf16[1024,128]{1,0:T(8,128)(2,1)S(1)} %get-tuple-element.98), channel_id=1, source_target_pairs={{0,16},{16,0},{1,17},{17,1},{2,18},{18,2},{3,19},{19,3},{4,20},{20... | collective-permute-start | bytes 786440 | tf_op jit(solution)/shard_map/ppermute | solution.py:658
  65.0 9.1 %copy-start.7 = (bf16[512,2688]{1,0:T(8,128)(2,1)S(1)}, bf16[512,2688]{1,0:T(8,128)(2,1)}, u32[]{:S(2)}) copy-start(bf16[512,2688]{1,0:T(8,128)(2,1)} %get-tuple-element.99.cott_ref) | copy-start | bytes 8257540
  74.0 2.6 %copy-start.1 = (bf16[2688,512]{1,0:T(8,128)(2,1)}, bf16[2688,512]{1,0:T(8,128)(2,1)S(1)}, u32[]{:S(2)}) copy-start(bf16[2688,512]{1,0:T(8,128)(2,1)S(1)} %get-tuple-element.116.mix_ref) | copy-start | bytes 8257540
  76.6 1.7 %collective-permute-start.6 = (bf16[2,640,128]{2,1,0:T(8,128)(2,1)S(1)}, bf16[2,640,128]{2,1,0:T(8,128)(2,1)S(1)}, u32[]{:S(2)}, u32[]{:S(2)}) collective-permute-start(bf16[2,640,128]{2,1,0:T(8,128)(2,1)S(1)} %get-tuple-element.108), channel_id=1, source_target_pairs={{0,8},{8,0},{1,9},{9,1},{2,10},{10,2},{3,11},{11,3},{4,12},{12,4},... | collective-permute-start | bytes 983048 | tf_op jit(solution)/shard_map/ppermute | solution.py:660
  78.9 6.3 %collective-permute-start.7 = (bf16[640,128]{1,0:T(8,128)(2,1)S(1)}, bf16[640,128]{1,0:T(8,128)(2,1)S(1)}, u32[]{:S(2)}, u32[]{:S(2)}) collective-permute-start(bf16[640,128]{1,0:T(8,128)(2,1)S(1)} %get-tuple-element.110), channel_id=1, source_target_pairs={{0,16},{16,0},{1,17},{17,1},{2,18},{18,2},{3,19},{19,3},{4,20},{20... | collective-permute-start | bytes 491528 | tf_op jit(solution)/shard_map/ppermute | solution.py:663
  86.1 16.9 %all-to-all-start.1 = ((bf16[8,208,128]{2,1,0:T(8,128)(2,1)}), bf16[8,208,128]{2,1,0:T(8,128)(2,1)S(1)}, u32[]{:S(2)}, u32[]{:S(2)}) async-start(bf16[8,208,128]{2,1,0:T(8,128)(2,1)} %merge.1), calls=%async_computation.1 | async-start | bytes 851968 | tf_op jit(solution)/shard_map/all_to_all | solution.py:599
  90.6 5.5 %collective-permute-start.9 = (bf16[144,512]{1,0:T(8,128)(2,1)S(1)}, bf16[144,512]{1,0:T(8,128)(2,1)S(1)}, u32[]{:S(2)}, u32[]{:S(2)}) collective-permute-start(bf16[144,512]{1,0:T(8,128)(2,1)S(1)} %get-tuple-element.125), channel_id=1, source_target_pairs={{8,0},{16,8},{24,16},{9,1},{17,9},{25,17},{10,2},{18,10},{26,18},{... | collective-permute-start | bytes 442376 | tf_op jit(solution)/shard_map/ppermute | solution.py:675
  91.9 4.0 %collective-permute-start.8 = (bf16[144,512]{1,0:T(8,128)(2,1)S(1)}, bf16[144,512]{1,0:T(8,128)(2,1)S(1)}, u32[]{:S(2)}, u32[]{:S(2)}) collective-permute-start(bf16[144,512]{1,0:T(8,128)(2,1)S(1)} %get-tuple-element.126), channel_id=1, source_target_pairs={{0,8},{8,16},{16,24},{1,9},{9,17},{17,25},{2,10},{10,18},{18,26},{... | collective-permute-start | bytes 442376 | tf_op jit(solution)/shard_map/ppermute | solution.py:674
  96.2 17.5 %copy-start.5 = (bf16[512,512]{1,0:T(8,128)(2,1)S(1)}, bf16[512,512]{1,0:T(8,128)(2,1)}, u32[]{:S(2)}) copy-start(bf16[512,512]{1,0:T(8,128)(2,1)} %wp_ref.3) | copy-start | bytes 1572868
  96.2 6.8 %collective-permute-start.10 = (f32[16,512]{1,0:T(8,128)S(1)}, f32[16,512]{1,0:T(8,128)S(1)}, u32[]{:S(2)}, u32[]{:S(2)}) collective-permute-start(f32[16,512]{1,0:T(8,128)S(1)} %scatter-add.15), channel_id=1, source_target_pairs={{0,1},{1,2},{2,3},{3,4},{4,5},{5,6},{6,7},{7,0},{8,9},{9,10},{10,1... | collective-permute-start | bytes 98312 | tf_op jit(solution)/shard_map/ppermute | solution.py:680
  98.2 4.8 %collective-permute-start.11 = (f32[16,512]{1,0:T(8,128)S(1)}, f32[16,512]{1,0:T(8,128)S(1)}, u32[]{:S(2)}, u32[]{:S(2)}) collective-permute-start(f32[16,512]{1,0:T(8,128)S(1)} %scatter-add.19), channel_id=1, source_target_pairs={{1,0},{2,1},{3,2},{4,3},{5,4},{6,5},{7,6},{0,7},{9,8},{10,9},{11,1... | collective-permute-start | bytes 98312 | tf_op jit(solution)/shard_map/ppermute | solution.py:681
  104.0 29.2 %all-to-all-start.2 = ((bf16[16,208,128]{2,1,0:T(8,128)(2,1)}), bf16[16,208,128]{2,1,0:T(8,128)(2,1)S(1)}, u32[]{:S(2)}, u32[]{:S(2)}) async-start(bf16[16,208,128]{2,1,0:T(8,128)(2,1)} %totals.1), calls=%async_computation.2 | async-start | bytes 1703936 | tf_op jit(solution)/shard_map/all_to_all | solution.py:599
  113.8 1.8 %copy-start.2 = (bf16[2688,512]{1,0:T(8,128)(2,1)S(1)}, bf16[2688,512]{1,0:T(8,128)(2,1)}, u32[]{:S(2)}) copy-start(bf16[2688,512]{1,0:T(8,128)(2,1)} %copy-done.1) | copy-start | bytes 8257540
  115.5 1.6 %copy-start.9 = (bf16[2048,512]{1,0:T(8,128)(2,1)S(1)}, bf16[2048,512]{1,0:T(8,128)(2,1)}, u32[]{:S(2)}) copy-start(bf16[2048,512]{1,0:T(8,128)(2,1)} %copy-done.8) | copy-start | bytes 6291460
  133.2 2.4 %collective-permute-start.12 = (bf16[16,208,128]{2,1,0:T(8,128)(2,1)S(1)}, bf16[16,208,128]{2,1,0:T(8,128)(2,1)S(1)}, u32[]{:S(2)}, u32[]{:S(2)}) collective-permute-start(bf16[16,208,128]{2,1,0:T(8,128)(2,1)S(1)} %all-to-all-done.2.own_ref), channel_id=1, source_target_pairs={{0,8},{8,0},{1,9},{9,1},{2,10},{10,2},{3,11},{11,3},{4,12},{12,4},... | collective-permute-start | bytes 2555912 | tf_op jit(solution)/shard_map/ppermute | solution.py:688

commit v4 on v3

--- a/solution.py
+++ b/solution.py
@@ -85,24 +85,38 @@
     )(places, rows)
 
 
-PAD = 16
-CHUNK = 32
-
-
-def shifted(ref, n, row, start, by, size):
-    return ref[n, row, pl.ds(start + by, size), :]
+GROUPS = 8
+CHUNK = 8 * GROUPS
+
+
+def column_of(place, per):
+    return per * (place % GROUPS) + place // GROUPS
+
+
+def place_of(column, per):
+    return GROUPS * (column % per) + column // per
+
+
+def one_hot(wanted, count):
+    hit = wanted == lax.broadcasted_iota(i32, (wanted.shape[0], count), 1)
+    return hit.astype(f32).astype(bf16)
 
 
 def grid_grad_kernel(
-    clat, clon, wide, one_ref, cot_ref, east_ref, west_ref, north_ref, south_ref, wp_ref, wd_ref,
-    cott_hbm, gm_hbm, gg_hbm, cott_ref, gm_ref, gg_ref, cot_ext, east, west, sems,
+    clat, clon, wide, cot_ref, east_ref, west_ref, north_ref, south_ref, wp_ref, wd_ref,
+    cott_hbm, gm_hbm, gg_hbm, cott_ref, gm_ref, gg_ref, cot_ext, cot_own, east, west, sems,
 ):
     width = wp_ref.shape[0]
+    per = clon // GROUPS
     w_point = wp_ref[...]
-    one = one_ref[0]
     east[...] = east_ref[...].astype(f32)
     west[...] = west_ref[...].astype(f32)
     line = lax.broadcasted_iota(i32, (wide - clon, width), 0)
+    place = lax.broadcasted_iota(i32, (wide, 1), 0)
+    column = column_of(place, per) - 1
+    spread_order = one_hot(jnp.where(column < 0, wide - 1, column), wide)
+    ends = jnp.where(place == clon + GROUPS - 1, clon, jnp.where(place == clon + GROUPS, wide - 1, -1))
+    point_order = one_hot(jnp.where(place < clon, column_of(place, per), ends), wide)
     puts = [
         pltpu.make_async_copy(source, target, sems.at[i])
         for i, (source, target) in enumerate(
@@ -110,27 +124,25 @@
         )
     ]
 
-    def mixed_grad(e, rows):
-        g = dot(rows, w_point, (1, 1)).astype(bf16).astype(f32)
+    def reorder(e, rows):
+        ordered = dot(spread_order, rows)
+        g = dot(ordered.astype(bf16), w_point, (1, 1)).astype(bf16).astype(f32)
         for n in range(width // LANES):
-            cols = slice(n * LANES, (n + 1) * LANES)
-            gm_ref[n, e, 0:PAD, :] = g[clon:, cols]
-            gm_ref[n, e, PAD : PAD + clon, :] = g[:clon, cols]
-            gm_ref[n, e, PAD + clon :, :] = g[clon:, cols]
+            gm_ref[n, e] = g[:, n * LANES : (n + 1) * LANES]
+        cot_ext[pl.ds(pl.multiple_of(e * wide, 16), wide), :] = dot(point_order, rows).astype(bf16)
+        return ordered
 
     def matmul(i, carry):
-        at = pl.multiple_of((i + 1) * wide, 16)
-        cot_ext[pl.ds(at, clon), :] = cot_ref[pl.ds(pl.multiple_of(i * clon, 16), clon), :]
+        at = pl.ds(pl.multiple_of(i * clon, 16), clon)
         tail = jnp.where(
             line == 0, east[pl.ds(i, 1), :], jnp.where(line == wide - clon - 1, west[pl.ds(i, 1), :], 0.0)
         )
-        cot_ext[pl.ds(at + clon, wide - clon), :] = tail.astype(bf16)
-        mixed_grad(i + 1, cot_ext[pl.ds(at, wide), :])
+        ordered = reorder(i + 1, jnp.concatenate([cot_ref[at, :], tail.astype(bf16)], axis=0))
+        cot_own[at, :] = ordered[GROUPS : GROUPS + clon].astype(bf16)
         return carry
 
-    for ref, e in ((north_ref, 0), (south_ref, clat + 1)):
-        cot_ext[e * wide : (e + 1) * wide, :] = ref[...]
-        mixed_grad(e, ref[...])
+    reorder(0, north_ref[...])
+    reorder(clat + 1, south_ref[...])
     used = (clat + 2) * wide
     cot_ext[used:, :] = jnp.zeros((cot_ext.shape[0] - used, width), bf16)
     lax.fori_loop(0, clat, matmul, 0)
@@ -139,14 +151,15 @@
     def conv(i, carry):
         for n in range(width // LANES):
             cols = slice(n * LANES, (n + 1) * LANES)
-            for j in range(0, clon, CHUNK):
-                at = pl.ds(pl.multiple_of(i * clon + j, CHUNK), CHUNK)
-                out = cot_ref[at, cols].astype(f32)
+            for c in range(0, clon, CHUNK):
+                at = pl.ds(pl.multiple_of(i * clon + c, 16), CHUNK)
+                out = cot_own[at, cols].astype(f32)
                 for a in range(3):
+                    g = gm_ref[n, i + 2 - a, c : c + CHUNK + 2 * GROUPS, :]
                     for b in range(3):
                         k = 3 * a + b
-                        g = shifted(gm_ref, n, i + 2 - a, PAD + j, (1 - b) * one, CHUNK)
-                        out = out + wd_ref[k : k + 1, cols] * g
+                        first = GROUPS * (2 - b)
+                        out = out + wd_ref[k : k + 1, cols] * g[first : first + CHUNK]
                 gg_ref[at, cols] = out.astype(bf16)
         return carry
 
@@ -164,27 +177,27 @@
         put.wait()
 
 
-def grid_grad(one, cot, sides, w_point, w_depth, clat, clon, wide):
+def grid_grad(cot, sides, w_point, w_depth, clat, clon, wide):
     width = w_point.shape[0]
     ext_rows = round_up((clat + 2) * wide, LANES)
     outs = (
         jax.ShapeDtypeStruct((width, ext_rows), bf16),
-        jax.ShapeDtypeStruct((width // LANES, clat + 2, clon + 2 * PAD, LANES), f32),
+        jax.ShapeDtypeStruct((width // LANES, clat + 2, wide, LANES), f32),
         jax.ShapeDtypeStruct((clat * clon, width), bf16),
     )
     return pl.pallas_call(
         functools.partial(grid_grad_kernel, clat, clon, wide),
         out_shape=outs,
-        in_specs=[smem()] + [vmem()] * 7,
+        in_specs=[vmem()] * 7,
         out_specs=(anywhere(),) * 3,
         scratch_shapes=[pltpu.VMEM(x.shape, x.dtype) for x in outs]
-        + [pltpu.VMEM((ext_rows, width), bf16)]
+        + [pltpu.VMEM((ext_rows, width), bf16), pltpu.VMEM((clat * clon, width), bf16)]
         + [pltpu.VMEM((clat, width), f32)] * 2
         + [pltpu.SemaphoreType.DMA((3,))],
-        compiler_params=params(50),
+        compiler_params=params(58),
         cost_estimate=cost(10),
         name="grid_grad",
-    )(one, cot, *sides, w_point, w_depth)
+    )(cot, *sides, w_point, w_depth)
 
 
 def write_halves(core, total, start, mine_ref, other_ref, first=0, size=None):
@@ -227,9 +240,9 @@
     for t in range(slots // step):
         at = slice(t * step, (t + 1) * step)
         rows = rows_ref[at, :]
-        place = rows[:, spec : spec + 1].astype(f32) * clon + rows[:, spec + 1 : spec + 2].astype(f32)
-        hits = place.astype(i32) == lax.broadcasted_iota(i32, (step, cells), 1)
-        hits = hits.astype(f32).astype(bf16)
+        line = rows[:, spec : spec + 1].astype(f32).astype(i32)
+        column = rows[:, spec + 1 : spec + 2].astype(f32).astype(i32)
+        hits = one_hot(line * clon + place_of(column, clon // GROUPS), cells)
         if t == 0:
             loads[0].wait()
         preact = dot(wit_ref[...], rows, (1, 1))
@@ -279,43 +292,58 @@
             pltpu.VMEM((width, width), f32),
             pltpu.SemaphoreType.DMA((len(weights),)),
         ],
-        compiler_params=params(24),
+        compiler_params=params(59),
         cost_estimate=cost(10),
         name="encode",
     )(ids, rows, *weights)
 
 
-def bins_kernel(spec, clon, rows_ref, emb_ref, grid_ref, grid_hbm, sem):
+def bins_kernel(spec, clat, clon, wide, rows_ref, emb_ref, wide_ref, grid_hbm, grid_ref, sem):
     slots, spec_wide = rows_ref.shape
-    cells = grid_ref.shape[0]
+    width = emb_ref.shape[0]
+    blocks = width // LANES
     last = rows_ref[:, spec_wide - LANES :]
     col = spec - (spec_wide - LANES)
     lane = lax.broadcasted_iota(i32, (16, LANES), 1)
     pick = jnp.where(lane == col, float(clon), jnp.where(lane == col + 1, 1.0, 0.0)).astype(bf16)
-    place = dot(pick, last, (1, 1))[0:1, :].astype(i32)
-    block = 4 * clon
+    cell = dot(pick, last, (1, 1))[0:1, :].astype(i32)
+    lines = 4
+    place = lax.broadcasted_iota(i32, (wide, 1), 0)
+    column = column_of(place, clon // GROUPS) - 1
+    inside = (column >= 0) & (column < clon)
+    wanted = [jnp.where(inside, column + k * clon, -clat * clon) for k in range(lines)]
+    wanted = jnp.concatenate(wanted, axis=0)
+    empty = jnp.zeros((blocks, 2, wide, LANES), f32)
+    wide_ref[:, 0:2] = empty
+    wide_ref[:, clat + 2 :] = empty
 
     def body(t, carry):
-        cell = lax.broadcasted_iota(i32, (block, slots), 0) + t * block
-        hits = (place == cell).astype(f32).astype(bf16)
-        grid = dot(hits, emb_ref[...], (1, 1)).astype(bf16)
-        grid_ref[pl.ds(pl.multiple_of(t * block, 16), block), :] = grid
+        hits = (cell == wanted + t * (lines * clon)).astype(f32).astype(bf16)
+        grid = dot(hits, emb_ref[...], (1, 1)).astype(bf16).astype(f32)
+        for k in range(lines):
+            line = grid[k * wide : (k + 1) * wide]
+            for n in range(blocks):
+                wide_ref[n, t * lines + k + 2] = line[:, n * LANES : (n + 1) * LANES]
+            at = pl.ds(pl.multiple_of((t * lines + k) * clon, 16), clon)
+            grid_ref[at, :] = line[GROUPS : GROUPS + clon].astype(bf16)
         return carry
 
-    lax.fori_loop(0, cells // block, body, 0)
+    lax.fori_loop(0, clat // lines, body, 0)
     put = pltpu.make_async_copy(grid_ref, grid_hbm, sem)
     put.start()
     put.wait()
 
 
-def bins(rows, emb, spec, cells, clon):
-    grid = jax.ShapeDtypeStruct((cells, emb.shape[0]), bf16)
-    return pl.pallas_call(
-        functools.partial(bins_kernel, spec, clon),
-        out_shape=(grid, grid),
+def bins(rows, emb, spec, clat, clon, wide):
+    width = emb.shape[0]
+    grid = jax.ShapeDtypeStruct((clat * clon, width), bf16)
+    wide_grid = jax.ShapeDtypeStruct((width // LANES, clat + 4, wide, LANES), f32)
+    return pl.pallas_call(
+        functools.partial(bins_kernel, spec, clat, clon, wide),
+        out_shape=(wide_grid, grid),
         in_specs=[vmem()] * 2,
         out_specs=(vmem(), anywhere()),
-        scratch_shapes=[pltpu.SemaphoreType.DMA],
+        scratch_shapes=[pltpu.VMEM(grid.shape, bf16), pltpu.SemaphoreType.DMA],
         compiler_params=params(12),
         cost_estimate=cost(4),
         name="bins",
@@ -323,11 +351,10 @@
 
 
 def mix_kernel(
-    clat, clon, wide, ids_ref, grid_ref, wd_ref, gm_ref, after_ref,
-    mix_ref, gd_ref, mix_hbm, east_hbm, west_hbm, east_ref, west_ref, padded, gd, sems,
+    clat, clon, wide, grid_ref, wd_ref, gm_ref, after_ref,
+    mix_ref, gd_ref, mix_hbm, east_hbm, west_hbm, east_ref, west_ref, gd, sems,
 ):
-    one = ids_ref[1]
-    width = grid_ref.shape[1]
+    width = wd_ref.shape[1]
     blocks = width // LANES
     puts = [
         pltpu.make_async_copy(source, target, sems.at[i])
@@ -336,53 +363,39 @@
         )
     ]
     gd[...] = jnp.zeros_like(gd)
-    side = jnp.zeros((blocks, clat + 4, PAD, LANES), f32)
-    padded[:, :, :PAD, :] = side
-    padded[:, :, PAD + clon :, :] = side
-    for e in (0, 1, clat + 2, clat + 3):
-        padded[:, e, PAD : PAD + clon, :] = jnp.zeros((blocks, clon, LANES), f32)
     used = (clat + 2) * wide
     mix_ref[used:, :] = jnp.zeros((mix_ref.shape[0] - used, width), bf16)
-
-    def widen(i, carry):
-        at = pl.ds(pl.multiple_of(i * clon, 16), clon)
-        for n in range(blocks):
-            part = grid_ref[at, n * LANES : (n + 1) * LANES].astype(f32)
-            padded[n, i + 2, PAD : PAD + clon, :] = part
-        return carry
-
-    lax.fori_loop(0, clat, widen, 0)
+    group = lax.broadcasted_iota(i32, (GROUPS, LANES), 0)
 
     def conv(e, carry):
         for n in range(blocks):
             cols = slice(n * LANES, (n + 1) * LANES)
             weights = [wd_ref[k : k + 1, cols] for k in range(9)]
             taps = [gd[8 * k : 8 * k + 8, cols] for k in range(9)]
-            for j in range(0, clon, CHUNK):
-                at = PAD + j
-                grads = [shifted(gm_ref, n, e, at, (1 - b) * one, CHUNK) for b in range(3)]
+            for c in range(0, clon, CHUNK):
+                grads = gm_ref[n, e, c : c + CHUNK + 2 * GROUPS, :]
                 mixed = None
                 for a in range(3):
+                    cells = grid_ref[n, e + a, c : c + CHUNK + 2 * GROUPS, :]
+                    middle = cells[GROUPS : GROUPS + CHUNK]
                     for b in range(3):
                         k = 3 * a + b
-                        cell = shifted(padded, n, e + a, at, (b - 1) * one, CHUNK)
-                        mixed = weights[k] * cell if mixed is None else mixed + weights[k] * cell
-                    middle = padded[n, e + a, at : at + CHUNK, :]
-                    for b in range(3):
-                        k = 3 * a + b
-                        part = (grads[b] * middle).reshape(CHUNK // 8, 8, LANES)
+                        term = weights[k] * cells[GROUPS * b : GROUPS * b + CHUNK]
+                        mixed = term if mixed is None else mixed + term
+                        first = GROUPS * (2 - b)
+                        part = (grads[first : first + CHUNK] * middle).reshape(CHUNK // 8, 8, LANES)
                         taps[k] = taps[k] + jnp.sum(part, axis=0)
-                out_at = pl.ds(pl.multiple_of(e * wide + j, 16), CHUNK)
+                out_at = pl.ds(pl.multiple_of(e * wide + c, 16), CHUNK)
                 mix_ref[out_at, cols] = mixed.astype(bf16)
             for k in range(9):
                 gd[8 * k : 8 * k + 8, cols] = taps[k]
             ends = []
-            for b, at in ((0, PAD + clon), (2, PAD - 8)):
+            for b, at, valid in ((0, clon, GROUPS - 1), (2, GROUPS, 0)):
                 end = None
                 for a in range(3):
-                    term = weights[3 * a + b] * shifted(padded, n, e + a, at, (b - 1) * one, 8)
+                    term = weights[3 * a + b] * grid_ref[n, e + a, at : at + GROUPS, :]
                     end = term if end is None else end + term
-                ends.append(end)
+                ends.append(jnp.where(group == valid, end, 0.0))
             east_ref[e, :, cols] = ends[0]
             west_ref[e, :, cols] = ends[1]
             out_at = pl.ds(pl.multiple_of(e * wide + clon, 16), wide - clon)
@@ -398,25 +411,21 @@
         put.wait()
 
 
-def mix(ids, grid, w_depth, g_mixed, after, clat, clon, wide):
-    width = grid.shape[1]
-    column = jax.ShapeDtypeStruct((clat + 2, 8, width), f32)
+def mix(grid, w_depth, g_mixed, after, clat, clon, wide):
+    width = w_depth.shape[1]
+    column = jax.ShapeDtypeStruct((clat + 2, GROUPS, width), f32)
     ext = jax.ShapeDtypeStruct((round_up((clat + 2) * wide, LANES), width), bf16)
     return pl.pallas_call(
         functools.partial(mix_kernel, clat, clon, wide),
         out_shape=(ext, jax.ShapeDtypeStruct((16, width), f32), ext, column, column),
-        in_specs=[smem()] + [vmem()] * 3 + [anywhere()],
+        in_specs=[vmem()] * 3 + [anywhere()],
         out_specs=(vmem(),) * 2 + (anywhere(),) * 3,
         scratch_shapes=[pltpu.VMEM(column.shape, column.dtype)] * 2
-        + [
-            pltpu.VMEM((width // LANES, clat + 4, clon + 2 * PAD, LANES), f32),
-            pltpu.VMEM((72, width), f32),
-            pltpu.SemaphoreType.DMA((3,)),
-        ],
-        compiler_params=params(16),
-        cost_estimate=cost(10),
+        + [pltpu.VMEM((72, width), f32), pltpu.SemaphoreType.DMA((3,))],
+        compiler_params=params(8),
+        cost_estimate=cost(8),
         name="mix",
-    )(ids, grid, w_depth, g_mixed, after)
+    )(grid, w_depth, g_mixed, after)
 
 
 def point_kernel(
@@ -454,6 +463,8 @@
     width = wp_ref.shape[0]
     w_point = wp_ref[...]
     line = lax.broadcasted_iota(i32, (clon, width), 0)
+    column = lax.broadcasted_iota(i32, (clon, 1), 0)
+    natural_order = one_hot(place_of(column, clon // GROUPS), clon)
 
     def body(i, carry):
         at = pl.ds(pl.multiple_of(i * clon, 16), clon)
@@ -464,7 +475,7 @@
             line == 0, left_ref[pl.ds(i, 1), :], jnp.where(line == clon - 1, right_ref[pl.ds(i, 1), :], 0.0)
         )
         out = grid_ref[at, :].astype(f32) + dot(mixed.astype(bf16), w_point)
-        out_ref[at, :] = out.astype(bf16)
+        out_ref[at, :] = dot(natural_order, out.astype(bf16)).astype(bf16)
         return carry
 
     lax.fori_loop(0, clat, body, 0)
@@ -483,7 +494,7 @@
 
 
 def split_kernel(ids_ref, mine_ref, got_ref, keep_ref, send_ref):
-    x = ids_ref[2]
+    x = ids_ref[1]
     for ref, i in ((keep_ref, x), (send_ref, 1 - x)):
         at = pl.ds(i, 1)
         ref[...] = (mine_ref[at].astype(f32) + got_ref[at].astype(f32))[0].astype(bf16)
@@ -502,7 +513,8 @@
     )(ids, mine, got)
 
 
-def merge_kernel(a_keep, a_got, b_keep, b_got, out_ref):
+def merge_kernel(a_keep, a_got, b_keep, b_got, *refs):
+    out_ref = refs[-1]
     count = out_ref.shape[0]
     start = 0
     for keep, got in ((a_keep, a_got), (b_keep, b_got)):
@@ -512,17 +524,17 @@
         start += size
 
 
-def merge(a_keep, a_got, b_keep, b_got, count):
+def merge(a_keep, a_got, b_keep, b_got, count, *after):
     rows = (a_keep.shape[0] + b_keep.shape[0]) // count
     return pl.pallas_call(
         merge_kernel,
         out_shape=jax.ShapeDtypeStruct((count, rows, LANES), bf16),
-        in_specs=[vmem()] * 4,
+        in_specs=[vmem()] * 4 + [anywhere()] * len(after),
         out_specs=vmem(),
         compiler_params=params(8),
         cost_estimate=cost(1),
         name="merge",
-    )(a_keep, a_got, b_keep, b_got)
+    )(a_keep, a_got, b_keep, b_got, *after)
 
 
 def totals_kernel(parts_ref, *refs):
@@ -607,8 +619,7 @@
     cells = clat * clon
     wide = clon + 16
     spec_wide = round_up(spec + 2, LANES)
-    ids = jnp.stack([lax.axis_index("core"), jnp.int32(1), lax.axis_index("x")])
-    one = jnp.ones((1,), i32)
+    ids = jnp.stack([lax.axis_index("core"), lax.axis_index("x")])
     east_way, west_way = neighbours("lon", True)
     south_way, north_way = neighbours(LAT, False)
 
@@ -632,7 +643,6 @@
     from_north = lax.ppermute(edge_row(clat - 1), LAT, south_way)
     from_south = lax.ppermute(edge_row(0), LAT, north_way)
     cot_t, g_mixed, g_grid = grid_grad(
-        one,
         cotangent.reshape(cells, width),
         (from_east, from_west, from_north, from_south),
         w_point, w_depth, clat, clon, wide,
@@ -649,36 +659,38 @@
         ids, arrived, (w_in_t, w_out.T, g_grid, w_out), spec, clon, rows_a, rest
     )
     got_a = lax.ppermute(other_a, "core", SWAP)
-    grid_here, grid = bins(arrived, emb, spec, cells, clon)
+    grid_here, grid = bins(arrived, emb, spec, clat, clon, wide)
     keep_a, send_a = split(ids, mine_a, got_a) if pairs else (mine_a, got_a)
 
     mix_here, grad_depth, mix_ext, east, west = mix(
-        ids, grid_here, w_depth, g_mixed, keep_a, clat, clon, wide
+        grid_here, w_depth, g_mixed, keep_a, clat, clon, wide
     )
     got_a = lax.ppermute(send_a, "x", SWAP) if pairs else send_a
     mine_b, other_b = point(ids, cot_t, mix_here, grad_depth, rest_halves, got_a, rows_b)
     got_b = lax.ppermute(other_b, "core", SWAP)
     if pairs:
         keep_b, send_b = split(ids, mine_b, got_b)
+        send_b, mix_ext = lax.optimization_barrier((send_b, mix_ext))
         got_b = lax.ppermute(send_b, "x", SWAP)
-        summed = merge(keep_a, got_a, keep_b, got_b, lax.axis_size("lon"))
+
+    top = lax.ppermute(mix_ext[(clat + 1) * wide : (clat + 2) * wide], LAT, south_way)
+    bottom = lax.ppermute(mix_ext[:wide], LAT, north_way)
+    if pairs:
+        summed = merge(keep_a, got_a, keep_b, got_b, lax.axis_size("lon"), top, bottom)
     else:
         sums = [
             (mine.astype(f32) + got.astype(f32)).astype(bf16).reshape(chips, -1, LANES)
             for mine, got in ((keep_a, send_a), (mine_b, got_b))
         ]
         summed = jnp.concatenate(sums, axis=1)
-    summed, mix_ext, east, west = lax.optimization_barrier((summed, mix_ext, east, west))
+    summed, top, bottom, east, west = lax.optimization_barrier((summed, top, bottom, east, west))
     parts = spread(summed, "lon" if pairs else CHIPS)
-
-    top = lax.ppermute(mix_ext[(clat + 1) * wide : (clat + 2) * wide], LAT, south_way)
-    bottom = lax.ppermute(mix_ext[:wide], LAT, north_way)
 
     def edge_column(own, at):
         return own[1:-1].at[0].add(top[at].astype(f32)).at[-1].add(bottom[at].astype(f32))
 
-    left = lax.ppermute(edge_column(east[:, 0], clon), "lon", east_way)
-    right = lax.ppermute(edge_column(west[:, 7], wide - 1), "lon", west_way)
+    left = lax.ppermute(edge_column(east[:, GROUPS - 1], clon + GROUPS - 1), "lon", east_way)
+    right = lax.ppermute(edge_column(west[:, 0], clon + GROUPS), "lon", west_way)
     full = spread(totals(parts, chips, left, right), CHIPS)
     latent = finish_latent(grid, mix_ext, (top, bottom, left, right), w_point, clat, clon, wide)
 

time: 139 us -> 140 us (level)
  starting transfers between devices: 38.3 us -> 33.3 us
  waiting for transfers between devices: 29.2 us -> 33.2 us
  Pallas kernels: 52.9 us -> 55.6 us
    ppermute x2, waiting for transfers between devices: 2 us -> 7.59 us  [the longest x1 7.58 us: on_device(): lax.ppermute(edge_column(east[:, GROUPS - 1], clon + GROUPS - 1), 'lon',...]
    all_to_all x2, starting transfers between devices: 13.2 us -> 8.18 us  [spread(): return lax.all_to_all(values, axes, split_axis=0, concat_axis=0, tiled=True)]
    ppermute x1, waiting for transfers between devices: 5.05 us -> 0.34 us  [on_device(): got_b = lax.ppermute(send_b, 'x', SWAP)]
    pallas_call x1, Pallas kernels: 9.02 us -> 6.44 us  [mix(): pl.pallas_call(functools.partial(mix_kernel, clat, clon, wide), out_shape...]
    pallas_call x1, Pallas kernels: 5.39 us -> 7.82 us  [finish_latent(): pl.pallas_call(functools.partial(latent_kernel, clat, clon, wide), out_sh...]
    pallas_call x1, Pallas kernels: 8.8 us -> 10.6 us  [encode(): pl.pallas_call(functools.partial(encode_kernel, spec, clon), out_shape=(j...]
    unnamed x30 -> x42, local copies, waits for them, and re-layouts: 9.04 us -> 9.46 us
  transfers between devices with their start and end apart: 16 -> 16, of which waited for: 7 -> 8; matrix products, arithmetic and copies ran while one was open for 5% -> 4% of each run, Pallas kernels for 26% -> 26%
where the time goes in v4:
time: 140 us; the launch traced here: 139 us
  Pallas kernels  55.6 us (40%)
  starting transfers between devices  33.3 us (24%)
  waiting for transfers between devices  33.2 us (24%)
  local copies, waits for them, and re-layouts  14.4 us (10%)
  other arithmetic  1.5 us (1%)
    pallas_call x1, Pallas kernels, grid_grad(): pl.pallas_call(functools.partial(grid_grad_kernel, clat, clon, wide), out...  15.8 us
    all_to_all x2, waiting for transfers between devices, spread(): return lax.all_to_all(values, axes, split_axis=0, concat_axis=0, tiled=True)  10.6 us
    pallas_call x1, Pallas kernels, encode(): pl.pallas_call(functools.partial(encode_kernel, spec, clon), out_shape=(j...  10.6 us
    unnamed x42, local copies, waits for them, and re-layouts  9.46 us
    all_to_all x1, waiting for transfers between devices, on_device(): lax.all_to_all(outgoing.reshape(tiles, cap, spec_wide), ('x', 'core', 'lo...  8.3 us
    all_to_all x2, starting transfers between devices, spread(): return lax.all_to_all(values, axes, split_axis=0, concat_axis=0, tiled=True)  8.18 us
    pallas_call x1, Pallas kernels, finish_latent(): pl.pallas_call(functools.partial(latent_kernel, clat, clon, wide), out_sh...  7.82 us
    ppermute x1, waiting for transfers between devices, on_device(): lax.ppermute(edge_column(east[:, GROUPS - 1], clon + GROUPS - 1), 'lon',...  7.58 us
  transfers between devices with their start and end apart: 16, of which 8 were waited for; matrix products, arithmetic and copies ran while one was open for 4% of the time, Pallas kernels for 26%

profile of v4, /device:TPU:0, one launch (start us, length us, event | category | flops | bytes accessed | tf_op | source)
XLA Modules:
  0.0 139.0 jit_solution(16259964774047331277)
XLA Ops:
  0.6 1.0 fusion.1
  1.7 3.0 %collective-permute-start = (bf16[16,512]{1,0:T(8,128)(2,1)S(1)}, bf16[16,512]{1,0:T(8,128)(2,1)S(1)}, u32[]{:S(2)}, u32[]{:S(2)}) collective-permute-start(bf16[16,512]{1,0:T(8,128)(2,1)S(1)} %bitcast.35), channel_id=1, source_target_pairs={{0,1},{1,2},{2,3},{3,4},{4,5},{5,6},{6,7},{7,0},{8,9},{9,10},{10,1... | collective-permute-start | bytes 49160 | tf_op jit(solution)/shard_map/ppermute | solution.py:626
  4.7 3.1 %collective-permute-start.1 = (bf16[16,512]{1,0:T(8,128)(2,1)S(1)}, bf16[16,512]{1,0:T(8,128)(2,1)S(1)}, u32[]{:S(2)}, u32[]{:S(2)}) collective-permute-start(bf16[16,512]{1,0:T(8,128)(2,1)S(1)} %bitcast.36), channel_id=1, source_target_pairs={{1,0},{2,1},{3,2},{4,3},{5,4},{6,5},{7,6},{0,7},{9,8},{10,9},{11,1... | collective-permute-start | bytes 49160 | tf_op jit(solution)/shard_map/ppermute | solution.py:627
  7.8 0.7 pad_add_fusion.places_ref
  8.5 1.1 copy-done.4
  9.6 3.0 %route.1 = bf16[1024,640]{1,0:T(8,128)(2,1)} custom-call(s32[2,512]{1,0:T(2,128)S(1)} %pad_add_fusion.places_ref, bf16[616,512]{1,0:T(8,128)(2,1)S(1)} %bitcast.31), custom_call_target="tpu_custom_call" | custom-call | flops 3460499968 | tf_op jit(solution)/shard_map/route/pallas_call | solution.py:77
  12.6 0.0 collective-permute-done.west_ref
  12.6 0.0 collective-permute-done.1.east_ref
  12.6 0.0 copy-start.19
  12.6 0.0 copy-start.16
  12.6 3.2 %all-to-all-start = ((bf16[32,32,640]{2,1,0:T(8,128)(2,1)}), bf16[32,32,640]{2,1,0:T(8,128)(2,1)S(1)}, u32[]{:S(2)}, u32[]{:S(2)}) async-start(bf16[32,32,640]{2,1,0:T(8,128)(2,1)} %bitcast.7), calls=%async_computation | async-start | bytes 2621440 | tf_op jit(solution)/shard_map/all_to_all | solution.py:634
  15.9 0.1 pad.19.clone
  15.9 1.0 slice_bitcast_fusion
  17.0 0.1 pad_maximum_fusion.1
  17.1 1.3 collective-permute-start.3
  18.4 3.7 %collective-permute-start.2 = (bf16[144,512]{1,0:T(8,128)(2,1)S(1)}, bf16[144,512]{1,0:T(8,128)(2,1)}, u32[]{:S(2)}, u32[]{:S(2)}) collective-permute-start(bf16[144,512]{1,0:T(8,128)(2,1)S(1)} %get-tuple-element.146), channel_id=1, source_target_pairs={{0,8},{8,16},{16,24},{1,9},{9,17},{17,25},{2,10},{10,18},{18,26},{... | collective-permute-start | bytes 442376 | tf_op jit(solution)/shard_map/ppermute | solution.py:643
  22.1 0.7 pad_add_fusion.1.ids_ref
  22.7 1.0 copy.16
  23.7 0.3 copy.15
  24.0 0.9 pad.12.wit_hbm
  25.0 15.8 %grid_grad.1 = (bf16[512,2688]{1,0:T(8,128)(2,1)}, f32[4,18,144,128]{3,2,1,0:T(8,128)}, bf16[2048,512]{1,0:T(8,128)(2,1)}) custom-call(bf16[2048,512]{1,0:T(8,128)(2,1)} %bitcast.34, bf16[16,512]{1,0:T(8,128)(2,1)} %copy-done.19, bf16[16,512]{1,0:T(8,128)(2,1)} %copy-done.18, bf16[144,512]{1,0:T(8,128)(2,1)} %collective-permute-done.2.north_ref, ...), custom_call_target="tpu_custom_call" | custom-call | flops 11534999552 | tf_op jit(solution)/shard_map/grid_grad/pallas_call | solution.py:188
  40.8 8.3 %all-to-all-done = bf16[32,32,640]{2,1,0:T(8,128)(2,1)S(1)} async-done(((bf16[32,32,640]{2,1,0:T(8,128)(2,1)}), bf16[32,32,640]{2,1,0:T(8,128)(2,1)S(1)}, u32[]{:S(2)}, u32[]{:S(2)}) %all-to-all-start) | async-done | bytes 1310752 | tf_op jit(solution)/shard_map/all_to_all | solution.py:634
  49.1 1.1 copy-done
  50.2 10.6 %encode.1 = (bf16[512,1024]{1,0:T(8,128)(2,1)}, bf16[2,1024,128]{2,1,0:T(8,128)(2,1)}, bf16[2,1024,128]{2,1,0:T(8,128)(2,1)}, bf16[2,112,128]{2,1,0:T(8,128)(2,1)}, bf16[2,112,128]{2,1,0:T(8,128)(2,1)}) custom-call(s32[2]{0:T(128)} %pad_add_fusion.1.ids_ref, bf16[1024,640]{1,0:T(8,128)(2,1)} %bitcast.29, bf16[512,640]{1,0:T(8,128)(2,1)} %pad.12.wit_hbm, ...), custom_call_target="tpu_custom_call" | custom-call | flops 11534999552 | tf_op jit(solution)/shard_map/encode/pallas_call | solution.py:283
  60.8 0.1 collective-permute-start.4
  60.9 1.3 copy-done.1
  62.2 1.2 copy-done.13
  63.4 3.7 %bins.1 = (f32[4,20,144,128]{3,2,1,0:T(8,128)S(1)}, bf16[2048,512]{1,0:T(8,128)(2,1)S(1)}) custom-call(bf16[1024,640]{1,0:T(8,128)(2,1)S(1)} %bitcast.30, bf16[512,1024]{1,0:T(8,128)(2,1)S(1)} %copy-done.13), custom_call_target="tpu_custom_call" | custom-call | flops 4614000128 | tf_op jit(solution)/shard_map/bins/pallas_call | solution.py:341
  67.1 0.0 copy-start.10
  67.1 1.3 copy-done.10
  68.4 0.0 copy-start.6
  68.4 0.7 split.2
  69.1 0.9 collective-permute-start.5
  70.0 6.4 %mix.1 = (bf16[2688,512]{1,0:T(8,128)(2,1)S(1)}, f32[16,512]{1,0:T(8,128)S(1)}, bf16[2688,512]{1,0:T(8,128)(2,1)S(1)}, f32[18,8,512]{2,1,0:T(8,128)S(1)}, f32[18,8,512]{2,1,0:T(8,128)S(1)}) custom-call(f32[4,20,144,128]{3,2,1,0:T(8,128)S(1)} %get-tuple-element.104.grid_ref, f32[9,512]{1,0:T(8,128)S(1)} %copy-done.6, f32[4,18,144,128]{3,2,1,0:T(8,128)S(1)} %copy-done.12, ...), custom_call_target="tpu_custom_call" | custom-call | flops 9228000256 | tf_op jit(solution)/shard_map/mix/pallas_call | solution.py:418
  76.5 1.4 collective-permute-done.5.after_ref.a_got
  77.9 2.5 %point.1 = (bf16[2,640,128]{2,1,0:T(8,128)(2,1)S(1)}, bf16[2,640,128]{2,1,0:T(8,128)(2,1)S(1)}) custom-call(s32[2]{0:T(128)S(1)} %copy-done.7, bf16[512,2688]{1,0:T(8,128)(2,1)S(1)} %copy-done.8, bf16[2688,512]{1,0:T(8,128)(2,1)S(1)} %get-tuple-element.106.mix_ref, f32[16,512]{1,0:T(8,128)S(1)} %get-tuple-element.107.gd_ref, ...), custom_call_target="tpu_custom_call" | custom-call | flops 3460499968 | tf_op jit(solution)/shard_map/point/pallas_call | solution.py:448
  80.4 0.1 collective-permute-start.6
  80.5 1.6 %collective-permute-done.6.got_ref = bf16[2,640,128]{2,1,0:T(8,128)(2,1)S(1)} collective-permute-done((bf16[2,640,128]{2,1,0:T(8,128)(2,1)S(1)}, bf16[2,640,128]{2,1,0:T(8,128)(2,1)S(1)}, u32[]{:S(2)}, u32[]{:S(2)}) %collective-permute-start.6) | collective-permute-done | bytes 327712 | tf_op jit(solution)/shard_map/ppermute | solution.py:670
  82.1 0.6 split.3
  82.7 0.6 collective-permute-start.7
  83.4 1.3 collective-permute-start.9
  84.7 3.0 %collective-permute-start.8 = (bf16[144,512]{1,0:T(8,128)(2,1)S(1)}, bf16[144,512]{1,0:T(8,128)(2,1)S(1)}, u32[]{:S(2)}, u32[]{:S(2)}) collective-permute-start(bf16[144,512]{1,0:T(8,128)(2,1)S(1)} %get-tuple-element.132), channel_id=1, source_target_pairs={{0,8},{8,16},{16,24},{1,9},{9,17},{17,25},{2,10},{10,18},{18,26},{... | collective-permute-start | bytes 442376 | tf_op jit(solution)/shard_map/ppermute | solution.py:676
  87.7 1.0 collective-permute-done.8.refs_0_.top_ref
  88.7 0.3 collective-permute-done.7.b_got
  89.0 0.9 merge.1
  89.9 3.5 %all-to-all-start.1 = ((bf16[8,208,128]{2,1,0:T(8,128)(2,1)}), bf16[8,208,128]{2,1,0:T(8,128)(2,1)S(1)}, u32[]{:S(2)}, u32[]{:S(2)}) async-start(bf16[8,208,128]{2,1,0:T(8,128)(2,1)} %merge.1), calls=%async_computation.1 | async-start | bytes 851968 | tf_op jit(solution)/shard_map/all_to_all | solution.py:611
  93.4 0.2 copy.17
  93.6 0.2 copy.18
  93.8 0.1 scatter-add.14
  93.9 0.1 scatter-add.16
  93.9 0.1 scatter-add.19
  94.0 0.1 scatter-add.15
  94.1 0.0 copy-start.5
  94.1 2.0 %collective-permute-start.10 = (f32[16,512]{1,0:T(8,128)S(1)}, f32[16,512]{1,0:T(8,128)S(1)}, u32[]{:S(2)}, u32[]{:S(2)}) collective-permute-start(f32[16,512]{1,0:T(8,128)S(1)} %scatter-add.15), channel_id=1, source_target_pairs={{0,1},{1,2},{2,3},{3,4},{4,5},{5,6},{6,7},{7,0},{8,9},{9,10},{10,1... | collective-permute-start | bytes 98312 | tf_op jit(solution)/shard_map/ppermute | solution.py:692
  96.1 2.8 %collective-permute-start.11 = (f32[16,512]{1,0:T(8,128)S(1)}, f32[16,512]{1,0:T(8,128)S(1)}, u32[]{:S(2)}, u32[]{:S(2)}) collective-permute-start(f32[16,512]{1,0:T(8,128)S(1)} %scatter-add.19), channel_id=1, source_target_pairs={{1,0},{2,1},{3,2},{4,3},{5,4},{6,5},{7,6},{0,7},{9,8},{10,9},{11,1... | collective-permute-start | bytes 98312 | tf_op jit(solution)/shard_map/ppermute | solution.py:693
  98.9 7.6 %collective-permute-done.10.refs_0_.left_ref = f32[16,512]{1,0:T(8,128)S(1)} collective-permute-done((f32[16,512]{1,0:T(8,128)S(1)}, f32[16,512]{1,0:T(8,128)S(1)}, u32[]{:S(2)}, u32[]{:S(2)}) %collective-permute-start.10) | collective-permute-done | bytes 32800 | tf_op jit(solution)/shard_map/ppermute | solution.py:692
  106.5 1.0 totals.1
  107.4 4.7 %all-to-all-start.2 = ((bf16[16,208,128]{2,1,0:T(8,128)(2,1)}), bf16[16,208,128]{2,1,0:T(8,128)(2,1)S(1)}, u32[]{:S(2)}, u32[]{:S(2)}) async-start(bf16[16,208,128]{2,1,0:T(8,128)(2,1)} %totals.1), calls=%async_computation.2 | async-start | bytes 1703936 | tf_op jit(solution)/shard_map/all_to_all | solution.py:611
  112.2 1.8 %copy-done.3 = bf16[2688,512]{1,0:T(8,128)(2,1)S(1)} copy-done((bf16[2688,512]{1,0:T(8,128)(2,1)S(1)}, bf16[2688,512]{1,0:T(8,128)(2,1)}, u32[]{:S(2)}) %copy-start.3) | copy-done | bytes 2752536
  113.9 1.6 %copy-done.11 = bf16[2048,512]{1,0:T(8,128)(2,1)S(1)} copy-done((bf16[2048,512]{1,0:T(8,128)(2,1)S(1)}, bf16[2048,512]{1,0:T(8,128)(2,1)}, u32[]{:S(2)}) %copy-start.11) | copy-done | bytes 2097176
  115.5 7.8 %latent.1 = bf16[2048,512]{1,0:T(8,128)(2,1)} custom-call(bf16[2048,512]{1,0:T(8,128)(2,1)S(1)} %copy-done.11, bf16[2688,512]{1,0:T(8,128)(2,1)S(1)} %copy-done.3, bf16[144,512]{1,0:T(8,128)(2,1)S(1)} %collective-permute-done.8.refs_0_.top_ref, bf16[144,512]{1,0:T(8,128)(2,1)S(1)} %collective-permute-done.9.refs_1_.bottom_ref, ...), custom_call_target="tpu_custom_call" | custom-call | flops 5767499776 | tf_op jit(solution)/shard_map/latent/pallas_call | solution.py:485
  123.3 10.6 %all-to-all-done.2.own_ref = bf16[16,208,128]{2,1,0:T(8,128)(2,1)S(1)} async-done(((bf16[16,208,128]{2,1,0:T(8,128)(2,1)}), bf16[16,208,128]{2,1,0:T(8,128)(2,1)S(1)}, u32[]{:S(2)}, u32[]{:S(2)}) %all-to-all-start.2) | async-done | bytes 852000 | tf_op jit(solution)/shard_map/all_to_all | solution.py:611
  134.0 2.4 %collective-permute-done.12.sibling_ref = bf16[16,208,128]{2,1,0:T(8,128)(2,1)S(1)} collective-permute-done((bf16[16,208,128]{2,1,0:T(8,128)(2,1)S(1)}, bf16[16,208,128]{2,1,0:T(8,128)(2,1)S(1)}, u32[]{:S(2)}, u32[]{:S(2)}) %collective-permute-start.12) | collective-permute-done | bytes 852000 | tf_op jit(solution)/shard_map/ppermute | solution.py:700
  136.3 2.7 %unpack.1 = (f32[616,512]{1,0:T(8,128)}, f32[512,512]{1,0:T(8,128)}, f32[512,512]{1,0:T(8,128)}, f32[9,512]{1,0:T(8,128)}) custom-call(s32[2]{0:T(128)S(1)} %copy-done.7, bf16[16,208,128]{2,1,0:T(8,128)(2,1)S(1)} %all-to-all-done.2.own_ref, bf16[16,208,128]{2,1,0:T(8,128)(2,1)S(1)} %collective-permute-done.12.sibling_ref), custom_call_target="tpu_custom_call" | custom-call | flops 3460499968 | tf_op jit(solution)/shard_map/unpack/pallas_call | solution.py:582
  (44 shorter events, 0.2 us)
Async XLA Ops:
  1.7 10.9 %collective-permute-start = (bf16[16,512]{1,0:T(8,128)(2,1)S(1)}, bf16[16,512]{1,0:T(8,128)(2,1)S(1)}, u32[]{:S(2)}, u32[]{:S(2)}) collective-permute-start(bf16[16,512]{1,0:T(8,128)(2,1)S(1)} %bitcast.35), channel_id=1, source_target_pairs={{0,1},{1,2},{2,3},{3,4},{4,5},{5,6},{6,7},{7,0},{8,9},{9,10},{10,1... | collective-permute-start | bytes 49160 | tf_op jit(solution)/shard_map/ppermute | solution.py:626
  4.7 7.9 %collective-permute-start.1 = (bf16[16,512]{1,0:T(8,128)(2,1)S(1)}, bf16[16,512]{1,0:T(8,128)(2,1)S(1)}, u32[]{:S(2)}, u32[]{:S(2)}) collective-permute-start(bf16[16,512]{1,0:T(8,128)(2,1)S(1)} %bitcast.36), channel_id=1, source_target_pairs={{1,0},{2,1},{3,2},{4,3},{5,4},{6,5},{7,6},{0,7},{9,8},{10,9},{11,1... | collective-permute-start | bytes 49160 | tf_op jit(solution)/shard_map/ppermute | solution.py:627
  8.5 1.1 copy-start.4
  12.6 10.2 %copy-start.17 = (bf16[512,512]{1,0:T(8,128)(2,1)S(1)}, bf16[512,512]{1,0:T(8,128)(2,1)}, u32[]{:S(2)}) copy-start(bf16[512,512]{1,0:T(8,128)(2,1)} %wo_hbm) | copy-start | bytes 1572868
  12.6 11.2 %copy-start.18 = (bf16[16,512]{1,0:T(8,128)(2,1)}, bf16[16,512]{1,0:T(8,128)(2,1)S(1)}, u32[]{:S(2)}) copy-start(bf16[16,512]{1,0:T(8,128)(2,1)S(1)} %collective-permute-done.west_ref) | copy-start | bytes 49156
  12.6 11.2 %copy-start.19 = (bf16[16,512]{1,0:T(8,128)(2,1)}, bf16[16,512]{1,0:T(8,128)(2,1)S(1)}, u32[]{:S(2)}) copy-start(bf16[16,512]{1,0:T(8,128)(2,1)S(1)} %collective-permute-done.1.east_ref) | copy-start | bytes 49156
  12.6 11.2 %copy-start.16 = (bf16[616,512]{1,0:T(8,128)(2,1)S(1)}, bf16[616,512]{1,0:T(8,128)(2,1)}, u32[]{:S(2)}) copy-start(bf16[616,512]{1,0:T(8,128)(2,1)} %param.19) | copy-start | bytes 1892356
  12.6 36.5 %all-to-all-start = ((bf16[32,32,640]{2,1,0:T(8,128)(2,1)}), bf16[32,32,640]{2,1,0:T(8,128)(2,1)S(1)}, u32[]{:S(2)}, u32[]{:S(2)}) async-start(bf16[32,32,640]{2,1,0:T(8,128)(2,1)} %bitcast.7), calls=%async_computation | async-start | bytes 2621440 | tf_op jit(solution)/shard_map/all_to_all | solution.py:634
  17.1 7.9 %collective-permute-start.3 = (bf16[144,512]{1,0:T(8,128)(2,1)S(1)}, bf16[144,512]{1,0:T(8,128)(2,1)}, u32[]{:S(2)}, u32[]{:S(2)}) collective-permute-start(bf16[144,512]{1,0:T(8,128)(2,1)S(1)} %get-tuple-element.145), channel_id=1, source_target_pairs={{8,0},{16,8},{24,16},{9,1},{17,9},{25,17},{10,2},{18,10},{26,18},{... | collective-permute-start | bytes 442376 | tf_op jit(solution)/shard_map/ppermute | solution.py:644
  18.4 6.6 %collective-permute-start.2 = (bf16[144,512]{1,0:T(8,128)(2,1)S(1)}, bf16[144,512]{1,0:T(8,128)(2,1)}, u32[]{:S(2)}, u32[]{:S(2)}) collective-permute-start(bf16[144,512]{1,0:T(8,128)(2,1)S(1)} %get-tuple-element.146), channel_id=1, source_target_pairs={{0,8},{8,16},{16,24},{1,9},{9,17},{17,25},{2,10},{10,18},{18,26},{... | collective-permute-start | bytes 442376 | tf_op jit(solution)/shard_map/ppermute | solution.py:643
  49.1 1.1 copy-start
  60.8 7.6 %collective-permute-start.4 = (bf16[2,1024,128]{2,1,0:T(8,128)(2,1)}, bf16[2,1024,128]{2,1,0:T(8,128)(2,1)S(1)}, u32[]{:S(2)}, u32[]{:S(2)}) collective-permute-start(bf16[2,1024,128]{2,1,0:T(8,128)(2,1)} %get-tuple-element.99), channel_id=1, source_target_pairs={{0,8},{8,0},{1,9},{9,1},{2,10},{10,2},{3,11},{11,3},{4,12},{12,4},... | collective-permute-start | bytes 1572872 | tf_op jit(solution)/shard_map/ppermute | solution.py:661
  60.8 1.3 copy-start.1
  62.2 1.2 copy-start.13
  63.4 5.0 %copy-start.7 = (s32[2]{0:T(128)S(1)}, s32[2]{0:T(128)}, u32[]{:S(2)}) copy-start(s32[2]{0:T(128)} %pad_add_fusion.1.ids_ref) | copy-start | bytes 28
  63.4 5.0 %copy-start.9 = (bf16[2,1024,128]{2,1,0:T(8,128)(2,1)S(1)}, bf16[2,1024,128]{2,1,0:T(8,128)(2,1)}, u32[]{:S(2)}) copy-start(bf16[2,1024,128]{2,1,0:T(8,128)(2,1)} %get-tuple-element.98.mine_ref) | copy-start | bytes 1572868
  63.4 6.6 %copy-start.12 = (f32[4,18,144,128]{3,2,1,0:T(8,128)S(1)}, f32[4,18,144,128]{3,2,1,0:T(8,128)}, u32[]{:S(2)}) copy-start(f32[4,18,144,128]{3,2,1,0:T(8,128)} %get-tuple-element.105.gm_ref) | copy-start | bytes 15925252
  67.1 1.3 copy-start.10
  68.4 1.6 %copy-start.6 = (f32[9,512]{1,0:T(8,128)S(1)}, f32[9,512]{1,0:T(8,128)}, u32[]{:S(2)}) copy-start(f32[9,512]{1,0:T(8,128)} %wd_ref.3) | copy-start | bytes 55300
  69.1 8.8 %collective-permute-start.5 = (bf16[1024,128]{1,0:T(8,128)(2,1)S(1)}, bf16[1024,128]{1,0:T(8,128)(2,1)S(1)}, u32[]{:S(2)}, u32[]{:S(2)}) collective-permute-start(bf16[1024,128]{1,0:T(8,128)(2,1)S(1)} %get-tuple-element.101), channel_id=1, source_target_pairs={{0,16},{16,0},{1,17},{17,1},{2,18},{18,2},{3,19},{19,3},{4,20},{20... | collective-permute-start | bytes 786440 | tf_op jit(solution)/shard_map/ppermute | solution.py:668
  70.0 7.9 %copy-start.8 = (bf16[512,2688]{1,0:T(8,128)(2,1)S(1)}, bf16[512,2688]{1,0:T(8,128)(2,1)}, u32[]{:S(2)}) copy-start(bf16[512,2688]{1,0:T(8,128)(2,1)} %get-tuple-element.102.cott_ref) | copy-start | bytes 8257540
  70.0 7.9 %copy-start.14 = (bf16[2,112,128]{2,1,0:T(8,128)(2,1)S(1)}, bf16[2,112,128]{2,1,0:T(8,128)(2,1)}, u32[]{:S(2)}) copy-start(bf16[2,112,128]{2,1,0:T(8,128)(2,1)} %get-tuple-element.108.mine_rest) | copy-start | bytes 172036
  70.0 7.9 %copy-start.15 = (bf16[2,112,128]{2,1,0:T(8,128)(2,1)S(1)}, bf16[2,112,128]{2,1,0:T(8,128)(2,1)}, u32[]{:S(2)}) copy-start(bf16[2,112,128]{2,1,0:T(8,128)(2,1)} %get-tuple-element.109.other_rest) | copy-start | bytes 172036
  76.5 6.9 %copy-start.2 = (bf16[2688,512]{1,0:T(8,128)(2,1)}, bf16[2688,512]{1,0:T(8,128)(2,1)S(1)}, u32[]{:S(2)}) copy-start(bf16[2688,512]{1,0:T(8,128)(2,1)S(1)} %get-tuple-element.116.mix_ref) | copy-start | bytes 8257540
  80.4 1.7 %collective-permute-start.6 = (bf16[2,640,128]{2,1,0:T(8,128)(2,1)S(1)}, bf16[2,640,128]{2,1,0:T(8,128)(2,1)S(1)}, u32[]{:S(2)}, u32[]{:S(2)}) collective-permute-start(bf16[2,640,128]{2,1,0:T(8,128)(2,1)S(1)} %get-tuple-element.111), channel_id=1, source_target_pairs={{0,8},{8,0},{1,9},{9,1},{2,10},{10,2},{3,11},{11,3},{4,12},{12,4},... | collective-permute-start | bytes 983048 | tf_op jit(solution)/shard_map/ppermute | solution.py:670
  82.7 6.3 %collective-permute-start.7 = (bf16[640,128]{1,0:T(8,128)(2,1)S(1)}, bf16[640,128]{1,0:T(8,128)(2,1)S(1)}, u32[]{:S(2)}, u32[]{:S(2)}) collective-permute-start(bf16[640,128]{1,0:T(8,128)(2,1)S(1)} %get-tuple-element.115), channel_id=1, source_target_pairs={{0,16},{16,0},{1,17},{17,1},{2,18},{18,2},{3,19},{19,3},{4,20},{20... | collective-permute-start | bytes 491528 | tf_op jit(solution)/shard_map/ppermute | solution.py:674
  83.4 4.3 %collective-permute-start.9 = (bf16[144,512]{1,0:T(8,128)(2,1)S(1)}, bf16[144,512]{1,0:T(8,128)(2,1)S(1)}, u32[]{:S(2)}, u32[]{:S(2)}) collective-permute-start(bf16[144,512]{1,0:T(8,128)(2,1)S(1)} %get-tuple-element.131), channel_id=1, source_target_pairs={{8,0},{16,8},{24,16},{9,1},{17,9},{25,17},{10,2},{18,10},{26,18},{... | collective-permute-start | bytes 442376 | tf_op jit(solution)/shard_map/ppermute | solution.py:677
  84.7 4.0 %collective-permute-start.8 = (bf16[144,512]{1,0:T(8,128)(2,1)S(1)}, bf16[144,512]{1,0:T(8,128)(2,1)S(1)}, u32[]{:S(2)}, u32[]{:S(2)}) collective-permute-start(bf16[144,512]{1,0:T(8,128)(2,1)S(1)} %get-tuple-element.132), channel_id=1, source_target_pairs={{0,8},{8,16},{16,24},{1,9},{9,17},{17,25},{2,10},{10,18},{18,26},{... | collective-permute-start | bytes 442376 | tf_op jit(solution)/shard_map/ppermute | solution.py:676
  89.9 16.6 %all-to-all-start.1 = ((bf16[8,208,128]{2,1,0:T(8,128)(2,1)}), bf16[8,208,128]{2,1,0:T(8,128)(2,1)S(1)}, u32[]{:S(2)}, u32[]{:S(2)}) async-start(bf16[8,208,128]{2,1,0:T(8,128)(2,1)} %merge.1), calls=%async_computation.1 | async-start | bytes 851968 | tf_op jit(solution)/shard_map/all_to_all | solution.py:611
  94.1 18.1 %copy-start.5 = (bf16[512,512]{1,0:T(8,128)(2,1)S(1)}, bf16[512,512]{1,0:T(8,128)(2,1)}, u32[]{:S(2)}) copy-start(bf16[512,512]{1,0:T(8,128)(2,1)} %wp_ref.3) | copy-start | bytes 1572868
  94.1 12.4 %collective-permute-start.10 = (f32[16,512]{1,0:T(8,128)S(1)}, f32[16,512]{1,0:T(8,128)S(1)}, u32[]{:S(2)}, u32[]{:S(2)}) collective-permute-start(f32[16,512]{1,0:T(8,128)S(1)} %scatter-add.15), channel_id=1, source_target_pairs={{0,1},{1,2},{2,3},{3,4},{4,5},{5,6},{6,7},{7,0},{8,9},{9,10},{10,1... | collective-permute-start | bytes 98312 | tf_op jit(solution)/shard_map/ppermute | solution.py:692
  96.1 10.4 %collective-permute-start.11 = (f32[16,512]{1,0:T(8,128)S(1)}, f32[16,512]{1,0:T(8,128)S(1)}, u32[]{:S(2)}, u32[]{:S(2)}) collective-permute-start(f32[16,512]{1,0:T(8,128)S(1)} %scatter-add.19), channel_id=1, source_target_pairs={{1,0},{2,1},{3,2},{4,3},{5,4},{6,5},{7,6},{0,7},{9,8},{10,9},{11,1... | collective-permute-start | bytes 98312 | tf_op jit(solution)/shard_map/ppermute | solution.py:693
  107.4 26.5 %all-to-all-start.2 = ((bf16[16,208,128]{2,1,0:T(8,128)(2,1)}), bf16[16,208,128]{2,1,0:T(8,128)(2,1)S(1)}, u32[]{:S(2)}, u32[]{:S(2)}) async-start(bf16[16,208,128]{2,1,0:T(8,128)(2,1)} %totals.1), calls=%async_computation.2 | async-start | bytes 1703936 | tf_op jit(solution)/shard_map/all_to_all | solution.py:611
  112.2 1.8 %copy-start.3 = (bf16[2688,512]{1,0:T(8,128)(2,1)S(1)}, bf16[2688,512]{1,0:T(8,128)(2,1)}, u32[]{:S(2)}) copy-start(bf16[2688,512]{1,0:T(8,128)(2,1)} %copy-done.2) | copy-start | bytes 8257540
  113.9 1.6 %copy-start.11 = (bf16[2048,512]{1,0:T(8,128)(2,1)S(1)}, bf16[2048,512]{1,0:T(8,128)(2,1)}, u32[]{:S(2)}) copy-start(bf16[2048,512]{1,0:T(8,128)(2,1)} %copy-done.10) | copy-start | bytes 6291460
  134.0 2.4 %collective-permute-start.12 = (bf16[16,208,128]{2,1,0:T(8,128)(2,1)S(1)}, bf16[16,208,128]{2,1,0:T(8,128)(2,1)S(1)}, u32[]{:S(2)}, u32[]{:S(2)}) collective-permute-start(bf16[16,208,128]{2,1,0:T(8,128)(2,1)S(1)} %all-to-all-done.2.own_ref), channel_id=1, source_target_pairs={{0,8},{8,0},{1,9},{9,1},{2,10},{10,2},{3,11},{11,3},{4,12},{12,4},... | collective-permute-start | bytes 2555912 | tf_op jit(solution)/shard_map/ppermute | solution.py:700

commit v5 on v4

--- a/solution.py
+++ b/solution.py
@@ -292,7 +292,7 @@
             pltpu.VMEM((width, width), f32),
             pltpu.SemaphoreType.DMA((len(weights),)),
         ],
-        compiler_params=params(59),
+        compiler_params=params(48),
         cost_estimate=cost(10),
         name="encode",
     )(ids, rows, *weights)
@@ -352,16 +352,11 @@
 
 def mix_kernel(
     clat, clon, wide, grid_ref, wd_ref, gm_ref, after_ref,
-    mix_ref, gd_ref, mix_hbm, east_hbm, west_hbm, east_ref, west_ref, gd, sems,
+    mix_ref, gd_ref, mix_hbm, east_out, west_out, east_ref, west_ref, gd, sem,
 ):
     width = wd_ref.shape[1]
     blocks = width // LANES
-    puts = [
-        pltpu.make_async_copy(source, target, sems.at[i])
-        for i, (source, target) in enumerate(
-            ((mix_ref, mix_hbm), (east_ref, east_hbm), (west_ref, west_hbm))
-        )
-    ]
+    put = pltpu.make_async_copy(mix_ref, mix_hbm, sem)
     gd[...] = jnp.zeros_like(gd)
     used = (clat + 2) * wide
     mix_ref[used:, :] = jnp.zeros((mix_ref.shape[0] - used, width), bf16)
@@ -403,25 +398,25 @@
         return carry
 
     lax.fori_loop(0, clat + 2, conv, 0)
-    for put in puts:
-        put.start()
+    put.start()
+    east_out[...] = east_ref[:, GROUPS - 1, :]
+    west_out[...] = west_ref[:, 0, :]
     taps = [jnp.sum(gd[8 * k : 8 * k + 8, :], axis=0, keepdims=True) for k in range(9)]
     gd_ref[...] = jnp.concatenate(taps + [jnp.zeros((7, width), f32)], axis=0)
-    for put in puts:
-        put.wait()
+    put.wait()
 
 
 def mix(grid, w_depth, g_mixed, after, clat, clon, wide):
     width = w_depth.shape[1]
-    column = jax.ShapeDtypeStruct((clat + 2, GROUPS, width), f32)
+    column = jax.ShapeDtypeStruct((clat + 2, width), f32)
     ext = jax.ShapeDtypeStruct((round_up((clat + 2) * wide, LANES), width), bf16)
     return pl.pallas_call(
         functools.partial(mix_kernel, clat, clon, wide),
         out_shape=(ext, jax.ShapeDtypeStruct((16, width), f32), ext, column, column),
         in_specs=[vmem()] * 3 + [anywhere()],
-        out_specs=(vmem(),) * 2 + (anywhere(),) * 3,
-        scratch_shapes=[pltpu.VMEM(column.shape, column.dtype)] * 2
-        + [pltpu.VMEM((72, width), f32), pltpu.SemaphoreType.DMA((3,))],
+        out_specs=(vmem(),) * 2 + (anywhere(),) + (vmem(),) * 2,
+        scratch_shapes=[pltpu.VMEM((clat + 2, GROUPS, width), f32)] * 2
+        + [pltpu.VMEM((72, width), f32), pltpu.SemaphoreType.DMA],
         compiler_params=params(8),
         cost_estimate=cost(8),
         name="mix",
@@ -469,10 +464,10 @@
     def body(i, carry):
         at = pl.ds(pl.multiple_of(i * clon, 16), clon)
         mixed = mix_ref[pl.ds(pl.multiple_of((i + 1) * wide, 16), clon), :].astype(f32)
-        mixed = mixed + (i == 0).astype(f32) * top_ref[:clon, :].astype(f32)
-        mixed = mixed + (i == clat - 1).astype(f32) * bottom_ref[:clon, :].astype(f32)
+        mixed = mixed + (i == 0).astype(f32) * top_ref[...].astype(f32)
+        mixed = mixed + (i == clat - 1).astype(f32) * bottom_ref[...].astype(f32)
         mixed = mixed + jnp.where(
-            line == 0, left_ref[pl.ds(i, 1), :], jnp.where(line == clon - 1, right_ref[pl.ds(i, 1), :], 0.0)
+            line == 0, left_ref[pl.ds(i + 1, 1), :], jnp.where(line == clon - 1, right_ref[pl.ds(i + 1, 1), :], 0.0)
         )
         out = grid_ref[at, :].astype(f32) + dot(mixed.astype(bf16), w_point)
         out_ref[at, :] = dot(natural_order, out.astype(bf16)).astype(bf16)
@@ -637,11 +632,11 @@
 
     fill = jnp.zeros((wide - clon - 2, width), bf16)
 
-    def edge_row(i):
+    def halo_row(i):
         return jnp.concatenate([cotangent[i], from_east[i, None], fill, from_west[i, None]], axis=0)
 
-    from_north = lax.ppermute(edge_row(clat - 1), LAT, south_way)
-    from_south = lax.ppermute(edge_row(0), LAT, north_way)
+    from_north = lax.ppermute(halo_row(clat - 1), LAT, south_way)
+    from_south = lax.ppermute(halo_row(0), LAT, north_way)
     cot_t, g_mixed, g_grid = grid_grad(
         cotangent.reshape(cells, width),
         (from_east, from_west, from_north, from_south),
@@ -670,28 +665,31 @@
     got_b = lax.ppermute(other_b, "core", SWAP)
     if pairs:
         keep_b, send_b = split(ids, mine_b, got_b)
-        send_b, mix_ext = lax.optimization_barrier((send_b, mix_ext))
+        send_b, east, west = lax.optimization_barrier((send_b, east, west))
         got_b = lax.ppermute(send_b, "x", SWAP)
 
-    top = lax.ppermute(mix_ext[(clat + 1) * wide : (clat + 2) * wide], LAT, south_way)
-    bottom = lax.ppermute(mix_ext[:wide], LAT, north_way)
+    left = lax.ppermute(east, "lon", east_way)
+    right = lax.ppermute(west, "lon", west_way)
     if pairs:
-        summed = merge(keep_a, got_a, keep_b, got_b, lax.axis_size("lon"), top, bottom)
+        summed = merge(keep_a, got_a, keep_b, got_b, lax.axis_size("lon"), left, right)
     else:
         sums = [
             (mine.astype(f32) + got.astype(f32)).astype(bf16).reshape(chips, -1, LANES)
             for mine, got in ((keep_a, send_a), (mine_b, got_b))
         ]
         summed = jnp.concatenate(sums, axis=1)
-    summed, top, bottom, east, west = lax.optimization_barrier((summed, top, bottom, east, west))
+    summed, left, right, mix_ext = lax.optimization_barrier((summed, left, right, mix_ext))
     parts = spread(summed, "lon" if pairs else CHIPS)
-
-    def edge_column(own, at):
-        return own[1:-1].at[0].add(top[at].astype(f32)).at[-1].add(bottom[at].astype(f32))
-
-    left = lax.ppermute(edge_column(east[:, GROUPS - 1], clon + GROUPS - 1), "lon", east_way)
-    right = lax.ppermute(edge_column(west[:, 0], clon + GROUPS), "lon", west_way)
-    full = spread(totals(parts, chips, left, right), CHIPS)
+    line = lax.broadcasted_iota(i32, (clon, width), 0)
+
+    def edge_row(e):
+        row = mix_ext[e * wide : e * wide + clon].astype(f32)
+        sides = jnp.where(line == 0, left[e], jnp.where(line == clon - 1, right[e], 0.0))
+        return (row + sides).astype(bf16)
+
+    top = lax.ppermute(edge_row(clat + 1), LAT, south_way)
+    bottom = lax.ppermute(edge_row(0), LAT, north_way)
+    full = spread(totals(parts, chips, top, bottom), CHIPS)
     latent = finish_latent(grid, mix_ext, (top, bottom, left, right), w_point, clat, clon, wide)
 
     obs_scale = float((rows_here * tiles) ** -0.5)

time: 140 us -> 136 us (0.971)
  local copies, waits for them, and re-layouts: 14.4 us -> 7.85 us
  waiting for transfers between devices: 33.2 us -> 37.4 us
  Pallas kernels: 55.6 us -> 53.9 us
    all_to_all x2, waiting for transfers between devices: 10.6 us -> 15.7 us  [spread(): return lax.all_to_all(values, axes, split_axis=0, concat_axis=0, tiled=True)]
    unnamed x42 -> x28, local copies, waits for them, and re-layouts: 9.46 us -> 5.11 us
    ppermute x6, starting transfers between devices: 14.1 us -> 11.5 us  [the longest x1 4.15 us: on_device(): right = lax.ppermute(west, 'lon', west_way)]
    all_to_all x2, starting transfers between devices: 8.18 us -> 10.7 us  [spread(): return lax.all_to_all(values, axes, split_axis=0, concat_axis=0, tiled=True)]
    pallas_call x1, Pallas kernels: 10.6 us -> 8.88 us  [encode(): pl.pallas_call(functools.partial(encode_kernel, spec, clon), out_shape=(j...]
  transfers between devices with their start and end apart: 16 -> 16, of which waited for: 8 -> 9; matrix products, arithmetic and copies ran while one was open for 4% -> 3% of each run, Pallas kernels for 26% -> 27%
where the time goes in v5:
time: 136 us; the launch traced here: 135 us
  Pallas kernels  53.9 us (40%)
  waiting for transfers between devices  37.4 us (28%)
  starting transfers between devices  33.2 us (24%)
  local copies, waits for them, and re-layouts  7.85 us (6%)
  other arithmetic  1.73 us (1%)
    pallas_call x1, Pallas kernels, grid_grad(): pl.pallas_call(functools.partial(grid_grad_kernel, clat, clon, wide), out...  15.8 us
    all_to_all x2, waiting for transfers between devices, spread(): return lax.all_to_all(values, axes, split_axis=0, concat_axis=0, tiled=True)  15.7 us
    all_to_all x2, starting transfers between devices, spread(): return lax.all_to_all(values, axes, split_axis=0, concat_axis=0, tiled=True)  10.7 us
    pallas_call x1, Pallas kernels, encode(): pl.pallas_call(functools.partial(encode_kernel, spec, clon), out_shape=(j...  8.88 us
    all_to_all x1, waiting for transfers between devices, on_device(): lax.all_to_all(outgoing.reshape(tiles, cap, spec_wide), ('x', 'core', 'lo...  8.79 us
    pallas_call x1, Pallas kernels, finish_latent(): pl.pallas_call(functools.partial(latent_kernel, clat, clon, wide), out_sh...  7.82 us
    pallas_call x1, Pallas kernels, mix(): pl.pallas_call(functools.partial(mix_kernel, clat, clon, wide), out_shape...  6.47 us
    unnamed x28, local copies, waits for them, and re-layouts  5.11 us
  transfers between devices with their start and end apart: 16, of which 9 were waited for; matrix products, arithmetic and copies ran while one was open for 3% of the time, Pallas kernels for 27%

profile of v5, /device:TPU:0, one launch (start us, length us, event | category | flops | bytes accessed | tf_op | source)
XLA Modules:
  0.0 135.0 jit_solution(18200203097956151889)
XLA Ops:
  0.6 1.0 fusion
  1.7 3.0 %collective-permute-start = (bf16[16,512]{1,0:T(8,128)(2,1)S(1)}, bf16[16,512]{1,0:T(8,128)(2,1)S(1)}, u32[]{:S(2)}, u32[]{:S(2)}) collective-permute-start(bf16[16,512]{1,0:T(8,128)(2,1)S(1)} %bitcast.31), channel_id=1, source_target_pairs={{0,1},{1,2},{2,3},{3,4},{4,5},{5,6},{6,7},{7,0},{8,9},{9,10},{10,1... | collective-permute-start | bytes 49160 | tf_op jit(solution)/shard_map/ppermute | solution.py:621
  4.7 3.1 %collective-permute-start.1 = (bf16[16,512]{1,0:T(8,128)(2,1)S(1)}, bf16[16,512]{1,0:T(8,128)(2,1)S(1)}, u32[]{:S(2)}, u32[]{:S(2)}) collective-permute-start(bf16[16,512]{1,0:T(8,128)(2,1)S(1)} %bitcast.32), channel_id=1, source_target_pairs={{1,0},{2,1},{3,2},{4,3},{5,4},{6,5},{7,6},{0,7},{9,8},{10,9},{11,1... | collective-permute-start | bytes 49160 | tf_op jit(solution)/shard_map/ppermute | solution.py:622
  7.8 0.7 pad_add_fusion.places_ref
  8.5 1.1 copy-done.3
  9.6 3.0 %route.1 = bf16[1024,640]{1,0:T(8,128)(2,1)} custom-call(s32[2,512]{1,0:T(2,128)S(1)} %pad_add_fusion.places_ref, bf16[616,512]{1,0:T(8,128)(2,1)S(1)} %bitcast.28), custom_call_target="tpu_custom_call" | custom-call | flops 3460499968 | tf_op jit(solution)/shard_map/route/pallas_call | solution.py:77
  12.6 0.0 collective-permute-done.west_ref
  12.6 0.0 collective-permute-done.1.east_ref
  12.6 0.0 copy-start.12
  12.6 3.2 %all-to-all-start = ((bf16[32,32,640]{2,1,0:T(8,128)(2,1)}), bf16[32,32,640]{2,1,0:T(8,128)(2,1)S(1)}, u32[]{:S(2)}, u32[]{:S(2)}) async-start(bf16[32,32,640]{2,1,0:T(8,128)(2,1)} %bitcast.7), calls=%async_computation | async-start | bytes 2621440 | tf_op jit(solution)/shard_map/all_to_all | solution.py:629
  15.8 0.0 copy-start
  15.9 0.1 pad.11.clone
  15.9 1.0 slice_bitcast_fusion
  17.0 0.8 pad_maximum_fusion.1
  17.8 2.8 %collective-permute-start.2 = (bf16[144,512]{1,0:T(8,128)(2,1)}, bf16[144,512]{1,0:T(8,128)(2,1)}, u32[]{:S(2)}, u32[]{:S(2)}) collective-permute-start(bf16[144,512]{1,0:T(8,128)(2,1)} %get-tuple-element.98), channel_id=1, source_target_pairs={{0,8},{8,16},{16,24},{1,9},{9,17},{17,25},{2,10},{10,18},{18,26},{... | collective-permute-start | bytes 442376 | tf_op jit(solution)/shard_map/ppermute | solution.py:638
  20.6 1.3 collective-permute-start.3
  21.9 0.1 pad_add_fusion.1.ids_ref
  22.0 0.3 copy.15
  22.3 0.1 pad.4.wit_hbm
  22.4 0.0 copy-done
  22.4 0.2 copy.16
  22.6 0.0 collective-permute-done.2.north_ref
  22.6 1.9 %collective-permute-done.3.south_ref = bf16[144,512]{1,0:T(8,128)(2,1)} collective-permute-done((bf16[144,512]{1,0:T(8,128)(2,1)S(1)}, bf16[144,512]{1,0:T(8,128)(2,1)}, u32[]{:S(2)}, u32[]{:S(2)}) %collective-permute-start.3) | collective-permute-done | bytes 147488 | tf_op jit(solution)/shard_map/ppermute | solution.py:639
  24.5 15.8 %grid_grad.1 = (bf16[512,2688]{1,0:T(8,128)(2,1)}, f32[4,18,144,128]{3,2,1,0:T(8,128)}, bf16[2048,512]{1,0:T(8,128)(2,1)}) custom-call(bf16[2048,512]{1,0:T(8,128)(2,1)} %bitcast.30, bf16[16,512]{1,0:T(8,128)(2,1)} %copy-done.12, bf16[16,512]{1,0:T(8,128)(2,1)} %copy-done.11, bf16[144,512]{1,0:T(8,128)(2,1)} %collective-permute-done.2.north_ref, ...), custom_call_target="tpu_custom_call" | custom-call | flops 11534999552 | tf_op jit(solution)/shard_map/grid_grad/pallas_call | solution.py:188
  40.3 8.8 %all-to-all-done = bf16[32,32,640]{2,1,0:T(8,128)(2,1)S(1)} async-done(((bf16[32,32,640]{2,1,0:T(8,128)(2,1)}), bf16[32,32,640]{2,1,0:T(8,128)(2,1)S(1)}, u32[]{:S(2)}, u32[]{:S(2)}) %all-to-all-start) | async-done | bytes 1310752 | tf_op jit(solution)/shard_map/all_to_all | solution.py:629
  49.1 8.9 %encode.1 = (bf16[512,1024]{1,0:T(8,128)(2,1)S(1)}, bf16[2,1024,128]{2,1,0:T(8,128)(2,1)S(1)}, bf16[2,1024,128]{2,1,0:T(8,128)(2,1)S(1)}, bf16[2,112,128]{2,1,0:T(8,128)(2,1)S(1)}, bf16[2,112,128]{2,1,0:T(8,128)(2,1)S(1)}) custom-call(s32[2]{0:T(128)S(1)} %pad_add_fusion.1.ids_ref, bf16[1024,640]{1,0:T(8,128)(2,1)S(1)} %bitcast.25, ...), custom_call_target="tpu_custom_call" | custom-call | flops 11534999552 | tf_op jit(solution)/shard_map/encode/pallas_call | solution.py:283
  57.9 0.1 collective-permute-start.4
  58.0 3.7 %bins.1 = (f32[4,20,144,128]{3,2,1,0:T(8,128)S(1)}, bf16[2048,512]{1,0:T(8,128)(2,1)S(1)}) custom-call(bf16[1024,640]{1,0:T(8,128)(2,1)S(1)} %bitcast.26, bf16[512,1024]{1,0:T(8,128)(2,1)S(1)} %get-tuple-element.55.emb_ref), custom_call_target="tpu_custom_call" | custom-call | flops 4614000128 | tf_op jit(solution)/shard_map/bins/pallas_call | solution.py:341
  61.7 0.0 copy-start.7
  61.7 0.0 collective-permute-done.4.got_ref
  61.7 0.0 copy-start.5
  61.7 0.7 split.2
  62.4 0.6 copy-done.7
  63.0 0.8 collective-permute-start.5
  63.9 6.5 %mix.1 = (bf16[2688,512]{1,0:T(8,128)(2,1)S(1)}, f32[16,512]{1,0:T(8,128)S(1)}, bf16[2688,512]{1,0:T(8,128)(2,1)S(1)}, f32[18,512]{1,0:T(8,128)S(1)}, f32[18,512]{1,0:T(8,128)S(1)}) custom-call(f32[4,20,144,128]{3,2,1,0:T(8,128)S(1)} %get-tuple-element.56.grid_ref, f32[9,512]{1,0:T(8,128)S(1)} %copy-done.5, f32[4,18,144,128]{3,2,1,0:T(8,128)S(1)} %copy-done.9, ...), custom_call_target="tpu_custom_call" | custom-call | flops 9228000256 | tf_op jit(solution)/shard_map/mix/pallas_call | solution.py:413
  70.4 1.4 %collective-permute-done.5.after_ref.a_got = bf16[1024,128]{1,0:T(8,128)(2,1)S(1)} collective-permute-done((bf16[1024,128]{1,0:T(8,128)(2,1)S(1)}, bf16[1024,128]{1,0:T(8,128)(2,1)S(1)}, u32[]{:S(2)}, u32[]{:S(2)}) %collective-permute-start.5) | collective-permute-done | bytes 262176 | tf_op jit(solution)/shard_map/ppermute | solution.py:663
  71.7 2.5 %point.1 = (bf16[2,640,128]{2,1,0:T(8,128)(2,1)S(1)}, bf16[2,640,128]{2,1,0:T(8,128)(2,1)S(1)}) custom-call(s32[2]{0:T(128)S(1)} %pad_add_fusion.1.ids_ref, bf16[512,2688]{1,0:T(8,128)(2,1)S(1)} %copy-done.6, bf16[2688,512]{1,0:T(8,128)(2,1)S(1)} %get-tuple-element.58.mix_ref, f32[16,512]{1,0:T(8,128)S(1)} %get-tuple-element.59.gd_ref, ...), custom_call_target="tpu_custom_call" | custom-call | flops 3460499968 | tf_op jit(solution)/shard_map/point/pallas_call | solution.py:443
  74.3 0.1 collective-permute-start.6
  74.3 1.6 %collective-permute-done.6.got_ref = bf16[2,640,128]{2,1,0:T(8,128)(2,1)S(1)} collective-permute-done((bf16[2,640,128]{2,1,0:T(8,128)(2,1)S(1)}, bf16[2,640,128]{2,1,0:T(8,128)(2,1)S(1)}, u32[]{:S(2)}, u32[]{:S(2)}) %collective-permute-start.6) | collective-permute-done | bytes 327712 | tf_op jit(solution)/shard_map/ppermute | solution.py:665
  76.0 0.6 split.3
  76.6 0.6 collective-permute-start.7
  77.2 0.6 collective-permute-start.8
  77.8 4.1 %collective-permute-start.9 = (f32[18,512]{1,0:T(8,128)S(1)}, f32[18,512]{1,0:T(8,128)S(1)}, u32[]{:S(2)}, u32[]{:S(2)}) collective-permute-start(f32[18,512]{1,0:T(8,128)S(1)} %get-tuple-element.70), channel_id=1, source_target_pairs={{1,0},{2,1},{3,2},{4,3},{5,4},{6,5},{7,6},{0,7},{9,8},{10,9},{11,1... | collective-permute-start | bytes 110600 | tf_op jit(solution)/shard_map/ppermute | solution.py:672
  81.9 2.1 %collective-permute-done.8.refs_0_.left_ref = f32[18,512]{1,0:T(8,128)S(1)} collective-permute-done((f32[18,512]{1,0:T(8,128)S(1)}, f32[18,512]{1,0:T(8,128)S(1)}, u32[]{:S(2)}, u32[]{:S(2)}) %collective-permute-start.8) | collective-permute-done | bytes 36896 | tf_op jit(solution)/shard_map/ppermute | solution.py:671
  84.0 0.0 collective-permute-done.9.refs_1_.right_ref
  84.0 0.0 collective-permute-done.7.b_got
  84.0 0.9 merge.1
  84.9 6.0 %all-to-all-start.1 = ((bf16[8,208,128]{2,1,0:T(8,128)(2,1)}), bf16[8,208,128]{2,1,0:T(8,128)(2,1)S(1)}, u32[]{:S(2)}, u32[]{:S(2)}) async-start(bf16[8,208,128]{2,1,0:T(8,128)(2,1)} %merge.1), calls=%async_computation.1 | async-start | bytes 851968 | tf_op jit(solution)/shard_map/all_to_all | solution.py:606
  90.9 0.2 add_convert_fusion
  91.1 1.3 collective-permute-start.10
  92.4 0.0 copy-start.4
  92.4 1.4 %collective-permute-start.11 = (bf16[128,512]{1,0:T(8,128)(2,1)S(1)}, bf16[128,512]{1,0:T(8,128)(2,1)S(1)}, u32[]{:S(2)}, u32[]{:S(2)}) collective-permute-start(bf16[128,512]{1,0:T(8,128)(2,1)S(1)} %get-tuple-element.83), channel_id=1, source_target_pairs={{8,0},{16,8},{24,16},{9,1},{17,9},{25,17},{10,2},{18,10},{26,18},{... | collective-permute-start | bytes 393224 | tf_op jit(solution)/shard_map/ppermute | solution.py:691
  93.8 0.0 collective-permute-done.10.refs_0_.top_ref
  93.8 3.6 %collective-permute-done.11.refs_1_.bottom_ref = bf16[128,512]{1,0:T(8,128)(2,1)S(1)} collective-permute-done((bf16[128,512]{1,0:T(8,128)(2,1)S(1)}, bf16[128,512]{1,0:T(8,128)(2,1)S(1)}, u32[]{:S(2)}, u32[]{:S(2)}) %collective-permute-start.11) | collective-permute-done | bytes 131104 | tf_op jit(solution)/shard_map/ppermute | solution.py:691
  97.5 4.4 %all-to-all-done.1.parts_ref = bf16[8,208,128]{2,1,0:T(8,128)(2,1)S(1)} async-done(((bf16[8,208,128]{2,1,0:T(8,128)(2,1)}), bf16[8,208,128]{2,1,0:T(8,128)(2,1)S(1)}, u32[]{:S(2)}, u32[]{:S(2)}) %all-to-all-start.1) | async-done | bytes 426016 | tf_op jit(solution)/shard_map/all_to_all | solution.py:606
  101.8 1.0 totals.1
  102.8 4.7 %all-to-all-start.2 = ((bf16[16,208,128]{2,1,0:T(8,128)(2,1)}), bf16[16,208,128]{2,1,0:T(8,128)(2,1)S(1)}, u32[]{:S(2)}, u32[]{:S(2)}) async-start(bf16[16,208,128]{2,1,0:T(8,128)(2,1)} %totals.1), calls=%async_computation.2 | async-start | bytes 1703936 | tf_op jit(solution)/shard_map/all_to_all | solution.py:606
  107.5 1.8 %copy-done.2 = bf16[2688,512]{1,0:T(8,128)(2,1)S(1)} copy-done((bf16[2688,512]{1,0:T(8,128)(2,1)S(1)}, bf16[2688,512]{1,0:T(8,128)(2,1)}, u32[]{:S(2)}) %copy-start.2) | copy-done | bytes 2752536
  109.3 1.6 %copy-done.8 = bf16[2048,512]{1,0:T(8,128)(2,1)S(1)} copy-done((bf16[2048,512]{1,0:T(8,128)(2,1)S(1)}, bf16[2048,512]{1,0:T(8,128)(2,1)}, u32[]{:S(2)}) %copy-start.8) | copy-done | bytes 2097176
  110.9 7.8 %latent.1 = bf16[2048,512]{1,0:T(8,128)(2,1)} custom-call(bf16[2048,512]{1,0:T(8,128)(2,1)S(1)} %copy-done.8, bf16[2688,512]{1,0:T(8,128)(2,1)S(1)} %copy-done.2, bf16[128,512]{1,0:T(8,128)(2,1)S(1)} %collective-permute-done.10.refs_0_.top_ref, bf16[128,512]{1,0:T(8,128)(2,1)S(1)} %collective-permute-done.11.refs_1_.bottom_ref, ...), custom_call_target="tpu_custom_call" | custom-call | flops 5767499776 | tf_op jit(solution)/shard_map/latent/pallas_call | solution.py:480
  118.7 11.3 %all-to-all-done.2.own_ref = bf16[16,208,128]{2,1,0:T(8,128)(2,1)S(1)} async-done(((bf16[16,208,128]{2,1,0:T(8,128)(2,1)}), bf16[16,208,128]{2,1,0:T(8,128)(2,1)S(1)}, u32[]{:S(2)}, u32[]{:S(2)}) %all-to-all-start.2) | async-done | bytes 852000 | tf_op jit(solution)/shard_map/all_to_all | solution.py:606
  130.0 0.0 collective-permute-start.12
  130.0 2.4 %collective-permute-done.12.sibling_ref = bf16[16,208,128]{2,1,0:T(8,128)(2,1)S(1)} collective-permute-done((bf16[16,208,128]{2,1,0:T(8,128)(2,1)S(1)}, bf16[16,208,128]{2,1,0:T(8,128)(2,1)S(1)}, u32[]{:S(2)}, u32[]{:S(2)}) %collective-permute-start.12) | collective-permute-done | bytes 852000 | tf_op jit(solution)/shard_map/ppermute | solution.py:698
  132.4 2.7 %unpack.1 = (f32[616,512]{1,0:T(8,128)}, f32[512,512]{1,0:T(8,128)}, f32[512,512]{1,0:T(8,128)}, f32[9,512]{1,0:T(8,128)}) custom-call(s32[2]{0:T(128)S(1)} %pad_add_fusion.1.ids_ref, bf16[16,208,128]{2,1,0:T(8,128)(2,1)S(1)} %all-to-all-done.2.own_ref, bf16[16,208,128]{2,1,0:T(8,128)(2,1)S(1)} %collective-permute-done.12.sibling_ref), custom_call_target="tpu_custom_call" | custom-call | flops 3460499968 | tf_op jit(solution)/shard_map/unpack/pallas_call | solution.py:577
  (23 shorter events, 0.1 us)
Async XLA Ops:
  1.7 10.9 %collective-permute-start = (bf16[16,512]{1,0:T(8,128)(2,1)S(1)}, bf16[16,512]{1,0:T(8,128)(2,1)S(1)}, u32[]{:S(2)}, u32[]{:S(2)}) collective-permute-start(bf16[16,512]{1,0:T(8,128)(2,1)S(1)} %bitcast.31), channel_id=1, source_target_pairs={{0,1},{1,2},{2,3},{3,4},{4,5},{5,6},{6,7},{7,0},{8,9},{9,10},{10,1... | collective-permute-start | bytes 49160 | tf_op jit(solution)/shard_map/ppermute | solution.py:621
  4.7 7.9 %collective-permute-start.1 = (bf16[16,512]{1,0:T(8,128)(2,1)S(1)}, bf16[16,512]{1,0:T(8,128)(2,1)S(1)}, u32[]{:S(2)}, u32[]{:S(2)}) collective-permute-start(bf16[16,512]{1,0:T(8,128)(2,1)S(1)} %bitcast.32), channel_id=1, source_target_pairs={{1,0},{2,1},{3,2},{4,3},{5,4},{6,5},{7,6},{0,7},{9,8},{10,9},{11,1... | collective-permute-start | bytes 49160 | tf_op jit(solution)/shard_map/ppermute | solution.py:622
  8.5 1.1 copy-start.3
  12.6 9.4 %copy-start.10 = (bf16[616,512]{1,0:T(8,128)(2,1)S(1)}, bf16[616,512]{1,0:T(8,128)(2,1)}, u32[]{:S(2)}) copy-start(bf16[616,512]{1,0:T(8,128)(2,1)} %param.11) | copy-start | bytes 1892356
  12.6 9.7 %copy-start.11 = (bf16[16,512]{1,0:T(8,128)(2,1)}, bf16[16,512]{1,0:T(8,128)(2,1)S(1)}, u32[]{:S(2)}) copy-start(bf16[16,512]{1,0:T(8,128)(2,1)S(1)} %collective-permute-done.west_ref) | copy-start | bytes 49156
  12.6 9.7 %copy-start.12 = (bf16[16,512]{1,0:T(8,128)(2,1)}, bf16[16,512]{1,0:T(8,128)(2,1)S(1)}, u32[]{:S(2)}) copy-start(bf16[16,512]{1,0:T(8,128)(2,1)S(1)} %collective-permute-done.1.east_ref) | copy-start | bytes 49156
  12.6 36.5 %all-to-all-start = ((bf16[32,32,640]{2,1,0:T(8,128)(2,1)}), bf16[32,32,640]{2,1,0:T(8,128)(2,1)S(1)}, u32[]{:S(2)}, u32[]{:S(2)}) async-start(bf16[32,32,640]{2,1,0:T(8,128)(2,1)} %bitcast.7), calls=%async_computation | async-start | bytes 2621440 | tf_op jit(solution)/shard_map/all_to_all | solution.py:629
  15.8 6.5 %copy-start = (bf16[512,512]{1,0:T(8,128)(2,1)S(1)}, bf16[512,512]{1,0:T(8,128)(2,1)}, u32[]{:S(2)}) copy-start(bf16[512,512]{1,0:T(8,128)(2,1)} %wo_hbm) | copy-start | bytes 1572868
  17.8 4.8 %collective-permute-start.2 = (bf16[144,512]{1,0:T(8,128)(2,1)}, bf16[144,512]{1,0:T(8,128)(2,1)}, u32[]{:S(2)}, u32[]{:S(2)}) collective-permute-start(bf16[144,512]{1,0:T(8,128)(2,1)} %get-tuple-element.98), channel_id=1, source_target_pairs={{0,8},{8,16},{16,24},{1,9},{9,17},{17,25},{2,10},{10,18},{18,26},{... | collective-permute-start | bytes 442376 | tf_op jit(solution)/shard_map/ppermute | solution.py:638
  20.6 3.9 %collective-permute-start.3 = (bf16[144,512]{1,0:T(8,128)(2,1)S(1)}, bf16[144,512]{1,0:T(8,128)(2,1)}, u32[]{:S(2)}, u32[]{:S(2)}) collective-permute-start(bf16[144,512]{1,0:T(8,128)(2,1)S(1)} %get-tuple-element.97), channel_id=1, source_target_pairs={{8,0},{16,8},{24,16},{9,1},{17,9},{25,17},{10,2},{18,10},{26,18},{... | collective-permute-start | bytes 442376 | tf_op jit(solution)/shard_map/ppermute | solution.py:639
  57.9 3.8 %collective-permute-start.4 = (bf16[2,1024,128]{2,1,0:T(8,128)(2,1)S(1)}, bf16[2,1024,128]{2,1,0:T(8,128)(2,1)S(1)}, u32[]{:S(2)}, u32[]{:S(2)}) collective-permute-start(bf16[2,1024,128]{2,1,0:T(8,128)(2,1)S(1)} %get-tuple-element.51), channel_id=1, source_target_pairs={{0,8},{8,0},{1,9},{9,1},{2,10},{10,2},{3,11},{11,3},{4,12},{12,4},... | collective-permute-start | bytes 1572872 | tf_op jit(solution)/shard_map/ppermute | solution.py:656
  58.0 5.9 %copy-start.9 = (f32[4,18,144,128]{3,2,1,0:T(8,128)S(1)}, f32[4,18,144,128]{3,2,1,0:T(8,128)}, u32[]{:S(2)}) copy-start(f32[4,18,144,128]{3,2,1,0:T(8,128)} %get-tuple-element.57.gm_ref) | copy-start | bytes 15925252
  61.7 1.3 copy-start.7
  61.7 2.1 %copy-start.5 = (f32[9,512]{1,0:T(8,128)S(1)}, f32[9,512]{1,0:T(8,128)}, u32[]{:S(2)}) copy-start(f32[9,512]{1,0:T(8,128)} %wd_ref.3) | copy-start | bytes 55300
  63.0 8.7 %collective-permute-start.5 = (bf16[1024,128]{1,0:T(8,128)(2,1)S(1)}, bf16[1024,128]{1,0:T(8,128)(2,1)S(1)}, u32[]{:S(2)}, u32[]{:S(2)}) collective-permute-start(bf16[1024,128]{1,0:T(8,128)(2,1)S(1)} %get-tuple-element.53), channel_id=1, source_target_pairs={{0,16},{16,0},{1,17},{17,1},{2,18},{18,2},{3,19},{19,3},{4,20},{20... | collective-permute-start | bytes 786440 | tf_op jit(solution)/shard_map/ppermute | solution.py:663
  63.9 7.9 %copy-start.6 = (bf16[512,2688]{1,0:T(8,128)(2,1)S(1)}, bf16[512,2688]{1,0:T(8,128)(2,1)}, u32[]{:S(2)}) copy-start(bf16[512,2688]{1,0:T(8,128)(2,1)} %get-tuple-element.54.cott_ref) | copy-start | bytes 8257540
  70.3 20.5 %copy-start.1 = (bf16[2688,512]{1,0:T(8,128)(2,1)}, bf16[2688,512]{1,0:T(8,128)(2,1)S(1)}, u32[]{:S(2)}) copy-start(bf16[2688,512]{1,0:T(8,128)(2,1)S(1)} %get-tuple-element.73.mix_ref) | copy-start | bytes 8257540
  74.3 1.7 %collective-permute-start.6 = (bf16[2,640,128]{2,1,0:T(8,128)(2,1)S(1)}, bf16[2,640,128]{2,1,0:T(8,128)(2,1)S(1)}, u32[]{:S(2)}, u32[]{:S(2)}) collective-permute-start(bf16[2,640,128]{2,1,0:T(8,128)(2,1)S(1)} %get-tuple-element.63), channel_id=1, source_target_pairs={{0,8},{8,0},{1,9},{9,1},{2,10},{10,2},{3,11},{11,3},{4,12},{12,4},... | collective-permute-start | bytes 983048 | tf_op jit(solution)/shard_map/ppermute | solution.py:665
  76.6 7.4 %collective-permute-start.7 = (bf16[640,128]{1,0:T(8,128)(2,1)S(1)}, bf16[640,128]{1,0:T(8,128)(2,1)S(1)}, u32[]{:S(2)}, u32[]{:S(2)}) collective-permute-start(bf16[640,128]{1,0:T(8,128)(2,1)S(1)} %get-tuple-element.68), channel_id=1, source_target_pairs={{0,16},{16,0},{1,17},{17,1},{2,18},{18,2},{3,19},{19,3},{4,20},{20... | collective-permute-start | bytes 491528 | tf_op jit(solution)/shard_map/ppermute | solution.py:669
  77.2 6.8 %collective-permute-start.8 = (f32[18,512]{1,0:T(8,128)S(1)}, f32[18,512]{1,0:T(8,128)S(1)}, u32[]{:S(2)}, u32[]{:S(2)}) collective-permute-start(f32[18,512]{1,0:T(8,128)S(1)} %get-tuple-element.69), channel_id=1, source_target_pairs={{0,1},{1,2},{2,3},{3,4},{4,5},{5,6},{6,7},{7,0},{8,9},{9,10},{10,1... | collective-permute-start | bytes 110600 | tf_op jit(solution)/shard_map/ppermute | solution.py:671
  77.8 6.2 %collective-permute-start.9 = (f32[18,512]{1,0:T(8,128)S(1)}, f32[18,512]{1,0:T(8,128)S(1)}, u32[]{:S(2)}, u32[]{:S(2)}) collective-permute-start(f32[18,512]{1,0:T(8,128)S(1)} %get-tuple-element.70), channel_id=1, source_target_pairs={{1,0},{2,1},{3,2},{4,3},{5,4},{6,5},{7,6},{0,7},{9,8},{10,9},{11,1... | collective-permute-start | bytes 110600 | tf_op jit(solution)/shard_map/ppermute | solution.py:672
  84.9 17.0 %all-to-all-start.1 = ((bf16[8,208,128]{2,1,0:T(8,128)(2,1)}), bf16[8,208,128]{2,1,0:T(8,128)(2,1)S(1)}, u32[]{:S(2)}, u32[]{:S(2)}) async-start(bf16[8,208,128]{2,1,0:T(8,128)(2,1)} %merge.1), calls=%async_computation.1 | async-start | bytes 851968 | tf_op jit(solution)/shard_map/all_to_all | solution.py:606
  91.1 2.8 %collective-permute-start.10 = (bf16[128,512]{1,0:T(8,128)(2,1)S(1)}, bf16[128,512]{1,0:T(8,128)(2,1)S(1)}, u32[]{:S(2)}, u32[]{:S(2)}) collective-permute-start(bf16[128,512]{1,0:T(8,128)(2,1)S(1)} %get-tuple-element.84), channel_id=1, source_target_pairs={{0,8},{8,16},{16,24},{1,9},{9,17},{17,25},{2,10},{10,18},{18,26},{... | collective-permute-start | bytes 393224 | tf_op jit(solution)/shard_map/ppermute | solution.py:690
  92.4 15.1 %copy-start.4 = (bf16[512,512]{1,0:T(8,128)(2,1)S(1)}, bf16[512,512]{1,0:T(8,128)(2,1)}, u32[]{:S(2)}) copy-start(bf16[512,512]{1,0:T(8,128)(2,1)} %wp_ref.3) | copy-start | bytes 1572868
  92.4 5.1 %collective-permute-start.11 = (bf16[128,512]{1,0:T(8,128)(2,1)S(1)}, bf16[128,512]{1,0:T(8,128)(2,1)S(1)}, u32[]{:S(2)}, u32[]{:S(2)}) collective-permute-start(bf16[128,512]{1,0:T(8,128)(2,1)S(1)} %get-tuple-element.83), channel_id=1, source_target_pairs={{8,0},{16,8},{24,16},{9,1},{17,9},{25,17},{10,2},{18,10},{26,18},{... | collective-permute-start | bytes 393224 | tf_op jit(solution)/shard_map/ppermute | solution.py:691
  102.8 27.2 %all-to-all-start.2 = ((bf16[16,208,128]{2,1,0:T(8,128)(2,1)}), bf16[16,208,128]{2,1,0:T(8,128)(2,1)S(1)}, u32[]{:S(2)}, u32[]{:S(2)}) async-start(bf16[16,208,128]{2,1,0:T(8,128)(2,1)} %totals.1), calls=%async_computation.2 | async-start | bytes 1703936 | tf_op jit(solution)/shard_map/all_to_all | solution.py:606
  107.5 1.8 %copy-start.2 = (bf16[2688,512]{1,0:T(8,128)(2,1)S(1)}, bf16[2688,512]{1,0:T(8,128)(2,1)}, u32[]{:S(2)}) copy-start(bf16[2688,512]{1,0:T(8,128)(2,1)} %copy-done.1) | copy-start | bytes 8257540
  109.3 1.6 %copy-start.8 = (bf16[2048,512]{1,0:T(8,128)(2,1)S(1)}, bf16[2048,512]{1,0:T(8,128)(2,1)}, u32[]{:S(2)}) copy-start(bf16[2048,512]{1,0:T(8,128)(2,1)} %copy-done.7) | copy-start | bytes 6291460
  130.0 2.4 %collective-permute-start.12 = (bf16[16,208,128]{2,1,0:T(8,128)(2,1)S(1)}, bf16[16,208,128]{2,1,0:T(8,128)(2,1)S(1)}, u32[]{:S(2)}, u32[]{:S(2)}) collective-permute-start(bf16[16,208,128]{2,1,0:T(8,128)(2,1)S(1)} %all-to-all-done.2.own_ref), channel_id=1, source_target_pairs={{0,8},{8,0},{1,9},{9,1},{2,10},{10,2},{3,11},{11,3},{4,12},{12,4},... | collective-permute-start | bytes 2555912 | tf_op jit(solution)/shard_map/ppermute | solution.py:698

commit v6 on v5

--- a/solution.py
+++ b/solution.py
@@ -228,14 +228,20 @@
 
 def encode_kernel(
     spec, clon, ids_ref, rows_ref, wit_hbm, wot_hbm, gg_hbm, wo_hbm,
-    emb_ref, mine_ref, other_ref, mine_rest, other_rest,
-    wit_ref, wot_ref, gg_ref, wo_ref, gi, gi_out, go, sems,
+    emb_hbm, cell_ref, mine_ref, other_ref, mine_rest, other_rest,
+    wit_ref, wot_ref, gg_ref, wo_ref, emb_ref, gi, gi_out, go, sems,
 ):
     loads = start_loads((wit_hbm, wot_hbm, gg_hbm, wo_hbm), (wit_ref, wot_ref, gg_ref, wo_ref), sems)
     core = ids_ref[0]
     slots, spec_wide = rows_ref.shape
     cells, width = gg_ref.shape
     step = min(512, slots)
+    put_emb = pltpu.make_async_copy(emb_ref, emb_hbm, sems.at[len(loads)])
+    last = rows_ref[:, spec_wide - LANES :]
+    col = spec - (spec_wide - LANES)
+    lane = lax.broadcasted_iota(i32, (16, LANES), 1)
+    pick = jnp.where(lane == col, float(clon), jnp.where(lane == col + 1, 1.0, 0.0)).astype(bf16)
+    cell_ref[...] = dot(pick, last, (1, 1))[0:8, :].astype(i32)
 
     for t in range(slots // step):
         at = slice(t * step, (t + 1) * step)
@@ -251,6 +257,8 @@
         if t == 0:
             loads[1].wait()
         emb_ref[:, at] = dot(wot_ref[...], hidden).astype(bf16)
+        if t == slots // step - 1:
+            put_emb.start()
         if t == 0:
             loads[2].wait()
         g_emb = dot(hits, gg_ref[...]).astype(bf16)
@@ -273,6 +281,7 @@
     write_halves(core, gi_out, width, mine_ref, other_ref, 0, head)
     write_halves(core, gi_out, 0, mine_rest, other_rest, head, mine_rest.shape[1])
     clear_tail(width + head, mine_ref, other_ref)
+    put_emb.wait()
 
 
 def encode(ids, rows, weights, spec, clon, out_rows, rest_rows):
@@ -282,15 +291,23 @@
     rest = jax.ShapeDtypeStruct((width // LANES // 2, rest_rows, LANES), bf16)
     return pl.pallas_call(
         functools.partial(encode_kernel, spec, clon),
-        out_shape=(jax.ShapeDtypeStruct((width, slots), bf16), half, half, rest, rest),
+        out_shape=(
+            jax.ShapeDtypeStruct((width, slots), bf16),
+            jax.ShapeDtypeStruct((8, slots), i32),
+            half,
+            half,
+            rest,
+            rest,
+        ),
         in_specs=[smem(), vmem()] + [anywhere()] * len(weights),
-        out_specs=(vmem(),) * 5,
+        out_specs=(anywhere(),) + (vmem(),) * 5,
         scratch_shapes=[pltpu.VMEM(x.shape, x.dtype) for x in weights]
         + [
+            pltpu.VMEM((width, slots), bf16),
             pltpu.VMEM((width, spec_wide), f32),
             pltpu.VMEM((spec_wide, width), f32),
             pltpu.VMEM((width, width), f32),
-            pltpu.SemaphoreType.DMA((len(weights),)),
+            pltpu.SemaphoreType.DMA((len(weights) + 1,)),
         ],
         compiler_params=params(48),
         cost_estimate=cost(10),
@@ -298,15 +315,10 @@
     )(ids, rows, *weights)
 
 
-def bins_kernel(spec, clat, clon, wide, rows_ref, emb_ref, wide_ref, grid_hbm, grid_ref, sem):
-    slots, spec_wide = rows_ref.shape
+def bins_kernel(clat, clon, wide, cell_ref, emb_ref, after_ref, wide_ref, grid_hbm, grid_ref, sem):
     width = emb_ref.shape[0]
     blocks = width // LANES
-    last = rows_ref[:, spec_wide - LANES :]
-    col = spec - (spec_wide - LANES)
-    lane = lax.broadcasted_iota(i32, (16, LANES), 1)
-    pick = jnp.where(lane == col, float(clon), jnp.where(lane == col + 1, 1.0, 0.0)).astype(bf16)
-    cell = dot(pick, last, (1, 1))[0:1, :].astype(i32)
+    cell = cell_ref[0:1, :]
     lines = 4
     place = lax.broadcasted_iota(i32, (wide, 1), 0)
     column = column_of(place, clon // GROUPS) - 1
@@ -334,24 +346,24 @@
     put.wait()
 
 
-def bins(rows, emb, spec, clat, clon, wide):
+def bins(cell, emb, after, clat, clon, wide):
     width = emb.shape[0]
     grid = jax.ShapeDtypeStruct((clat * clon, width), bf16)
     wide_grid = jax.ShapeDtypeStruct((width // LANES, clat + 4, wide, LANES), f32)
     return pl.pallas_call(
-        functools.partial(bins_kernel, spec, clat, clon, wide),
+        functools.partial(bins_kernel, clat, clon, wide),
         out_shape=(wide_grid, grid),
-        in_specs=[vmem()] * 2,
+        in_specs=[vmem()] * 2 + [anywhere()],
         out_specs=(vmem(), anywhere()),
         scratch_shapes=[pltpu.VMEM(grid.shape, bf16), pltpu.SemaphoreType.DMA],
         compiler_params=params(12),
         cost_estimate=cost(4),
         name="bins",
-    )(rows, emb)
+    )(cell, emb, after)
 
 
 def mix_kernel(
-    clat, clon, wide, grid_ref, wd_ref, gm_ref, after_ref,
+    clat, clon, wide, grid_ref, wd_ref, gm_ref,
     mix_ref, gd_ref, mix_hbm, east_out, west_out, east_ref, west_ref, gd, sem,
 ):
     width = wd_ref.shape[1]
@@ -406,25 +418,25 @@
     put.wait()
 
 
-def mix(grid, w_depth, g_mixed, after, clat, clon, wide):
+def mix(grid, w_depth, g_mixed, clat, clon, wide):
     width = w_depth.shape[1]
     column = jax.ShapeDtypeStruct((clat + 2, width), f32)
     ext = jax.ShapeDtypeStruct((round_up((clat + 2) * wide, LANES), width), bf16)
     return pl.pallas_call(
         functools.partial(mix_kernel, clat, clon, wide),
         out_shape=(ext, jax.ShapeDtypeStruct((16, width), f32), ext, column, column),
-        in_specs=[vmem()] * 3 + [anywhere()],
+        in_specs=[vmem()] * 3,
         out_specs=(vmem(),) * 2 + (anywhere(),) + (vmem(),) * 2,
         scratch_shapes=[pltpu.VMEM((clat + 2, GROUPS, width), f32)] * 2
         + [pltpu.VMEM((72, width), f32), pltpu.SemaphoreType.DMA],
         compiler_params=params(8),
         cost_estimate=cost(8),
         name="mix",
-    )(grid, w_depth, g_mixed, after)
+    )(grid, w_depth, g_mixed)
 
 
 def point_kernel(
-    ids_ref, cott_ref, mix_ref, gd_ref, mine_rest, other_rest, after_ref, mine_ref, other_ref, gp
+    ids_ref, cott_ref, mix_ref, gd_ref, mine_rest, other_rest, mine_ref, other_ref, gp
 ):
     core = ids_ref[0]
     width = mix_ref.shape[1]
@@ -437,19 +449,19 @@
     clear_tail(width + rest + 16, mine_ref, other_ref)
 
 
-def point(ids, cot_t, mix_ext, grad_depth, rest, after, out_rows):
+def point(ids, cot_t, mix_ext, grad_depth, rest, out_rows):
     width = mix_ext.shape[1]
     half = jax.ShapeDtypeStruct((width // LANES // 2, out_rows, LANES), bf16)
     return pl.pallas_call(
         point_kernel,
         out_shape=(half, half),
-        in_specs=[smem()] + [vmem()] * 5 + [anywhere()],
+        in_specs=[smem()] + [vmem()] * 5,
         out_specs=(vmem(),) * 2,
         scratch_shapes=[pltpu.VMEM((width, width), f32)],
         compiler_params=params(12),
         cost_estimate=cost(3),
         name="point",
-    )(ids, cot_t, mix_ext, grad_depth, *rest, after)
+    )(ids, cot_t, mix_ext, grad_depth, *rest)
 
 
 def latent_kernel(
@@ -488,66 +500,46 @@
     )(grid, mix_ext, *sides, w_point)
 
 
-def split_kernel(ids_ref, mine_ref, got_ref, keep_ref, send_ref):
-    x = ids_ref[1]
-    for ref, i in ((keep_ref, x), (send_ref, 1 - x)):
-        at = pl.ds(i, 1)
-        ref[...] = (mine_ref[at].astype(f32) + got_ref[at].astype(f32))[0].astype(bf16)
-
-
-def split(ids, mine, got):
-    half = jax.ShapeDtypeStruct(mine.shape[1:], bf16)
-    return pl.pallas_call(
-        split_kernel,
-        out_shape=(half, half),
-        in_specs=[smem()] + [vmem()] * 2,
-        out_specs=(vmem(),) * 2,
-        compiler_params=params(8),
-        cost_estimate=cost(1),
-        name="split",
-    )(ids, mine, got)
-
-
-def merge_kernel(a_keep, a_got, b_keep, b_got, *refs):
-    out_ref = refs[-1]
-    count = out_ref.shape[0]
-    start = 0
-    for keep, got in ((a_keep, a_got), (b_keep, b_got)):
-        total = (keep[...].astype(f32) + got[...].astype(f32)).astype(bf16)
-        size = total.shape[0] // count
-        out_ref[:, start : start + size, :] = total.reshape(count, size, LANES)
-        start += size
-
-
-def merge(a_keep, a_got, b_keep, b_got, count, *after):
-    rows = (a_keep.shape[0] + b_keep.shape[0]) // count
-    return pl.pallas_call(
-        merge_kernel,
-        out_shape=jax.ShapeDtypeStruct((count, rows, LANES), bf16),
-        in_specs=[vmem()] * 4 + [anywhere()] * len(after),
+SWAP = [(0, 1), (1, 0)]
+
+
+def add_kernel(mine_ref, got_ref, out_ref):
+    out_ref[...] = (mine_ref[...].astype(f32) + got_ref[...].astype(f32)).astype(bf16)
+
+
+def core_sum(mine, other):
+    return pl.pallas_call(
+        add_kernel,
+        out_shape=jax.ShapeDtypeStruct(mine.shape, bf16),
+        in_specs=[vmem()] * 2,
         out_specs=vmem(),
         compiler_params=params(8),
         cost_estimate=cost(1),
-        name="merge",
-    )(a_keep, a_got, b_keep, b_got, *after)
-
-
-def totals_kernel(parts_ref, *refs):
+        name="core_sum",
+    )(mine, lax.ppermute(other, "core", SWAP))
+
+
+def totals_kernel(a_ref, b_ref, *refs):
     out_ref = refs[-1]
-    total = jnp.sum(parts_ref[...].astype(f32), axis=0).astype(bf16)
-    out_ref[...] = jnp.broadcast_to(total[None], out_ref.shape)
-
-
-def totals(parts, chips, *after):
+    start = 0
+    for ref in (a_ref, b_ref):
+        size = ref.shape[1]
+        total = jnp.sum(ref[...].astype(f32), axis=0).astype(bf16)
+        out_ref[:, start : start + size, :] = jnp.broadcast_to(total[None], ref.shape)
+        start += size
+
+
+def totals(parts_a, parts_b, *after):
+    chips, rows_a, _ = parts_a.shape
     return pl.pallas_call(
         totals_kernel,
-        out_shape=jax.ShapeDtypeStruct((chips,) + parts.shape[1:], bf16),
-        in_specs=[vmem()] + [anywhere()] * len(after),
+        out_shape=jax.ShapeDtypeStruct((chips, rows_a + parts_b.shape[1], LANES), bf16),
+        in_specs=[vmem()] * 2 + [anywhere()] * len(after),
         out_specs=vmem(),
         compiler_params=params(8),
         cost_estimate=cost(1),
         name="totals",
-    )(parts, *after)
+    )(parts_a, parts_b, *after)
 
 
 def unpack_kernel(
@@ -599,11 +591,10 @@
 CHIPS = ("x", "lon")
 
 
-SWAP = [(0, 1), (1, 0)]
-
-
-def spread(values, axes):
-    return lax.all_to_all(values, axes, split_axis=0, concat_axis=0, tiled=True)
+def spread(values):
+    chips = lax.axis_size(CHIPS)
+    values = values.reshape(chips, values.size // (chips * LANES), LANES)
+    return lax.all_to_all(values, CHIPS, split_axis=0, concat_axis=0, tiled=True)
 
 
 def on_device(spectra, owner, cell, w_in, w_out, w_point, w_depth, cotangent):
@@ -614,7 +605,7 @@
     cells = clat * clon
     wide = clon + 16
     spec_wide = round_up(spec + 2, LANES)
-    ids = jnp.stack([lax.axis_index("core"), lax.axis_index("x")])
+    ids = lax.axis_index("core").reshape(1)
     east_way, west_way = neighbours("lon", True)
     south_way, north_way = neighbours(LAT, False)
 
@@ -644,42 +635,32 @@
     )
     w_in_t = jnp.pad(w_in.T, ((0, 0), (0, spec_wide - spec)))
 
-    chips, pairs = lax.axis_size(CHIPS), lax.axis_size("x") == 2
     align = 16 * tiles * LANES // width
     head = spec - spec % LANES
     rest = round_up(spec - head, 16)
     rows_a = round_up(width + head, align)
     rows_b = round_up(width + rest + 16, align)
-    emb, mine_a, other_a, *rest_halves = encode(
+    emb, cells_got, mine, other, *rest_halves = encode(
         ids, arrived, (w_in_t, w_out.T, g_grid, w_out), spec, clon, rows_a, rest
     )
-    got_a = lax.ppermute(other_a, "core", SWAP)
-    grid_here, grid = bins(arrived, emb, spec, clat, clon, wide)
-    keep_a, send_a = split(ids, mine_a, got_a) if pairs else (mine_a, got_a)
-
+    sum_a = core_sum(mine, other)
+    parts_a = spread(sum_a)
+
+    grid_here, grid = bins(cells_got, emb, sum_a, clat, clon, wide)
     mix_here, grad_depth, mix_ext, east, west = mix(
-        grid_here, w_depth, g_mixed, keep_a, clat, clon, wide
-    )
-    got_a = lax.ppermute(send_a, "x", SWAP) if pairs else send_a
-    mine_b, other_b = point(ids, cot_t, mix_here, grad_depth, rest_halves, got_a, rows_b)
-    got_b = lax.ppermute(other_b, "core", SWAP)
-    if pairs:
-        keep_b, send_b = split(ids, mine_b, got_b)
-        send_b, east, west = lax.optimization_barrier((send_b, east, west))
-        got_b = lax.ppermute(send_b, "x", SWAP)
+        grid_here, w_depth, g_mixed, clat, clon, wide
+    )
+    mine, other = point(ids, cot_t, mix_here, grad_depth, rest_halves, rows_b)
+    sum_b = core_sum(mine, other)
+    sum_b, parts_a, east, west, mix_ext = lax.optimization_barrier(
+        (sum_b, parts_a, east, west, mix_ext)
+    )
+    parts_b = spread(sum_b)
 
     left = lax.ppermute(east, "lon", east_way)
     right = lax.ppermute(west, "lon", west_way)
-    if pairs:
-        summed = merge(keep_a, got_a, keep_b, got_b, lax.axis_size("lon"), left, right)
-    else:
-        sums = [
-            (mine.astype(f32) + got.astype(f32)).astype(bf16).reshape(chips, -1, LANES)
-            for mine, got in ((keep_a, send_a), (mine_b, got_b))
-        ]
-        summed = jnp.concatenate(sums, axis=1)
-    summed, left, right, mix_ext = lax.optimization_barrier((summed, left, right, mix_ext))
-    parts = spread(summed, "lon" if pairs else CHIPS)
+    sent = totals(parts_a, parts_b, left, right)
+    full = spread(sent)
     line = lax.broadcasted_iota(i32, (clon, width), 0)
 
     def edge_row(e):
@@ -689,7 +670,6 @@
 
     top = lax.ppermute(edge_row(clat + 1), LAT, south_way)
     bottom = lax.ppermute(edge_row(0), LAT, north_way)
-    full = spread(totals(parts, chips, top, bottom), CHIPS)
     latent = finish_latent(grid, mix_ext, (top, bottom, left, right), w_point, clat, clon, wide)
 
     obs_scale = float((rows_here * tiles) ** -0.5)

time: 136 us -> 136 us (level)
  waiting for transfers between devices: 37.4 us -> 30.8 us
  local copies, waits for them, and re-layouts: 7.85 us -> 12.3 us
  starting transfers between devices: 33.2 us -> 37 us
  Pallas kernels: 53.9 us -> 52.3 us
    all_to_all x2 -> x3, waiting for transfers between devices: 15.7 us -> 3.22 us  [spread(): lax.all_to_all(values, CHIPS, split_axis=0, concat_axis=0, tiled=True)]
    ppermute x1, waiting for transfers between devices: 2.06 us -> 6.8 us  [on_device(): left = lax.ppermute(east, 'lon', east_way)]
    unnamed x28 -> x32, local copies, waits for them, and re-layouts: 5.11 us -> 9.54 us
    all_to_all x2 -> x3, starting transfers between devices: 10.7 us -> 14.2 us  [spread(): lax.all_to_all(values, CHIPS, split_axis=0, concat_axis=0, tiled=True)]
    ppermute x1, starting transfers between devices: 0.01 us -> 1.66 us  [on_device(): sibling = lax.ppermute(full, 'core', SWAP)]
    pallas_call x5 -> x4, Pallas kernels: 6.78 us -> 6.3 us  [the longest x1 3.57 us: bins(): pl.pallas_call(functools.partial(bins_kernel, clat, clon, wide), out_shap...]
    ppermute x4 -> x2, waiting for transfers between devices: 2.99 us -> 3.39 us  [core_sum(): lax.ppermute(other, 'core', SWAP)]
  transfers between devices with their start and end apart: 16 -> 15, of which waited for: 9 -> 9; matrix products, arithmetic and copies ran while one was open for 3% -> 3% of each run, Pallas kernels for 27% -> 29%
where the time goes in v6:
time: 136 us; the launch traced here: 135 us
  Pallas kernels  52.3 us (38%)
  starting transfers between devices  37 us (27%)
  waiting for transfers between devices  30.8 us (23%)
  local copies, waits for them, and re-layouts  12.3 us (9%)
  other arithmetic  1.96 us (1%)
    pallas_call x1, Pallas kernels, grid_grad(): pl.pallas_call(functools.partial(grid_grad_kernel, clat, clon, wide), out...  15.8 us
    all_to_all x3, starting transfers between devices, spread(): lax.all_to_all(values, CHIPS, split_axis=0, concat_axis=0, tiled=True)  14.2 us
    unnamed x32, local copies, waits for them, and re-layouts  9.54 us
    all_to_all x1, waiting for transfers between devices, on_device(): lax.all_to_all(outgoing.reshape(tiles, cap, spec_wide), ('x', 'core', 'lo...  9.43 us
    pallas_call x1, Pallas kernels, encode(): pl.pallas_call(functools.partial(encode_kernel, spec, clon), out_shape=(j...  9.03 us
    pallas_call x1, Pallas kernels, finish_latent(): pl.pallas_call(functools.partial(latent_kernel, clat, clon, wide), out_sh...  7.81 us
    ppermute x1, waiting for transfers between devices, on_device(): left = lax.ppermute(east, 'lon', east_way)  6.8 us
    pallas_call x1, Pallas kernels, mix(): pl.pallas_call(functools.partial(mix_kernel, clat, clon, wide), out_shape...  6.31 us
  transfers between devices with their start and end apart: 15, of which 9 were waited for; matrix products, arithmetic and copies ran while one was open for 3% of the time, Pallas kernels for 29%

profile of v6, /device:TPU:0, one launch (start us, length us, event | category | flops | bytes accessed | tf_op | source)
XLA Modules:
  0.0 135.3 jit_solution(11973737322015674786)
XLA Ops:
  0.6 1.0 fusion
  1.7 3.0 %collective-permute-start = (bf16[16,512]{1,0:T(8,128)(2,1)S(1)}, bf16[16,512]{1,0:T(8,128)(2,1)S(1)}, u32[]{:S(2)}, u32[]{:S(2)}) collective-permute-start(bf16[16,512]{1,0:T(8,128)(2,1)S(1)} %bitcast.31), channel_id=1, source_target_pairs={{0,1},{1,2},{2,3},{3,4},{4,5},{5,6},{6,7},{7,0},{8,9},{9,10},{10,1... | collective-permute-start | bytes 49160 | tf_op jit(solution)/shard_map/ppermute | solution.py:612
  4.7 3.1 %collective-permute-start.1 = (bf16[16,512]{1,0:T(8,128)(2,1)S(1)}, bf16[16,512]{1,0:T(8,128)(2,1)S(1)}, u32[]{:S(2)}, u32[]{:S(2)}) collective-permute-start(bf16[16,512]{1,0:T(8,128)(2,1)S(1)} %bitcast.32), channel_id=1, source_target_pairs={{1,0},{2,1},{3,2},{4,3},{5,4},{6,5},{7,6},{0,7},{9,8},{10,9},{11,1... | collective-permute-start | bytes 49160 | tf_op jit(solution)/shard_map/ppermute | solution.py:613
  7.8 0.7 pad_add_fusion.places_ref
  8.5 1.1 copy-done.3
  9.6 3.0 %route.1 = bf16[1024,640]{1,0:T(8,128)(2,1)} custom-call(s32[2,512]{1,0:T(2,128)S(1)} %pad_add_fusion.places_ref, bf16[616,512]{1,0:T(8,128)(2,1)S(1)} %bitcast.28), custom_call_target="tpu_custom_call" | custom-call | flops 3460499968 | tf_op jit(solution)/shard_map/route/pallas_call | solution.py:77
  12.6 0.0 collective-permute-done.west_ref
  12.6 0.0 collective-permute-done.1.east_ref
  12.6 0.0 copy-start.14
  12.6 3.3 %all-to-all-start = ((bf16[32,32,640]{2,1,0:T(8,128)(2,1)}), bf16[32,32,640]{2,1,0:T(8,128)(2,1)S(1)}, u32[]{:S(2)}, u32[]{:S(2)}) async-start(bf16[32,32,640]{2,1,0:T(8,128)(2,1)} %bitcast.9), calls=%async_computation | async-start | bytes 2621440 | tf_op jit(solution)/shard_map/all_to_all | solution.py:620
  15.9 0.0 copy-start
  15.9 0.1 pad.11.clone
  16.0 1.0 slice_bitcast_fusion
  17.0 0.1 pad_maximum_fusion.1
  17.2 2.8 %collective-permute-start.2 = (bf16[144,512]{1,0:T(8,128)(2,1)S(1)}, bf16[144,512]{1,0:T(8,128)(2,1)}, u32[]{:S(2)}, u32[]{:S(2)}) collective-permute-start(bf16[144,512]{1,0:T(8,128)(2,1)S(1)} %get-tuple-element.88), channel_id=1, source_target_pairs={{0,8},{8,16},{16,24},{1,9},{9,17},{17,25},{2,10},{10,18},{18,26},{... | collective-permute-start | bytes 442376 | tf_op jit(solution)/shard_map/ppermute | solution.py:629
  20.0 1.3 collective-permute-start.3
  21.3 0.0 copy-done.12
  21.3 0.3 copy.15
  21.6 0.0 copy-done.13
  21.6 0.1 pad.4.wit_hbm
  21.7 0.2 copy.16
  21.9 0.0 collective-permute-done.2.north_ref
  21.9 2.0 %collective-permute-done.3.south_ref = bf16[144,512]{1,0:T(8,128)(2,1)} collective-permute-done((bf16[144,512]{1,0:T(8,128)(2,1)S(1)}, bf16[144,512]{1,0:T(8,128)(2,1)}, u32[]{:S(2)}, u32[]{:S(2)}) %collective-permute-start.3) | collective-permute-done | bytes 147488 | tf_op jit(solution)/shard_map/ppermute | solution.py:630
  23.9 15.8 %grid_grad.1 = (bf16[512,2688]{1,0:T(8,128)(2,1)}, f32[4,18,144,128]{3,2,1,0:T(8,128)}, bf16[2048,512]{1,0:T(8,128)(2,1)}) custom-call(bf16[2048,512]{1,0:T(8,128)(2,1)} %bitcast.30, bf16[16,512]{1,0:T(8,128)(2,1)} %copy-done.14, bf16[16,512]{1,0:T(8,128)(2,1)} %copy-done.13, bf16[144,512]{1,0:T(8,128)(2,1)} %collective-permute-done.2.north_ref, ...), custom_call_target="tpu_custom_call" | custom-call | flops 11534999552 | tf_op jit(solution)/shard_map/grid_grad/pallas_call | solution.py:188
  39.6 9.4 %all-to-all-done = bf16[32,32,640]{2,1,0:T(8,128)(2,1)S(1)} async-done(((bf16[32,32,640]{2,1,0:T(8,128)(2,1)}), bf16[32,32,640]{2,1,0:T(8,128)(2,1)S(1)}, u32[]{:S(2)}, u32[]{:S(2)}) %all-to-all-start) | async-done | bytes 1310752 | tf_op jit(solution)/shard_map/all_to_all | solution.py:620
  49.1 9.0 %encode.1 = (bf16[512,1024]{1,0:T(8,128)(2,1)S(1)}, s32[8,1024]{1,0:T(8,128)S(1)}, bf16[2,1024,128]{2,1,0:T(8,128)(2,1)S(1)}, bf16[2,1024,128]{2,1,0:T(8,128)(2,...) custom-call(s32[1]{0:T(128)} %bitcast.ids_ref, bf16[1024,640]{1,0:T(8,128)(2,1)S(1)} %bitcast.26, ...), custom_call_target="tpu_custom_call" | custom-call | flops 11534999552 | tf_op jit(solution)/shard_map/encode/pallas_call | solution.py:292
  58.1 0.0 copy-start.10
  58.1 0.1 collective-permute-start.4
  58.2 1.9 %collective-permute-done.4.got_ref = bf16[2,1024,128]{2,1,0:T(8,128)(2,1)S(1)} collective-permute-done((bf16[2,1024,128]{2,1,0:T(8,128)(2,1)S(1)}, bf16[2,1024,128]{2,1,0:T(8,128)(2,1)S(1)}, u32[]{:S(2)}, u32[]{:S(2)}) %collective-permute-start.4) | collective-permute-done | bytes 524320 | tf_op jit(solution)/shard_map/ppermute | solution.py:519
  60.1 0.9 core_sum.2.after_ref
  61.0 0.0 copy-done.10
  61.0 3.8 %all-to-all-start.1 = ((bf16[16,128,128]{2,1,0:T(8,128)(2,1)}), bf16[16,128,128]{2,1,0:T(8,128)(2,1)S(1)}, u32[]{:S(2)}, u32[]{:S(2)}) async-start(bf16[16,128,128]{2,1,0:T(8,128)(2,1)} %bitcast.13), calls=%async_computation.1 | async-start | bytes 1048576 | tf_op jit(solution)/shard_map/all_to_all | solution.py:597
  64.8 0.0 copy-start.11
  64.8 1.2 copy-done.11
  66.0 3.6 %bins.1 = (f32[4,20,144,128]{3,2,1,0:T(8,128)S(1)}, bf16[2048,512]{1,0:T(8,128)(2,1)S(1)}) custom-call(s32[8,1024]{1,0:T(8,128)S(1)} %get-tuple-element.46.cell_ref, bf16[512,1024]{1,0:T(8,128)(2,1)S(1)} %copy-done.11, bf16[2,1024,128]{2,1,0:T(8,128)(2,1)} %core_sum.2.after_ref), custom_call_target="tpu_custom_call" | custom-call | flops 4614000128 | tf_op jit(solution)/shard_map/bins/pallas_call | solution.py:353
  69.6 0.0 copy-start.7
  69.6 1.3 copy-done.7
  70.9 2.5 %copy-done.9 = f32[4,18,144,128]{3,2,1,0:T(8,128)S(1)} copy-done((f32[4,18,144,128]{3,2,1,0:T(8,128)S(1)}, f32[4,18,144,128]{3,2,1,0:T(8,128)}, u32[]{:S(2)}) %copy-start.9) | copy-done | bytes 5308440
  73.4 6.3 %mix.1 = (bf16[2688,512]{1,0:T(8,128)(2,1)S(1)}, f32[16,512]{1,0:T(8,128)S(1)}, bf16[2688,512]{1,0:T(8,128)(2,1)S(1)}, f32[18,512]{1,0:T(8,128)S(1)}, f32[18,512]{1,0:T(8,128)S(1)}) custom-call(f32[4,20,144,128]{3,2,1,0:T(8,128)S(1)} %get-tuple-element.50.grid_ref, f32[9,512]{1,0:T(8,128)S(1)} %copy-done.5, f32[4,18,144,128]{3,2,1,0:T(8,128)S(1)} %copy-done.9), custom_call_target="tpu_custom_call" | custom-call | flops 9228000256 | tf_op jit(solution)/shard_map/mix/pallas_call | solution.py:425
  79.8 2.0 %point.1 = (bf16[2,640,128]{2,1,0:T(8,128)(2,1)S(1)}, bf16[2,640,128]{2,1,0:T(8,128)(2,1)S(1)}) custom-call(s32[1]{0:T(128)} %bitcast.ids_ref, bf16[512,2688]{1,0:T(8,128)(2,1)S(1)} %copy-done.6, bf16[2688,512]{1,0:T(8,128)(2,1)S(1)} %get-tuple-element.52.mix_ref, f32[16,512]{1,0:T(8,128)S(1)} %get-tuple-element.53.gd_ref, ...), custom_call_target="tpu_custom_call" | custom-call | flops 3460499968 | tf_op jit(solution)/shard_map/point/pallas_call | solution.py:455
  81.8 0.2 collective-permute-start.5
  82.0 1.5 %collective-permute-done.5.got_ref = bf16[2,640,128]{2,1,0:T(8,128)(2,1)S(1)} collective-permute-done((bf16[2,640,128]{2,1,0:T(8,128)(2,1)S(1)}, bf16[2,640,128]{2,1,0:T(8,128)(2,1)S(1)}, u32[]{:S(2)}, u32[]{:S(2)}) %collective-permute-start.5) | collective-permute-done | bytes 327712 | tf_op jit(solution)/shard_map/ppermute | solution.py:519
  83.5 0.8 core_sum.3
  84.3 0.0 all-to-all-done.1.a_ref
  84.3 6.7 %all-to-all-start.2 = ((bf16[16,80,128]{2,1,0:T(8,128)(2,1)}), bf16[16,80,128]{2,1,0:T(8,128)(2,1)S(1)}, u32[]{:S(2)}, u32[]{:S(2)}) async-start(bf16[16,80,128]{2,1,0:T(8,128)(2,1)} %bitcast.14), calls=%async_computation.2 | async-start | bytes 655360 | tf_op jit(solution)/shard_map/all_to_all | solution.py:597
  91.0 1.9 %collective-permute-start.6 = (f32[18,512]{1,0:T(8,128)S(1)}, f32[18,512]{1,0:T(8,128)S(1)}, u32[]{:S(2)}, u32[]{:S(2)}) collective-permute-start(f32[18,512]{1,0:T(8,128)S(1)} %get-tuple-element.63), channel_id=1, source_target_pairs={{0,1},{1,2},{2,3},{3,4},{4,5},{5,6},{6,7},{7,0},{8,9},{9,10},{10,1... | collective-permute-start | bytes 110600 | tf_op jit(solution)/shard_map/ppermute | solution.py:660
  92.9 2.8 %collective-permute-start.7 = (f32[18,512]{1,0:T(8,128)S(1)}, f32[18,512]{1,0:T(8,128)S(1)}, u32[]{:S(2)}, u32[]{:S(2)}) collective-permute-start(f32[18,512]{1,0:T(8,128)S(1)} %get-tuple-element.64), channel_id=1, source_target_pairs={{1,0},{2,1},{3,2},{4,3},{5,4},{6,5},{7,6},{0,7},{9,8},{10,9},{11,1... | collective-permute-start | bytes 110600 | tf_op jit(solution)/shard_map/ppermute | solution.py:661
  95.7 6.8 %collective-permute-done.6.refs_0_.left_ref = f32[18,512]{1,0:T(8,128)S(1)} collective-permute-done((f32[18,512]{1,0:T(8,128)S(1)}, f32[18,512]{1,0:T(8,128)S(1)}, u32[]{:S(2)}, u32[]{:S(2)}) %collective-permute-start.6) | collective-permute-done | bytes 36896 | tf_op jit(solution)/shard_map/ppermute | solution.py:660
  102.5 0.0 collective-permute-done.7.refs_1_.right_ref
  102.5 1.1 all-to-all-done.2.b_ref
  103.6 1.0 totals.1
  104.7 3.8 %all-to-all-start.3 = ((bf16[16,208,128]{2,1,0:T(8,128)(2,1)}), bf16[16,208,128]{2,1,0:T(8,128)(2,1)S(1)}, u32[]{:S(2)}, u32[]{:S(2)}) async-start(bf16[16,208,128]{2,1,0:T(8,128)(2,1)} %totals.1), calls=%async_computation.3 | async-start | bytes 1703936 | tf_op jit(solution)/shard_map/all_to_all | solution.py:597
  108.5 1.1 add_convert_fusion
  109.6 1.3 collective-permute-start.8
  110.9 1.3 collective-permute-start.9
  112.2 0.0 collective-permute-done.8.top_ref
  112.2 4.0 %collective-permute-done.9.bottom_ref = bf16[128,512]{1,0:T(8,128)(2,1)S(1)} collective-permute-done((bf16[128,512]{1,0:T(8,128)(2,1)S(1)}, bf16[128,512]{1,0:T(8,128)(2,1)S(1)}, u32[]{:S(2)}, u32[]{:S(2)}) %collective-permute-start.9) | collective-permute-done | bytes 131104 | tf_op jit(solution)/shard_map/ppermute | solution.py:672
  116.2 1.8 %copy-done.2 = bf16[2688,512]{1,0:T(8,128)(2,1)S(1)} copy-done((bf16[2688,512]{1,0:T(8,128)(2,1)S(1)}, bf16[2688,512]{1,0:T(8,128)(2,1)}, u32[]{:S(2)}) %copy-start.2) | copy-done | bytes 2752536
  118.0 1.6 %copy-done.8 = bf16[2048,512]{1,0:T(8,128)(2,1)S(1)} copy-done((bf16[2048,512]{1,0:T(8,128)(2,1)S(1)}, bf16[2048,512]{1,0:T(8,128)(2,1)}, u32[]{:S(2)}) %copy-start.8) | copy-done | bytes 2097176
  119.6 7.8 %latent.1 = bf16[2048,512]{1,0:T(8,128)(2,1)} custom-call(bf16[2048,512]{1,0:T(8,128)(2,1)S(1)} %copy-done.8, bf16[2688,512]{1,0:T(8,128)(2,1)S(1)} %copy-done.2, bf16[128,512]{1,0:T(8,128)(2,1)S(1)} %collective-permute-done.8.top_ref, bf16[128,512]{1,0:T(8,128)(2,1)S(1)} %collective-permute-done.9.bottom_ref, ...), custom_call_target="tpu_custom_call" | custom-call | flops 5767499776 | tf_op jit(solution)/shard_map/latent/pallas_call | solution.py:492
  127.4 2.1 %all-to-all-done.3.own_ref = bf16[16,208,128]{2,1,0:T(8,128)(2,1)S(1)} async-done(((bf16[16,208,128]{2,1,0:T(8,128)(2,1)}), bf16[16,208,128]{2,1,0:T(8,128)(2,1)S(1)}, u32[]{:S(2)}, u32[]{:S(2)}) %all-to-all-start.3) | async-done | bytes 852000 | tf_op jit(solution)/shard_map/all_to_all | solution.py:597
  129.5 1.7 %collective-permute-start.10 = (bf16[16,208,128]{2,1,0:T(8,128)(2,1)S(1)}, bf16[16,208,128]{2,1,0:T(8,128)(2,1)S(1)}, u32[]{:S(2)}, u32[]{:S(2)}) collective-permute-start(bf16[16,208,128]{2,1,0:T(8,128)(2,1)S(1)} %all-to-all-done.3.own_ref), channel_id=1, source_target_pairs={{0,8},{8,0},{1,9},{9,1},{2,10},{10,2},{3,11},{11,3},{4,12},{12,4},... | collective-permute-start | bytes 2555912 | tf_op jit(solution)/shard_map/ppermute | solution.py:678
  131.2 2.0 %collective-permute-done.10.sibling_ref = bf16[16,208,128]{2,1,0:T(8,128)(2,1)S(1)} collective-permute-done((bf16[16,208,128]{2,1,0:T(8,128)(2,1)S(1)}, bf16[16,208,128]{2,1,0:T(8,128)(2,1)S(1)}, u32[]{:S(2)}, u32[]{:S(2)}) %collective-permute-start.10) | collective-permute-done | bytes 852000 | tf_op jit(solution)/shard_map/ppermute | solution.py:678
  133.2 2.1 %unpack.1 = (f32[616,512]{1,0:T(8,128)}, f32[512,512]{1,0:T(8,128)}, f32[512,512]{1,0:T(8,128)}, f32[9,512]{1,0:T(8,128)}) custom-call(s32[1]{0:T(128)} %bitcast.ids_ref, bf16[16,208,128]{2,1,0:T(8,128)(2,1)S(1)} %all-to-all-done.3.own_ref, bf16[16,208,128]{2,1,0:T(8,128)(2,1)S(1)} %collective-permute-done.10.sibling_ref), custom_call_target="tpu_custom_call" | custom-call | flops 3460499968 | tf_op jit(solution)/shard_map/unpack/pallas_call | solution.py:569
  (23 shorter events, 0.1 us)
Async XLA Ops:
  1.7 10.9 %collective-permute-start = (bf16[16,512]{1,0:T(8,128)(2,1)S(1)}, bf16[16,512]{1,0:T(8,128)(2,1)S(1)}, u32[]{:S(2)}, u32[]{:S(2)}) collective-permute-start(bf16[16,512]{1,0:T(8,128)(2,1)S(1)} %bitcast.31), channel_id=1, source_target_pairs={{0,1},{1,2},{2,3},{3,4},{4,5},{5,6},{6,7},{7,0},{8,9},{9,10},{10,1... | collective-permute-start | bytes 49160 | tf_op jit(solution)/shard_map/ppermute | solution.py:612
  4.7 7.9 %collective-permute-start.1 = (bf16[16,512]{1,0:T(8,128)(2,1)S(1)}, bf16[16,512]{1,0:T(8,128)(2,1)S(1)}, u32[]{:S(2)}, u32[]{:S(2)}) collective-permute-start(bf16[16,512]{1,0:T(8,128)(2,1)S(1)} %bitcast.32), channel_id=1, source_target_pairs={{1,0},{2,1},{3,2},{4,3},{5,4},{6,5},{7,6},{0,7},{9,8},{10,9},{11,1... | collective-permute-start | bytes 49160 | tf_op jit(solution)/shard_map/ppermute | solution.py:613
  8.5 1.1 copy-start.3
  12.6 8.7 %copy-start.12 = (bf16[616,512]{1,0:T(8,128)(2,1)S(1)}, bf16[616,512]{1,0:T(8,128)(2,1)}, u32[]{:S(2)}) copy-start(bf16[616,512]{1,0:T(8,128)(2,1)} %param.11) | copy-start | bytes 1892356
  12.6 9.0 %copy-start.13 = (bf16[16,512]{1,0:T(8,128)(2,1)}, bf16[16,512]{1,0:T(8,128)(2,1)S(1)}, u32[]{:S(2)}) copy-start(bf16[16,512]{1,0:T(8,128)(2,1)S(1)} %collective-permute-done.west_ref) | copy-start | bytes 49156
  12.6 9.0 %copy-start.14 = (bf16[16,512]{1,0:T(8,128)(2,1)}, bf16[16,512]{1,0:T(8,128)(2,1)S(1)}, u32[]{:S(2)}) copy-start(bf16[16,512]{1,0:T(8,128)(2,1)S(1)} %collective-permute-done.1.east_ref) | copy-start | bytes 49156
  12.6 36.5 %all-to-all-start = ((bf16[32,32,640]{2,1,0:T(8,128)(2,1)}), bf16[32,32,640]{2,1,0:T(8,128)(2,1)S(1)}, u32[]{:S(2)}, u32[]{:S(2)}) async-start(bf16[32,32,640]{2,1,0:T(8,128)(2,1)} %bitcast.9), calls=%async_computation | async-start | bytes 2621440 | tf_op jit(solution)/shard_map/all_to_all | solution.py:620
  15.9 5.8 %copy-start = (bf16[512,512]{1,0:T(8,128)(2,1)S(1)}, bf16[512,512]{1,0:T(8,128)(2,1)}, u32[]{:S(2)}) copy-start(bf16[512,512]{1,0:T(8,128)(2,1)} %wo_hbm) | copy-start | bytes 1572868
  17.2 4.7 %collective-permute-start.2 = (bf16[144,512]{1,0:T(8,128)(2,1)S(1)}, bf16[144,512]{1,0:T(8,128)(2,1)}, u32[]{:S(2)}, u32[]{:S(2)}) collective-permute-start(bf16[144,512]{1,0:T(8,128)(2,1)S(1)} %get-tuple-element.88), channel_id=1, source_target_pairs={{0,8},{8,16},{16,24},{1,9},{9,17},{17,25},{2,10},{10,18},{18,26},{... | collective-permute-start | bytes 442376 | tf_op jit(solution)/shard_map/ppermute | solution.py:629
  20.0 3.9 %collective-permute-start.3 = (bf16[144,512]{1,0:T(8,128)(2,1)S(1)}, bf16[144,512]{1,0:T(8,128)(2,1)}, u32[]{:S(2)}, u32[]{:S(2)}) collective-permute-start(bf16[144,512]{1,0:T(8,128)(2,1)S(1)} %get-tuple-element.87), channel_id=1, source_target_pairs={{8,0},{16,8},{24,16},{9,1},{17,9},{25,17},{10,2},{18,10},{26,18},{... | collective-permute-start | bytes 442376 | tf_op jit(solution)/shard_map/ppermute | solution.py:630
  58.1 2.9 %copy-start.10 = (bf16[512,1024]{1,0:T(8,128)(2,1)}, bf16[512,1024]{1,0:T(8,128)(2,1)S(1)}, u32[]{:S(2)}) copy-start(bf16[512,1024]{1,0:T(8,128)(2,1)S(1)} %get-tuple-element.47.emb_ref) | copy-start | bytes 3145732
  58.1 2.0 %collective-permute-start.4 = (bf16[2,1024,128]{2,1,0:T(8,128)(2,1)S(1)}, bf16[2,1024,128]{2,1,0:T(8,128)(2,1)S(1)}, u32[]{:S(2)}, u32[]{:S(2)}) collective-permute-start(bf16[2,1024,128]{2,1,0:T(8,128)(2,1)S(1)} %get-tuple-element.49), channel_id=1, source_target_pairs={{0,8},{8,0},{1,9},{9,1},{2,10},{10,2},{3,11},{11,3},{4,12},{12,4},... | collective-permute-start | bytes 1572872 | tf_op jit(solution)/shard_map/ppermute | solution.py:519
  61.0 23.2 %all-to-all-start.1 = ((bf16[16,128,128]{2,1,0:T(8,128)(2,1)}), bf16[16,128,128]{2,1,0:T(8,128)(2,1)S(1)}, u32[]{:S(2)}, u32[]{:S(2)}) async-start(bf16[16,128,128]{2,1,0:T(8,128)(2,1)} %bitcast.13), calls=%async_computation.1 | async-start | bytes 1048576 | tf_op jit(solution)/shard_map/all_to_all | solution.py:597
  64.8 1.2 copy-start.11
  66.0 4.9 %copy-start.5 = (f32[9,512]{1,0:T(8,128)S(1)}, f32[9,512]{1,0:T(8,128)}, u32[]{:S(2)}) copy-start(f32[9,512]{1,0:T(8,128)} %wd_ref.3) | copy-start | bytes 55300
  69.6 1.3 copy-start.7
  70.9 2.5 %copy-start.9 = (f32[4,18,144,128]{3,2,1,0:T(8,128)S(1)}, f32[4,18,144,128]{3,2,1,0:T(8,128)}, u32[]{:S(2)}) copy-start(f32[4,18,144,128]{3,2,1,0:T(8,128)} %get-tuple-element.51.gm_ref) | copy-start | bytes 15925252
  73.4 6.3 %copy-start.6 = (bf16[512,2688]{1,0:T(8,128)(2,1)S(1)}, bf16[512,2688]{1,0:T(8,128)(2,1)}, u32[]{:S(2)}) copy-start(bf16[512,2688]{1,0:T(8,128)(2,1)} %get-tuple-element.41.cott_ref) | copy-start | bytes 8257540
  79.7 2.0 %copy-start.1 = (bf16[2688,512]{1,0:T(8,128)(2,1)}, bf16[2688,512]{1,0:T(8,128)(2,1)S(1)}, u32[]{:S(2)}) copy-start(bf16[2688,512]{1,0:T(8,128)(2,1)S(1)} %get-tuple-element.66.mix_ref) | copy-start | bytes 8257540
  81.8 1.7 %collective-permute-start.5 = (bf16[2,640,128]{2,1,0:T(8,128)(2,1)S(1)}, bf16[2,640,128]{2,1,0:T(8,128)(2,1)S(1)}, u32[]{:S(2)}, u32[]{:S(2)}) collective-permute-start(bf16[2,640,128]{2,1,0:T(8,128)(2,1)S(1)} %get-tuple-element.57), channel_id=1, source_target_pairs={{0,8},{8,0},{1,9},{9,1},{2,10},{10,2},{3,11},{11,3},{4,12},{12,4},... | collective-permute-start | bytes 983048 | tf_op jit(solution)/shard_map/ppermute | solution.py:519
  84.3 19.4 %all-to-all-start.2 = ((bf16[16,80,128]{2,1,0:T(8,128)(2,1)}), bf16[16,80,128]{2,1,0:T(8,128)(2,1)S(1)}, u32[]{:S(2)}, u32[]{:S(2)}) async-start(bf16[16,80,128]{2,1,0:T(8,128)(2,1)} %bitcast.14), calls=%async_computation.2 | async-start | bytes 655360 | tf_op jit(solution)/shard_map/all_to_all | solution.py:597
  91.0 11.6 %collective-permute-start.6 = (f32[18,512]{1,0:T(8,128)S(1)}, f32[18,512]{1,0:T(8,128)S(1)}, u32[]{:S(2)}, u32[]{:S(2)}) collective-permute-start(f32[18,512]{1,0:T(8,128)S(1)} %get-tuple-element.63), channel_id=1, source_target_pairs={{0,1},{1,2},{2,3},{3,4},{4,5},{5,6},{6,7},{7,0},{8,9},{9,10},{10,1... | collective-permute-start | bytes 110600 | tf_op jit(solution)/shard_map/ppermute | solution.py:660
  92.9 9.7 %collective-permute-start.7 = (f32[18,512]{1,0:T(8,128)S(1)}, f32[18,512]{1,0:T(8,128)S(1)}, u32[]{:S(2)}, u32[]{:S(2)}) collective-permute-start(f32[18,512]{1,0:T(8,128)S(1)} %get-tuple-element.64), channel_id=1, source_target_pairs={{1,0},{2,1},{3,2},{4,3},{5,4},{6,5},{7,6},{0,7},{9,8},{10,9},{11,1... | collective-permute-start | bytes 110600 | tf_op jit(solution)/shard_map/ppermute | solution.py:661
  104.7 11.6 %copy-start.4 = (bf16[512,512]{1,0:T(8,128)(2,1)S(1)}, bf16[512,512]{1,0:T(8,128)(2,1)}, u32[]{:S(2)}) copy-start(bf16[512,512]{1,0:T(8,128)(2,1)} %wp_ref.3) | copy-start | bytes 1572868
  104.7 24.9 %all-to-all-start.3 = ((bf16[16,208,128]{2,1,0:T(8,128)(2,1)}), bf16[16,208,128]{2,1,0:T(8,128)(2,1)S(1)}, u32[]{:S(2)}, u32[]{:S(2)}) async-start(bf16[16,208,128]{2,1,0:T(8,128)(2,1)} %totals.1), calls=%async_computation.3 | async-start | bytes 1703936 | tf_op jit(solution)/shard_map/all_to_all | solution.py:597
  109.6 2.6 %collective-permute-start.8 = (bf16[128,512]{1,0:T(8,128)(2,1)S(1)}, bf16[128,512]{1,0:T(8,128)(2,1)S(1)}, u32[]{:S(2)}, u32[]{:S(2)}) collective-permute-start(bf16[128,512]{1,0:T(8,128)(2,1)S(1)} %get-tuple-element.74), channel_id=1, source_target_pairs={{0,8},{8,16},{16,24},{1,9},{9,17},{17,25},{2,10},{10,18},{18,26},{... | collective-permute-start | bytes 393224 | tf_op jit(solution)/shard_map/ppermute | solution.py:671
  110.9 5.3 %collective-permute-start.9 = (bf16[128,512]{1,0:T(8,128)(2,1)S(1)}, bf16[128,512]{1,0:T(8,128)(2,1)S(1)}, u32[]{:S(2)}, u32[]{:S(2)}) collective-permute-start(bf16[128,512]{1,0:T(8,128)(2,1)S(1)} %get-tuple-element.73), channel_id=1, source_target_pairs={{8,0},{16,8},{24,16},{9,1},{17,9},{25,17},{10,2},{18,10},{26,18},{... | collective-permute-start | bytes 393224 | tf_op jit(solution)/shard_map/ppermute | solution.py:672
  116.2 1.8 %copy-start.2 = (bf16[2688,512]{1,0:T(8,128)(2,1)S(1)}, bf16[2688,512]{1,0:T(8,128)(2,1)}, u32[]{:S(2)}) copy-start(bf16[2688,512]{1,0:T(8,128)(2,1)} %copy-done.1) | copy-start | bytes 8257540
  118.0 1.6 %copy-start.8 = (bf16[2048,512]{1,0:T(8,128)(2,1)S(1)}, bf16[2048,512]{1,0:T(8,128)(2,1)}, u32[]{:S(2)}) copy-start(bf16[2048,512]{1,0:T(8,128)(2,1)} %copy-done.7) | copy-start | bytes 6291460
  129.5 3.7 %collective-permute-start.10 = (bf16[16,208,128]{2,1,0:T(8,128)(2,1)S(1)}, bf16[16,208,128]{2,1,0:T(8,128)(2,1)S(1)}, u32[]{:S(2)}, u32[]{:S(2)}) collective-permute-start(bf16[16,208,128]{2,1,0:T(8,128)(2,1)S(1)} %all-to-all-done.3.own_ref), channel_id=1, source_target_pairs={{0,8},{8,0},{1,9},{9,1},{2,10},{10,2},{3,11},{11,3},{4,12},{12,4},... | collective-permute-start | bytes 2555912 | tf_op jit(solution)/shard_map/ppermute | solution.py:678

commit v7 on v6

--- a/solution.py
+++ b/solution.py
@@ -315,9 +315,19 @@
     )(ids, rows, *weights)
 
 
-def bins_kernel(clat, clon, wide, cell_ref, emb_ref, after_ref, wide_ref, grid_hbm, grid_ref, sem):
+def mix_kernel(
+    clat, clon, wide, ids_ref, cell_ref, wd_ref, mine_rest, other_rest,
+    emb_hbm, gm_hbm, cott_hbm, after_ref,
+    mine_ref, other_ref, east_out, west_out, grid_hbm, mix_hbm,
+    emb_ref, gm_ref, cott_ref, wide_ref, grid_ref, mix_ref, east_ref, west_ref, gp, gd, sems,
+):
+    loads = start_loads((emb_hbm, gm_hbm, cott_hbm), (emb_ref, gm_ref, cott_ref), sems)
+    put_grid = pltpu.make_async_copy(grid_ref, grid_hbm, sems.at[3])
+    put_mix = pltpu.make_async_copy(mix_ref, mix_hbm, sems.at[4])
+    core = ids_ref[0]
     width = emb_ref.shape[0]
     blocks = width // LANES
+
     cell = cell_ref[0:1, :]
     lines = 4
     place = lax.broadcasted_iota(i32, (wide, 1), 0)
@@ -328,8 +338,12 @@
     empty = jnp.zeros((blocks, 2, wide, LANES), f32)
     wide_ref[:, 0:2] = empty
     wide_ref[:, clat + 2 :] = empty
-
-    def body(t, carry):
+    gd[...] = jnp.zeros_like(gd)
+    used = (clat + 2) * wide
+    mix_ref[used:, :] = jnp.zeros((mix_ref.shape[0] - used, width), bf16)
+    loads[0].wait()
+
+    def bins(t, carry):
         hits = (cell == wanted + t * (lines * clon)).astype(f32).astype(bf16)
         grid = dot(hits, emb_ref[...], (1, 1)).astype(bf16).astype(f32)
         for k in range(lines):
@@ -340,38 +354,9 @@
             grid_ref[at, :] = line[GROUPS : GROUPS + clon].astype(bf16)
         return carry
 
-    lax.fori_loop(0, clat // lines, body, 0)
-    put = pltpu.make_async_copy(grid_ref, grid_hbm, sem)
-    put.start()
-    put.wait()
-
-
-def bins(cell, emb, after, clat, clon, wide):
-    width = emb.shape[0]
-    grid = jax.ShapeDtypeStruct((clat * clon, width), bf16)
-    wide_grid = jax.ShapeDtypeStruct((width // LANES, clat + 4, wide, LANES), f32)
-    return pl.pallas_call(
-        functools.partial(bins_kernel, clat, clon, wide),
-        out_shape=(wide_grid, grid),
-        in_specs=[vmem()] * 2 + [anywhere()],
-        out_specs=(vmem(), anywhere()),
-        scratch_shapes=[pltpu.VMEM(grid.shape, bf16), pltpu.SemaphoreType.DMA],
-        compiler_params=params(12),
-        cost_estimate=cost(4),
-        name="bins",
-    )(cell, emb, after)
-
-
-def mix_kernel(
-    clat, clon, wide, grid_ref, wd_ref, gm_ref,
-    mix_ref, gd_ref, mix_hbm, east_out, west_out, east_ref, west_ref, gd, sem,
-):
-    width = wd_ref.shape[1]
-    blocks = width // LANES
-    put = pltpu.make_async_copy(mix_ref, mix_hbm, sem)
-    gd[...] = jnp.zeros_like(gd)
-    used = (clat + 2) * wide
-    mix_ref[used:, :] = jnp.zeros((mix_ref.shape[0] - used, width), bf16)
+    lax.fori_loop(0, clat // lines, bins, 0)
+    put_grid.start()
+    loads[1].wait()
     group = lax.broadcasted_iota(i32, (GROUPS, LANES), 0)
 
     def conv(e, carry):
@@ -383,7 +368,7 @@
                 grads = gm_ref[n, e, c : c + CHUNK + 2 * GROUPS, :]
                 mixed = None
                 for a in range(3):
-                    cells = grid_ref[n, e + a, c : c + CHUNK + 2 * GROUPS, :]
+                    cells = wide_ref[n, e + a, c : c + CHUNK + 2 * GROUPS, :]
                     middle = cells[GROUPS : GROUPS + CHUNK]
                     for b in range(3):
                         k = 3 * a + b
@@ -400,7 +385,7 @@
             for b, at, valid in ((0, clon, GROUPS - 1), (2, GROUPS, 0)):
                 end = None
                 for a in range(3):
-                    term = weights[3 * a + b] * grid_ref[n, e + a, at : at + GROUPS, :]
+                    term = weights[3 * a + b] * wide_ref[n, e + a, at : at + GROUPS, :]
                     end = term if end is None else end + term
                 ends.append(jnp.where(group == valid, end, 0.0))
             east_ref[e, :, cols] = ends[0]
@@ -410,58 +395,49 @@
         return carry
 
     lax.fori_loop(0, clat + 2, conv, 0)
-    put.start()
+    put_mix.start()
+    loads[2].wait()
+    gp[...] = dot(cott_ref[...], mix_ref[...]).T
     east_out[...] = east_ref[:, GROUPS - 1, :]
     west_out[...] = west_ref[:, 0, :]
     taps = [jnp.sum(gd[8 * k : 8 * k + 8, :], axis=0, keepdims=True) for k in range(9)]
-    gd_ref[...] = jnp.concatenate(taps + [jnp.zeros((7, width), f32)], axis=0)
-    put.wait()
-
-
-def mix(grid, w_depth, g_mixed, clat, clon, wide):
-    width = w_depth.shape[1]
-    column = jax.ShapeDtypeStruct((clat + 2, width), f32)
-    ext = jax.ShapeDtypeStruct((round_up((clat + 2) * wide, LANES), width), bf16)
-    return pl.pallas_call(
-        functools.partial(mix_kernel, clat, clon, wide),
-        out_shape=(ext, jax.ShapeDtypeStruct((16, width), f32), ext, column, column),
-        in_specs=[vmem()] * 3,
-        out_specs=(vmem(),) * 2 + (anywhere(),) + (vmem(),) * 2,
-        scratch_shapes=[pltpu.VMEM((clat + 2, GROUPS, width), f32)] * 2
-        + [pltpu.VMEM((72, width), f32), pltpu.SemaphoreType.DMA],
-        compiler_params=params(8),
-        cost_estimate=cost(8),
-        name="mix",
-    )(grid, w_depth, g_mixed)
-
-
-def point_kernel(
-    ids_ref, cott_ref, mix_ref, gd_ref, mine_rest, other_rest, mine_ref, other_ref, gp
-):
-    core = ids_ref[0]
-    width = mix_ref.shape[1]
+    gd[0:16, :] = jnp.concatenate(taps + [jnp.zeros((7, width), f32)], axis=0)
     rest = mine_rest.shape[1]
-    gp[...] = dot(cott_ref[...], mix_ref[...]).T
     write_halves(core, gp, 0, mine_ref, other_ref)
     mine_ref[:, width : width + rest, :] = mine_rest[...]
     other_ref[:, width : width + rest, :] = other_rest[...]
-    write_halves(core, gd_ref, width + rest, mine_ref, other_ref, 0, 16)
+    write_halves(core, gd, width + rest, mine_ref, other_ref, 0, 16)
     clear_tail(width + rest + 16, mine_ref, other_ref)
-
-
-def point(ids, cot_t, mix_ext, grad_depth, rest, out_rows):
-    width = mix_ext.shape[1]
+    put_grid.wait()
+    put_mix.wait()
+
+
+def mix(ids, cell, w_depth, rest, emb, g_mixed, cot_t, after, clat, clon, wide, out_rows):
+    width = w_depth.shape[1]
     half = jax.ShapeDtypeStruct((width // LANES // 2, out_rows, LANES), bf16)
-    return pl.pallas_call(
-        point_kernel,
-        out_shape=(half, half),
-        in_specs=[smem()] + [vmem()] * 5,
-        out_specs=(vmem(),) * 2,
-        scratch_shapes=[pltpu.VMEM((width, width), f32)],
-        compiler_params=params(12),
-        cost_estimate=cost(3),
-        name="point",
-    )(ids, cot_t, mix_ext, grad_depth, *rest)
+    column = jax.ShapeDtypeStruct((clat + 2, width), f32)
+    grid = jax.ShapeDtypeStruct((clat * clon, width), bf16)
+    ext = jax.ShapeDtypeStruct(cot_t.shape[::-1], bf16)
+    return pl.pallas_call(
+        functools.partial(mix_kernel, clat, clon, wide),
+        out_shape=(half, half, column, column, grid, ext),
+        in_specs=[smem()] + [vmem()] * 4 + [anywhere()] * 4,
+        out_specs=(vmem(),) * 4 + (anywhere(),) * 2,
+        scratch_shapes=[pltpu.VMEM(x.shape, x.dtype) for x in (emb, g_mixed, cot_t)]
+        + [
+            pltpu.VMEM((width // LANES, clat + 4, wide, LANES), f32),
+            pltpu.VMEM(grid.shape, bf16),
+            pltpu.VMEM(ext.shape, bf16),
+            pltpu.VMEM((clat + 2, GROUPS, width), f32),
+            pltpu.VMEM((clat + 2, GROUPS, width), f32),
+            pltpu.VMEM((width, width), f32),
+            pltpu.VMEM((72, width), f32),
+            pltpu.SemaphoreType.DMA((5,)),
+        ],
+        compiler_params=params(56),
+        cost_estimate=cost(13),
+        name="mix",
+    )(ids, cell, w_depth, *rest, emb, g_mixed, cot_t, after)
 
 
 def latent_kernel(
@@ -485,7 +461,7 @@
         out_ref[at, :] = dot(natural_order, out.astype(bf16)).astype(bf16)
         return carry
 
-    lax.fori_loop(0, clat, body, 0)
+    lax.fori_loop(0, clat, body, 0, unroll=2)
 
 
 def finish_latent(grid, mix_ext, sides, w_point, clat, clon, wide):
@@ -646,11 +622,10 @@
     sum_a = core_sum(mine, other)
     parts_a = spread(sum_a)
 
-    grid_here, grid = bins(cells_got, emb, sum_a, clat, clon, wide)
-    mix_here, grad_depth, mix_ext, east, west = mix(
-        grid_here, w_depth, g_mixed, clat, clon, wide
-    )
-    mine, other = point(ids, cot_t, mix_here, grad_depth, rest_halves, rows_b)
+    mine, other, east, west, grid, mix_ext = mix(
+        ids, cells_got, w_depth, rest_halves, emb, g_mixed, cot_t, sum_a,
+        clat, clon, wide, rows_b,
+    )
     sum_b = core_sum(mine, other)
     sum_b, parts_a, east, west, mix_ext = lax.optimization_barrier(
         (sum_b, parts_a, east, west, mix_ext)

time: 136 us -> 133 us (0.978)
  local copies, waits for them, and re-layouts: 12.3 us -> 10 us
  starting transfers between devices: 37 us -> 35.1 us
    pallas_call x1, Pallas kernels: 6.31 us -> 14.2 us  [mix(): pl.pallas_call(functools.partial(mix_kernel, clat, clon, wide), out_shape...]
    pallas_call x2 -> x0, Pallas kernels: 5.56 us -> none  [the longest x1 3.57 us: bins(): pl.pallas_call(functools.partial(bins_kernel, clat, clon, wide), out_shap...]
    unnamed x32 -> x34, local copies, waits for them, and re-layouts: 9.54 us -> 5.49 us
  transfers between devices with their start and end apart: 15 -> 15, of which waited for: 9 -> 9; matrix products, arithmetic and copies ran while one was open for 3% -> 4% of each run, Pallas kernels for 29% -> 30%
where the time goes in v7:
time: 133 us
  Pallas kernels  53.4 us (40%)
  starting transfers between devices  35.1 us (26%)
  waiting for transfers between devices  31.1 us (23%)
  local copies, waits for them, and re-layouts  10 us (8%)
  other arithmetic  1.96 us (1%)
    pallas_call x1, Pallas kernels, grid_grad(): pl.pallas_call(functools.partial(grid_grad_kernel, clat, clon, wide), out...  15.8 us
    all_to_all x3, starting transfers between devices, spread(): lax.all_to_all(values, CHIPS, split_axis=0, concat_axis=0, tiled=True)  14.2 us
    pallas_call x1, Pallas kernels, mix(): pl.pallas_call(functools.partial(mix_kernel, clat, clon, wide), out_shape...  14.2 us
    all_to_all x1, waiting for transfers between devices, on_device(): lax.all_to_all(outgoing.reshape(tiles, cap, spec_wide), ('x', 'core', 'lo...  9.49 us
    pallas_call x1, Pallas kernels, encode(): pl.pallas_call(functools.partial(encode_kernel, spec, clon), out_shape=(j...  9.03 us
    ppermute x1, waiting for transfers between devices, on_device(): left = lax.ppermute(east, 'lon', east_way)  6.79 us
    pallas_call x1, Pallas kernels, finish_latent(): pl.pallas_call(functools.partial(latent_kernel, clat, clon, wide), out_sh...  6.58 us
    unnamed x34, local copies, waits for them, and re-layouts  5.49 us
  transfers between devices with their start and end apart: 15, of which 9 were waited for; matrix products, arithmetic and copies ran while one was open for 4% of the time, Pallas kernels for 30%

profile of v7, /device:TPU:0, one launch (start us, length us, event | category | flops | bytes accessed | tf_op | source)
XLA Modules:
  0.0 132.5 jit_solution(4919889240751754111)
XLA Ops:
  0.6 1.0 fusion
  1.7 3.0 %collective-permute-start = (bf16[16,512]{1,0:T(8,128)(2,1)S(1)}, bf16[16,512]{1,0:T(8,128)(2,1)S(1)}, u32[]{:S(2)}, u32[]{:S(2)}) collective-permute-start(bf16[16,512]{1,0:T(8,128)(2,1)S(1)} %bitcast.31), channel_id=1, source_target_pairs={{0,1},{1,2},{2,3},{3,4},{4,5},{5,6},{6,7},{7,0},{8,9},{9,10},{10,1... | collective-permute-start | bytes 49160 | tf_op jit(solution)/shard_map/ppermute | solution.py:588
  4.7 3.1 %collective-permute-start.1 = (bf16[16,512]{1,0:T(8,128)(2,1)S(1)}, bf16[16,512]{1,0:T(8,128)(2,1)S(1)}, u32[]{:S(2)}, u32[]{:S(2)}) collective-permute-start(bf16[16,512]{1,0:T(8,128)(2,1)S(1)} %bitcast.32), channel_id=1, source_target_pairs={{1,0},{2,1},{3,2},{4,3},{5,4},{6,5},{7,6},{0,7},{9,8},{10,9},{11,1... | collective-permute-start | bytes 49160 | tf_op jit(solution)/shard_map/ppermute | solution.py:589
  7.8 0.7 pad_add_fusion.places_ref
  8.5 1.1 copy-done.2
  9.6 3.0 %route.1 = bf16[1024,640]{1,0:T(8,128)(2,1)} custom-call(s32[2,512]{1,0:T(2,128)S(1)} %pad_add_fusion.places_ref, bf16[616,512]{1,0:T(8,128)(2,1)S(1)} %bitcast.28), custom_call_target="tpu_custom_call" | custom-call | flops 3460499968 | tf_op jit(solution)/shard_map/route/pallas_call | solution.py:77
  12.6 0.0 collective-permute-done.west_ref
  12.6 0.0 collective-permute-done.1.east_ref
  12.6 0.0 copy-start.12
  12.6 0.0 copy-start.10
  12.6 3.3 %all-to-all-start = ((bf16[32,32,640]{2,1,0:T(8,128)(2,1)}), bf16[32,32,640]{2,1,0:T(8,128)(2,1)S(1)}, u32[]{:S(2)}, u32[]{:S(2)}) async-start(bf16[32,32,640]{2,1,0:T(8,128)(2,1)} %bitcast.6), calls=%async_computation | async-start | bytes 2621440 | tf_op jit(solution)/shard_map/all_to_all | solution.py:596
  15.9 0.1 pad.11.clone
  16.0 1.0 slice_bitcast_fusion
  17.0 0.1 pad_maximum_fusion.1
  17.1 2.2 %collective-permute-start.2 = (bf16[144,512]{1,0:T(8,128)(2,1)S(1)}, bf16[144,512]{1,0:T(8,128)(2,1)S(1)}, u32[]{:S(2)}, u32[]{:S(2)}) collective-permute-start(bf16[144,512]{1,0:T(8,128)(2,1)S(1)} %get-tuple-element.82), channel_id=1, source_target_pairs={{0,8},{8,16},{16,24},{1,9},{9,17},{17,25},{2,10},{10,18},{18,26},{... | collective-permute-start | bytes 442376 | tf_op jit(solution)/shard_map/ppermute | solution.py:605
  19.3 1.3 collective-permute-start.3
  20.6 0.0 copy-done
  20.6 0.2 copy.16
  20.8 0.0 copy-done.11
  20.8 0.0 copy-done.12
  20.8 0.0 copy-done.10
  20.8 1.1 copy.15
  21.9 1.1 pad.4.wit_hbm
  23.1 0.0 collective-permute-done.2.north_ref
  23.1 0.0 copy-start.13
  23.1 0.7 collective-permute-done.3.south_ref
  23.8 15.8 %grid_grad.1 = (bf16[512,2688]{1,0:T(8,128)(2,1)}, f32[4,18,144,128]{3,2,1,0:T(8,128)}, bf16[2048,512]{1,0:T(8,128)(2,1)}) custom-call(bf16[2048,512]{1,0:T(8,128)(2,1)} %bitcast.30, bf16[16,512]{1,0:T(8,128)(2,1)} %copy-done.12, bf16[16,512]{1,0:T(8,128)(2,1)} %copy-done.11, bf16[144,512]{1,0:T(8,128)(2,1)} %copy-done.13, ...), custom_call_target="tpu_custom_call" | custom-call | flops 11534999552 | tf_op jit(solution)/shard_map/grid_grad/pallas_call | solution.py:188
  39.6 9.5 %all-to-all-done = bf16[32,32,640]{2,1,0:T(8,128)(2,1)S(1)} async-done(((bf16[32,32,640]{2,1,0:T(8,128)(2,1)}), bf16[32,32,640]{2,1,0:T(8,128)(2,1)S(1)}, u32[]{:S(2)}, u32[]{:S(2)}) %all-to-all-start) | async-done | bytes 1310752 | tf_op jit(solution)/shard_map/all_to_all | solution.py:596
  49.1 9.0 %encode.1 = (bf16[512,1024]{1,0:T(8,128)(2,1)S(1)}, s32[8,1024]{1,0:T(8,128)S(1)}, bf16[2,1024,128]{2,1,0:T(8,128)(2,1)S(1)}, bf16[2,1024,128]{2,1,0:T(8,128)(2,...) custom-call(s32[1]{0:T(128)} %bitcast.ids_ref, bf16[1024,640]{1,0:T(8,128)(2,1)S(1)} %bitcast.26, ...), custom_call_target="tpu_custom_call" | custom-call | flops 11534999552 | tf_op jit(solution)/shard_map/encode/pallas_call | solution.py:292
  58.1 0.0 copy-start.6
  58.1 0.0 copy-start.7
  58.1 0.0 copy-start.8
  58.2 0.0 copy-start.9
  58.2 0.1 collective-permute-start.4
  58.2 1.9 %collective-permute-done.4.got_ref = bf16[2,1024,128]{2,1,0:T(8,128)(2,1)S(1)} collective-permute-done((bf16[2,1024,128]{2,1,0:T(8,128)(2,1)S(1)}, bf16[2,1024,128]{2,1,0:T(8,128)(2,1)S(1)}, u32[]{:S(2)}, u32[]{:S(2)}) %collective-permute-start.4) | collective-permute-done | bytes 524320 | tf_op jit(solution)/shard_map/ppermute | solution.py:495
  60.1 0.9 core_sum.2.after_ref
  61.1 0.0 copy-done.7
  61.1 3.8 %all-to-all-start.1 = ((bf16[16,128,128]{2,1,0:T(8,128)(2,1)}), bf16[16,128,128]{2,1,0:T(8,128)(2,1)S(1)}, u32[]{:S(2)}, u32[]{:S(2)}) async-start(bf16[16,128,128]{2,1,0:T(8,128)(2,1)} %bitcast.13), calls=%async_computation.1 | async-start | bytes 1048576 | tf_op jit(solution)/shard_map/all_to_all | solution.py:573
  64.8 14.2 %mix.1 = (bf16[2,640,128]{2,1,0:T(8,128)(2,1)}, bf16[2,640,128]{2,1,0:T(8,128)(2,1)}, f32[18,512]{1,0:T(8,128)}, f32[18,512]{1,0:T(8,128)}, bf16[2048,512]{1,0:T(8,128)(2,1)}, /*index=5*/bf16[2688,512]{1,0:T(8,128)(2,1)}) custom-call(s32[1]{0:T(128)} %bitcast.ids_ref, s32[8,1024]{1,0:T(8,128)} %copy-done.9, f32[9,512]{1,0:T(8,128)} %wd_ref.3, ...), custom_call_target="tpu_custom_call" | custom-call | flops 14995500032 | tf_op jit(solution)/shard_map/mix/pallas_call | solution.py:421
  79.0 0.2 collective-permute-start.5
  79.2 1.7 %collective-permute-done.5.got_ref = bf16[2,640,128]{2,1,0:T(8,128)(2,1)S(1)} collective-permute-done((bf16[2,640,128]{2,1,0:T(8,128)(2,1)}, bf16[2,640,128]{2,1,0:T(8,128)(2,1)S(1)}, u32[]{:S(2)}, u32[]{:S(2)}) %collective-permute-start.5) | collective-permute-done | bytes 327712 | tf_op jit(solution)/shard_map/ppermute | solution.py:495
  80.9 1.0 copy-done.4
  81.9 0.8 core_sum.3
  82.7 0.0 all-to-all-done.1.a_ref
  82.7 6.7 %all-to-all-start.2 = ((bf16[16,80,128]{2,1,0:T(8,128)(2,1)}), bf16[16,80,128]{2,1,0:T(8,128)(2,1)S(1)}, u32[]{:S(2)}, u32[]{:S(2)}) async-start(bf16[16,80,128]{2,1,0:T(8,128)(2,1)} %bitcast.14), calls=%async_computation.2 | async-start | bytes 655360 | tf_op jit(solution)/shard_map/all_to_all | solution.py:573
  89.4 2.0 %collective-permute-start.6 = (f32[18,512]{1,0:T(8,128)S(1)}, f32[18,512]{1,0:T(8,128)S(1)}, u32[]{:S(2)}, u32[]{:S(2)}) collective-permute-start(f32[18,512]{1,0:T(8,128)S(1)} %copy-done.15), channel_id=1, source_target_pairs={{0,1},{1,2},{2,3},{3,4},{4,5},{5,6},{6,7},{7,0},{8,9},{9,10},{10,1... | collective-permute-start | bytes 110600 | tf_op jit(solution)/shard_map/ppermute | solution.py:635
  91.4 2.8 %collective-permute-start.7 = (f32[18,512]{1,0:T(8,128)S(1)}, f32[18,512]{1,0:T(8,128)S(1)}, u32[]{:S(2)}, u32[]{:S(2)}) collective-permute-start(f32[18,512]{1,0:T(8,128)S(1)} %copy-done.14), channel_id=1, source_target_pairs={{1,0},{2,1},{3,2},{4,3},{5,4},{6,5},{7,6},{0,7},{9,8},{10,9},{11,1... | collective-permute-start | bytes 110600 | tf_op jit(solution)/shard_map/ppermute | solution.py:636
  94.2 6.8 %collective-permute-done.6.refs_0_.left_ref = f32[18,512]{1,0:T(8,128)S(1)} collective-permute-done((f32[18,512]{1,0:T(8,128)S(1)}, f32[18,512]{1,0:T(8,128)S(1)}, u32[]{:S(2)}, u32[]{:S(2)}) %collective-permute-start.6) | collective-permute-done | bytes 36896 | tf_op jit(solution)/shard_map/ppermute | solution.py:635
  101.0 0.0 collective-permute-done.7.refs_1_.right_ref
  101.0 1.1 all-to-all-done.2.b_ref
  102.1 1.0 totals.1
  103.1 3.8 %all-to-all-start.3 = ((bf16[16,208,128]{2,1,0:T(8,128)(2,1)}), bf16[16,208,128]{2,1,0:T(8,128)(2,1)S(1)}, u32[]{:S(2)}, u32[]{:S(2)}) async-start(bf16[16,208,128]{2,1,0:T(8,128)(2,1)} %totals.1), calls=%async_computation.3 | async-start | bytes 1703936 | tf_op jit(solution)/shard_map/all_to_all | solution.py:573
  106.9 1.1 add_convert_fusion
  108.1 1.3 collective-permute-start.8
  109.4 1.3 collective-permute-start.9
  110.7 0.0 collective-permute-done.8.top_ref
  110.7 4.0 %collective-permute-done.9.bottom_ref = bf16[128,512]{1,0:T(8,128)(2,1)S(1)} collective-permute-done((bf16[128,512]{1,0:T(8,128)(2,1)S(1)}, bf16[128,512]{1,0:T(8,128)(2,1)S(1)}, u32[]{:S(2)}, u32[]{:S(2)}) %collective-permute-start.9) | collective-permute-done | bytes 131104 | tf_op jit(solution)/shard_map/ppermute | solution.py:647
  114.7 1.8 %copy-done.1 = bf16[2688,512]{1,0:T(8,128)(2,1)S(1)} copy-done((bf16[2688,512]{1,0:T(8,128)(2,1)S(1)}, bf16[2688,512]{1,0:T(8,128)(2,1)}, u32[]{:S(2)}) %copy-start.1) | copy-done | bytes 2752536
  116.5 1.6 %copy-done.5 = bf16[2048,512]{1,0:T(8,128)(2,1)S(1)} copy-done((bf16[2048,512]{1,0:T(8,128)(2,1)S(1)}, bf16[2048,512]{1,0:T(8,128)(2,1)}, u32[]{:S(2)}) %copy-start.5) | copy-done | bytes 2097176
  118.1 6.6 %latent.1 = bf16[2048,512]{1,0:T(8,128)(2,1)} custom-call(bf16[2048,512]{1,0:T(8,128)(2,1)S(1)} %copy-done.5, bf16[2688,512]{1,0:T(8,128)(2,1)S(1)} %copy-done.1, bf16[128,512]{1,0:T(8,128)(2,1)S(1)} %collective-permute-done.8.top_ref, bf16[128,512]{1,0:T(8,128)(2,1)S(1)} %collective-permute-done.9.bottom_ref, ...), custom_call_target="tpu_custom_call" | custom-call | flops 5767499776 | tf_op jit(solution)/shard_map/latent/pallas_call | solution.py:468
  124.6 3.4 %all-to-all-done.3.own_ref = bf16[16,208,128]{2,1,0:T(8,128)(2,1)S(1)} async-done(((bf16[16,208,128]{2,1,0:T(8,128)(2,1)}), bf16[16,208,128]{2,1,0:T(8,128)(2,1)S(1)}, u32[]{:S(2)}, u32[]{:S(2)}) %all-to-all-start.3) | async-done | bytes 852000 | tf_op jit(solution)/shard_map/all_to_all | solution.py:573
  128.0 0.4 collective-permute-start.10
  128.4 2.0 %collective-permute-done.10.sibling_ref = bf16[16,208,128]{2,1,0:T(8,128)(2,1)S(1)} collective-permute-done((bf16[16,208,128]{2,1,0:T(8,128)(2,1)S(1)}, bf16[16,208,128]{2,1,0:T(8,128)(2,1)S(1)}, u32[]{:S(2)}, u32[]{:S(2)}) %collective-permute-start.10) | collective-permute-done | bytes 852000 | tf_op jit(solution)/shard_map/ppermute | solution.py:653
  130.4 2.1 %unpack.1 = (f32[616,512]{1,0:T(8,128)}, f32[512,512]{1,0:T(8,128)}, f32[512,512]{1,0:T(8,128)}, f32[9,512]{1,0:T(8,128)}) custom-call(s32[1]{0:T(128)} %bitcast.ids_ref, bf16[16,208,128]{2,1,0:T(8,128)(2,1)S(1)} %all-to-all-done.3.own_ref, bf16[16,208,128]{2,1,0:T(8,128)(2,1)S(1)} %collective-permute-done.10.sibling_ref), custom_call_target="tpu_custom_call" | custom-call | flops 3460499968 | tf_op jit(solution)/shard_map/unpack/pallas_call | solution.py:545
  (23 shorter events, 0.1 us)
Async XLA Ops:
  1.7 10.9 %collective-permute-start = (bf16[16,512]{1,0:T(8,128)(2,1)S(1)}, bf16[16,512]{1,0:T(8,128)(2,1)S(1)}, u32[]{:S(2)}, u32[]{:S(2)}) collective-permute-start(bf16[16,512]{1,0:T(8,128)(2,1)S(1)} %bitcast.31), channel_id=1, source_target_pairs={{0,1},{1,2},{2,3},{3,4},{4,5},{5,6},{6,7},{7,0},{8,9},{9,10},{10,1... | collective-permute-start | bytes 49160 | tf_op jit(solution)/shard_map/ppermute | solution.py:588
  4.7 7.9 %collective-permute-start.1 = (bf16[16,512]{1,0:T(8,128)(2,1)S(1)}, bf16[16,512]{1,0:T(8,128)(2,1)S(1)}, u32[]{:S(2)}, u32[]{:S(2)}) collective-permute-start(bf16[16,512]{1,0:T(8,128)(2,1)S(1)} %bitcast.32), channel_id=1, source_target_pairs={{1,0},{2,1},{3,2},{4,3},{5,4},{6,5},{7,6},{0,7},{9,8},{10,9},{11,1... | collective-permute-start | bytes 49160 | tf_op jit(solution)/shard_map/ppermute | solution.py:589
  8.5 1.1 copy-start.2
  12.6 8.0 %copy-start = (bf16[512,512]{1,0:T(8,128)(2,1)S(1)}, bf16[512,512]{1,0:T(8,128)(2,1)}, u32[]{:S(2)}) copy-start(bf16[512,512]{1,0:T(8,128)(2,1)} %wo_hbm) | copy-start | bytes 1572868
  12.6 8.2 %copy-start.11 = (bf16[16,512]{1,0:T(8,128)(2,1)}, bf16[16,512]{1,0:T(8,128)(2,1)S(1)}, u32[]{:S(2)}) copy-start(bf16[16,512]{1,0:T(8,128)(2,1)S(1)} %collective-permute-done.west_ref) | copy-start | bytes 49156
  12.6 8.2 %copy-start.12 = (bf16[16,512]{1,0:T(8,128)(2,1)}, bf16[16,512]{1,0:T(8,128)(2,1)S(1)}, u32[]{:S(2)}) copy-start(bf16[16,512]{1,0:T(8,128)(2,1)S(1)} %collective-permute-done.1.east_ref) | copy-start | bytes 49156
  12.6 8.2 %copy-start.10 = (bf16[616,512]{1,0:T(8,128)(2,1)S(1)}, bf16[616,512]{1,0:T(8,128)(2,1)}, u32[]{:S(2)}) copy-start(bf16[616,512]{1,0:T(8,128)(2,1)} %param.11) | copy-start | bytes 1892356
  12.6 36.5 %all-to-all-start = ((bf16[32,32,640]{2,1,0:T(8,128)(2,1)}), bf16[32,32,640]{2,1,0:T(8,128)(2,1)S(1)}, u32[]{:S(2)}, u32[]{:S(2)}) async-start(bf16[32,32,640]{2,1,0:T(8,128)(2,1)} %bitcast.6), calls=%async_computation | async-start | bytes 2621440 | tf_op jit(solution)/shard_map/all_to_all | solution.py:596
  17.1 6.0 %collective-permute-start.2 = (bf16[144,512]{1,0:T(8,128)(2,1)S(1)}, bf16[144,512]{1,0:T(8,128)(2,1)S(1)}, u32[]{:S(2)}, u32[]{:S(2)}) collective-permute-start(bf16[144,512]{1,0:T(8,128)(2,1)S(1)} %get-tuple-element.82), channel_id=1, source_target_pairs={{0,8},{8,16},{16,24},{1,9},{9,17},{17,25},{2,10},{10,18},{18,26},{... | collective-permute-start | bytes 442376 | tf_op jit(solution)/shard_map/ppermute | solution.py:605
  19.3 4.5 %collective-permute-start.3 = (bf16[144,512]{1,0:T(8,128)(2,1)S(1)}, bf16[144,512]{1,0:T(8,128)(2,1)}, u32[]{:S(2)}, u32[]{:S(2)}) collective-permute-start(bf16[144,512]{1,0:T(8,128)(2,1)S(1)} %get-tuple-element.81), channel_id=1, source_target_pairs={{8,0},{16,8},{24,16},{9,1},{17,9},{25,17},{10,2},{18,10},{26,18},{... | collective-permute-start | bytes 442376 | tf_op jit(solution)/shard_map/ppermute | solution.py:606
  23.1 0.7 copy-start.13
  58.1 2.9 %copy-start.6 = (bf16[512,1024]{1,0:T(8,128)(2,1)}, bf16[512,1024]{1,0:T(8,128)(2,1)S(1)}, u32[]{:S(2)}) copy-start(bf16[512,1024]{1,0:T(8,128)(2,1)S(1)} %get-tuple-element.45.emb_hbm) | copy-start | bytes 3145732
  58.1 2.9 %copy-start.7 = (bf16[2,112,128]{2,1,0:T(8,128)(2,1)}, bf16[2,112,128]{2,1,0:T(8,128)(2,1)S(1)}, u32[]{:S(2)}) copy-start(bf16[2,112,128]{2,1,0:T(8,128)(2,1)S(1)} %get-tuple-element.43.mine_rest) | copy-start | bytes 172036
  58.1 2.9 %copy-start.8 = (bf16[2,112,128]{2,1,0:T(8,128)(2,1)}, bf16[2,112,128]{2,1,0:T(8,128)(2,1)S(1)}, u32[]{:S(2)}) copy-start(bf16[2,112,128]{2,1,0:T(8,128)(2,1)S(1)} %get-tuple-element.44.other_rest) | copy-start | bytes 172036
  58.2 2.9 %copy-start.9 = (s32[8,1024]{1,0:T(8,128)}, s32[8,1024]{1,0:T(8,128)S(1)}, u32[]{:S(2)}) copy-start(s32[8,1024]{1,0:T(8,128)S(1)} %get-tuple-element.42.cell_ref) | copy-start | bytes 98308
  58.2 2.0 %collective-permute-start.4 = (bf16[2,1024,128]{2,1,0:T(8,128)(2,1)S(1)}, bf16[2,1024,128]{2,1,0:T(8,128)(2,1)S(1)}, u32[]{:S(2)}, u32[]{:S(2)}) collective-permute-start(bf16[2,1024,128]{2,1,0:T(8,128)(2,1)S(1)} %get-tuple-element.49), channel_id=1, source_target_pairs={{0,8},{8,0},{1,9},{9,1},{2,10},{10,2},{3,11},{11,3},{4,12},{12,4},... | collective-permute-start | bytes 1572872 | tf_op jit(solution)/shard_map/ppermute | solution.py:495
  61.1 21.6 %all-to-all-start.1 = ((bf16[16,128,128]{2,1,0:T(8,128)(2,1)}), bf16[16,128,128]{2,1,0:T(8,128)(2,1)S(1)}, u32[]{:S(2)}, u32[]{:S(2)}) async-start(bf16[16,128,128]{2,1,0:T(8,128)(2,1)} %bitcast.13), calls=%async_computation.1 | async-start | bytes 1048576 | tf_op jit(solution)/shard_map/all_to_all | solution.py:573
  79.0 1.9 %collective-permute-start.5 = (bf16[2,640,128]{2,1,0:T(8,128)(2,1)}, bf16[2,640,128]{2,1,0:T(8,128)(2,1)S(1)}, u32[]{:S(2)}, u32[]{:S(2)}) collective-permute-start(bf16[2,640,128]{2,1,0:T(8,128)(2,1)} %get-tuple-element.51), channel_id=1, source_target_pairs={{0,8},{8,0},{1,9},{9,1},{2,10},{10,2},{3,11},{11,3},{4,12},{12,4},... | collective-permute-start | bytes 983048 | tf_op jit(solution)/shard_map/ppermute | solution.py:495
  80.9 1.0 copy-start.4
  81.9 7.5 %copy-start.15 = (f32[18,512]{1,0:T(8,128)S(1)}, f32[18,512]{1,0:T(8,128)}, u32[]{:S(2)}) copy-start(f32[18,512]{1,0:T(8,128)} %get-tuple-element.57) | copy-start | bytes 110596
  81.9 9.5 %copy-start.14 = (f32[18,512]{1,0:T(8,128)S(1)}, f32[18,512]{1,0:T(8,128)}, u32[]{:S(2)}) copy-start(f32[18,512]{1,0:T(8,128)} %get-tuple-element.58) | copy-start | bytes 110596
  82.7 19.4 %all-to-all-start.2 = ((bf16[16,80,128]{2,1,0:T(8,128)(2,1)}), bf16[16,80,128]{2,1,0:T(8,128)(2,1)S(1)}, u32[]{:S(2)}, u32[]{:S(2)}) async-start(bf16[16,80,128]{2,1,0:T(8,128)(2,1)} %bitcast.14), calls=%async_computation.2 | async-start | bytes 655360 | tf_op jit(solution)/shard_map/all_to_all | solution.py:573
  89.4 11.6 %collective-permute-start.6 = (f32[18,512]{1,0:T(8,128)S(1)}, f32[18,512]{1,0:T(8,128)S(1)}, u32[]{:S(2)}, u32[]{:S(2)}) collective-permute-start(f32[18,512]{1,0:T(8,128)S(1)} %copy-done.15), channel_id=1, source_target_pairs={{0,1},{1,2},{2,3},{3,4},{4,5},{5,6},{6,7},{7,0},{8,9},{9,10},{10,1... | collective-permute-start | bytes 110600 | tf_op jit(solution)/shard_map/ppermute | solution.py:635
  91.4 9.6 %collective-permute-start.7 = (f32[18,512]{1,0:T(8,128)S(1)}, f32[18,512]{1,0:T(8,128)S(1)}, u32[]{:S(2)}, u32[]{:S(2)}) collective-permute-start(f32[18,512]{1,0:T(8,128)S(1)} %copy-done.14), channel_id=1, source_target_pairs={{1,0},{2,1},{3,2},{4,3},{5,4},{6,5},{7,6},{0,7},{9,8},{10,9},{11,1... | collective-permute-start | bytes 110600 | tf_op jit(solution)/shard_map/ppermute | solution.py:636
  103.1 11.6 %copy-start.3 = (bf16[512,512]{1,0:T(8,128)(2,1)S(1)}, bf16[512,512]{1,0:T(8,128)(2,1)}, u32[]{:S(2)}) copy-start(bf16[512,512]{1,0:T(8,128)(2,1)} %wp_ref.3) | copy-start | bytes 1572868
  103.1 24.9 %all-to-all-start.3 = ((bf16[16,208,128]{2,1,0:T(8,128)(2,1)}), bf16[16,208,128]{2,1,0:T(8,128)(2,1)S(1)}, u32[]{:S(2)}, u32[]{:S(2)}) async-start(bf16[16,208,128]{2,1,0:T(8,128)(2,1)} %totals.1), calls=%async_computation.3 | async-start | bytes 1703936 | tf_op jit(solution)/shard_map/all_to_all | solution.py:573
  108.1 2.6 %collective-permute-start.8 = (bf16[128,512]{1,0:T(8,128)(2,1)S(1)}, bf16[128,512]{1,0:T(8,128)(2,1)S(1)}, u32[]{:S(2)}, u32[]{:S(2)}) collective-permute-start(bf16[128,512]{1,0:T(8,128)(2,1)S(1)} %get-tuple-element.68), channel_id=1, source_target_pairs={{0,8},{8,16},{16,24},{1,9},{9,17},{17,25},{2,10},{10,18},{18,26},{... | collective-permute-start | bytes 393224 | tf_op jit(solution)/shard_map/ppermute | solution.py:646
  109.4 5.3 %collective-permute-start.9 = (bf16[128,512]{1,0:T(8,128)(2,1)S(1)}, bf16[128,512]{1,0:T(8,128)(2,1)S(1)}, u32[]{:S(2)}, u32[]{:S(2)}) collective-permute-start(bf16[128,512]{1,0:T(8,128)(2,1)S(1)} %get-tuple-element.67), channel_id=1, source_target_pairs={{8,0},{16,8},{24,16},{9,1},{17,9},{25,17},{10,2},{18,10},{26,18},{... | collective-permute-start | bytes 393224 | tf_op jit(solution)/shard_map/ppermute | solution.py:647
  114.7 1.8 %copy-start.1 = (bf16[2688,512]{1,0:T(8,128)(2,1)S(1)}, bf16[2688,512]{1,0:T(8,128)(2,1)}, u32[]{:S(2)}) copy-start(bf16[2688,512]{1,0:T(8,128)(2,1)} %get-tuple-element.60.mix_ref) | copy-start | bytes 8257540
  116.5 1.6 %copy-start.5 = (bf16[2048,512]{1,0:T(8,128)(2,1)S(1)}, bf16[2048,512]{1,0:T(8,128)(2,1)}, u32[]{:S(2)}) copy-start(bf16[2048,512]{1,0:T(8,128)(2,1)} %get-tuple-element.59.grid_ref) | copy-start | bytes 6291460
  128.0 2.4 %collective-permute-start.10 = (bf16[16,208,128]{2,1,0:T(8,128)(2,1)S(1)}, bf16[16,208,128]{2,1,0:T(8,128)(2,1)S(1)}, u32[]{:S(2)}, u32[]{:S(2)}) collective-permute-start(bf16[16,208,128]{2,1,0:T(8,128)(2,1)S(1)} %all-to-all-done.3.own_ref), channel_id=1, source_target_pairs={{0,8},{8,0},{1,9},{9,1},{2,10},{10,2},{3,11},{11,3},{4,12},{12,4},... | collective-permute-start | bytes 2555912 | tf_op jit(solution)/shard_map/ppermute | solution.py:653

commit v8 on v7

--- a/solution.py
+++ b/solution.py
@@ -226,22 +226,20 @@
     return loads
 
 
-def encode_kernel(
-    spec, clon, ids_ref, rows_ref, wit_hbm, wot_hbm, gg_hbm, wo_hbm,
-    emb_hbm, cell_ref, mine_ref, other_ref, mine_rest, other_rest,
-    wit_ref, wot_ref, gg_ref, wo_ref, emb_ref, gi, gi_out, go, sems,
+def owner_kernel(
+    spec, clat, clon, wide, core_ref, rows_ref, wd_ref, wit_hbm, wot_hbm, gg_hbm, wo_hbm, gm_hbm, cott_hbm,
+    mine_ref, other_ref, east_out, west_out, grid_hbm, mix_hbm,
+    wit_ref, wot_ref, gg_ref, wo_ref, gm_ref, cott_ref,
+    emb_ref, gi, gi_out, go, wide_ref, grid_ref, mix_ref, east_ref, west_ref, gp, gd, sems,
 ):
     loads = start_loads((wit_hbm, wot_hbm, gg_hbm, wo_hbm), (wit_ref, wot_ref, gg_ref, wo_ref), sems)
-    core = ids_ref[0]
+    put_grid = pltpu.make_async_copy(grid_ref, grid_hbm, sems.at[6])
+    put_mix = pltpu.make_async_copy(mix_ref, mix_hbm, sems.at[7])
+    core = core_ref[0]
     slots, spec_wide = rows_ref.shape
     cells, width = gg_ref.shape
+    blocks = width // LANES
     step = min(512, slots)
-    put_emb = pltpu.make_async_copy(emb_ref, emb_hbm, sems.at[len(loads)])
-    last = rows_ref[:, spec_wide - LANES :]
-    col = spec - (spec_wide - LANES)
-    lane = lax.broadcasted_iota(i32, (16, LANES), 1)
-    pick = jnp.where(lane == col, float(clon), jnp.where(lane == col + 1, 1.0, 0.0)).astype(bf16)
-    cell_ref[...] = dot(pick, last, (1, 1))[0:8, :].astype(i32)
 
     for t in range(slots // step):
         at = slice(t * step, (t + 1) * step)
@@ -257,14 +255,13 @@
         if t == 0:
             loads[1].wait()
         emb_ref[:, at] = dot(wot_ref[...], hidden).astype(bf16)
-        if t == slots // step - 1:
-            put_emb.start()
         if t == 0:
             loads[2].wait()
         g_emb = dot(hits, gg_ref[...]).astype(bf16)
         g_out = dot(hidden, g_emb)
         if t == 0:
             loads[3].wait()
+            late = start_loads((gm_hbm, cott_hbm), (gm_ref, cott_ref), sems.at[pl.ds(4, 2)])
         g_hid = dot(wo_ref[...], g_emb, (1, 1))
         g_pre = (g_hid * (sig * (1.0 + preact * (1.0 - sig)))).astype(bf16)
         g_in = dot(g_pre, rows)
@@ -275,60 +272,11 @@
             go[...] += g_out
             gi[...] += g_in
 
-    gi_out[...] = gi[...].T
-    head = spec_wide - LANES
-    write_halves(core, go, 0, mine_ref, other_ref)
-    write_halves(core, gi_out, width, mine_ref, other_ref, 0, head)
-    write_halves(core, gi_out, 0, mine_rest, other_rest, head, mine_rest.shape[1])
-    clear_tail(width + head, mine_ref, other_ref)
-    put_emb.wait()
-
-
-def encode(ids, rows, weights, spec, clon, out_rows, rest_rows):
-    slots, spec_wide = rows.shape
-    width = weights[-1].shape[0]
-    half = jax.ShapeDtypeStruct((width // LANES // 2, out_rows, LANES), bf16)
-    rest = jax.ShapeDtypeStruct((width // LANES // 2, rest_rows, LANES), bf16)
-    return pl.pallas_call(
-        functools.partial(encode_kernel, spec, clon),
-        out_shape=(
-            jax.ShapeDtypeStruct((width, slots), bf16),
-            jax.ShapeDtypeStruct((8, slots), i32),
-            half,
-            half,
-            rest,
-            rest,
-        ),
-        in_specs=[smem(), vmem()] + [anywhere()] * len(weights),
-        out_specs=(anywhere(),) + (vmem(),) * 5,
-        scratch_shapes=[pltpu.VMEM(x.shape, x.dtype) for x in weights]
-        + [
-            pltpu.VMEM((width, slots), bf16),
-            pltpu.VMEM((width, spec_wide), f32),
-            pltpu.VMEM((spec_wide, width), f32),
-            pltpu.VMEM((width, width), f32),
-            pltpu.SemaphoreType.DMA((len(weights) + 1,)),
-        ],
-        compiler_params=params(48),
-        cost_estimate=cost(10),
-        name="encode",
-    )(ids, rows, *weights)
-
-
-def mix_kernel(
-    clat, clon, wide, ids_ref, cell_ref, wd_ref, mine_rest, other_rest,
-    emb_hbm, gm_hbm, cott_hbm, after_ref,
-    mine_ref, other_ref, east_out, west_out, grid_hbm, mix_hbm,
-    emb_ref, gm_ref, cott_ref, wide_ref, grid_ref, mix_ref, east_ref, west_ref, gp, gd, sems,
-):
-    loads = start_loads((emb_hbm, gm_hbm, cott_hbm), (emb_ref, gm_ref, cott_ref), sems)
-    put_grid = pltpu.make_async_copy(grid_ref, grid_hbm, sems.at[3])
-    put_mix = pltpu.make_async_copy(mix_ref, mix_hbm, sems.at[4])
-    core = ids_ref[0]
-    width = emb_ref.shape[0]
-    blocks = width // LANES
-
-    cell = cell_ref[0:1, :]
+    last = rows_ref[:, spec_wide - LANES :]
+    col = spec - (spec_wide - LANES)
+    lane = lax.broadcasted_iota(i32, (16, LANES), 1)
+    pick = jnp.where(lane == col, float(clon), jnp.where(lane == col + 1, 1.0, 0.0)).astype(bf16)
+    cell = dot(pick, last, (1, 1))[0:1, :].astype(i32)
     lines = 4
     place = lax.broadcasted_iota(i32, (wide, 1), 0)
     column = column_of(place, clon // GROUPS) - 1
@@ -341,7 +289,6 @@
     gd[...] = jnp.zeros_like(gd)
     used = (clat + 2) * wide
     mix_ref[used:, :] = jnp.zeros((mix_ref.shape[0] - used, width), bf16)
-    loads[0].wait()
 
     def bins(t, carry):
         hits = (cell == wanted + t * (lines * clon)).astype(f32).astype(bf16)
@@ -356,7 +303,7 @@
 
     lax.fori_loop(0, clat // lines, bins, 0)
     put_grid.start()
-    loads[1].wait()
+    late[0].wait()
     group = lax.broadcasted_iota(i32, (GROUPS, LANES), 0)
 
     def conv(e, carry):
@@ -396,35 +343,40 @@
 
     lax.fori_loop(0, clat + 2, conv, 0)
     put_mix.start()
-    loads[2].wait()
+    late[1].wait()
     gp[...] = dot(cott_ref[...], mix_ref[...]).T
+    gi_out[...] = gi[...].T
     east_out[...] = east_ref[:, GROUPS - 1, :]
     west_out[...] = west_ref[:, 0, :]
     taps = [jnp.sum(gd[8 * k : 8 * k + 8, :], axis=0, keepdims=True) for k in range(9)]
     gd[0:16, :] = jnp.concatenate(taps + [jnp.zeros((7, width), f32)], axis=0)
-    rest = mine_rest.shape[1]
-    write_halves(core, gp, 0, mine_ref, other_ref)
-    mine_ref[:, width : width + rest, :] = mine_rest[...]
-    other_ref[:, width : width + rest, :] = other_rest[...]
-    write_halves(core, gd, width + rest, mine_ref, other_ref, 0, 16)
-    clear_tail(width + rest + 16, mine_ref, other_ref)
+    start = 0
+    for total, size in ((go, width), (gi_out, round_up(spec, 16)), (gp, width), (gd, 16)):
+        write_halves(core, total, start, mine_ref, other_ref, 0, size)
+        start += size
+    clear_tail(start, mine_ref, other_ref)
     put_grid.wait()
     put_mix.wait()
 
 
-def mix(ids, cell, w_depth, rest, emb, g_mixed, cot_t, after, clat, clon, wide, out_rows):
+def owner_part(core, rows, w_depth, operands, spec, clat, clon, wide, out_rows):
+    slots, spec_wide = rows.shape
     width = w_depth.shape[1]
     half = jax.ShapeDtypeStruct((width // LANES // 2, out_rows, LANES), bf16)
     column = jax.ShapeDtypeStruct((clat + 2, width), f32)
     grid = jax.ShapeDtypeStruct((clat * clon, width), bf16)
-    ext = jax.ShapeDtypeStruct(cot_t.shape[::-1], bf16)
+    ext = jax.ShapeDtypeStruct(operands[-1].shape[::-1], bf16)
     return pl.pallas_call(
-        functools.partial(mix_kernel, clat, clon, wide),
+        functools.partial(owner_kernel, spec, clat, clon, wide),
         out_shape=(half, half, column, column, grid, ext),
-        in_specs=[smem()] + [vmem()] * 4 + [anywhere()] * 4,
+        in_specs=[smem()] + [vmem()] * 2 + [anywhere()] * len(operands),
         out_specs=(vmem(),) * 4 + (anywhere(),) * 2,
-        scratch_shapes=[pltpu.VMEM(x.shape, x.dtype) for x in (emb, g_mixed, cot_t)]
+        scratch_shapes=[pltpu.VMEM(x.shape, x.dtype) for x in operands]
         + [
+            pltpu.VMEM((width, slots), bf16),
+            pltpu.VMEM((width, spec_wide), f32),
+            pltpu.VMEM((spec_wide, width), f32),
+            pltpu.VMEM((width, width), f32),
             pltpu.VMEM((width // LANES, clat + 4, wide, LANES), f32),
             pltpu.VMEM(grid.shape, bf16),
             pltpu.VMEM(ext.shape, bf16),
@@ -432,12 +384,12 @@
             pltpu.VMEM((clat + 2, GROUPS, width), f32),
             pltpu.VMEM((width, width), f32),
             pltpu.VMEM((72, width), f32),
-            pltpu.SemaphoreType.DMA((5,)),
+            pltpu.SemaphoreType.DMA((8,)),
         ],
-        compiler_params=params(56),
-        cost_estimate=cost(13),
-        name="mix",
-    )(ids, cell, w_depth, *rest, emb, g_mixed, cot_t, after)
+        compiler_params=params(48),
+        cost_estimate=cost(21),
+        name="owner",
+    )(core, rows, w_depth, *operands)
 
 
 def latent_kernel(
@@ -495,55 +447,49 @@
     )(mine, lax.ppermute(other, "core", SWAP))
 
 
-def totals_kernel(a_ref, b_ref, *refs):
+def totals_kernel(parts_ref, *refs):
     out_ref = refs[-1]
-    start = 0
-    for ref in (a_ref, b_ref):
-        size = ref.shape[1]
-        total = jnp.sum(ref[...].astype(f32), axis=0).astype(bf16)
-        out_ref[:, start : start + size, :] = jnp.broadcast_to(total[None], ref.shape)
-        start += size
-
-
-def totals(parts_a, parts_b, *after):
-    chips, rows_a, _ = parts_a.shape
+    total = jnp.sum(parts_ref[...].astype(f32), axis=0).astype(bf16)
+    out_ref[...] = jnp.broadcast_to(total[None], parts_ref.shape)
+
+
+def totals(parts, *after):
     return pl.pallas_call(
         totals_kernel,
-        out_shape=jax.ShapeDtypeStruct((chips, rows_a + parts_b.shape[1], LANES), bf16),
-        in_specs=[vmem()] * 2 + [anywhere()] * len(after),
+        out_shape=jax.ShapeDtypeStruct(parts.shape, bf16),
+        in_specs=[vmem()] + [anywhere()] * len(after),
         out_specs=vmem(),
         compiler_params=params(8),
         cost_estimate=cost(1),
         name="totals",
-    )(parts_a, parts_b, *after)
+    )(parts, *after)
 
 
 def unpack_kernel(
-    rows_a, rest, obs_scale, cell_scale, ids_ref, own_ref, sibling_ref, gi_ref, go_ref, gp_ref, gd_ref
+    obs_scale, cell_scale, core_ref, own_ref, sibling_ref, gi_ref, go_ref, gp_ref, gd_ref
 ):
-    spec, width = gi_ref.shape
+    width = gi_ref.shape[1]
     chips = own_ref.shape[0]
     count = width // (2 * LANES)
     per = chips // count
-    core = ids_ref[0]
-    cut = rows_a // per
-    head = spec - spec % LANES
+    core = core_ref[0]
     for ref, half in ((own_ref, core), (sibling_ref, 1 - core)):
         for n in range(count):
             cols = pl.ds(pl.multiple_of((half * count + n) * LANES, LANES), LANES)
             block = ref[n * per : (n + 1) * per].astype(f32)
-            a = block[:, :cut].reshape(rows_a, LANES)
-            b = block[:, cut:].reshape(per * (block.shape[1] - cut), LANES)
-            go_ref[:, cols] = a[:width] * obs_scale
-            gi_ref[:head, cols] = a[width : width + head] * obs_scale
-            gp_ref[:, cols] = b[:width] * cell_scale
-            gi_ref[head:, cols] = b[width : width + spec - head] * obs_scale
-            gd_ref[:, cols] = b[width + rest : width + rest + gd_ref.shape[0]] * cell_scale
-
-
-def unpack(ids, own, sibling, spec, width, rows_a, rest, obs_scale, cell_scale):
+            block = block.reshape(per * block.shape[1], LANES)
+            start = 0
+            for out_ref, scale in (
+                (go_ref, obs_scale), (gi_ref, obs_scale), (gp_ref, cell_scale), (gd_ref, cell_scale)
+            ):
+                size = out_ref.shape[0]
+                out_ref[:, cols] = block[start : start + size] * scale
+                start += round_up(size, 16)
+
+
+def unpack(core, own, sibling, spec, width, obs_scale, cell_scale):
     return pl.pallas_call(
-        functools.partial(unpack_kernel, rows_a, rest, obs_scale, cell_scale),
+        functools.partial(unpack_kernel, obs_scale, cell_scale),
         out_shape=tuple(
             jax.ShapeDtypeStruct((rows, width), f32) for rows in (spec, width, width, 9)
         ),
@@ -552,7 +498,7 @@
         compiler_params=params(8),
         cost_estimate=cost(3),
         name="unpack",
-    )(ids, own, sibling)
+    )(core, own, sibling)
 
 
 def neighbours(axes, periodic):
@@ -581,7 +527,7 @@
     cells = clat * clon
     wide = clon + 16
     spec_wide = round_up(spec + 2, LANES)
-    ids = lax.axis_index("core").reshape(1)
+    core = lax.axis_index("core").reshape(1)
     east_way, west_way = neighbours("lon", True)
     south_way, north_way = neighbours(LAT, False)
 
@@ -611,30 +557,18 @@
     )
     w_in_t = jnp.pad(w_in.T, ((0, 0), (0, spec_wide - spec)))
 
-    align = 16 * tiles * LANES // width
-    head = spec - spec % LANES
-    rest = round_up(spec - head, 16)
-    rows_a = round_up(width + head, align)
-    rows_b = round_up(width + rest + 16, align)
-    emb, cells_got, mine, other, *rest_halves = encode(
-        ids, arrived, (w_in_t, w_out.T, g_grid, w_out), spec, clon, rows_a, rest
+    out_rows = round_up(2 * width + round_up(spec, 16) + 16, 16 * tiles * LANES // width)
+    operands = w_in_t, w_out.T, g_grid, w_out, g_mixed, cot_t
+    mine, other, east, west, grid, mix_ext = owner_part(
+        core, arrived, w_depth, operands, spec, clat, clon, wide, out_rows
     )
-    sum_a = core_sum(mine, other)
-    parts_a = spread(sum_a)
-
-    mine, other, east, west, grid, mix_ext = mix(
-        ids, cells_got, w_depth, rest_halves, emb, g_mixed, cot_t, sum_a,
-        clat, clon, wide, rows_b,
-    )
-    sum_b = core_sum(mine, other)
-    sum_b, parts_a, east, west, mix_ext = lax.optimization_barrier(
-        (sum_b, parts_a, east, west, mix_ext)
-    )
-    parts_b = spread(sum_b)
+    summed = core_sum(mine, other)
+    summed, east, west, mix_ext = lax.optimization_barrier((summed, east, west, mix_ext))
+    parts = spread(summed)
 
     left = lax.ppermute(east, "lon", east_way)
     right = lax.ppermute(west, "lon", west_way)
-    sent = totals(parts_a, parts_b, left, right)
+    sent = totals(parts, left, right)
     full = spread(sent)
     line = lax.broadcasted_iota(i32, (clon, width), 0)
 
@@ -652,7 +586,7 @@
     full, latent = lax.optimization_barrier((full, latent))
     sibling = lax.ppermute(full, "core", SWAP)
     grad_in, grad_out, grad_point, grad_depth = unpack(
-        ids, full, sibling, spec, width, rows_a, rest, obs_scale, cell_scale
+        core, full, sibling, spec, width, obs_scale, cell_scale
     )
     return latent.reshape(clat, clon, width), grad_in, grad_out, grad_point, grad_depth
 

time: 133 us -> 131 us (0.985)
  waiting for transfers between devices: 31.1 us -> 40.4 us
  starting transfers between devices: 35.1 us -> 28.8 us
  Pallas kernels: 53.4 us -> 49.1 us
    ppermute x1, waiting for transfers between devices: 6.79 us -> 15.4 us  [on_device(): left = lax.ppermute(east, 'lon', east_way)]
    all_to_all x3 -> x2, starting transfers between devices: 14.2 us -> 7.38 us  [spread(): lax.all_to_all(values, CHIPS, split_axis=0, concat_axis=0, tiled=True)]
    pallas_call x4 -> x3, Pallas kernels: 26.3 us -> 22.6 us  [the longest x1 19.5 us: owner_part(): pl.pallas_call(functools.partial(owner_kernel, spec, clat, clon, wide), o...]
    all_to_all x3 -> x2, waiting for transfers between devices: 4.45 us -> 7.06 us  [spread(): lax.all_to_all(values, CHIPS, split_axis=0, concat_axis=0, tiled=True)]
    ppermute x2 -> x1, waiting for transfers between devices: 3.6 us -> 2.37 us  [core_sum(): lax.ppermute(other, 'core', SWAP)]
    unnamed x34 -> x20, local copies, waits for them, and re-layouts: 5.49 us -> 4.48 us
  transfers between devices with their start and end apart: 15 -> 13, of which waited for: 9 -> 8; matrix products, arithmetic and copies ran while one was open for 4% -> 4% of each run, Pallas kernels for 30% -> 19%
where the time goes in v8:
time: 131 us; the launch traced here: 130 us
  Pallas kernels  49.1 us (37%)
  waiting for transfers between devices  40.4 us (31%)
  starting transfers between devices  28.8 us (22%)
  local copies, waits for them, and re-layouts  9.04 us (7%)
  other arithmetic  1.96 us (1%)
    pallas_call x1, Pallas kernels, owner_part(): pl.pallas_call(functools.partial(owner_kernel, spec, clat, clon, wide), o...  19.5 us
    pallas_call x1, Pallas kernels, grid_grad(): pl.pallas_call(functools.partial(grid_grad_kernel, clat, clon, wide), out...  15.7 us
    ppermute x1, waiting for transfers between devices, on_device(): left = lax.ppermute(east, 'lon', east_way)  15.4 us
    all_to_all x1, waiting for transfers between devices, on_device(): lax.all_to_all(outgoing.reshape(tiles, cap, spec_wide), ('x', 'core', 'lo...  9.53 us
    all_to_all x2, starting transfers between devices, spread(): lax.all_to_all(values, CHIPS, split_axis=0, concat_axis=0, tiled=True)  7.38 us
    all_to_all x2, waiting for transfers between devices, spread(): lax.all_to_all(values, CHIPS, split_axis=0, concat_axis=0, tiled=True)  7.06 us
    pallas_call x1, Pallas kernels, finish_latent(): pl.pallas_call(functools.partial(latent_kernel, clat, clon, wide), out_sh...  6.58 us
    unnamed x20, local copies, waits for them, and re-layouts  4.48 us
  transfers between devices with their start and end apart: 13, of which 8 were waited for; matrix products, arithmetic and copies ran while one was open for 4% of the time, Pallas kernels for 19%

profile of v8, /device:TPU:0, one launch (start us, length us, event | category | flops | bytes accessed | tf_op | source)
XLA Modules:
  0.0 130.1 jit_solution(18338727179101337913)
XLA Ops:
  0.6 1.0 fusion
  1.7 3.0 %collective-permute-start = (bf16[16,512]{1,0:T(8,128)(2,1)S(1)}, bf16[16,512]{1,0:T(8,128)(2,1)S(1)}, u32[]{:S(2)}, u32[]{:S(2)}) collective-permute-start(bf16[16,512]{1,0:T(8,128)(2,1)S(1)} %bitcast.30), channel_id=1, source_target_pairs={{0,1},{1,2},{2,3},{3,4},{4,5},{5,6},{6,7},{7,0},{8,9},{9,10},{10,1... | collective-permute-start | bytes 49160 | tf_op jit(solution)/shard_map/ppermute | solution.py:534
  4.7 3.1 %collective-permute-start.1 = (bf16[16,512]{1,0:T(8,128)(2,1)S(1)}, bf16[16,512]{1,0:T(8,128)(2,1)S(1)}, u32[]{:S(2)}, u32[]{:S(2)}) collective-permute-start(bf16[16,512]{1,0:T(8,128)(2,1)S(1)} %bitcast.31), channel_id=1, source_target_pairs={{1,0},{2,1},{3,2},{4,3},{5,4},{6,5},{7,6},{0,7},{9,8},{10,9},{11,1... | collective-permute-start | bytes 49160 | tf_op jit(solution)/shard_map/ppermute | solution.py:535
  7.8 0.7 pad_add_fusion.places_ref
  8.5 0.0 copy-start.2
  8.5 1.1 copy-done.2
  9.6 3.0 %route.1 = bf16[1024,640]{1,0:T(8,128)(2,1)} custom-call(s32[2,512]{1,0:T(2,128)S(1)} %pad_add_fusion.places_ref, bf16[616,512]{1,0:T(8,128)(2,1)S(1)} %bitcast.27), custom_call_target="tpu_custom_call" | custom-call | flops 3460499968 | tf_op jit(solution)/shard_map/route/pallas_call | solution.py:77
  12.6 0.0 copy-start
  12.6 0.0 collective-permute-done.west_ref
  12.6 0.0 copy-start.7
  12.6 0.0 collective-permute-done.1.east_ref
  12.6 0.0 copy-start.8
  12.6 0.0 copy-start.6
  12.6 3.2 %all-to-all-start = ((bf16[32,32,640]{2,1,0:T(8,128)(2,1)}), bf16[32,32,640]{2,1,0:T(8,128)(2,1)S(1)}, u32[]{:S(2)}, u32[]{:S(2)}) async-start(bf16[32,32,640]{2,1,0:T(8,128)(2,1)} %bitcast.6), calls=%async_computation | async-start | bytes 2621440 | tf_op jit(solution)/shard_map/all_to_all | solution.py:542
  15.9 0.1 pad.11.clone
  16.0 1.0 slice_bitcast_fusion
  17.0 0.1 pad_maximum_fusion.1
  17.1 2.8 %collective-permute-start.2 = (bf16[144,512]{1,0:T(8,128)(2,1)S(1)}, bf16[144,512]{1,0:T(8,128)(2,1)}, u32[]{:S(2)}, u32[]{:S(2)}) collective-permute-start(bf16[144,512]{1,0:T(8,128)(2,1)S(1)} %get-tuple-element.68), channel_id=1, source_target_pairs={{0,8},{8,16},{16,24},{1,9},{9,17},{17,25},{2,10},{10,18},{18,26},{... | collective-permute-start | bytes 442376 | tf_op jit(solution)/shard_map/ppermute | solution.py:551
  19.9 1.3 collective-permute-start.3
  21.2 0.0 copy-done
  21.2 0.2 copy.16
  21.4 0.0 copy-done.7
  21.5 0.0 copy-done.8
  21.5 0.0 copy-done.6
  21.5 1.1 copy.15
  22.6 1.1 pad.4.wit_hbm
  23.7 0.0 collective-permute-done.2.north_ref
  23.7 0.1 collective-permute-done.3.south_ref
  23.8 0.0 copy-start.4
  23.8 15.7 %grid_grad.1 = (bf16[512,2688]{1,0:T(8,128)(2,1)}, f32[4,18,144,128]{3,2,1,0:T(8,128)}, bf16[2048,512]{1,0:T(8,128)(2,1)}) custom-call(bf16[2048,512]{1,0:T(8,128)(2,1)} %bitcast.29, bf16[16,512]{1,0:T(8,128)(2,1)} %copy-done.8, bf16[16,512]{1,0:T(8,128)(2,1)} %copy-done.7, bf16[144,512]{1,0:T(8,128)(2,1)} %collective-permute-done.2.north_ref, ...), custom_call_target="tpu_custom_call" | custom-call | flops 11534999552 | tf_op jit(solution)/shard_map/grid_grad/pallas_call | solution.py:188
  39.6 9.5 %all-to-all-done = bf16[32,32,640]{2,1,0:T(8,128)(2,1)S(1)} async-done(((bf16[32,32,640]{2,1,0:T(8,128)(2,1)}), bf16[32,32,640]{2,1,0:T(8,128)(2,1)S(1)}, u32[]{:S(2)}, u32[]{:S(2)}) %all-to-all-start) | async-done | bytes 1310752 | tf_op jit(solution)/shard_map/all_to_all | solution.py:542
  49.1 0.0 copy-done.4
  49.1 19.5 %owner.1 = (bf16[2,1664,128]{2,1,0:T(8,128)(2,1)S(1)}, bf16[2,1664,128]{2,1,0:T(8,128)(2,1)S(1)}, f32[18,512]{1,0:T(8,128)S(1)}, f32[18,512]{1,0:T(8,128)S(1)}, ...) custom-call(s32[1]{0:T(128)} %bitcast.core_ref, bf16[1024,640]{1,0:T(8,128)(2,1)S(1)} %bitcast.25, ...), custom_call_target="tpu_custom_call" | custom-call | flops 24223500288 | tf_op jit(solution)/shard_map/owner/pallas_call | solution.py:369
  68.6 0.1 collective-permute-start.4
  68.7 2.4 %collective-permute-done.4.got_ref = bf16[2,1664,128]{2,1,0:T(8,128)(2,1)S(1)} collective-permute-done((bf16[2,1664,128]{2,1,0:T(8,128)(2,1)S(1)}, bf16[2,1664,128]{2,1,0:T(8,128)(2,1)S(1)}, u32[]{:S(2)}, u32[]{:S(2)}) %collective-permute-start.4) | collective-permute-done | bytes 852000 | tf_op jit(solution)/shard_map/ppermute | solution.py:447
  71.1 1.1 core_sum.1
  72.2 3.6 %all-to-all-start.1 = ((bf16[16,208,128]{2,1,0:T(8,128)(2,1)}), bf16[16,208,128]{2,1,0:T(8,128)(2,1)S(1)}, u32[]{:S(2)}, u32[]{:S(2)}) async-start(bf16[16,208,128]{2,1,0:T(8,128)(2,1)} %bitcast.13), calls=%async_computation.1 | async-start | bytes 1703936 | tf_op jit(solution)/shard_map/all_to_all | solution.py:519
  75.8 1.8 %collective-permute-start.5 = (f32[18,512]{1,0:T(8,128)S(1)}, f32[18,512]{1,0:T(8,128)S(1)}, u32[]{:S(2)}, u32[]{:S(2)}) collective-permute-start(f32[18,512]{1,0:T(8,128)S(1)} %get-tuple-element.43), channel_id=1, source_target_pairs={{0,1},{1,2},{2,3},{3,4},{4,5},{5,6},{6,7},{7,0},{8,9},{9,10},{10,1... | collective-permute-start | bytes 110600 | tf_op jit(solution)/shard_map/ppermute | solution.py:569
  77.6 3.0 %collective-permute-start.6 = (f32[18,512]{1,0:T(8,128)S(1)}, f32[18,512]{1,0:T(8,128)S(1)}, u32[]{:S(2)}, u32[]{:S(2)}) collective-permute-start(f32[18,512]{1,0:T(8,128)S(1)} %get-tuple-element.44), channel_id=1, source_target_pairs={{1,0},{2,1},{3,2},{4,3},{5,4},{6,5},{7,6},{0,7},{9,8},{10,9},{11,1... | collective-permute-start | bytes 110600 | tf_op jit(solution)/shard_map/ppermute | solution.py:570
  80.6 15.4 %collective-permute-done.5.refs_0_.left_ref = f32[18,512]{1,0:T(8,128)S(1)} collective-permute-done((f32[18,512]{1,0:T(8,128)S(1)}, f32[18,512]{1,0:T(8,128)S(1)}, u32[]{:S(2)}, u32[]{:S(2)}) %collective-permute-start.5) | collective-permute-done | bytes 36896 | tf_op jit(solution)/shard_map/ppermute | solution.py:569
  96.0 0.0 collective-permute-done.6.refs_1_.right_ref
  96.0 3.1 %all-to-all-done.1.parts_ref = bf16[16,208,128]{2,1,0:T(8,128)(2,1)S(1)} async-done(((bf16[16,208,128]{2,1,0:T(8,128)(2,1)}), bf16[16,208,128]{2,1,0:T(8,128)(2,1)S(1)}, u32[]{:S(2)}, u32[]{:S(2)}) %all-to-all-start.1) | async-done | bytes 852000 | tf_op jit(solution)/shard_map/all_to_all | solution.py:519
  99.1 1.0 totals.1
  100.1 0.0 copy-start.3
  100.1 3.8 %all-to-all-start.2 = ((bf16[16,208,128]{2,1,0:T(8,128)(2,1)}), bf16[16,208,128]{2,1,0:T(8,128)(2,1)S(1)}, u32[]{:S(2)}, u32[]{:S(2)}) async-start(bf16[16,208,128]{2,1,0:T(8,128)(2,1)} %totals.1), calls=%async_computation.2 | async-start | bytes 1703936 | tf_op jit(solution)/shard_map/all_to_all | solution.py:519
  103.9 1.1 add_convert_fusion
  105.0 1.5 %collective-permute-start.7 = (bf16[128,512]{1,0:T(8,128)(2,1)S(1)}, bf16[128,512]{1,0:T(8,128)(2,1)S(1)}, u32[]{:S(2)}, u32[]{:S(2)}) collective-permute-start(bf16[128,512]{1,0:T(8,128)(2,1)S(1)} %get-tuple-element.54), channel_id=1, source_target_pairs={{0,8},{8,16},{16,24},{1,9},{9,17},{17,25},{2,10},{10,18},{18,26},{... | collective-permute-start | bytes 393224 | tf_op jit(solution)/shard_map/ppermute | solution.py:580
  106.5 1.3 collective-permute-start.8
  107.8 0.0 collective-permute-done.7.top_ref
  107.8 3.8 %collective-permute-done.8.bottom_ref = bf16[128,512]{1,0:T(8,128)(2,1)S(1)} collective-permute-done((bf16[128,512]{1,0:T(8,128)(2,1)S(1)}, bf16[128,512]{1,0:T(8,128)(2,1)S(1)}, u32[]{:S(2)}, u32[]{:S(2)}) %collective-permute-start.8) | collective-permute-done | bytes 131104 | tf_op jit(solution)/shard_map/ppermute | solution.py:581
  111.7 0.0 copy-done.3
  111.7 0.0 copy-start.1
  111.7 1.8 %copy-done.1 = bf16[2688,512]{1,0:T(8,128)(2,1)S(1)} copy-done((bf16[2688,512]{1,0:T(8,128)(2,1)S(1)}, bf16[2688,512]{1,0:T(8,128)(2,1)}, u32[]{:S(2)}) %copy-start.1) | copy-done | bytes 2752536
  113.4 0.0 copy-start.5
  113.4 1.6 %copy-done.5 = bf16[2048,512]{1,0:T(8,128)(2,1)S(1)} copy-done((bf16[2048,512]{1,0:T(8,128)(2,1)S(1)}, bf16[2048,512]{1,0:T(8,128)(2,1)}, u32[]{:S(2)}) %copy-start.5) | copy-done | bytes 2097176
  115.0 6.6 %latent.1 = bf16[2048,512]{1,0:T(8,128)(2,1)} custom-call(bf16[2048,512]{1,0:T(8,128)(2,1)S(1)} %copy-done.5, bf16[2688,512]{1,0:T(8,128)(2,1)S(1)} %copy-done.1, bf16[128,512]{1,0:T(8,128)(2,1)S(1)} %collective-permute-done.7.top_ref, bf16[128,512]{1,0:T(8,128)(2,1)S(1)} %collective-permute-done.8.bottom_ref, ...), custom_call_target="tpu_custom_call" | custom-call | flops 5767499776 | tf_op jit(solution)/shard_map/latent/pallas_call | solution.py:420
  121.6 4.0 %all-to-all-done.2.own_ref = bf16[16,208,128]{2,1,0:T(8,128)(2,1)S(1)} async-done(((bf16[16,208,128]{2,1,0:T(8,128)(2,1)}), bf16[16,208,128]{2,1,0:T(8,128)(2,1)S(1)}, u32[]{:S(2)}, u32[]{:S(2)}) %all-to-all-start.2) | async-done | bytes 852000 | tf_op jit(solution)/shard_map/all_to_all | solution.py:519
  125.6 0.3 collective-permute-start.9
  125.9 2.1 %collective-permute-done.9.sibling_ref = bf16[16,208,128]{2,1,0:T(8,128)(2,1)S(1)} collective-permute-done((bf16[16,208,128]{2,1,0:T(8,128)(2,1)S(1)}, bf16[16,208,128]{2,1,0:T(8,128)(2,1)S(1)}, u32[]{:S(2)}, u32[]{:S(2)}) %collective-permute-start.9) | collective-permute-done | bytes 852000 | tf_op jit(solution)/shard_map/ppermute | solution.py:587
  128.0 2.1 %unpack.1 = (f32[616,512]{1,0:T(8,128)}, f32[512,512]{1,0:T(8,128)}, f32[512,512]{1,0:T(8,128)}, f32[9,512]{1,0:T(8,128)}) custom-call(s32[1]{0:T(128)} %bitcast.core_ref, bf16[16,208,128]{2,1,0:T(8,128)(2,1)S(1)} %all-to-all-done.2.own_ref, bf16[16,208,128]{2,1,0:T(8,128)(2,1)S(1)} %collective-permute-done.9.sibling_ref), custom_call_target="tpu_custom_call" | custom-call | flops 3460499968 | tf_op jit(solution)/shard_map/unpack/pallas_call | solution.py:491
  (7 shorter events, 0.0 us)
Async XLA Ops:
  1.7 10.9 %collective-permute-start = (bf16[16,512]{1,0:T(8,128)(2,1)S(1)}, bf16[16,512]{1,0:T(8,128)(2,1)S(1)}, u32[]{:S(2)}, u32[]{:S(2)}) collective-permute-start(bf16[16,512]{1,0:T(8,128)(2,1)S(1)} %bitcast.30), channel_id=1, source_target_pairs={{0,1},{1,2},{2,3},{3,4},{4,5},{5,6},{6,7},{7,0},{8,9},{9,10},{10,1... | collective-permute-start | bytes 49160 | tf_op jit(solution)/shard_map/ppermute | solution.py:534
  4.7 7.9 %collective-permute-start.1 = (bf16[16,512]{1,0:T(8,128)(2,1)S(1)}, bf16[16,512]{1,0:T(8,128)(2,1)S(1)}, u32[]{:S(2)}, u32[]{:S(2)}) collective-permute-start(bf16[16,512]{1,0:T(8,128)(2,1)S(1)} %bitcast.31), channel_id=1, source_target_pairs={{1,0},{2,1},{3,2},{4,3},{5,4},{6,5},{7,6},{0,7},{9,8},{10,9},{11,1... | collective-permute-start | bytes 49160 | tf_op jit(solution)/shard_map/ppermute | solution.py:535
  8.5 1.1 copy-start.2
  12.6 8.6 %copy-start = (bf16[512,512]{1,0:T(8,128)(2,1)S(1)}, bf16[512,512]{1,0:T(8,128)(2,1)}, u32[]{:S(2)}) copy-start(bf16[512,512]{1,0:T(8,128)(2,1)} %wo_hbm) | copy-start | bytes 1572868
  12.6 8.8 %copy-start.7 = (bf16[16,512]{1,0:T(8,128)(2,1)}, bf16[16,512]{1,0:T(8,128)(2,1)S(1)}, u32[]{:S(2)}) copy-start(bf16[16,512]{1,0:T(8,128)(2,1)S(1)} %collective-permute-done.west_ref) | copy-start | bytes 49156
  12.6 8.8 %copy-start.8 = (bf16[16,512]{1,0:T(8,128)(2,1)}, bf16[16,512]{1,0:T(8,128)(2,1)S(1)}, u32[]{:S(2)}) copy-start(bf16[16,512]{1,0:T(8,128)(2,1)S(1)} %collective-permute-done.1.east_ref) | copy-start | bytes 49156
  12.6 8.8 %copy-start.6 = (bf16[616,512]{1,0:T(8,128)(2,1)S(1)}, bf16[616,512]{1,0:T(8,128)(2,1)}, u32[]{:S(2)}) copy-start(bf16[616,512]{1,0:T(8,128)(2,1)} %param.11) | copy-start | bytes 1892356
  12.6 36.5 %all-to-all-start = ((bf16[32,32,640]{2,1,0:T(8,128)(2,1)}), bf16[32,32,640]{2,1,0:T(8,128)(2,1)S(1)}, u32[]{:S(2)}, u32[]{:S(2)}) async-start(bf16[32,32,640]{2,1,0:T(8,128)(2,1)} %bitcast.6), calls=%async_computation | async-start | bytes 2621440 | tf_op jit(solution)/shard_map/all_to_all | solution.py:542
  17.1 6.6 %collective-permute-start.2 = (bf16[144,512]{1,0:T(8,128)(2,1)S(1)}, bf16[144,512]{1,0:T(8,128)(2,1)}, u32[]{:S(2)}, u32[]{:S(2)}) collective-permute-start(bf16[144,512]{1,0:T(8,128)(2,1)S(1)} %get-tuple-element.68), channel_id=1, source_target_pairs={{0,8},{8,16},{16,24},{1,9},{9,17},{17,25},{2,10},{10,18},{18,26},{... | collective-permute-start | bytes 442376 | tf_op jit(solution)/shard_map/ppermute | solution.py:551
  19.9 3.9 %collective-permute-start.3 = (bf16[144,512]{1,0:T(8,128)(2,1)S(1)}, bf16[144,512]{1,0:T(8,128)(2,1)}, u32[]{:S(2)}, u32[]{:S(2)}) collective-permute-start(bf16[144,512]{1,0:T(8,128)(2,1)S(1)} %get-tuple-element.67), channel_id=1, source_target_pairs={{8,0},{16,8},{24,16},{9,1},{17,9},{25,17},{10,2},{18,10},{26,18},{... | collective-permute-start | bytes 442376 | tf_op jit(solution)/shard_map/ppermute | solution.py:552
  23.8 25.3 %copy-start.4 = (f32[9,512]{1,0:T(8,128)S(1)}, f32[9,512]{1,0:T(8,128)}, u32[]{:S(2)}) copy-start(f32[9,512]{1,0:T(8,128)} %wd_ref.3) | copy-start | bytes 55300
  68.6 2.4 %collective-permute-start.4 = (bf16[2,1664,128]{2,1,0:T(8,128)(2,1)S(1)}, bf16[2,1664,128]{2,1,0:T(8,128)(2,1)S(1)}, u32[]{:S(2)}, u32[]{:S(2)}) collective-permute-start(bf16[2,1664,128]{2,1,0:T(8,128)(2,1)S(1)} %get-tuple-element.38), channel_id=1, source_target_pairs={{0,8},{8,0},{1,9},{9,1},{2,10},{10,2},{3,11},{11,3},{4,12},{12,4},... | collective-permute-start | bytes 2555912 | tf_op jit(solution)/shard_map/ppermute | solution.py:447
  72.2 26.9 %all-to-all-start.1 = ((bf16[16,208,128]{2,1,0:T(8,128)(2,1)}), bf16[16,208,128]{2,1,0:T(8,128)(2,1)S(1)}, u32[]{:S(2)}, u32[]{:S(2)}) async-start(bf16[16,208,128]{2,1,0:T(8,128)(2,1)} %bitcast.13), calls=%async_computation.1 | async-start | bytes 1703936 | tf_op jit(solution)/shard_map/all_to_all | solution.py:519
  75.8 20.2 %collective-permute-start.5 = (f32[18,512]{1,0:T(8,128)S(1)}, f32[18,512]{1,0:T(8,128)S(1)}, u32[]{:S(2)}, u32[]{:S(2)}) collective-permute-start(f32[18,512]{1,0:T(8,128)S(1)} %get-tuple-element.43), channel_id=1, source_target_pairs={{0,1},{1,2},{2,3},{3,4},{4,5},{5,6},{6,7},{7,0},{8,9},{9,10},{10,1... | collective-permute-start | bytes 110600 | tf_op jit(solution)/shard_map/ppermute | solution.py:569
  77.6 18.4 %collective-permute-start.6 = (f32[18,512]{1,0:T(8,128)S(1)}, f32[18,512]{1,0:T(8,128)S(1)}, u32[]{:S(2)}, u32[]{:S(2)}) collective-permute-start(f32[18,512]{1,0:T(8,128)S(1)} %get-tuple-element.44), channel_id=1, source_target_pairs={{1,0},{2,1},{3,2},{4,3},{5,4},{6,5},{7,6},{0,7},{9,8},{10,9},{11,1... | collective-permute-start | bytes 110600 | tf_op jit(solution)/shard_map/ppermute | solution.py:570
  100.1 11.6 %copy-start.3 = (bf16[512,512]{1,0:T(8,128)(2,1)S(1)}, bf16[512,512]{1,0:T(8,128)(2,1)}, u32[]{:S(2)}) copy-start(bf16[512,512]{1,0:T(8,128)(2,1)} %wp_ref.3) | copy-start | bytes 1572868
  100.1 25.5 %all-to-all-start.2 = ((bf16[16,208,128]{2,1,0:T(8,128)(2,1)}), bf16[16,208,128]{2,1,0:T(8,128)(2,1)S(1)}, u32[]{:S(2)}, u32[]{:S(2)}) async-start(bf16[16,208,128]{2,1,0:T(8,128)(2,1)} %totals.1), calls=%async_computation.2 | async-start | bytes 1703936 | tf_op jit(solution)/shard_map/all_to_all | solution.py:519
  105.0 2.8 %collective-permute-start.7 = (bf16[128,512]{1,0:T(8,128)(2,1)S(1)}, bf16[128,512]{1,0:T(8,128)(2,1)S(1)}, u32[]{:S(2)}, u32[]{:S(2)}) collective-permute-start(bf16[128,512]{1,0:T(8,128)(2,1)S(1)} %get-tuple-element.54), channel_id=1, source_target_pairs={{0,8},{8,16},{16,24},{1,9},{9,17},{17,25},{2,10},{10,18},{18,26},{... | collective-permute-start | bytes 393224 | tf_op jit(solution)/shard_map/ppermute | solution.py:580
  106.5 5.1 %collective-permute-start.8 = (bf16[128,512]{1,0:T(8,128)(2,1)S(1)}, bf16[128,512]{1,0:T(8,128)(2,1)S(1)}, u32[]{:S(2)}, u32[]{:S(2)}) collective-permute-start(bf16[128,512]{1,0:T(8,128)(2,1)S(1)} %get-tuple-element.53), channel_id=1, source_target_pairs={{8,0},{16,8},{24,16},{9,1},{17,9},{25,17},{10,2},{18,10},{26,18},{... | collective-permute-start | bytes 393224 | tf_op jit(solution)/shard_map/ppermute | solution.py:581
  111.7 1.8 %copy-start.1 = (bf16[2688,512]{1,0:T(8,128)(2,1)S(1)}, bf16[2688,512]{1,0:T(8,128)(2,1)}, u32[]{:S(2)}) copy-start(bf16[2688,512]{1,0:T(8,128)(2,1)} %get-tuple-element.46.mix_ref) | copy-start | bytes 8257540
  113.4 1.6 %copy-start.5 = (bf16[2048,512]{1,0:T(8,128)(2,1)S(1)}, bf16[2048,512]{1,0:T(8,128)(2,1)}, u32[]{:S(2)}) copy-start(bf16[2048,512]{1,0:T(8,128)(2,1)} %get-tuple-element.45.grid_ref) | copy-start | bytes 6291460
  125.6 2.4 %collective-permute-start.9 = (bf16[16,208,128]{2,1,0:T(8,128)(2,1)S(1)}, bf16[16,208,128]{2,1,0:T(8,128)(2,1)S(1)}, u32[]{:S(2)}, u32[]{:S(2)}) collective-permute-start(bf16[16,208,128]{2,1,0:T(8,128)(2,1)S(1)} %all-to-all-done.2.own_ref), channel_id=1, source_target_pairs={{0,8},{8,0},{1,9},{9,1},{2,10},{10,2},{3,11},{11,3},{4,12},{12,4},... | collective-permute-start | bytes 2555912 | tf_op jit(solution)/shard_map/ppermute | solution.py:587

commit v9 on v8

--- a/solution.py
+++ b/solution.py
@@ -230,9 +230,9 @@
     spec, clat, clon, wide, core_ref, rows_ref, wd_ref, wit_hbm, wot_hbm, gg_hbm, wo_hbm, gm_hbm, cott_hbm,
     mine_ref, other_ref, east_out, west_out, grid_hbm, mix_hbm,
     wit_ref, wot_ref, gg_ref, wo_ref, gm_ref, cott_ref,
-    emb_ref, gi, gi_out, go, wide_ref, grid_ref, mix_ref, east_ref, west_ref, gp, gd, sems,
+    emb_ref, hid_ref, slope_ref, gi, gi_out, go, wide_ref, grid_ref, mix_ref, east_ref, west_ref, gp, gd, sems,
 ):
-    loads = start_loads((wit_hbm, wot_hbm, gg_hbm, wo_hbm), (wit_ref, wot_ref, gg_ref, wo_ref), sems)
+    first = start_loads((wit_hbm, wot_hbm), (wit_ref, wot_ref), sems)
     put_grid = pltpu.make_async_copy(grid_ref, grid_hbm, sems.at[6])
     put_mix = pltpu.make_async_copy(mix_ref, mix_hbm, sems.at[7])
     core = core_ref[0]
@@ -241,36 +241,21 @@
     blocks = width // LANES
     step = min(512, slots)
 
+    go[...] = jnp.zeros_like(go)
+    gi[...] = jnp.zeros_like(gi)
+    for load in first:
+        load.wait()
+    late = start_loads(
+        (gg_hbm, wo_hbm, gm_hbm, cott_hbm), (gg_ref, wo_ref, gm_ref, cott_ref), sems.at[pl.ds(2, 4)]
+    )
     for t in range(slots // step):
         at = slice(t * step, (t + 1) * step)
-        rows = rows_ref[at, :]
-        line = rows[:, spec : spec + 1].astype(f32).astype(i32)
-        column = rows[:, spec + 1 : spec + 2].astype(f32).astype(i32)
-        hits = one_hot(line * clon + place_of(column, clon // GROUPS), cells)
-        if t == 0:
-            loads[0].wait()
-        preact = dot(wit_ref[...], rows, (1, 1))
+        preact = dot(wit_ref[...], rows_ref[at, :], (1, 1))
         sig = 1.0 / (1.0 + jnp.exp(-preact))
         hidden = (preact * sig).astype(bf16)
-        if t == 0:
-            loads[1].wait()
+        hid_ref[:, at] = hidden
+        slope_ref[:, at] = sig * (1.0 + preact * (1.0 - sig))
         emb_ref[:, at] = dot(wot_ref[...], hidden).astype(bf16)
-        if t == 0:
-            loads[2].wait()
-        g_emb = dot(hits, gg_ref[...]).astype(bf16)
-        g_out = dot(hidden, g_emb)
-        if t == 0:
-            loads[3].wait()
-            late = start_loads((gm_hbm, cott_hbm), (gm_ref, cott_ref), sems.at[pl.ds(4, 2)])
-        g_hid = dot(wo_ref[...], g_emb, (1, 1))
-        g_pre = (g_hid * (sig * (1.0 + preact * (1.0 - sig)))).astype(bf16)
-        g_in = dot(g_pre, rows)
-        if t == 0:
-            go[...] = g_out
-            gi[...] = g_in
-        else:
-            go[...] += g_out
-            gi[...] += g_in
 
     last = rows_ref[:, spec_wide - LANES :]
     col = spec - (spec_wide - LANES)
@@ -303,10 +288,11 @@
 
     lax.fori_loop(0, clat // lines, bins, 0)
     put_grid.start()
-    late[0].wait()
+    for load in late[:3]:
+        load.wait()
     group = lax.broadcasted_iota(i32, (GROUPS, LANES), 0)
 
-    def conv(e, carry):
+    def conv(e):
         for n in range(blocks):
             cols = slice(n * LANES, (n + 1) * LANES)
             weights = [wd_ref[k : k + 1, cols] for k in range(9)]
@@ -339,11 +325,36 @@
             west_ref[e, :, cols] = ends[1]
             out_at = pl.ds(pl.multiple_of(e * wide + clon, 16), wide - clon)
             mix_ref[out_at, cols] = jnp.concatenate(ends, axis=0).astype(bf16)
-        return carry
-
-    lax.fori_loop(0, clat + 2, conv, 0)
+
+    part = min(256, slots)
+    count = slots // part
+    each = (clat + 2) // count
+
+    def both(t, carry):
+        at = pl.ds(pl.multiple_of(t * part, part), part)
+        rows = rows_ref[at, :]
+        line = rows[:, spec : spec + 1].astype(f32).astype(i32)
+        column = rows[:, spec + 1 : spec + 2].astype(f32).astype(i32)
+        hits = one_hot(line * clon + place_of(column, clon // GROUPS), cells)
+        g_emb = dot(hits, gg_ref[...]).astype(bf16)
+        done = each // 2
+        for k in range(done):
+            conv(t * each + k)
+        go[...] += dot(hid_ref[:, at], g_emb)
+        g_pre = (dot(wo_ref[...], g_emb, (1, 1)) * slope_ref[:, at]).astype(bf16)
+        for k in range(done, each):
+            conv(t * each + k)
+        gi[...] += dot(g_pre, rows)
+        return carry
+
+    def remaining(e, carry):
+        conv(e)
+        return carry
+
+    lax.fori_loop(0, count, both, 0)
+    lax.fori_loop(count * each, clat + 2, remaining, 0)
     put_mix.start()
-    late[1].wait()
+    late[3].wait()
     gp[...] = dot(cott_ref[...], mix_ref[...]).T
     gi_out[...] = gi[...].T
     east_out[...] = east_ref[:, GROUPS - 1, :]
@@ -374,6 +385,8 @@
         scratch_shapes=[pltpu.VMEM(x.shape, x.dtype) for x in operands]
         + [
             pltpu.VMEM((width, slots), bf16),
+            pltpu.VMEM((width, slots), bf16),
+            pltpu.VMEM((width, slots), f32),
             pltpu.VMEM((width, spec_wide), f32),
             pltpu.VMEM((spec_wide, width), f32),
             pltpu.VMEM((width, width), f32),

time: 131 us -> 132 us (level)
  no operation moved by 1% of the time
where the time goes in v9:
time: 132 us; the launch traced here: 131 us
  Pallas kernels  50.1 us (38%)
  waiting for transfers between devices  40.4 us (31%)
  starting transfers between devices  28.8 us (22%)
  local copies, waits for them, and re-layouts  9.04 us (7%)
  other arithmetic  1.96 us (1%)
    pallas_call x1, Pallas kernels, owner_part(): pl.pallas_call(functools.partial(owner_kernel, spec, clat, clon, wide), o...  20.5 us
    pallas_call x1, Pallas kernels, grid_grad(): pl.pallas_call(functools.partial(grid_grad_kernel, clat, clon, wide), out...  15.7 us
    ppermute x1, waiting for transfers between devices, on_device(): left = lax.ppermute(east, 'lon', east_way)  15.4 us
    all_to_all x1, waiting for transfers between devices, on_device(): lax.all_to_all(outgoing.reshape(tiles, cap, spec_wide), ('x', 'core', 'lo...  9.53 us
    all_to_all x2, starting transfers between devices, spread(): lax.all_to_all(values, CHIPS, split_axis=0, concat_axis=0, tiled=True)  7.38 us
    all_to_all x2, waiting for transfers between devices, spread(): lax.all_to_all(values, CHIPS, split_axis=0, concat_axis=0, tiled=True)  7.06 us
    pallas_call x1, Pallas kernels, finish_latent(): pl.pallas_call(functools.partial(latent_kernel, clat, clon, wide), out_sh...  6.58 us
    unnamed x20, local copies, waits for them, and re-layouts  4.48 us
  transfers between devices with their start and end apart: 13, of which 8 were waited for; matrix products, arithmetic and copies ran while one was open for 4% of the time, Pallas kernels for 19%

profile of v9, /device:TPU:0, one launch (start us, length us, event | category | flops | bytes accessed | tf_op | source)
XLA Modules:
  0.0 131.1 jit_solution(8545682880703460443)
XLA Ops:
  0.6 1.0 fusion
  1.7 3.0 %collective-permute-start = (bf16[16,512]{1,0:T(8,128)(2,1)S(1)}, bf16[16,512]{1,0:T(8,128)(2,1)S(1)}, u32[]{:S(2)}, u32[]{:S(2)}) collective-permute-start(bf16[16,512]{1,0:T(8,128)(2,1)S(1)} %bitcast.30), channel_id=1, source_target_pairs={{0,1},{1,2},{2,3},{3,4},{4,5},{5,6},{6,7},{7,0},{8,9},{9,10},{10,1... | collective-permute-start | bytes 49160 | tf_op jit(solution)/shard_map/ppermute | solution.py:547
  4.7 3.1 %collective-permute-start.1 = (bf16[16,512]{1,0:T(8,128)(2,1)S(1)}, bf16[16,512]{1,0:T(8,128)(2,1)S(1)}, u32[]{:S(2)}, u32[]{:S(2)}) collective-permute-start(bf16[16,512]{1,0:T(8,128)(2,1)S(1)} %bitcast.31), channel_id=1, source_target_pairs={{1,0},{2,1},{3,2},{4,3},{5,4},{6,5},{7,6},{0,7},{9,8},{10,9},{11,1... | collective-permute-start | bytes 49160 | tf_op jit(solution)/shard_map/ppermute | solution.py:548
  7.8 0.7 pad_add_fusion.places_ref
  8.5 0.0 copy-start.2
  8.5 1.1 copy-done.2
  9.6 3.0 %route.1 = bf16[1024,640]{1,0:T(8,128)(2,1)} custom-call(s32[2,512]{1,0:T(2,128)S(1)} %pad_add_fusion.places_ref, bf16[616,512]{1,0:T(8,128)(2,1)S(1)} %bitcast.27), custom_call_target="tpu_custom_call" | custom-call | flops 3460499968 | tf_op jit(solution)/shard_map/route/pallas_call | solution.py:77
  12.6 0.0 copy-start
  12.6 0.0 collective-permute-done.west_ref
  12.6 0.0 copy-start.7
  12.6 0.0 collective-permute-done.1.east_ref
  12.6 0.0 copy-start.8
  12.6 0.0 copy-start.6
  12.6 3.2 %all-to-all-start = ((bf16[32,32,640]{2,1,0:T(8,128)(2,1)}), bf16[32,32,640]{2,1,0:T(8,128)(2,1)S(1)}, u32[]{:S(2)}, u32[]{:S(2)}) async-start(bf16[32,32,640]{2,1,0:T(8,128)(2,1)} %bitcast.6), calls=%async_computation | async-start | bytes 2621440 | tf_op jit(solution)/shard_map/all_to_all | solution.py:555
  15.9 0.1 pad.11.clone
  16.0 1.0 slice_bitcast_fusion
  17.0 0.1 pad_maximum_fusion.1
  17.1 2.8 %collective-permute-start.2 = (bf16[144,512]{1,0:T(8,128)(2,1)S(1)}, bf16[144,512]{1,0:T(8,128)(2,1)}, u32[]{:S(2)}, u32[]{:S(2)}) collective-permute-start(bf16[144,512]{1,0:T(8,128)(2,1)S(1)} %get-tuple-element.68), channel_id=1, source_target_pairs={{0,8},{8,16},{16,24},{1,9},{9,17},{17,25},{2,10},{10,18},{18,26},{... | collective-permute-start | bytes 442376 | tf_op jit(solution)/shard_map/ppermute | solution.py:564
  19.9 1.3 collective-permute-start.3
  21.2 0.0 copy-done
  21.2 0.2 copy.16
  21.4 0.0 copy-done.7
  21.5 0.0 copy-done.8
  21.5 0.0 copy-done.6
  21.5 1.1 copy.15
  22.6 1.1 pad.4.wit_hbm
  23.7 0.0 collective-permute-done.2.north_ref
  23.7 0.1 collective-permute-done.3.south_ref
  23.8 0.0 copy-start.4
  23.8 15.7 %grid_grad.1 = (bf16[512,2688]{1,0:T(8,128)(2,1)}, f32[4,18,144,128]{3,2,1,0:T(8,128)}, bf16[2048,512]{1,0:T(8,128)(2,1)}) custom-call(bf16[2048,512]{1,0:T(8,128)(2,1)} %bitcast.29, bf16[16,512]{1,0:T(8,128)(2,1)} %copy-done.8, bf16[16,512]{1,0:T(8,128)(2,1)} %copy-done.7, bf16[144,512]{1,0:T(8,128)(2,1)} %collective-permute-done.2.north_ref, ...), custom_call_target="tpu_custom_call" | custom-call | flops 11534999552 | tf_op jit(solution)/shard_map/grid_grad/pallas_call | solution.py:188
  39.6 9.5 %all-to-all-done = bf16[32,32,640]{2,1,0:T(8,128)(2,1)S(1)} async-done(((bf16[32,32,640]{2,1,0:T(8,128)(2,1)}), bf16[32,32,640]{2,1,0:T(8,128)(2,1)S(1)}, u32[]{:S(2)}, u32[]{:S(2)}) %all-to-all-start) | async-done | bytes 1310752 | tf_op jit(solution)/shard_map/all_to_all | solution.py:555
  49.1 0.0 copy-done.4
  49.1 20.5 %owner.1 = (bf16[2,1664,128]{2,1,0:T(8,128)(2,1)S(1)}, bf16[2,1664,128]{2,1,0:T(8,128)(2,1)S(1)}, f32[18,512]{1,0:T(8,128)S(1)}, f32[18,512]{1,0:T(8,128)S(1)}, ...) custom-call(s32[1]{0:T(128)} %bitcast.core_ref, bf16[1024,640]{1,0:T(8,128)(2,1)S(1)} %bitcast.25, ...), custom_call_target="tpu_custom_call" | custom-call | flops 24223500288 | tf_op jit(solution)/shard_map/owner/pallas_call | solution.py:380
  69.7 0.1 collective-permute-start.4
  69.7 2.4 %collective-permute-done.4.got_ref = bf16[2,1664,128]{2,1,0:T(8,128)(2,1)S(1)} collective-permute-done((bf16[2,1664,128]{2,1,0:T(8,128)(2,1)S(1)}, bf16[2,1664,128]{2,1,0:T(8,128)(2,1)S(1)}, u32[]{:S(2)}, u32[]{:S(2)}) %collective-permute-start.4) | collective-permute-done | bytes 852000 | tf_op jit(solution)/shard_map/ppermute | solution.py:460
  72.1 1.1 core_sum.1
  73.2 3.6 %all-to-all-start.1 = ((bf16[16,208,128]{2,1,0:T(8,128)(2,1)}), bf16[16,208,128]{2,1,0:T(8,128)(2,1)S(1)}, u32[]{:S(2)}, u32[]{:S(2)}) async-start(bf16[16,208,128]{2,1,0:T(8,128)(2,1)} %bitcast.13), calls=%async_computation.1 | async-start | bytes 1703936 | tf_op jit(solution)/shard_map/all_to_all | solution.py:532
  76.8 1.8 %collective-permute-start.5 = (f32[18,512]{1,0:T(8,128)S(1)}, f32[18,512]{1,0:T(8,128)S(1)}, u32[]{:S(2)}, u32[]{:S(2)}) collective-permute-start(f32[18,512]{1,0:T(8,128)S(1)} %get-tuple-element.43), channel_id=1, source_target_pairs={{0,1},{1,2},{2,3},{3,4},{4,5},{5,6},{6,7},{7,0},{8,9},{9,10},{10,1... | collective-permute-start | bytes 110600 | tf_op jit(solution)/shard_map/ppermute | solution.py:582
  78.6 3.0 %collective-permute-start.6 = (f32[18,512]{1,0:T(8,128)S(1)}, f32[18,512]{1,0:T(8,128)S(1)}, u32[]{:S(2)}, u32[]{:S(2)}) collective-permute-start(f32[18,512]{1,0:T(8,128)S(1)} %get-tuple-element.44), channel_id=1, source_target_pairs={{1,0},{2,1},{3,2},{4,3},{5,4},{6,5},{7,6},{0,7},{9,8},{10,9},{11,1... | collective-permute-start | bytes 110600 | tf_op jit(solution)/shard_map/ppermute | solution.py:583
  81.6 15.4 %collective-permute-done.5.refs_0_.left_ref = f32[18,512]{1,0:T(8,128)S(1)} collective-permute-done((f32[18,512]{1,0:T(8,128)S(1)}, f32[18,512]{1,0:T(8,128)S(1)}, u32[]{:S(2)}, u32[]{:S(2)}) %collective-permute-start.5) | collective-permute-done | bytes 36896 | tf_op jit(solution)/shard_map/ppermute | solution.py:582
  97.1 0.0 collective-permute-done.6.refs_1_.right_ref
  97.1 3.1 %all-to-all-done.1.parts_ref = bf16[16,208,128]{2,1,0:T(8,128)(2,1)S(1)} async-done(((bf16[16,208,128]{2,1,0:T(8,128)(2,1)}), bf16[16,208,128]{2,1,0:T(8,128)(2,1)S(1)}, u32[]{:S(2)}, u32[]{:S(2)}) %all-to-all-start.1) | async-done | bytes 852000 | tf_op jit(solution)/shard_map/all_to_all | solution.py:532
  100.1 1.0 totals.1
  101.1 0.0 copy-start.3
  101.1 3.8 %all-to-all-start.2 = ((bf16[16,208,128]{2,1,0:T(8,128)(2,1)}), bf16[16,208,128]{2,1,0:T(8,128)(2,1)S(1)}, u32[]{:S(2)}, u32[]{:S(2)}) async-start(bf16[16,208,128]{2,1,0:T(8,128)(2,1)} %totals.1), calls=%async_computation.2 | async-start | bytes 1703936 | tf_op jit(solution)/shard_map/all_to_all | solution.py:532
  104.9 1.1 add_convert_fusion
  106.1 1.5 %collective-permute-start.7 = (bf16[128,512]{1,0:T(8,128)(2,1)S(1)}, bf16[128,512]{1,0:T(8,128)(2,1)S(1)}, u32[]{:S(2)}, u32[]{:S(2)}) collective-permute-start(bf16[128,512]{1,0:T(8,128)(2,1)S(1)} %get-tuple-element.54), channel_id=1, source_target_pairs={{0,8},{8,16},{16,24},{1,9},{9,17},{17,25},{2,10},{10,18},{18,26},{... | collective-permute-start | bytes 393224 | tf_op jit(solution)/shard_map/ppermute | solution.py:593
  107.6 1.3 collective-permute-start.8
  108.9 0.0 collective-permute-done.7.top_ref
  108.9 3.8 %collective-permute-done.8.bottom_ref = bf16[128,512]{1,0:T(8,128)(2,1)S(1)} collective-permute-done((bf16[128,512]{1,0:T(8,128)(2,1)S(1)}, bf16[128,512]{1,0:T(8,128)(2,1)S(1)}, u32[]{:S(2)}, u32[]{:S(2)}) %collective-permute-start.8) | collective-permute-done | bytes 131104 | tf_op jit(solution)/shard_map/ppermute | solution.py:594
  112.7 0.0 copy-done.3
  112.7 0.0 copy-start.1
  112.7 1.8 %copy-done.1 = bf16[2688,512]{1,0:T(8,128)(2,1)S(1)} copy-done((bf16[2688,512]{1,0:T(8,128)(2,1)S(1)}, bf16[2688,512]{1,0:T(8,128)(2,1)}, u32[]{:S(2)}) %copy-start.1) | copy-done | bytes 2752536
  114.5 0.0 copy-start.5
  114.5 1.6 %copy-done.5 = bf16[2048,512]{1,0:T(8,128)(2,1)S(1)} copy-done((bf16[2048,512]{1,0:T(8,128)(2,1)S(1)}, bf16[2048,512]{1,0:T(8,128)(2,1)}, u32[]{:S(2)}) %copy-start.5) | copy-done | bytes 2097176
  116.1 6.6 %latent.1 = bf16[2048,512]{1,0:T(8,128)(2,1)} custom-call(bf16[2048,512]{1,0:T(8,128)(2,1)S(1)} %copy-done.5, bf16[2688,512]{1,0:T(8,128)(2,1)S(1)} %copy-done.1, bf16[128,512]{1,0:T(8,128)(2,1)S(1)} %collective-permute-done.7.top_ref, bf16[128,512]{1,0:T(8,128)(2,1)S(1)} %collective-permute-done.8.bottom_ref, ...), custom_call_target="tpu_custom_call" | custom-call | flops 5767499776 | tf_op jit(solution)/shard_map/latent/pallas_call | solution.py:433
  122.6 4.0 %all-to-all-done.2.own_ref = bf16[16,208,128]{2,1,0:T(8,128)(2,1)S(1)} async-done(((bf16[16,208,128]{2,1,0:T(8,128)(2,1)}), bf16[16,208,128]{2,1,0:T(8,128)(2,1)S(1)}, u32[]{:S(2)}, u32[]{:S(2)}) %all-to-all-start.2) | async-done | bytes 852000 | tf_op jit(solution)/shard_map/all_to_all | solution.py:532
  126.7 0.3 collective-permute-start.9
  127.0 2.1 %collective-permute-done.9.sibling_ref = bf16[16,208,128]{2,1,0:T(8,128)(2,1)S(1)} collective-permute-done((bf16[16,208,128]{2,1,0:T(8,128)(2,1)S(1)}, bf16[16,208,128]{2,1,0:T(8,128)(2,1)S(1)}, u32[]{:S(2)}, u32[]{:S(2)}) %collective-permute-start.9) | collective-permute-done | bytes 852000 | tf_op jit(solution)/shard_map/ppermute | solution.py:600
  129.0 2.1 %unpack.1 = (f32[616,512]{1,0:T(8,128)}, f32[512,512]{1,0:T(8,128)}, f32[512,512]{1,0:T(8,128)}, f32[9,512]{1,0:T(8,128)}) custom-call(s32[1]{0:T(128)} %bitcast.core_ref, bf16[16,208,128]{2,1,0:T(8,128)(2,1)S(1)} %all-to-all-done.2.own_ref, bf16[16,208,128]{2,1,0:T(8,128)(2,1)S(1)} %collective-permute-done.9.sibling_ref), custom_call_target="tpu_custom_call" | custom-call | flops 3460499968 | tf_op jit(solution)/shard_map/unpack/pallas_call | solution.py:504
  (7 shorter events, 0.0 us)
Async XLA Ops:
  1.7 10.9 %collective-permute-start = (bf16[16,512]{1,0:T(8,128)(2,1)S(1)}, bf16[16,512]{1,0:T(8,128)(2,1)S(1)}, u32[]{:S(2)}, u32[]{:S(2)}) collective-permute-start(bf16[16,512]{1,0:T(8,128)(2,1)S(1)} %bitcast.30), channel_id=1, source_target_pairs={{0,1},{1,2},{2,3},{3,4},{4,5},{5,6},{6,7},{7,0},{8,9},{9,10},{10,1... | collective-permute-start | bytes 49160 | tf_op jit(solution)/shard_map/ppermute | solution.py:547
  4.7 7.9 %collective-permute-start.1 = (bf16[16,512]{1,0:T(8,128)(2,1)S(1)}, bf16[16,512]{1,0:T(8,128)(2,1)S(1)}, u32[]{:S(2)}, u32[]{:S(2)}) collective-permute-start(bf16[16,512]{1,0:T(8,128)(2,1)S(1)} %bitcast.31), channel_id=1, source_target_pairs={{1,0},{2,1},{3,2},{4,3},{5,4},{6,5},{7,6},{0,7},{9,8},{10,9},{11,1... | collective-permute-start | bytes 49160 | tf_op jit(solution)/shard_map/ppermute | solution.py:548
  8.5 1.1 copy-start.2
  12.6 8.6 %copy-start = (bf16[512,512]{1,0:T(8,128)(2,1)S(1)}, bf16[512,512]{1,0:T(8,128)(2,1)}, u32[]{:S(2)}) copy-start(bf16[512,512]{1,0:T(8,128)(2,1)} %wo_hbm) | copy-start | bytes 1572868
  12.6 8.8 %copy-start.7 = (bf16[16,512]{1,0:T(8,128)(2,1)}, bf16[16,512]{1,0:T(8,128)(2,1)S(1)}, u32[]{:S(2)}) copy-start(bf16[16,512]{1,0:T(8,128)(2,1)S(1)} %collective-permute-done.west_ref) | copy-start | bytes 49156
  12.6 8.8 %copy-start.8 = (bf16[16,512]{1,0:T(8,128)(2,1)}, bf16[16,512]{1,0:T(8,128)(2,1)S(1)}, u32[]{:S(2)}) copy-start(bf16[16,512]{1,0:T(8,128)(2,1)S(1)} %collective-permute-done.1.east_ref) | copy-start | bytes 49156
  12.6 8.8 %copy-start.6 = (bf16[616,512]{1,0:T(8,128)(2,1)S(1)}, bf16[616,512]{1,0:T(8,128)(2,1)}, u32[]{:S(2)}) copy-start(bf16[616,512]{1,0:T(8,128)(2,1)} %param.11) | copy-start | bytes 1892356
  12.6 36.5 %all-to-all-start = ((bf16[32,32,640]{2,1,0:T(8,128)(2,1)}), bf16[32,32,640]{2,1,0:T(8,128)(2,1)S(1)}, u32[]{:S(2)}, u32[]{:S(2)}) async-start(bf16[32,32,640]{2,1,0:T(8,128)(2,1)} %bitcast.6), calls=%async_computation | async-start | bytes 2621440 | tf_op jit(solution)/shard_map/all_to_all | solution.py:555
  17.1 6.6 %collective-permute-start.2 = (bf16[144,512]{1,0:T(8,128)(2,1)S(1)}, bf16[144,512]{1,0:T(8,128)(2,1)}, u32[]{:S(2)}, u32[]{:S(2)}) collective-permute-start(bf16[144,512]{1,0:T(8,128)(2,1)S(1)} %get-tuple-element.68), channel_id=1, source_target_pairs={{0,8},{8,16},{16,24},{1,9},{9,17},{17,25},{2,10},{10,18},{18,26},{... | collective-permute-start | bytes 442376 | tf_op jit(solution)/shard_map/ppermute | solution.py:564
  19.9 3.9 %collective-permute-start.3 = (bf16[144,512]{1,0:T(8,128)(2,1)S(1)}, bf16[144,512]{1,0:T(8,128)(2,1)}, u32[]{:S(2)}, u32[]{:S(2)}) collective-permute-start(bf16[144,512]{1,0:T(8,128)(2,1)S(1)} %get-tuple-element.67), channel_id=1, source_target_pairs={{8,0},{16,8},{24,16},{9,1},{17,9},{25,17},{10,2},{18,10},{26,18},{... | collective-permute-start | bytes 442376 | tf_op jit(solution)/shard_map/ppermute | solution.py:565
  23.8 25.3 %copy-start.4 = (f32[9,512]{1,0:T(8,128)S(1)}, f32[9,512]{1,0:T(8,128)}, u32[]{:S(2)}) copy-start(f32[9,512]{1,0:T(8,128)} %wd_ref.3) | copy-start | bytes 55300
  69.7 2.4 %collective-permute-start.4 = (bf16[2,1664,128]{2,1,0:T(8,128)(2,1)S(1)}, bf16[2,1664,128]{2,1,0:T(8,128)(2,1)S(1)}, u32[]{:S(2)}, u32[]{:S(2)}) collective-permute-start(bf16[2,1664,128]{2,1,0:T(8,128)(2,1)S(1)} %get-tuple-element.38), channel_id=1, source_target_pairs={{0,8},{8,0},{1,9},{9,1},{2,10},{10,2},{3,11},{11,3},{4,12},{12,4},... | collective-permute-start | bytes 2555912 | tf_op jit(solution)/shard_map/ppermute | solution.py:460
  73.2 26.9 %all-to-all-start.1 = ((bf16[16,208,128]{2,1,0:T(8,128)(2,1)}), bf16[16,208,128]{2,1,0:T(8,128)(2,1)S(1)}, u32[]{:S(2)}, u32[]{:S(2)}) async-start(bf16[16,208,128]{2,1,0:T(8,128)(2,1)} %bitcast.13), calls=%async_computation.1 | async-start | bytes 1703936 | tf_op jit(solution)/shard_map/all_to_all | solution.py:532
  76.8 20.2 %collective-permute-start.5 = (f32[18,512]{1,0:T(8,128)S(1)}, f32[18,512]{1,0:T(8,128)S(1)}, u32[]{:S(2)}, u32[]{:S(2)}) collective-permute-start(f32[18,512]{1,0:T(8,128)S(1)} %get-tuple-element.43), channel_id=1, source_target_pairs={{0,1},{1,2},{2,3},{3,4},{4,5},{5,6},{6,7},{7,0},{8,9},{9,10},{10,1... | collective-permute-start | bytes 110600 | tf_op jit(solution)/shard_map/ppermute | solution.py:582
  78.6 18.4 %collective-permute-start.6 = (f32[18,512]{1,0:T(8,128)S(1)}, f32[18,512]{1,0:T(8,128)S(1)}, u32[]{:S(2)}, u32[]{:S(2)}) collective-permute-start(f32[18,512]{1,0:T(8,128)S(1)} %get-tuple-element.44), channel_id=1, source_target_pairs={{1,0},{2,1},{3,2},{4,3},{5,4},{6,5},{7,6},{0,7},{9,8},{10,9},{11,1... | collective-permute-start | bytes 110600 | tf_op jit(solution)/shard_map/ppermute | solution.py:583
  101.1 11.6 %copy-start.3 = (bf16[512,512]{1,0:T(8,128)(2,1)S(1)}, bf16[512,512]{1,0:T(8,128)(2,1)}, u32[]{:S(2)}) copy-start(bf16[512,512]{1,0:T(8,128)(2,1)} %wp_ref.3) | copy-start | bytes 1572868
  101.1 25.5 %all-to-all-start.2 = ((bf16[16,208,128]{2,1,0:T(8,128)(2,1)}), bf16[16,208,128]{2,1,0:T(8,128)(2,1)S(1)}, u32[]{:S(2)}, u32[]{:S(2)}) async-start(bf16[16,208,128]{2,1,0:T(8,128)(2,1)} %totals.1), calls=%async_computation.2 | async-start | bytes 1703936 | tf_op jit(solution)/shard_map/all_to_all | solution.py:532
  106.1 2.8 %collective-permute-start.7 = (bf16[128,512]{1,0:T(8,128)(2,1)S(1)}, bf16[128,512]{1,0:T(8,128)(2,1)S(1)}, u32[]{:S(2)}, u32[]{:S(2)}) collective-permute-start(bf16[128,512]{1,0:T(8,128)(2,1)S(1)} %get-tuple-element.54), channel_id=1, source_target_pairs={{0,8},{8,16},{16,24},{1,9},{9,17},{17,25},{2,10},{10,18},{18,26},{... | collective-permute-start | bytes 393224 | tf_op jit(solution)/shard_map/ppermute | solution.py:593
  107.6 5.1 %collective-permute-start.8 = (bf16[128,512]{1,0:T(8,128)(2,1)S(1)}, bf16[128,512]{1,0:T(8,128)(2,1)S(1)}, u32[]{:S(2)}, u32[]{:S(2)}) collective-permute-start(bf16[128,512]{1,0:T(8,128)(2,1)S(1)} %get-tuple-element.53), channel_id=1, source_target_pairs={{8,0},{16,8},{24,16},{9,1},{17,9},{25,17},{10,2},{18,10},{26,18},{... | collective-permute-start | bytes 393224 | tf_op jit(solution)/shard_map/ppermute | solution.py:594
  112.7 1.8 %copy-start.1 = (bf16[2688,512]{1,0:T(8,128)(2,1)S(1)}, bf16[2688,512]{1,0:T(8,128)(2,1)}, u32[]{:S(2)}) copy-start(bf16[2688,512]{1,0:T(8,128)(2,1)} %get-tuple-element.46.mix_ref) | copy-start | bytes 8257540
  114.5 1.6 %copy-start.5 = (bf16[2048,512]{1,0:T(8,128)(2,1)S(1)}, bf16[2048,512]{1,0:T(8,128)(2,1)}, u32[]{:S(2)}) copy-start(bf16[2048,512]{1,0:T(8,128)(2,1)} %get-tuple-element.45.grid_ref) | copy-start | bytes 6291460
  126.7 2.4 %collective-permute-start.9 = (bf16[16,208,128]{2,1,0:T(8,128)(2,1)S(1)}, bf16[16,208,128]{2,1,0:T(8,128)(2,1)S(1)}, u32[]{:S(2)}, u32[]{:S(2)}) collective-permute-start(bf16[16,208,128]{2,1,0:T(8,128)(2,1)S(1)} %all-to-all-done.2.own_ref), channel_id=1, source_target_pairs={{0,8},{8,0},{1,9},{9,1},{2,10},{10,2},{3,11},{11,3},{4,12},{12,4},... | collective-permute-start | bytes 2555912 | tf_op jit(solution)/shard_map/ppermute | solution.py:600

commit v10 on v8

--- a/solution.py
+++ b/solution.py
@@ -44,16 +44,16 @@
     return pl.BlockSpec(memory_space=pltpu.VMEM)
 
 
-def route_kernel(tiles, cap, clon, places_ref, rows_ref, out_ref):
+def route_kernel(tiles, cap, clon, owner_ref, cell_ref, rows_ref, out_ref):
     spec, n = rows_ref.shape
     head = out_ref.shape[1] - LANES
-    owner = places_ref[0:1, :]
+    owner = owner_ref[...]
     hits = owner == lax.broadcasted_iota(i32, (tiles, n), 0)
     above = lax.broadcasted_iota(i32, (n, n), 0) < lax.broadcasted_iota(i32, (n, n), 1)
     count = dot(hits.astype(f32).astype(bf16), above.astype(f32).astype(bf16))
     rank = jnp.sum(jnp.where(hits, count, 0.0), axis=0, keepdims=True)
     slot = owner * cap + rank.astype(i32)
-    cell = places_ref[1:2, :]
+    cell = cell_ref[...]
     line = lax.broadcasted_iota(i32, (LANES - (spec - head), n), 0)
     high = cell // clon
     spots = jnp.where(line == 0, high, jnp.where(line == 1, cell - high * clon, 0)).astype(f32)
@@ -73,16 +73,16 @@
     lax.fori_loop(0, tiles * cap // step, body, 0)
 
 
-def route(places, rows, tiles, cap, clon, spec_wide):
+def route(owner, cell, rows, tiles, cap, clon, spec_wide):
     return pl.pallas_call(
         functools.partial(route_kernel, tiles, cap, clon),
         out_shape=jax.ShapeDtypeStruct((tiles * cap, spec_wide), bf16),
-        in_specs=[vmem()] * 2,
+        in_specs=[vmem()] * 3,
         out_specs=vmem(),
-        compiler_params=params(12),
+        compiler_params=params(60),
         cost_estimate=cost(3),
         name="route",
-    )(places, rows)
+    )(owner, cell, rows)
 
 
 GROUPS = 8
@@ -232,7 +232,7 @@
     wit_ref, wot_ref, gg_ref, wo_ref, gm_ref, cott_ref,
     emb_ref, gi, gi_out, go, wide_ref, grid_ref, mix_ref, east_ref, west_ref, gp, gd, sems,
 ):
-    loads = start_loads((wit_hbm, wot_hbm, gg_hbm, wo_hbm), (wit_ref, wot_ref, gg_ref, wo_ref), sems)
+    loads = start_loads((wit_hbm, wot_hbm), (wit_ref, wot_ref), sems)
     put_grid = pltpu.make_async_copy(grid_ref, grid_hbm, sems.at[6])
     put_mix = pltpu.make_async_copy(mix_ref, mix_hbm, sems.at[7])
     core = core_ref[0]
@@ -249,6 +249,7 @@
         hits = one_hot(line * clon + place_of(column, clon // GROUPS), cells)
         if t == 0:
             loads[0].wait()
+            loads += start_loads((gg_hbm, wo_hbm), (gg_ref, wo_ref), sems.at[pl.ds(2, 2)])
         preact = dot(wit_ref[...], rows, (1, 1))
         sig = 1.0 / (1.0 + jnp.exp(-preact))
         hidden = (preact * sig).astype(bf16)
@@ -341,11 +342,11 @@
             mix_ref[out_at, cols] = jnp.concatenate(ends, axis=0).astype(bf16)
         return carry
 
-    lax.fori_loop(0, clat + 2, conv, 0)
+    lax.fori_loop(0, clat + 2, conv, 0, unroll=2)
     put_mix.start()
     late[1].wait()
-    gp[...] = dot(cott_ref[...], mix_ref[...]).T
-    gi_out[...] = gi[...].T
+    gp[...] = dot(cott_ref[...], mix_ref[...]).astype(bf16).T
+    gi_out[...] = gi[...].astype(bf16).T
     east_out[...] = east_ref[:, GROUPS - 1, :]
     west_out[...] = west_ref[:, 0, :]
     taps = [jnp.sum(gd[8 * k : 8 * k + 8, :], axis=0, keepdims=True) for k in range(9)]
@@ -375,14 +376,14 @@
         + [
             pltpu.VMEM((width, slots), bf16),
             pltpu.VMEM((width, spec_wide), f32),
-            pltpu.VMEM((spec_wide, width), f32),
+            pltpu.VMEM((spec_wide, width), bf16),
             pltpu.VMEM((width, width), f32),
             pltpu.VMEM((width // LANES, clat + 4, wide, LANES), f32),
             pltpu.VMEM(grid.shape, bf16),
             pltpu.VMEM(ext.shape, bf16),
             pltpu.VMEM((clat + 2, GROUPS, width), f32),
             pltpu.VMEM((clat + 2, GROUPS, width), f32),
-            pltpu.VMEM((width, width), f32),
+            pltpu.VMEM((width, width), bf16),
             pltpu.VMEM((72, width), f32),
             pltpu.SemaphoreType.DMA((8,)),
         ],
@@ -534,8 +535,9 @@
     from_west = lax.ppermute(cotangent[:, -1], "lon", east_way)
     from_east = lax.ppermute(cotangent[:, 0], "lon", west_way)
 
-    places = jnp.concatenate([owner.reshape(1, rows_here), cell.reshape(1, rows_here)], axis=0)
-    outgoing = route(places, spectra.T, tiles, cap, clon, spec_wide)
+    outgoing = route(
+        owner.reshape(1, rows_here), cell.reshape(1, rows_here), spectra.T, tiles, cap, clon, spec_wide
+    )
     outgoing, from_west, from_east, w_in, w_out = lax.optimization_barrier(
         (outgoing, from_west, from_east, w_in, w_out)
     )

time: 131 us -> 130 us (level)
    unnamed x20 -> x18, local copies, waits for them, and re-layouts: 4.48 us -> 3.41 us
  transfers between devices with their start and end apart: 13 -> 13, of which waited for: 8 -> 8; matrix products, arithmetic and copies ran while one was open for 4% -> 4% of each run, Pallas kernels for 19% -> 20%
where the time goes in v10:
time: 130 us
  Pallas kernels  50.1 us (39%)
  waiting for transfers between devices  40.4 us (31%)
  starting transfers between devices  29.2 us (22%)
  local copies, waits for them, and re-layouts  7.96 us (6%)
    pallas_call x1, Pallas kernels, owner_part(): pl.pallas_call(functools.partial(owner_kernel, spec, clat, clon, wide), o...  19.4 us
    pallas_call x1, Pallas kernels, grid_grad(): pl.pallas_call(functools.partial(grid_grad_kernel, clat, clon, wide), out...  15.7 us
    ppermute x1, waiting for transfers between devices, on_device(): left = lax.ppermute(east, 'lon', east_way)  15.4 us
    all_to_all x1, waiting for transfers between devices, on_device(): lax.all_to_all(outgoing.reshape(tiles, cap, spec_wide), ('x', 'core', 'lo...  9.54 us
    all_to_all x2, starting transfers between devices, spread(): lax.all_to_all(values, CHIPS, split_axis=0, concat_axis=0, tiled=True)  7.38 us
    all_to_all x2, waiting for transfers between devices, spread(): lax.all_to_all(values, CHIPS, split_axis=0, concat_axis=0, tiled=True)  7.06 us
    pallas_call x1, Pallas kernels, finish_latent(): pl.pallas_call(functools.partial(latent_kernel, clat, clon, wide), out_sh...  6.58 us
    pallas_call x1, Pallas kernels, route(): pl.pallas_call(functools.partial(route_kernel, tiles, cap, clon), out_sha...  4.11 us
  transfers between devices with their start and end apart: 13, of which 8 were waited for; matrix products, arithmetic and copies ran while one was open for 4% of the time, Pallas kernels for 20%

profile of v10, /device:TPU:0, one launch (start us, length us, event | category | flops | bytes accessed | tf_op | source)
XLA Modules:
  0.0 129.8 jit_solution(14233419076744275374)
XLA Ops:
  0.6 1.0 fusion
  1.7 3.0 %collective-permute-start = (bf16[16,512]{1,0:T(8,128)(2,1)S(1)}, bf16[16,512]{1,0:T(8,128)(2,1)S(1)}, u32[]{:S(2)}, u32[]{:S(2)}) collective-permute-start(bf16[16,512]{1,0:T(8,128)(2,1)S(1)} %bitcast.30), channel_id=1, source_target_pairs={{0,1},{1,2},{2,3},{3,4},{4,5},{5,6},{6,7},{7,0},{8,9},{9,10},{10,1... | collective-permute-start | bytes 49160 | tf_op jit(solution)/shard_map/ppermute | solution.py:535
  4.7 3.1 %collective-permute-start.1 = (bf16[16,512]{1,0:T(8,128)(2,1)S(1)}, bf16[16,512]{1,0:T(8,128)(2,1)S(1)}, u32[]{:S(2)}, u32[]{:S(2)}) collective-permute-start(bf16[16,512]{1,0:T(8,128)(2,1)S(1)} %bitcast.31), channel_id=1, source_target_pairs={{1,0},{2,1},{3,2},{4,3},{5,4},{6,5},{7,6},{0,7},{9,8},{10,9},{11,1... | collective-permute-start | bytes 49160 | tf_op jit(solution)/shard_map/ppermute | solution.py:536
  7.8 4.1 %route.1 = bf16[1024,640]{1,0:T(8,128)(2,1)} custom-call(s32[1,512]{1,0:T(1,128)} %bitcast.37, s32[1,512]{1,0:T(1,128)} %bitcast.38, bf16[616,512]{1,0:T(8,128)(2,1)} %bitcast.36), custom_call_target="tpu_custom_call" | custom-call | flops 3460499968 | tf_op jit(solution)/shard_map/route/pallas_call | solution.py:77
  11.9 0.0 copy-start
  11.9 0.0 collective-permute-done.west_ref
  11.9 0.0 copy-start.6
  11.9 0.0 collective-permute-done.1.east_ref
  11.9 0.0 copy-start.7
  12.0 0.0 copy-start.5
  12.0 3.7 %all-to-all-start = ((bf16[32,32,640]{2,1,0:T(8,128)(2,1)}), bf16[32,32,640]{2,1,0:T(8,128)(2,1)S(1)}, u32[]{:S(2)}, u32[]{:S(2)}) async-start(bf16[32,32,640]{2,1,0:T(8,128)(2,1)} %bitcast.28), calls=%async_computation | async-start | bytes 2621440 | tf_op jit(solution)/shard_map/all_to_all | solution.py:544
  15.7 0.1 pad.11.clone
  15.7 1.0 slice_bitcast_fusion
  16.7 0.1 pad_maximum_fusion.1
  16.9 2.8 %collective-permute-start.2 = (bf16[144,512]{1,0:T(8,128)(2,1)S(1)}, bf16[144,512]{1,0:T(8,128)(2,1)}, u32[]{:S(2)}, u32[]{:S(2)}) collective-permute-start(bf16[144,512]{1,0:T(8,128)(2,1)S(1)} %get-tuple-element.68), channel_id=1, source_target_pairs={{0,8},{8,16},{16,24},{1,9},{9,17},{17,25},{2,10},{10,18},{18,26},{... | collective-permute-start | bytes 442376 | tf_op jit(solution)/shard_map/ppermute | solution.py:553
  19.7 1.3 collective-permute-start.3
  21.0 0.0 copy-done
  21.0 0.2 copy.16
  21.2 0.0 copy-done.6
  21.2 0.0 copy-done.7
  21.2 0.0 copy-done.5
  21.2 1.1 copy.15
  22.3 1.1 pad.4.wit_hbm
  23.5 0.0 collective-permute-done.2.north_ref
  23.5 0.1 collective-permute-done.3.south_ref
  23.6 0.0 copy-start.3
  23.6 15.7 %grid_grad.1 = (bf16[512,2688]{1,0:T(8,128)(2,1)}, f32[4,18,144,128]{3,2,1,0:T(8,128)}, bf16[2048,512]{1,0:T(8,128)(2,1)}) custom-call(bf16[2048,512]{1,0:T(8,128)(2,1)} %bitcast.29, bf16[16,512]{1,0:T(8,128)(2,1)} %copy-done.7, bf16[16,512]{1,0:T(8,128)(2,1)} %copy-done.6, bf16[144,512]{1,0:T(8,128)(2,1)} %collective-permute-done.2.north_ref, ...), custom_call_target="tpu_custom_call" | custom-call | flops 11534999552 | tf_op jit(solution)/shard_map/grid_grad/pallas_call | solution.py:188
  39.3 9.5 %all-to-all-done = bf16[32,32,640]{2,1,0:T(8,128)(2,1)S(1)} async-done(((bf16[32,32,640]{2,1,0:T(8,128)(2,1)}), bf16[32,32,640]{2,1,0:T(8,128)(2,1)S(1)}, u32[]{:S(2)}, u32[]{:S(2)}) %all-to-all-start) | async-done | bytes 1310752 | tf_op jit(solution)/shard_map/all_to_all | solution.py:544
  48.8 0.0 copy-done.3
  48.9 19.4 %owner.1 = (bf16[2,1664,128]{2,1,0:T(8,128)(2,1)S(1)}, bf16[2,1664,128]{2,1,0:T(8,128)(2,1)S(1)}, f32[18,512]{1,0:T(8,128)S(1)}, f32[18,512]{1,0:T(8,128)S(1)}, ...) custom-call(s32[1]{0:T(128)} %bitcast.core_ref, bf16[1024,640]{1,0:T(8,128)(2,1)S(1)} %bitcast.25, ...), custom_call_target="tpu_custom_call" | custom-call | flops 24223500288 | tf_op jit(solution)/shard_map/owner/pallas_call | solution.py:370
  68.3 0.1 collective-permute-start.4
  68.4 2.4 %collective-permute-done.4.got_ref = bf16[2,1664,128]{2,1,0:T(8,128)(2,1)S(1)} collective-permute-done((bf16[2,1664,128]{2,1,0:T(8,128)(2,1)S(1)}, bf16[2,1664,128]{2,1,0:T(8,128)(2,1)S(1)}, u32[]{:S(2)}, u32[]{:S(2)}) %collective-permute-start.4) | collective-permute-done | bytes 852000 | tf_op jit(solution)/shard_map/ppermute | solution.py:448
  70.7 1.1 core_sum.1
  71.8 3.6 %all-to-all-start.1 = ((bf16[16,208,128]{2,1,0:T(8,128)(2,1)}), bf16[16,208,128]{2,1,0:T(8,128)(2,1)S(1)}, u32[]{:S(2)}, u32[]{:S(2)}) async-start(bf16[16,208,128]{2,1,0:T(8,128)(2,1)} %bitcast.13), calls=%async_computation.1 | async-start | bytes 1703936 | tf_op jit(solution)/shard_map/all_to_all | solution.py:520
  75.5 1.8 %collective-permute-start.5 = (f32[18,512]{1,0:T(8,128)S(1)}, f32[18,512]{1,0:T(8,128)S(1)}, u32[]{:S(2)}, u32[]{:S(2)}) collective-permute-start(f32[18,512]{1,0:T(8,128)S(1)} %get-tuple-element.43), channel_id=1, source_target_pairs={{0,1},{1,2},{2,3},{3,4},{4,5},{5,6},{6,7},{7,0},{8,9},{9,10},{10,1... | collective-permute-start | bytes 110600 | tf_op jit(solution)/shard_map/ppermute | solution.py:571
  77.3 3.0 %collective-permute-start.6 = (f32[18,512]{1,0:T(8,128)S(1)}, f32[18,512]{1,0:T(8,128)S(1)}, u32[]{:S(2)}, u32[]{:S(2)}) collective-permute-start(f32[18,512]{1,0:T(8,128)S(1)} %get-tuple-element.44), channel_id=1, source_target_pairs={{1,0},{2,1},{3,2},{4,3},{5,4},{6,5},{7,6},{0,7},{9,8},{10,9},{11,1... | collective-permute-start | bytes 110600 | tf_op jit(solution)/shard_map/ppermute | solution.py:572
  80.2 15.4 %collective-permute-done.5.refs_0_.left_ref = f32[18,512]{1,0:T(8,128)S(1)} collective-permute-done((f32[18,512]{1,0:T(8,128)S(1)}, f32[18,512]{1,0:T(8,128)S(1)}, u32[]{:S(2)}, u32[]{:S(2)}) %collective-permute-start.5) | collective-permute-done | bytes 36896 | tf_op jit(solution)/shard_map/ppermute | solution.py:571
  95.7 0.0 collective-permute-done.6.refs_1_.right_ref
  95.7 3.1 %all-to-all-done.1.parts_ref = bf16[16,208,128]{2,1,0:T(8,128)(2,1)S(1)} async-done(((bf16[16,208,128]{2,1,0:T(8,128)(2,1)}), bf16[16,208,128]{2,1,0:T(8,128)(2,1)S(1)}, u32[]{:S(2)}, u32[]{:S(2)}) %all-to-all-start.1) | async-done | bytes 852000 | tf_op jit(solution)/shard_map/all_to_all | solution.py:520
  98.7 1.0 totals.1
  99.8 0.0 copy-start.2
  99.8 3.8 %all-to-all-start.2 = ((bf16[16,208,128]{2,1,0:T(8,128)(2,1)}), bf16[16,208,128]{2,1,0:T(8,128)(2,1)S(1)}, u32[]{:S(2)}, u32[]{:S(2)}) async-start(bf16[16,208,128]{2,1,0:T(8,128)(2,1)} %totals.1), calls=%async_computation.2 | async-start | bytes 1703936 | tf_op jit(solution)/shard_map/all_to_all | solution.py:520
  103.6 1.1 add_convert_fusion
  104.7 1.5 %collective-permute-start.7 = (bf16[128,512]{1,0:T(8,128)(2,1)S(1)}, bf16[128,512]{1,0:T(8,128)(2,1)S(1)}, u32[]{:S(2)}, u32[]{:S(2)}) collective-permute-start(bf16[128,512]{1,0:T(8,128)(2,1)S(1)} %get-tuple-element.54), channel_id=1, source_target_pairs={{0,8},{8,16},{16,24},{1,9},{9,17},{17,25},{2,10},{10,18},{18,26},{... | collective-permute-start | bytes 393224 | tf_op jit(solution)/shard_map/ppermute | solution.py:582
  106.2 1.3 collective-permute-start.8
  107.5 0.0 collective-permute-done.7.top_ref
  107.5 3.8 %collective-permute-done.8.bottom_ref = bf16[128,512]{1,0:T(8,128)(2,1)S(1)} collective-permute-done((bf16[128,512]{1,0:T(8,128)(2,1)S(1)}, bf16[128,512]{1,0:T(8,128)(2,1)S(1)}, u32[]{:S(2)}, u32[]{:S(2)}) %collective-permute-start.8) | collective-permute-done | bytes 131104 | tf_op jit(solution)/shard_map/ppermute | solution.py:583
  111.3 0.0 copy-done.2
  111.3 0.0 copy-start.1
  111.3 1.8 %copy-done.1 = bf16[2688,512]{1,0:T(8,128)(2,1)S(1)} copy-done((bf16[2688,512]{1,0:T(8,128)(2,1)S(1)}, bf16[2688,512]{1,0:T(8,128)(2,1)}, u32[]{:S(2)}) %copy-start.1) | copy-done | bytes 2752536
  113.1 0.0 copy-start.4
  113.1 1.6 %copy-done.4 = bf16[2048,512]{1,0:T(8,128)(2,1)S(1)} copy-done((bf16[2048,512]{1,0:T(8,128)(2,1)S(1)}, bf16[2048,512]{1,0:T(8,128)(2,1)}, u32[]{:S(2)}) %copy-start.4) | copy-done | bytes 2097176
  114.7 6.6 %latent.1 = bf16[2048,512]{1,0:T(8,128)(2,1)} custom-call(bf16[2048,512]{1,0:T(8,128)(2,1)S(1)} %copy-done.4, bf16[2688,512]{1,0:T(8,128)(2,1)S(1)} %copy-done.1, bf16[128,512]{1,0:T(8,128)(2,1)S(1)} %collective-permute-done.7.top_ref, bf16[128,512]{1,0:T(8,128)(2,1)S(1)} %collective-permute-done.8.bottom_ref, ...), custom_call_target="tpu_custom_call" | custom-call | flops 5767499776 | tf_op jit(solution)/shard_map/latent/pallas_call | solution.py:421
  121.3 4.0 %all-to-all-done.2.own_ref = bf16[16,208,128]{2,1,0:T(8,128)(2,1)S(1)} async-done(((bf16[16,208,128]{2,1,0:T(8,128)(2,1)}), bf16[16,208,128]{2,1,0:T(8,128)(2,1)S(1)}, u32[]{:S(2)}, u32[]{:S(2)}) %all-to-all-start.2) | async-done | bytes 852000 | tf_op jit(solution)/shard_map/all_to_all | solution.py:520
  125.3 0.3 collective-permute-start.9
  125.6 2.1 %collective-permute-done.9.sibling_ref = bf16[16,208,128]{2,1,0:T(8,128)(2,1)S(1)} collective-permute-done((bf16[16,208,128]{2,1,0:T(8,128)(2,1)S(1)}, bf16[16,208,128]{2,1,0:T(8,128)(2,1)S(1)}, u32[]{:S(2)}, u32[]{:S(2)}) %collective-permute-start.9) | collective-permute-done | bytes 852000 | tf_op jit(solution)/shard_map/ppermute | solution.py:589
  127.7 2.1 %unpack.1 = (f32[616,512]{1,0:T(8,128)}, f32[512,512]{1,0:T(8,128)}, f32[512,512]{1,0:T(8,128)}, f32[9,512]{1,0:T(8,128)}) custom-call(s32[1]{0:T(128)} %bitcast.core_ref, bf16[16,208,128]{2,1,0:T(8,128)(2,1)S(1)} %all-to-all-done.2.own_ref, bf16[16,208,128]{2,1,0:T(8,128)(2,1)S(1)} %collective-permute-done.9.sibling_ref), custom_call_target="tpu_custom_call" | custom-call | flops 3460499968 | tf_op jit(solution)/shard_map/unpack/pallas_call | solution.py:492
  (7 shorter events, 0.0 us)
Async XLA Ops:
  1.7 10.3 %collective-permute-start = (bf16[16,512]{1,0:T(8,128)(2,1)S(1)}, bf16[16,512]{1,0:T(8,128)(2,1)S(1)}, u32[]{:S(2)}, u32[]{:S(2)}) collective-permute-start(bf16[16,512]{1,0:T(8,128)(2,1)S(1)} %bitcast.30), channel_id=1, source_target_pairs={{0,1},{1,2},{2,3},{3,4},{4,5},{5,6},{6,7},{7,0},{8,9},{9,10},{10,1... | collective-permute-start | bytes 49160 | tf_op jit(solution)/shard_map/ppermute | solution.py:535
  4.7 7.2 %collective-permute-start.1 = (bf16[16,512]{1,0:T(8,128)(2,1)S(1)}, bf16[16,512]{1,0:T(8,128)(2,1)S(1)}, u32[]{:S(2)}, u32[]{:S(2)}) collective-permute-start(bf16[16,512]{1,0:T(8,128)(2,1)S(1)} %bitcast.31), channel_id=1, source_target_pairs={{1,0},{2,1},{3,2},{4,3},{5,4},{6,5},{7,6},{0,7},{9,8},{10,9},{11,1... | collective-permute-start | bytes 49160 | tf_op jit(solution)/shard_map/ppermute | solution.py:536
  11.9 9.1 %copy-start = (bf16[512,512]{1,0:T(8,128)(2,1)S(1)}, bf16[512,512]{1,0:T(8,128)(2,1)}, u32[]{:S(2)}) copy-start(bf16[512,512]{1,0:T(8,128)(2,1)} %wo_hbm) | copy-start | bytes 1572868
  11.9 9.3 %copy-start.6 = (bf16[16,512]{1,0:T(8,128)(2,1)}, bf16[16,512]{1,0:T(8,128)(2,1)S(1)}, u32[]{:S(2)}) copy-start(bf16[16,512]{1,0:T(8,128)(2,1)S(1)} %collective-permute-done.west_ref) | copy-start | bytes 49156
  11.9 9.3 %copy-start.7 = (bf16[16,512]{1,0:T(8,128)(2,1)}, bf16[16,512]{1,0:T(8,128)(2,1)S(1)}, u32[]{:S(2)}) copy-start(bf16[16,512]{1,0:T(8,128)(2,1)S(1)} %collective-permute-done.1.east_ref) | copy-start | bytes 49156
  12.0 9.3 %copy-start.5 = (bf16[616,512]{1,0:T(8,128)(2,1)S(1)}, bf16[616,512]{1,0:T(8,128)(2,1)}, u32[]{:S(2)}) copy-start(bf16[616,512]{1,0:T(8,128)(2,1)} %param.11) | copy-start | bytes 1892356
  12.0 36.9 %all-to-all-start = ((bf16[32,32,640]{2,1,0:T(8,128)(2,1)}), bf16[32,32,640]{2,1,0:T(8,128)(2,1)S(1)}, u32[]{:S(2)}, u32[]{:S(2)}) async-start(bf16[32,32,640]{2,1,0:T(8,128)(2,1)} %bitcast.28), calls=%async_computation | async-start | bytes 2621440 | tf_op jit(solution)/shard_map/all_to_all | solution.py:544
  16.9 6.6 %collective-permute-start.2 = (bf16[144,512]{1,0:T(8,128)(2,1)S(1)}, bf16[144,512]{1,0:T(8,128)(2,1)}, u32[]{:S(2)}, u32[]{:S(2)}) collective-permute-start(bf16[144,512]{1,0:T(8,128)(2,1)S(1)} %get-tuple-element.68), channel_id=1, source_target_pairs={{0,8},{8,16},{16,24},{1,9},{9,17},{17,25},{2,10},{10,18},{18,26},{... | collective-permute-start | bytes 442376 | tf_op jit(solution)/shard_map/ppermute | solution.py:553
  19.7 3.9 %collective-permute-start.3 = (bf16[144,512]{1,0:T(8,128)(2,1)S(1)}, bf16[144,512]{1,0:T(8,128)(2,1)}, u32[]{:S(2)}, u32[]{:S(2)}) collective-permute-start(bf16[144,512]{1,0:T(8,128)(2,1)S(1)} %get-tuple-element.67), channel_id=1, source_target_pairs={{8,0},{16,8},{24,16},{9,1},{17,9},{25,17},{10,2},{18,10},{26,18},{... | collective-permute-start | bytes 442376 | tf_op jit(solution)/shard_map/ppermute | solution.py:554
  23.6 25.3 %copy-start.3 = (f32[9,512]{1,0:T(8,128)S(1)}, f32[9,512]{1,0:T(8,128)}, u32[]{:S(2)}) copy-start(f32[9,512]{1,0:T(8,128)} %wd_ref.3) | copy-start | bytes 55300
  68.3 2.4 %collective-permute-start.4 = (bf16[2,1664,128]{2,1,0:T(8,128)(2,1)S(1)}, bf16[2,1664,128]{2,1,0:T(8,128)(2,1)S(1)}, u32[]{:S(2)}, u32[]{:S(2)}) collective-permute-start(bf16[2,1664,128]{2,1,0:T(8,128)(2,1)S(1)} %get-tuple-element.38), channel_id=1, source_target_pairs={{0,8},{8,0},{1,9},{9,1},{2,10},{10,2},{3,11},{11,3},{4,12},{12,4},... | collective-permute-start | bytes 2555912 | tf_op jit(solution)/shard_map/ppermute | solution.py:448
  71.8 26.9 %all-to-all-start.1 = ((bf16[16,208,128]{2,1,0:T(8,128)(2,1)}), bf16[16,208,128]{2,1,0:T(8,128)(2,1)S(1)}, u32[]{:S(2)}, u32[]{:S(2)}) async-start(bf16[16,208,128]{2,1,0:T(8,128)(2,1)} %bitcast.13), calls=%async_computation.1 | async-start | bytes 1703936 | tf_op jit(solution)/shard_map/all_to_all | solution.py:520
  75.5 20.2 %collective-permute-start.5 = (f32[18,512]{1,0:T(8,128)S(1)}, f32[18,512]{1,0:T(8,128)S(1)}, u32[]{:S(2)}, u32[]{:S(2)}) collective-permute-start(f32[18,512]{1,0:T(8,128)S(1)} %get-tuple-element.43), channel_id=1, source_target_pairs={{0,1},{1,2},{2,3},{3,4},{4,5},{5,6},{6,7},{7,0},{8,9},{9,10},{10,1... | collective-permute-start | bytes 110600 | tf_op jit(solution)/shard_map/ppermute | solution.py:571
  77.3 18.4 %collective-permute-start.6 = (f32[18,512]{1,0:T(8,128)S(1)}, f32[18,512]{1,0:T(8,128)S(1)}, u32[]{:S(2)}, u32[]{:S(2)}) collective-permute-start(f32[18,512]{1,0:T(8,128)S(1)} %get-tuple-element.44), channel_id=1, source_target_pairs={{1,0},{2,1},{3,2},{4,3},{5,4},{6,5},{7,6},{0,7},{9,8},{10,9},{11,1... | collective-permute-start | bytes 110600 | tf_op jit(solution)/shard_map/ppermute | solution.py:572
  99.8 11.6 %copy-start.2 = (bf16[512,512]{1,0:T(8,128)(2,1)S(1)}, bf16[512,512]{1,0:T(8,128)(2,1)}, u32[]{:S(2)}) copy-start(bf16[512,512]{1,0:T(8,128)(2,1)} %wp_ref.3) | copy-start | bytes 1572868
  99.8 25.5 %all-to-all-start.2 = ((bf16[16,208,128]{2,1,0:T(8,128)(2,1)}), bf16[16,208,128]{2,1,0:T(8,128)(2,1)S(1)}, u32[]{:S(2)}, u32[]{:S(2)}) async-start(bf16[16,208,128]{2,1,0:T(8,128)(2,1)} %totals.1), calls=%async_computation.2 | async-start | bytes 1703936 | tf_op jit(solution)/shard_map/all_to_all | solution.py:520
  104.7 2.8 %collective-permute-start.7 = (bf16[128,512]{1,0:T(8,128)(2,1)S(1)}, bf16[128,512]{1,0:T(8,128)(2,1)S(1)}, u32[]{:S(2)}, u32[]{:S(2)}) collective-permute-start(bf16[128,512]{1,0:T(8,128)(2,1)S(1)} %get-tuple-element.54), channel_id=1, source_target_pairs={{0,8},{8,16},{16,24},{1,9},{9,17},{17,25},{2,10},{10,18},{18,26},{... | collective-permute-start | bytes 393224 | tf_op jit(solution)/shard_map/ppermute | solution.py:582
  106.2 5.1 %collective-permute-start.8 = (bf16[128,512]{1,0:T(8,128)(2,1)S(1)}, bf16[128,512]{1,0:T(8,128)(2,1)S(1)}, u32[]{:S(2)}, u32[]{:S(2)}) collective-permute-start(bf16[128,512]{1,0:T(8,128)(2,1)S(1)} %get-tuple-element.53), channel_id=1, source_target_pairs={{8,0},{16,8},{24,16},{9,1},{17,9},{25,17},{10,2},{18,10},{26,18},{... | collective-permute-start | bytes 393224 | tf_op jit(solution)/shard_map/ppermute | solution.py:583
  111.3 1.8 %copy-start.1 = (bf16[2688,512]{1,0:T(8,128)(2,1)S(1)}, bf16[2688,512]{1,0:T(8,128)(2,1)}, u32[]{:S(2)}) copy-start(bf16[2688,512]{1,0:T(8,128)(2,1)} %get-tuple-element.46.mix_ref) | copy-start | bytes 8257540
  113.1 1.6 %copy-start.4 = (bf16[2048,512]{1,0:T(8,128)(2,1)S(1)}, bf16[2048,512]{1,0:T(8,128)(2,1)}, u32[]{:S(2)}) copy-start(bf16[2048,512]{1,0:T(8,128)(2,1)} %get-tuple-element.45.grid_ref) | copy-start | bytes 6291460
  125.3 2.4 %collective-permute-start.9 = (bf16[16,208,128]{2,1,0:T(8,128)(2,1)S(1)}, bf16[16,208,128]{2,1,0:T(8,128)(2,1)S(1)}, u32[]{:S(2)}, u32[]{:S(2)}) collective-permute-start(bf16[16,208,128]{2,1,0:T(8,128)(2,1)S(1)} %all-to-all-done.2.own_ref), channel_id=1, source_target_pairs={{0,8},{8,0},{1,9},{9,1},{2,10},{10,2},{3,11},{11,3},{4,12},{12,4},... | collective-permute-start | bytes 2555912 | tf_op jit(solution)/shard_map/ppermute | solution.py:589

commit v11 on v10

--- a/solution.py
+++ b/solution.py
@@ -44,10 +44,13 @@
     return pl.BlockSpec(memory_space=pltpu.VMEM)
 
 
-def route_kernel(tiles, cap, clon, owner_ref, cell_ref, rows_ref, out_ref):
+def route_kernel(tiles, n_lon, cap, clon, owner_ref, cell_ref, rows_hbm, out_ref, rows_ref, sem):
+    load = pltpu.make_async_copy(rows_hbm, rows_ref, sem)
+    load.start()
     spec, n = rows_ref.shape
     head = out_ref.shape[1] - LANES
     owner = owner_ref[...]
+    owner = (owner % n_lon) * (tiles // n_lon) + owner // n_lon
     hits = owner == lax.broadcasted_iota(i32, (tiles, n), 0)
     above = lax.broadcasted_iota(i32, (n, n), 0) < lax.broadcasted_iota(i32, (n, n), 1)
     count = dot(hits.astype(f32).astype(bf16), above.astype(f32).astype(bf16))
@@ -57,6 +60,7 @@
     line = lax.broadcasted_iota(i32, (LANES - (spec - head), n), 0)
     high = cell // clon
     spots = jnp.where(line == 0, high, jnp.where(line == 1, cell - high * clon, 0)).astype(f32)
+    load.wait()
     last = jnp.concatenate([rows_ref[head:, :].astype(f32), spots], axis=0).astype(bf16)
     first = rows_ref[:head, :]
     step = min(256, tiles * cap)
@@ -73,12 +77,13 @@
     lax.fori_loop(0, tiles * cap // step, body, 0)
 
 
-def route(owner, cell, rows, tiles, cap, clon, spec_wide):
+def route(owner, cell, rows, tiles, n_lon, cap, clon, spec_wide):
     return pl.pallas_call(
-        functools.partial(route_kernel, tiles, cap, clon),
+        functools.partial(route_kernel, tiles, n_lon, cap, clon),
         out_shape=jax.ShapeDtypeStruct((tiles * cap, spec_wide), bf16),
-        in_specs=[vmem()] * 3,
+        in_specs=[vmem()] * 2 + [anywhere()],
         out_specs=vmem(),
+        scratch_shapes=[pltpu.VMEM(rows.shape, rows.dtype), pltpu.SemaphoreType.DMA],
         compiler_params=params(60),
         cost_estimate=cost(3),
         name="route",
@@ -511,7 +516,7 @@
 
 
 LAT = ("x", "core")
-CHIPS = ("x", "lon")
+CHIPS = ("lon", "x")
 
 
 def spread(values):
@@ -536,13 +541,14 @@
     from_east = lax.ppermute(cotangent[:, 0], "lon", west_way)
 
     outgoing = route(
-        owner.reshape(1, rows_here), cell.reshape(1, rows_here), spectra.T, tiles, cap, clon, spec_wide
+        owner.reshape(1, rows_here), cell.reshape(1, rows_here), spectra.T,
+        tiles, lax.axis_size("lon"), cap, clon, spec_wide,
     )
     outgoing, from_west, from_east, w_in, w_out = lax.optimization_barrier(
         (outgoing, from_west, from_east, w_in, w_out)
     )
     arrived = lax.all_to_all(
-        outgoing.reshape(tiles, cap, spec_wide), ("x", "core", "lon"), 0, 0, tiled=True
+        outgoing.reshape(tiles, cap, spec_wide), ("lon", "x", "core"), 0, 0, tiled=True
     ).reshape(tiles * cap, spec_wide)
 
     fill = jnp.zeros((wide - clon - 2, width), bf16)

time: 130 us -> 135 us (1.038)
  the two profiles are of different devices: /device:TPU:0 before, /device:TPU:21 now
where the time goes in v11:
time: 135 us; the launch traced here: 134 us
  Pallas kernels  50.5 us (37%)
  starting transfers between devices  37.6 us (28%)
  waiting for transfers between devices  35.6 us (26%)
  local copies, waits for them, and re-layouts  7.97 us (6%)
    pallas_call x1, Pallas kernels, owner_part(): pl.pallas_call(functools.partial(owner_kernel, spec, clat, clon, wide), o...  19.4 us
    pallas_call x1, Pallas kernels, grid_grad(): pl.pallas_call(functools.partial(grid_grad_kernel, clat, clon, wide), out...  15.7 us
    all_to_all x2, starting transfers between devices, spread(): lax.all_to_all(values, CHIPS, split_axis=0, concat_axis=0, tiled=True)  14.3 us
    ppermute x1, waiting for transfers between devices, on_device(): bottom = lax.ppermute(edge_row(0), LAT, north_way)  9.19 us
    ppermute x1, waiting for transfers between devices, on_device(): left = lax.ppermute(east, 'lon', east_way)  7.69 us
    ppermute x1, waiting for transfers between devices, on_device(): right = lax.ppermute(west, 'lon', west_way)  7.28 us
    all_to_all x1, starting transfers between devices, on_device(): lax.all_to_all(outgoing.reshape(tiles, cap, spec_wide), ('lon', 'x', 'cor...  6.77 us
    pallas_call x1, Pallas kernels, finish_latent(): pl.pallas_call(functools.partial(latent_kernel, clat, clon, wide), out_sh...  6.58 us
  transfers between devices with their start and end apart: 13, of which 9 were waited for; matrix products, arithmetic and copies ran while one was open for 4% of the time, Pallas kernels for 20%

profile of v11, /device:TPU:21, one launch (start us, length us, event | category | flops | bytes accessed | tf_op | source)
XLA Modules:
  0.0 133.8 jit_solution(18444258035733463855)
XLA Ops:
  0.6 1.0 fusion
  1.7 1.3 collective-permute-start
  3.0 0.2 collective-permute-start.1
  3.2 4.6 %route.1 = bf16[1024,640]{1,0:T(8,128)(2,1)} custom-call(s32[1,512]{1,0:T(1,128)} %bitcast.37, s32[1,512]{1,0:T(1,128)} %bitcast.38, bf16[616,512]{1,0:T(8,128)(2,1)} %bitcast.36), custom_call_target="tpu_custom_call" | custom-call | flops 3460499968 | tf_op jit(solution)/shard_map/route/pallas_call | solution.py:81
  7.8 0.0 copy-start
  7.8 0.0 collective-permute-done.west_ref
  7.8 0.0 copy-start.6
  7.8 0.0 collective-permute-done.1.east_ref
  7.8 0.0 copy-start.7
  7.8 0.0 copy-start.5
  7.8 6.8 %all-to-all-start = ((bf16[32,32,640]{2,1,0:T(8,128)(2,1)}), bf16[32,32,640]{2,1,0:T(8,128)(2,1)S(1)}, u32[]{:S(2)}, u32[]{:S(2)}) async-start(bf16[32,32,640]{2,1,0:T(8,128)(2,1)} %bitcast.28), calls=%async_computation | async-start | bytes 2621440 | tf_op jit(solution)/shard_map/all_to_all | solution.py:550
  14.6 0.1 pad.11.clone
  14.7 1.0 slice_bitcast_fusion
  15.7 0.1 pad_maximum_fusion.1
  15.8 3.4 %collective-permute-start.2 = (bf16[144,512]{1,0:T(8,128)(2,1)S(1)}, bf16[144,512]{1,0:T(8,128)(2,1)}, u32[]{:S(2)}, u32[]{:S(2)}) collective-permute-start(bf16[144,512]{1,0:T(8,128)(2,1)S(1)} %get-tuple-element.68), channel_id=1, source_target_pairs={{0,8},{8,16},{16,24},{1,9},{9,17},{17,25},{2,10},{10,18},{18,26},{... | collective-permute-start | bytes 442376 | tf_op jit(solution)/shard_map/ppermute | solution.py:559
  19.2 1.9 %collective-permute-start.3 = (bf16[144,512]{1,0:T(8,128)(2,1)S(1)}, bf16[144,512]{1,0:T(8,128)(2,1)}, u32[]{:S(2)}, u32[]{:S(2)}) collective-permute-start(bf16[144,512]{1,0:T(8,128)(2,1)S(1)} %get-tuple-element.67), channel_id=1, source_target_pairs={{8,0},{16,8},{24,16},{9,1},{17,9},{25,17},{10,2},{18,10},{26,18},{... | collective-permute-start | bytes 442376 | tf_op jit(solution)/shard_map/ppermute | solution.py:560
  21.1 0.0 copy-done
  21.1 0.2 copy.16
  21.4 0.0 copy-done.6
  21.4 0.0 copy-done.7
  21.4 0.0 copy-done.5
  21.4 1.1 copy.15
  22.5 1.1 pad.4.wit_hbm
  23.6 2.0 %collective-permute-done.2.north_ref = bf16[144,512]{1,0:T(8,128)(2,1)} collective-permute-done((bf16[144,512]{1,0:T(8,128)(2,1)S(1)}, bf16[144,512]{1,0:T(8,128)(2,1)}, u32[]{:S(2)}, u32[]{:S(2)}) %collective-permute-start.2) | collective-permute-done | bytes 147488 | tf_op jit(solution)/shard_map/ppermute | solution.py:559
  25.6 1.7 %collective-permute-done.3.south_ref = bf16[144,512]{1,0:T(8,128)(2,1)} collective-permute-done((bf16[144,512]{1,0:T(8,128)(2,1)S(1)}, bf16[144,512]{1,0:T(8,128)(2,1)}, u32[]{:S(2)}, u32[]{:S(2)}) %collective-permute-start.3) | collective-permute-done | bytes 147488 | tf_op jit(solution)/shard_map/ppermute | solution.py:560
  27.3 0.0 copy-start.3
  27.3 15.7 %grid_grad.1 = (bf16[512,2688]{1,0:T(8,128)(2,1)}, f32[4,18,144,128]{3,2,1,0:T(8,128)}, bf16[2048,512]{1,0:T(8,128)(2,1)}) custom-call(bf16[2048,512]{1,0:T(8,128)(2,1)} %bitcast.29, bf16[16,512]{1,0:T(8,128)(2,1)} %copy-done.7, bf16[16,512]{1,0:T(8,128)(2,1)} %copy-done.6, bf16[144,512]{1,0:T(8,128)(2,1)} %collective-permute-done.2.north_ref, ...), custom_call_target="tpu_custom_call" | custom-call | flops 11534999552 | tf_op jit(solution)/shard_map/grid_grad/pallas_call | solution.py:193
  43.0 0.0 all-to-all-done
  43.0 0.0 copy-done.3
  43.0 19.4 %owner.1 = (bf16[2,1664,128]{2,1,0:T(8,128)(2,1)S(1)}, bf16[2,1664,128]{2,1,0:T(8,128)(2,1)S(1)}, f32[18,512]{1,0:T(8,128)S(1)}, f32[18,512]{1,0:T(8,128)S(1)}, ...) custom-call(s32[1]{0:T(128)} %bitcast.core_ref, bf16[1024,640]{1,0:T(8,128)(2,1)S(1)} %bitcast.25, ...), custom_call_target="tpu_custom_call" | custom-call | flops 24223500288 | tf_op jit(solution)/shard_map/owner/pallas_call | solution.py:375
  62.5 0.9 collective-permute-start.4
  63.4 2.0 %collective-permute-done.4.got_ref = bf16[2,1664,128]{2,1,0:T(8,128)(2,1)S(1)} collective-permute-done((bf16[2,1664,128]{2,1,0:T(8,128)(2,1)S(1)}, bf16[2,1664,128]{2,1,0:T(8,128)(2,1)S(1)}, u32[]{:S(2)}, u32[]{:S(2)}) %collective-permute-start.4) | collective-permute-done | bytes 852000 | tf_op jit(solution)/shard_map/ppermute | solution.py:453
  65.4 1.1 core_sum.1
  66.5 7.4 %all-to-all-start.1 = ((bf16[16,208,128]{2,1,0:T(8,128)(2,1)}), bf16[16,208,128]{2,1,0:T(8,128)(2,1)S(1)}, u32[]{:S(2)}, u32[]{:S(2)}) async-start(bf16[16,208,128]{2,1,0:T(8,128)(2,1)} %bitcast.13), calls=%async_computation.1 | async-start | bytes 1703936 | tf_op jit(solution)/shard_map/all_to_all | solution.py:525
  73.9 1.2 collective-permute-start.5
  75.1 0.3 collective-permute-start.6
  75.4 7.7 %collective-permute-done.5.refs_0_.left_ref = f32[18,512]{1,0:T(8,128)S(1)} collective-permute-done((f32[18,512]{1,0:T(8,128)S(1)}, f32[18,512]{1,0:T(8,128)S(1)}, u32[]{:S(2)}, u32[]{:S(2)}) %collective-permute-start.5) | collective-permute-done | bytes 36896 | tf_op jit(solution)/shard_map/ppermute | solution.py:577
  83.1 7.3 %collective-permute-done.6.refs_1_.right_ref = f32[18,512]{1,0:T(8,128)S(1)} collective-permute-done((f32[18,512]{1,0:T(8,128)S(1)}, f32[18,512]{1,0:T(8,128)S(1)}, u32[]{:S(2)}, u32[]{:S(2)}) %collective-permute-start.6) | collective-permute-done | bytes 36896 | tf_op jit(solution)/shard_map/ppermute | solution.py:578
  90.3 2.7 %all-to-all-done.1.parts_ref = bf16[16,208,128]{2,1,0:T(8,128)(2,1)S(1)} async-done(((bf16[16,208,128]{2,1,0:T(8,128)(2,1)}), bf16[16,208,128]{2,1,0:T(8,128)(2,1)S(1)}, u32[]{:S(2)}, u32[]{:S(2)}) %all-to-all-start.1) | async-done | bytes 852000 | tf_op jit(solution)/shard_map/all_to_all | solution.py:525
  93.1 1.0 totals.1
  94.1 0.0 copy-start.2
  94.1 6.9 %all-to-all-start.2 = ((bf16[16,208,128]{2,1,0:T(8,128)(2,1)}), bf16[16,208,128]{2,1,0:T(8,128)(2,1)S(1)}, u32[]{:S(2)}, u32[]{:S(2)}) async-start(bf16[16,208,128]{2,1,0:T(8,128)(2,1)} %totals.1), calls=%async_computation.2 | async-start | bytes 1703936 | tf_op jit(solution)/shard_map/all_to_all | solution.py:525
  101.1 1.1 add_convert_fusion
  102.2 5.4 %collective-permute-start.7 = (bf16[128,512]{1,0:T(8,128)(2,1)S(1)}, bf16[128,512]{1,0:T(8,128)(2,1)S(1)}, u32[]{:S(2)}, u32[]{:S(2)}) collective-permute-start(bf16[128,512]{1,0:T(8,128)(2,1)S(1)} %get-tuple-element.54), channel_id=1, source_target_pairs={{0,8},{8,16},{16,24},{1,9},{9,17},{17,25},{2,10},{10,18},{18,26},{... | collective-permute-start | bytes 393224 | tf_op jit(solution)/shard_map/ppermute | solution.py:588
  107.6 1.9 %collective-permute-start.8 = (bf16[128,512]{1,0:T(8,128)(2,1)S(1)}, bf16[128,512]{1,0:T(8,128)(2,1)S(1)}, u32[]{:S(2)}, u32[]{:S(2)}) collective-permute-start(bf16[128,512]{1,0:T(8,128)(2,1)S(1)} %get-tuple-element.53), channel_id=1, source_target_pairs={{8,0},{16,8},{24,16},{9,1},{17,9},{25,17},{10,2},{18,10},{26,18},{... | collective-permute-start | bytes 393224 | tf_op jit(solution)/shard_map/ppermute | solution.py:589
  109.5 0.7 collective-permute-done.7.top_ref
  110.2 9.2 %collective-permute-done.8.bottom_ref = bf16[128,512]{1,0:T(8,128)(2,1)S(1)} collective-permute-done((bf16[128,512]{1,0:T(8,128)(2,1)S(1)}, bf16[128,512]{1,0:T(8,128)(2,1)S(1)}, u32[]{:S(2)}, u32[]{:S(2)}) %collective-permute-start.8) | collective-permute-done | bytes 131104 | tf_op jit(solution)/shard_map/ppermute | solution.py:589
  119.4 0.0 copy-done.2
  119.4 0.0 copy-start.1
  119.4 1.8 %copy-done.1 = bf16[2688,512]{1,0:T(8,128)(2,1)S(1)} copy-done((bf16[2688,512]{1,0:T(8,128)(2,1)S(1)}, bf16[2688,512]{1,0:T(8,128)(2,1)}, u32[]{:S(2)}) %copy-start.1) | copy-done | bytes 2752536
  121.2 0.0 copy-start.4
  121.2 1.6 %copy-done.4 = bf16[2048,512]{1,0:T(8,128)(2,1)S(1)} copy-done((bf16[2048,512]{1,0:T(8,128)(2,1)S(1)}, bf16[2048,512]{1,0:T(8,128)(2,1)}, u32[]{:S(2)}) %copy-start.4) | copy-done | bytes 2097176
  122.8 6.6 %latent.1 = bf16[2048,512]{1,0:T(8,128)(2,1)} custom-call(bf16[2048,512]{1,0:T(8,128)(2,1)S(1)} %copy-done.4, bf16[2688,512]{1,0:T(8,128)(2,1)S(1)} %copy-done.1, bf16[128,512]{1,0:T(8,128)(2,1)S(1)} %collective-permute-done.7.top_ref, bf16[128,512]{1,0:T(8,128)(2,1)S(1)} %collective-permute-done.8.bottom_ref, ...), custom_call_target="tpu_custom_call" | custom-call | flops 5767499776 | tf_op jit(solution)/shard_map/latent/pallas_call | solution.py:426
  129.3 0.0 all-to-all-done.2.own_ref
  129.3 0.0 collective-permute-start.9
  129.4 2.4 %collective-permute-done.9.sibling_ref = bf16[16,208,128]{2,1,0:T(8,128)(2,1)S(1)} collective-permute-done((bf16[16,208,128]{2,1,0:T(8,128)(2,1)S(1)}, bf16[16,208,128]{2,1,0:T(8,128)(2,1)S(1)}, u32[]{:S(2)}, u32[]{:S(2)}) %collective-permute-start.9) | collective-permute-done | bytes 852000 | tf_op jit(solution)/shard_map/ppermute | solution.py:595
  131.7 2.1 %unpack.1 = (f32[616,512]{1,0:T(8,128)}, f32[512,512]{1,0:T(8,128)}, f32[512,512]{1,0:T(8,128)}, f32[9,512]{1,0:T(8,128)}) custom-call(s32[1]{0:T(128)} %bitcast.core_ref, bf16[16,208,128]{2,1,0:T(8,128)(2,1)S(1)} %all-to-all-done.2.own_ref, bf16[16,208,128]{2,1,0:T(8,128)(2,1)S(1)} %collective-permute-done.9.sibling_ref), custom_call_target="tpu_custom_call" | custom-call | flops 3460499968 | tf_op jit(solution)/shard_map/unpack/pallas_call | solution.py:497
  (7 shorter events, 0.0 us)
Async XLA Ops:
  1.7 6.1 %collective-permute-start = (bf16[16,512]{1,0:T(8,128)(2,1)S(1)}, bf16[16,512]{1,0:T(8,128)(2,1)S(1)}, u32[]{:S(2)}, u32[]{:S(2)}) collective-permute-start(bf16[16,512]{1,0:T(8,128)(2,1)S(1)} %bitcast.30), channel_id=1, source_target_pairs={{0,1},{1,2},{2,3},{3,4},{4,5},{5,6},{6,7},{7,0},{8,9},{9,10},{10,1... | collective-permute-start | bytes 49160 | tf_op jit(solution)/shard_map/ppermute | solution.py:540
  3.0 4.8 %collective-permute-start.1 = (bf16[16,512]{1,0:T(8,128)(2,1)S(1)}, bf16[16,512]{1,0:T(8,128)(2,1)S(1)}, u32[]{:S(2)}, u32[]{:S(2)}) collective-permute-start(bf16[16,512]{1,0:T(8,128)(2,1)S(1)} %bitcast.31), channel_id=1, source_target_pairs={{1,0},{2,1},{3,2},{4,3},{5,4},{6,5},{7,6},{0,7},{9,8},{10,9},{11,1... | collective-permute-start | bytes 49160 | tf_op jit(solution)/shard_map/ppermute | solution.py:541
  7.8 13.4 %copy-start = (bf16[512,512]{1,0:T(8,128)(2,1)S(1)}, bf16[512,512]{1,0:T(8,128)(2,1)}, u32[]{:S(2)}) copy-start(bf16[512,512]{1,0:T(8,128)(2,1)} %wo_hbm) | copy-start | bytes 1572868
  7.8 13.6 %copy-start.6 = (bf16[16,512]{1,0:T(8,128)(2,1)}, bf16[16,512]{1,0:T(8,128)(2,1)S(1)}, u32[]{:S(2)}) copy-start(bf16[16,512]{1,0:T(8,128)(2,1)S(1)} %collective-permute-done.west_ref) | copy-start | bytes 49156
  7.8 13.6 %copy-start.7 = (bf16[16,512]{1,0:T(8,128)(2,1)}, bf16[16,512]{1,0:T(8,128)(2,1)S(1)}, u32[]{:S(2)}) copy-start(bf16[16,512]{1,0:T(8,128)(2,1)S(1)} %collective-permute-done.1.east_ref) | copy-start | bytes 49156
  7.8 13.6 %copy-start.5 = (bf16[616,512]{1,0:T(8,128)(2,1)S(1)}, bf16[616,512]{1,0:T(8,128)(2,1)}, u32[]{:S(2)}) copy-start(bf16[616,512]{1,0:T(8,128)(2,1)} %param.11) | copy-start | bytes 1892356
  7.8 35.2 %all-to-all-start = ((bf16[32,32,640]{2,1,0:T(8,128)(2,1)}), bf16[32,32,640]{2,1,0:T(8,128)(2,1)S(1)}, u32[]{:S(2)}, u32[]{:S(2)}) async-start(bf16[32,32,640]{2,1,0:T(8,128)(2,1)} %bitcast.28), calls=%async_computation | async-start | bytes 2621440 | tf_op jit(solution)/shard_map/all_to_all | solution.py:550
  15.8 9.7 %collective-permute-start.2 = (bf16[144,512]{1,0:T(8,128)(2,1)S(1)}, bf16[144,512]{1,0:T(8,128)(2,1)}, u32[]{:S(2)}, u32[]{:S(2)}) collective-permute-start(bf16[144,512]{1,0:T(8,128)(2,1)S(1)} %get-tuple-element.68), channel_id=1, source_target_pairs={{0,8},{8,16},{16,24},{1,9},{9,17},{17,25},{2,10},{10,18},{18,26},{... | collective-permute-start | bytes 442376 | tf_op jit(solution)/shard_map/ppermute | solution.py:559
  19.2 8.1 %collective-permute-start.3 = (bf16[144,512]{1,0:T(8,128)(2,1)S(1)}, bf16[144,512]{1,0:T(8,128)(2,1)}, u32[]{:S(2)}, u32[]{:S(2)}) collective-permute-start(bf16[144,512]{1,0:T(8,128)(2,1)S(1)} %get-tuple-element.67), channel_id=1, source_target_pairs={{8,0},{16,8},{24,16},{9,1},{17,9},{25,17},{10,2},{18,10},{26,18},{... | collective-permute-start | bytes 442376 | tf_op jit(solution)/shard_map/ppermute | solution.py:560
  27.3 15.8 %copy-start.3 = (f32[9,512]{1,0:T(8,128)S(1)}, f32[9,512]{1,0:T(8,128)}, u32[]{:S(2)}) copy-start(f32[9,512]{1,0:T(8,128)} %wd_ref.3) | copy-start | bytes 55300
  62.5 2.9 %collective-permute-start.4 = (bf16[2,1664,128]{2,1,0:T(8,128)(2,1)S(1)}, bf16[2,1664,128]{2,1,0:T(8,128)(2,1)S(1)}, u32[]{:S(2)}, u32[]{:S(2)}) collective-permute-start(bf16[2,1664,128]{2,1,0:T(8,128)(2,1)S(1)} %get-tuple-element.38), channel_id=1, source_target_pairs={{0,8},{8,0},{1,9},{9,1},{2,10},{10,2},{3,11},{11,3},{4,12},{12,4},... | collective-permute-start | bytes 2555912 | tf_op jit(solution)/shard_map/ppermute | solution.py:453
  66.5 26.5 %all-to-all-start.1 = ((bf16[16,208,128]{2,1,0:T(8,128)(2,1)}), bf16[16,208,128]{2,1,0:T(8,128)(2,1)S(1)}, u32[]{:S(2)}, u32[]{:S(2)}) async-start(bf16[16,208,128]{2,1,0:T(8,128)(2,1)} %bitcast.13), calls=%async_computation.1 | async-start | bytes 1703936 | tf_op jit(solution)/shard_map/all_to_all | solution.py:525
  73.9 9.2 %collective-permute-start.5 = (f32[18,512]{1,0:T(8,128)S(1)}, f32[18,512]{1,0:T(8,128)S(1)}, u32[]{:S(2)}, u32[]{:S(2)}) collective-permute-start(f32[18,512]{1,0:T(8,128)S(1)} %get-tuple-element.43), channel_id=1, source_target_pairs={{0,1},{1,2},{2,3},{3,4},{4,5},{5,6},{6,7},{7,0},{8,9},{9,10},{10,1... | collective-permute-start | bytes 110600 | tf_op jit(solution)/shard_map/ppermute | solution.py:577
  75.1 15.3 %collective-permute-start.6 = (f32[18,512]{1,0:T(8,128)S(1)}, f32[18,512]{1,0:T(8,128)S(1)}, u32[]{:S(2)}, u32[]{:S(2)}) collective-permute-start(f32[18,512]{1,0:T(8,128)S(1)} %get-tuple-element.44), channel_id=1, source_target_pairs={{1,0},{2,1},{3,2},{4,3},{5,4},{6,5},{7,6},{0,7},{9,8},{10,9},{11,1... | collective-permute-start | bytes 110600 | tf_op jit(solution)/shard_map/ppermute | solution.py:578
  94.1 25.3 %copy-start.2 = (bf16[512,512]{1,0:T(8,128)(2,1)S(1)}, bf16[512,512]{1,0:T(8,128)(2,1)}, u32[]{:S(2)}) copy-start(bf16[512,512]{1,0:T(8,128)(2,1)} %wp_ref.3) | copy-start | bytes 1572868
  94.1 35.3 %all-to-all-start.2 = ((bf16[16,208,128]{2,1,0:T(8,128)(2,1)}), bf16[16,208,128]{2,1,0:T(8,128)(2,1)S(1)}, u32[]{:S(2)}, u32[]{:S(2)}) async-start(bf16[16,208,128]{2,1,0:T(8,128)(2,1)} %totals.1), calls=%async_computation.2 | async-start | bytes 1703936 | tf_op jit(solution)/shard_map/all_to_all | solution.py:525
  102.2 8.0 %collective-permute-start.7 = (bf16[128,512]{1,0:T(8,128)(2,1)S(1)}, bf16[128,512]{1,0:T(8,128)(2,1)S(1)}, u32[]{:S(2)}, u32[]{:S(2)}) collective-permute-start(bf16[128,512]{1,0:T(8,128)(2,1)S(1)} %get-tuple-element.54), channel_id=1, source_target_pairs={{0,8},{8,16},{16,24},{1,9},{9,17},{17,25},{2,10},{10,18},{18,26},{... | collective-permute-start | bytes 393224 | tf_op jit(solution)/shard_map/ppermute | solution.py:588
  107.6 11.8 %collective-permute-start.8 = (bf16[128,512]{1,0:T(8,128)(2,1)S(1)}, bf16[128,512]{1,0:T(8,128)(2,1)S(1)}, u32[]{:S(2)}, u32[]{:S(2)}) collective-permute-start(bf16[128,512]{1,0:T(8,128)(2,1)S(1)} %get-tuple-element.53), channel_id=1, source_target_pairs={{8,0},{16,8},{24,16},{9,1},{17,9},{25,17},{10,2},{18,10},{26,18},{... | collective-permute-start | bytes 393224 | tf_op jit(solution)/shard_map/ppermute | solution.py:589
  119.4 1.8 %copy-start.1 = (bf16[2688,512]{1,0:T(8,128)(2,1)S(1)}, bf16[2688,512]{1,0:T(8,128)(2,1)}, u32[]{:S(2)}) copy-start(bf16[2688,512]{1,0:T(8,128)(2,1)} %get-tuple-element.46.mix_ref) | copy-start | bytes 8257540
  121.2 1.6 %copy-start.4 = (bf16[2048,512]{1,0:T(8,128)(2,1)S(1)}, bf16[2048,512]{1,0:T(8,128)(2,1)}, u32[]{:S(2)}) copy-start(bf16[2048,512]{1,0:T(8,128)(2,1)} %get-tuple-element.45.grid_ref) | copy-start | bytes 6291460
  129.3 2.4 %collective-permute-start.9 = (bf16[16,208,128]{2,1,0:T(8,128)(2,1)S(1)}, bf16[16,208,128]{2,1,0:T(8,128)(2,1)S(1)}, u32[]{:S(2)}, u32[]{:S(2)}) collective-permute-start(bf16[16,208,128]{2,1,0:T(8,128)(2,1)S(1)} %all-to-all-done.2.own_ref), channel_id=1, source_target_pairs={{0,8},{8,0},{1,9},{9,1},{2,10},{10,2},{3,11},{11,3},{4,12},{12,4},... | collective-permute-start | bytes 2555912 | tf_op jit(solution)/shard_map/ppermute | solution.py:595

commit v12 on v11

--- a/solution.py
+++ b/solution.py
@@ -44,9 +44,7 @@
     return pl.BlockSpec(memory_space=pltpu.VMEM)
 
 
-def route_kernel(tiles, n_lon, cap, clon, owner_ref, cell_ref, rows_hbm, out_ref, rows_ref, sem):
-    load = pltpu.make_async_copy(rows_hbm, rows_ref, sem)
-    load.start()
+def route_kernel(tiles, n_lon, cap, clon, owner_ref, cell_ref, rows_ref, out_ref):
     spec, n = rows_ref.shape
     head = out_ref.shape[1] - LANES
     owner = owner_ref[...]
@@ -60,7 +58,6 @@
     line = lax.broadcasted_iota(i32, (LANES - (spec - head), n), 0)
     high = cell // clon
     spots = jnp.where(line == 0, high, jnp.where(line == 1, cell - high * clon, 0)).astype(f32)
-    load.wait()
     last = jnp.concatenate([rows_ref[head:, :].astype(f32), spots], axis=0).astype(bf16)
     first = rows_ref[:head, :]
     step = min(256, tiles * cap)
@@ -81,9 +78,8 @@
     return pl.pallas_call(
         functools.partial(route_kernel, tiles, n_lon, cap, clon),
         out_shape=jax.ShapeDtypeStruct((tiles * cap, spec_wide), bf16),
-        in_specs=[vmem()] * 2 + [anywhere()],
+        in_specs=[vmem()] * 3,
         out_specs=vmem(),
-        scratch_shapes=[pltpu.VMEM(rows.shape, rows.dtype), pltpu.SemaphoreType.DMA],
         compiler_params=params(60),
         cost_estimate=cost(3),
         name="route",
@@ -516,7 +512,7 @@
 
 
 LAT = ("x", "core")
-CHIPS = ("lon", "x")
+CHIPS = ("x", "lon")
 
 
 def spread(values):

time: 135 us -> 130 us (0.963)
  the two profiles are of different devices: /device:TPU:21 before, /device:TPU:0 now
where the time goes in v12:
time: 130 us; the launch traced here: 129 us
  Pallas kernels  50.1 us (39%)
  waiting for transfers between devices  39.2 us (30%)
  starting transfers between devices  30 us (23%)
  local copies, waits for them, and re-layouts  7.96 us (6%)
    pallas_call x1, Pallas kernels, owner_part(): pl.pallas_call(functools.partial(owner_kernel, spec, clat, clon, wide), o...  19.4 us
    pallas_call x1, Pallas kernels, grid_grad(): pl.pallas_call(functools.partial(grid_grad_kernel, clat, clon, wide), out...  15.7 us
    ppermute x1, waiting for transfers between devices, on_device(): left = lax.ppermute(east, 'lon', east_way)  15.2 us
    all_to_all x1, waiting for transfers between devices, on_device(): lax.all_to_all(outgoing.reshape(tiles, cap, spec_wide), ('lon', 'x', 'cor...  8.46 us
    all_to_all x2, starting transfers between devices, spread(): lax.all_to_all(values, CHIPS, split_axis=0, concat_axis=0, tiled=True)  8.35 us
    all_to_all x2, waiting for transfers between devices, spread(): lax.all_to_all(values, CHIPS, split_axis=0, concat_axis=0, tiled=True)  7.06 us
    pallas_call x1, Pallas kernels, finish_latent(): pl.pallas_call(functools.partial(latent_kernel, clat, clon, wide), out_sh...  6.58 us
    pallas_call x1, Pallas kernels, route(): pl.pallas_call(functools.partial(route_kernel, tiles, n_lon, cap, clon),...  4.13 us
  transfers between devices with their start and end apart: 13, of which 8 were waited for; matrix products, arithmetic and copies ran while one was open for 4% of the time, Pallas kernels for 20%

profile of v12, /device:TPU:0, one launch (start us, length us, event | category | flops | bytes accessed | tf_op | source)
XLA Modules:
  0.0 129.5 jit_solution(13561623950293394577)
XLA Ops:
  0.6 1.0 fusion
  1.7 3.0 %collective-permute-start = (bf16[16,512]{1,0:T(8,128)(2,1)S(1)}, bf16[16,512]{1,0:T(8,128)(2,1)S(1)}, u32[]{:S(2)}, u32[]{:S(2)}) collective-permute-start(bf16[16,512]{1,0:T(8,128)(2,1)S(1)} %bitcast.30), channel_id=1, source_target_pairs={{0,1},{1,2},{2,3},{3,4},{4,5},{5,6},{6,7},{7,0},{8,9},{9,10},{10,1... | collective-permute-start | bytes 49160 | tf_op jit(solution)/shard_map/ppermute | solution.py:536
  4.7 3.1 %collective-permute-start.1 = (bf16[16,512]{1,0:T(8,128)(2,1)S(1)}, bf16[16,512]{1,0:T(8,128)(2,1)S(1)}, u32[]{:S(2)}, u32[]{:S(2)}) collective-permute-start(bf16[16,512]{1,0:T(8,128)(2,1)S(1)} %bitcast.31), channel_id=1, source_target_pairs={{1,0},{2,1},{3,2},{4,3},{5,4},{6,5},{7,6},{0,7},{9,8},{10,9},{11,1... | collective-permute-start | bytes 49160 | tf_op jit(solution)/shard_map/ppermute | solution.py:537
  7.8 4.1 %route.1 = bf16[1024,640]{1,0:T(8,128)(2,1)} custom-call(s32[1,512]{1,0:T(1,128)} %bitcast.37, s32[1,512]{1,0:T(1,128)} %bitcast.38, bf16[616,512]{1,0:T(8,128)(2,1)} %bitcast.36), custom_call_target="tpu_custom_call" | custom-call | flops 3460499968 | tf_op jit(solution)/shard_map/route/pallas_call | solution.py:78
  11.9 0.0 copy-start
  11.9 0.0 collective-permute-done.west_ref
  11.9 0.0 copy-start.6
  11.9 0.0 collective-permute-done.1.east_ref
  12.0 0.0 copy-start.7
  12.0 0.0 copy-start.5
  12.0 3.7 %all-to-all-start = ((bf16[32,32,640]{2,1,0:T(8,128)(2,1)}), bf16[32,32,640]{2,1,0:T(8,128)(2,1)S(1)}, u32[]{:S(2)}, u32[]{:S(2)}) async-start(bf16[32,32,640]{2,1,0:T(8,128)(2,1)} %bitcast.28), calls=%async_computation | async-start | bytes 2621440 | tf_op jit(solution)/shard_map/all_to_all | solution.py:546
  15.7 0.1 pad.11.clone
  15.7 1.0 slice_bitcast_fusion
  16.7 0.1 pad_maximum_fusion.1
  16.9 2.8 %collective-permute-start.2 = (bf16[144,512]{1,0:T(8,128)(2,1)S(1)}, bf16[144,512]{1,0:T(8,128)(2,1)}, u32[]{:S(2)}, u32[]{:S(2)}) collective-permute-start(bf16[144,512]{1,0:T(8,128)(2,1)S(1)} %get-tuple-element.68), channel_id=1, source_target_pairs={{0,8},{8,16},{16,24},{1,9},{9,17},{17,25},{2,10},{10,18},{18,26},{... | collective-permute-start | bytes 442376 | tf_op jit(solution)/shard_map/ppermute | solution.py:555
  19.7 1.3 collective-permute-start.3
  21.0 0.0 copy-done
  21.0 0.2 copy.16
  21.2 0.0 copy-done.6
  21.2 0.0 copy-done.7
  21.2 0.0 copy-done.5
  21.2 1.1 copy.15
  22.3 1.1 pad.4.wit_hbm
  23.5 0.0 collective-permute-done.2.north_ref
  23.5 0.1 collective-permute-done.3.south_ref
  23.6 0.0 copy-start.3
  23.6 15.7 %grid_grad.1 = (bf16[512,2688]{1,0:T(8,128)(2,1)}, f32[4,18,144,128]{3,2,1,0:T(8,128)}, bf16[2048,512]{1,0:T(8,128)(2,1)}) custom-call(bf16[2048,512]{1,0:T(8,128)(2,1)} %bitcast.29, bf16[16,512]{1,0:T(8,128)(2,1)} %copy-done.7, bf16[16,512]{1,0:T(8,128)(2,1)} %copy-done.6, bf16[144,512]{1,0:T(8,128)(2,1)} %collective-permute-done.2.north_ref, ...), custom_call_target="tpu_custom_call" | custom-call | flops 11534999552 | tf_op jit(solution)/shard_map/grid_grad/pallas_call | solution.py:189
  39.3 8.5 %all-to-all-done = bf16[32,32,640]{2,1,0:T(8,128)(2,1)S(1)} async-done(((bf16[32,32,640]{2,1,0:T(8,128)(2,1)}), bf16[32,32,640]{2,1,0:T(8,128)(2,1)S(1)}, u32[]{:S(2)}, u32[]{:S(2)}) %all-to-all-start) | async-done | bytes 1310752 | tf_op jit(solution)/shard_map/all_to_all | solution.py:546
  47.8 0.0 copy-done.3
  47.8 19.4 %owner.1 = (bf16[2,1664,128]{2,1,0:T(8,128)(2,1)S(1)}, bf16[2,1664,128]{2,1,0:T(8,128)(2,1)S(1)}, f32[18,512]{1,0:T(8,128)S(1)}, f32[18,512]{1,0:T(8,128)S(1)}, ...) custom-call(s32[1]{0:T(128)} %bitcast.core_ref, bf16[1024,640]{1,0:T(8,128)(2,1)S(1)} %bitcast.25, ...), custom_call_target="tpu_custom_call" | custom-call | flops 24223500288 | tf_op jit(solution)/shard_map/owner/pallas_call | solution.py:371
  67.2 0.1 collective-permute-start.4
  67.3 2.4 %collective-permute-done.4.got_ref = bf16[2,1664,128]{2,1,0:T(8,128)(2,1)S(1)} collective-permute-done((bf16[2,1664,128]{2,1,0:T(8,128)(2,1)S(1)}, bf16[2,1664,128]{2,1,0:T(8,128)(2,1)S(1)}, u32[]{:S(2)}, u32[]{:S(2)}) %collective-permute-start.4) | collective-permute-done | bytes 852000 | tf_op jit(solution)/shard_map/ppermute | solution.py:449
  69.7 1.1 core_sum.1
  70.8 4.6 %all-to-all-start.1 = ((bf16[16,208,128]{2,1,0:T(8,128)(2,1)}), bf16[16,208,128]{2,1,0:T(8,128)(2,1)S(1)}, u32[]{:S(2)}, u32[]{:S(2)}) async-start(bf16[16,208,128]{2,1,0:T(8,128)(2,1)} %bitcast.13), calls=%async_computation.1 | async-start | bytes 1703936 | tf_op jit(solution)/shard_map/all_to_all | solution.py:521
  75.4 1.9 %collective-permute-start.5 = (f32[18,512]{1,0:T(8,128)S(1)}, f32[18,512]{1,0:T(8,128)S(1)}, u32[]{:S(2)}, u32[]{:S(2)}) collective-permute-start(f32[18,512]{1,0:T(8,128)S(1)} %get-tuple-element.43), channel_id=1, source_target_pairs={{0,1},{1,2},{2,3},{3,4},{4,5},{5,6},{6,7},{7,0},{8,9},{9,10},{10,1... | collective-permute-start | bytes 110600 | tf_op jit(solution)/shard_map/ppermute | solution.py:573
  77.3 2.8 %collective-permute-start.6 = (f32[18,512]{1,0:T(8,128)S(1)}, f32[18,512]{1,0:T(8,128)S(1)}, u32[]{:S(2)}, u32[]{:S(2)}) collective-permute-start(f32[18,512]{1,0:T(8,128)S(1)} %get-tuple-element.44), channel_id=1, source_target_pairs={{1,0},{2,1},{3,2},{4,3},{5,4},{6,5},{7,6},{0,7},{9,8},{10,9},{11,1... | collective-permute-start | bytes 110600 | tf_op jit(solution)/shard_map/ppermute | solution.py:574
  80.1 15.2 %collective-permute-done.5.refs_0_.left_ref = f32[18,512]{1,0:T(8,128)S(1)} collective-permute-done((f32[18,512]{1,0:T(8,128)S(1)}, f32[18,512]{1,0:T(8,128)S(1)}, u32[]{:S(2)}, u32[]{:S(2)}) %collective-permute-start.5) | collective-permute-done | bytes 36896 | tf_op jit(solution)/shard_map/ppermute | solution.py:573
  95.4 0.0 collective-permute-done.6.refs_1_.right_ref
  95.4 3.2 %all-to-all-done.1.parts_ref = bf16[16,208,128]{2,1,0:T(8,128)(2,1)S(1)} async-done(((bf16[16,208,128]{2,1,0:T(8,128)(2,1)}), bf16[16,208,128]{2,1,0:T(8,128)(2,1)S(1)}, u32[]{:S(2)}, u32[]{:S(2)}) %all-to-all-start.1) | async-done | bytes 852000 | tf_op jit(solution)/shard_map/all_to_all | solution.py:521
  98.5 1.0 totals.1
  99.5 0.0 copy-start.2
  99.5 3.8 %all-to-all-start.2 = ((bf16[16,208,128]{2,1,0:T(8,128)(2,1)}), bf16[16,208,128]{2,1,0:T(8,128)(2,1)S(1)}, u32[]{:S(2)}, u32[]{:S(2)}) async-start(bf16[16,208,128]{2,1,0:T(8,128)(2,1)} %totals.1), calls=%async_computation.2 | async-start | bytes 1703936 | tf_op jit(solution)/shard_map/all_to_all | solution.py:521
  103.3 1.1 add_convert_fusion
  104.5 1.4 %collective-permute-start.7 = (bf16[128,512]{1,0:T(8,128)(2,1)S(1)}, bf16[128,512]{1,0:T(8,128)(2,1)S(1)}, u32[]{:S(2)}, u32[]{:S(2)}) collective-permute-start(bf16[128,512]{1,0:T(8,128)(2,1)S(1)} %get-tuple-element.54), channel_id=1, source_target_pairs={{0,8},{8,16},{16,24},{1,9},{9,17},{17,25},{2,10},{10,18},{18,26},{... | collective-permute-start | bytes 393224 | tf_op jit(solution)/shard_map/ppermute | solution.py:584
  105.9 1.3 collective-permute-start.8
  107.2 0.0 collective-permute-done.7.top_ref
  107.2 3.9 %collective-permute-done.8.bottom_ref = bf16[128,512]{1,0:T(8,128)(2,1)S(1)} collective-permute-done((bf16[128,512]{1,0:T(8,128)(2,1)S(1)}, bf16[128,512]{1,0:T(8,128)(2,1)S(1)}, u32[]{:S(2)}, u32[]{:S(2)}) %collective-permute-start.8) | collective-permute-done | bytes 131104 | tf_op jit(solution)/shard_map/ppermute | solution.py:585
  111.1 0.0 copy-done.2
  111.1 0.0 copy-start.1
  111.1 1.8 %copy-done.1 = bf16[2688,512]{1,0:T(8,128)(2,1)S(1)} copy-done((bf16[2688,512]{1,0:T(8,128)(2,1)S(1)}, bf16[2688,512]{1,0:T(8,128)(2,1)}, u32[]{:S(2)}) %copy-start.1) | copy-done | bytes 2752536
  112.9 0.0 copy-start.4
  112.9 1.6 %copy-done.4 = bf16[2048,512]{1,0:T(8,128)(2,1)S(1)} copy-done((bf16[2048,512]{1,0:T(8,128)(2,1)S(1)}, bf16[2048,512]{1,0:T(8,128)(2,1)}, u32[]{:S(2)}) %copy-start.4) | copy-done | bytes 2097176
  114.5 6.6 %latent.1 = bf16[2048,512]{1,0:T(8,128)(2,1)} custom-call(bf16[2048,512]{1,0:T(8,128)(2,1)S(1)} %copy-done.4, bf16[2688,512]{1,0:T(8,128)(2,1)S(1)} %copy-done.1, bf16[128,512]{1,0:T(8,128)(2,1)S(1)} %collective-permute-done.7.top_ref, bf16[128,512]{1,0:T(8,128)(2,1)S(1)} %collective-permute-done.8.bottom_ref, ...), custom_call_target="tpu_custom_call" | custom-call | flops 5767499776 | tf_op jit(solution)/shard_map/latent/pallas_call | solution.py:422
  121.1 3.9 %all-to-all-done.2.own_ref = bf16[16,208,128]{2,1,0:T(8,128)(2,1)S(1)} async-done(((bf16[16,208,128]{2,1,0:T(8,128)(2,1)}), bf16[16,208,128]{2,1,0:T(8,128)(2,1)S(1)}, u32[]{:S(2)}, u32[]{:S(2)}) %all-to-all-start.2) | async-done | bytes 852000 | tf_op jit(solution)/shard_map/all_to_all | solution.py:521
  125.0 0.3 collective-permute-start.9
  125.3 2.1 %collective-permute-done.9.sibling_ref = bf16[16,208,128]{2,1,0:T(8,128)(2,1)S(1)} collective-permute-done((bf16[16,208,128]{2,1,0:T(8,128)(2,1)S(1)}, bf16[16,208,128]{2,1,0:T(8,128)(2,1)S(1)}, u32[]{:S(2)}, u32[]{:S(2)}) %collective-permute-start.9) | collective-permute-done | bytes 852000 | tf_op jit(solution)/shard_map/ppermute | solution.py:591
  127.3 2.1 %unpack.1 = (f32[616,512]{1,0:T(8,128)}, f32[512,512]{1,0:T(8,128)}, f32[512,512]{1,0:T(8,128)}, f32[9,512]{1,0:T(8,128)}) custom-call(s32[1]{0:T(128)} %bitcast.core_ref, bf16[16,208,128]{2,1,0:T(8,128)(2,1)S(1)} %all-to-all-done.2.own_ref, bf16[16,208,128]{2,1,0:T(8,128)(2,1)S(1)} %collective-permute-done.9.sibling_ref), custom_call_target="tpu_custom_call" | custom-call | flops 3460499968 | tf_op jit(solution)/shard_map/unpack/pallas_call | solution.py:493
  (7 shorter events, 0.0 us)
Async XLA Ops:
  1.7 10.3 %collective-permute-start = (bf16[16,512]{1,0:T(8,128)(2,1)S(1)}, bf16[16,512]{1,0:T(8,128)(2,1)S(1)}, u32[]{:S(2)}, u32[]{:S(2)}) collective-permute-start(bf16[16,512]{1,0:T(8,128)(2,1)S(1)} %bitcast.30), channel_id=1, source_target_pairs={{0,1},{1,2},{2,3},{3,4},{4,5},{5,6},{6,7},{7,0},{8,9},{9,10},{10,1... | collective-permute-start | bytes 49160 | tf_op jit(solution)/shard_map/ppermute | solution.py:536
  4.7 7.3 %collective-permute-start.1 = (bf16[16,512]{1,0:T(8,128)(2,1)S(1)}, bf16[16,512]{1,0:T(8,128)(2,1)S(1)}, u32[]{:S(2)}, u32[]{:S(2)}) collective-permute-start(bf16[16,512]{1,0:T(8,128)(2,1)S(1)} %bitcast.31), channel_id=1, source_target_pairs={{1,0},{2,1},{3,2},{4,3},{5,4},{6,5},{7,6},{0,7},{9,8},{10,9},{11,1... | collective-permute-start | bytes 49160 | tf_op jit(solution)/shard_map/ppermute | solution.py:537
  11.9 9.0 %copy-start = (bf16[512,512]{1,0:T(8,128)(2,1)S(1)}, bf16[512,512]{1,0:T(8,128)(2,1)}, u32[]{:S(2)}) copy-start(bf16[512,512]{1,0:T(8,128)(2,1)} %wo_hbm) | copy-start | bytes 1572868
  11.9 9.3 %copy-start.6 = (bf16[16,512]{1,0:T(8,128)(2,1)}, bf16[16,512]{1,0:T(8,128)(2,1)S(1)}, u32[]{:S(2)}) copy-start(bf16[16,512]{1,0:T(8,128)(2,1)S(1)} %collective-permute-done.west_ref) | copy-start | bytes 49156
  12.0 9.2 %copy-start.7 = (bf16[16,512]{1,0:T(8,128)(2,1)}, bf16[16,512]{1,0:T(8,128)(2,1)S(1)}, u32[]{:S(2)}) copy-start(bf16[16,512]{1,0:T(8,128)(2,1)S(1)} %collective-permute-done.1.east_ref) | copy-start | bytes 49156
  12.0 9.2 %copy-start.5 = (bf16[616,512]{1,0:T(8,128)(2,1)S(1)}, bf16[616,512]{1,0:T(8,128)(2,1)}, u32[]{:S(2)}) copy-start(bf16[616,512]{1,0:T(8,128)(2,1)} %param.11) | copy-start | bytes 1892356
  12.0 35.8 %all-to-all-start = ((bf16[32,32,640]{2,1,0:T(8,128)(2,1)}), bf16[32,32,640]{2,1,0:T(8,128)(2,1)S(1)}, u32[]{:S(2)}, u32[]{:S(2)}) async-start(bf16[32,32,640]{2,1,0:T(8,128)(2,1)} %bitcast.28), calls=%async_computation | async-start | bytes 2621440 | tf_op jit(solution)/shard_map/all_to_all | solution.py:546
  16.9 6.6 %collective-permute-start.2 = (bf16[144,512]{1,0:T(8,128)(2,1)S(1)}, bf16[144,512]{1,0:T(8,128)(2,1)}, u32[]{:S(2)}, u32[]{:S(2)}) collective-permute-start(bf16[144,512]{1,0:T(8,128)(2,1)S(1)} %get-tuple-element.68), channel_id=1, source_target_pairs={{0,8},{8,16},{16,24},{1,9},{9,17},{17,25},{2,10},{10,18},{18,26},{... | collective-permute-start | bytes 442376 | tf_op jit(solution)/shard_map/ppermute | solution.py:555
  19.7 3.9 %collective-permute-start.3 = (bf16[144,512]{1,0:T(8,128)(2,1)S(1)}, bf16[144,512]{1,0:T(8,128)(2,1)}, u32[]{:S(2)}, u32[]{:S(2)}) collective-permute-start(bf16[144,512]{1,0:T(8,128)(2,1)S(1)} %get-tuple-element.67), channel_id=1, source_target_pairs={{8,0},{16,8},{24,16},{9,1},{17,9},{25,17},{10,2},{18,10},{26,18},{... | collective-permute-start | bytes 442376 | tf_op jit(solution)/shard_map/ppermute | solution.py:556
  23.6 24.2 %copy-start.3 = (f32[9,512]{1,0:T(8,128)S(1)}, f32[9,512]{1,0:T(8,128)}, u32[]{:S(2)}) copy-start(f32[9,512]{1,0:T(8,128)} %wd_ref.3) | copy-start | bytes 55300
  67.2 2.4 %collective-permute-start.4 = (bf16[2,1664,128]{2,1,0:T(8,128)(2,1)S(1)}, bf16[2,1664,128]{2,1,0:T(8,128)(2,1)S(1)}, u32[]{:S(2)}, u32[]{:S(2)}) collective-permute-start(bf16[2,1664,128]{2,1,0:T(8,128)(2,1)S(1)} %get-tuple-element.38), channel_id=1, source_target_pairs={{0,8},{8,0},{1,9},{9,1},{2,10},{10,2},{3,11},{11,3},{4,12},{12,4},... | collective-permute-start | bytes 2555912 | tf_op jit(solution)/shard_map/ppermute | solution.py:449
  70.8 27.8 %all-to-all-start.1 = ((bf16[16,208,128]{2,1,0:T(8,128)(2,1)}), bf16[16,208,128]{2,1,0:T(8,128)(2,1)S(1)}, u32[]{:S(2)}, u32[]{:S(2)}) async-start(bf16[16,208,128]{2,1,0:T(8,128)(2,1)} %bitcast.13), calls=%async_computation.1 | async-start | bytes 1703936 | tf_op jit(solution)/shard_map/all_to_all | solution.py:521
  75.4 20.0 %collective-permute-start.5 = (f32[18,512]{1,0:T(8,128)S(1)}, f32[18,512]{1,0:T(8,128)S(1)}, u32[]{:S(2)}, u32[]{:S(2)}) collective-permute-start(f32[18,512]{1,0:T(8,128)S(1)} %get-tuple-element.43), channel_id=1, source_target_pairs={{0,1},{1,2},{2,3},{3,4},{4,5},{5,6},{6,7},{7,0},{8,9},{9,10},{10,1... | collective-permute-start | bytes 110600 | tf_op jit(solution)/shard_map/ppermute | solution.py:573
  77.3 18.1 %collective-permute-start.6 = (f32[18,512]{1,0:T(8,128)S(1)}, f32[18,512]{1,0:T(8,128)S(1)}, u32[]{:S(2)}, u32[]{:S(2)}) collective-permute-start(f32[18,512]{1,0:T(8,128)S(1)} %get-tuple-element.44), channel_id=1, source_target_pairs={{1,0},{2,1},{3,2},{4,3},{5,4},{6,5},{7,6},{0,7},{9,8},{10,9},{11,1... | collective-permute-start | bytes 110600 | tf_op jit(solution)/shard_map/ppermute | solution.py:574
  99.5 11.6 %copy-start.2 = (bf16[512,512]{1,0:T(8,128)(2,1)S(1)}, bf16[512,512]{1,0:T(8,128)(2,1)}, u32[]{:S(2)}) copy-start(bf16[512,512]{1,0:T(8,128)(2,1)} %wp_ref.3) | copy-start | bytes 1572868
  99.5 25.4 %all-to-all-start.2 = ((bf16[16,208,128]{2,1,0:T(8,128)(2,1)}), bf16[16,208,128]{2,1,0:T(8,128)(2,1)S(1)}, u32[]{:S(2)}, u32[]{:S(2)}) async-start(bf16[16,208,128]{2,1,0:T(8,128)(2,1)} %totals.1), calls=%async_computation.2 | async-start | bytes 1703936 | tf_op jit(solution)/shard_map/all_to_all | solution.py:521
  104.5 2.7 %collective-permute-start.7 = (bf16[128,512]{1,0:T(8,128)(2,1)S(1)}, bf16[128,512]{1,0:T(8,128)(2,1)S(1)}, u32[]{:S(2)}, u32[]{:S(2)}) collective-permute-start(bf16[128,512]{1,0:T(8,128)(2,1)S(1)} %get-tuple-element.54), channel_id=1, source_target_pairs={{0,8},{8,16},{16,24},{1,9},{9,17},{17,25},{2,10},{10,18},{18,26},{... | collective-permute-start | bytes 393224 | tf_op jit(solution)/shard_map/ppermute | solution.py:584
  105.9 5.2 %collective-permute-start.8 = (bf16[128,512]{1,0:T(8,128)(2,1)S(1)}, bf16[128,512]{1,0:T(8,128)(2,1)S(1)}, u32[]{:S(2)}, u32[]{:S(2)}) collective-permute-start(bf16[128,512]{1,0:T(8,128)(2,1)S(1)} %get-tuple-element.53), channel_id=1, source_target_pairs={{8,0},{16,8},{24,16},{9,1},{17,9},{25,17},{10,2},{18,10},{26,18},{... | collective-permute-start | bytes 393224 | tf_op jit(solution)/shard_map/ppermute | solution.py:585
  111.1 1.8 %copy-start.1 = (bf16[2688,512]{1,0:T(8,128)(2,1)S(1)}, bf16[2688,512]{1,0:T(8,128)(2,1)}, u32[]{:S(2)}) copy-start(bf16[2688,512]{1,0:T(8,128)(2,1)} %get-tuple-element.46.mix_ref) | copy-start | bytes 8257540
  112.9 1.6 %copy-start.4 = (bf16[2048,512]{1,0:T(8,128)(2,1)S(1)}, bf16[2048,512]{1,0:T(8,128)(2,1)}, u32[]{:S(2)}) copy-start(bf16[2048,512]{1,0:T(8,128)(2,1)} %get-tuple-element.45.grid_ref) | copy-start | bytes 6291460
  125.0 2.4 %collective-permute-start.9 = (bf16[16,208,128]{2,1,0:T(8,128)(2,1)S(1)}, bf16[16,208,128]{2,1,0:T(8,128)(2,1)S(1)}, u32[]{:S(2)}, u32[]{:S(2)}) collective-permute-start(bf16[16,208,128]{2,1,0:T(8,128)(2,1)S(1)} %all-to-all-done.2.own_ref), channel_id=1, source_target_pairs={{0,8},{8,0},{1,9},{9,1},{2,10},{10,2},{3,11},{11,3},{4,12},{12,4},... | collective-permute-start | bytes 2555912 | tf_op jit(solution)/shard_map/ppermute | solution.py:591
